TPU v7x, 32 devices: a whole 2x2x4 slice. The times are simulated.
32 devices in a mesh: seq: 8 (over y, x, core), head: 4 (over z).
Axes of the slice: x: 2, y: 2, z: 4, core: 2. Of those that a mesh axis runs over, the one named last changes fastest.
Arguments:
- slab_query: bfloat16 [1024, 8192], P('seq', 'head'), may hold values from -6 to 6
- slab_key: bfloat16 [1024, 8192], P('seq', 'head'), may hold values from -6 to 6
- slab_value: bfloat16 [1024, 8192], P('seq', 'head'), may hold values from -6 to 6
- slab_levels: bfloat16 [6, 64, 1024], P(None, 'head', 'seq'), may hold values from 0.1 to 10
- norm_gain: bfloat16 [8192], P('head'), may hold values from 0.5 to 1.5
- user_query: bfloat16 [32, 64, 8192], P('seq', None, 'head'), may hold values from -6 to 6
- user_key: bfloat16 [32, 64, 8192], P('seq', None, 'head'), may hold values from -6 to 6
- user_value: bfloat16 [32, 64, 8192], P('seq', None, 'head'), may hold values from -6 to 6
- user_levels: bfloat16 [32, 6, 64, 64], P('seq', None, 'head'), may hold values from 0.1 to 10
- prefix_lengths: int32 [32], P('seq'), may hold values from 1 to 7, as said below
Outputs:
- slab_out: bfloat16 [1024, 8192], P('seq', 'head')
- user_out: bfloat16 [32, 64, 8192], P('seq', None, 'head')
Inputs may be any that keep to these rules, and one draw needn't show every extreme that they name: `prefix_lengths`: the 4 users that lie on one index of seq have distinct prefix lengths; one prefix length is held by one user of every index of seq.
All inputs are finite; a program needn't handle non-finite values.
Results may differ from a plain program's by a relative error of at most 0.012.
Values may be sent and summed in bfloat16 or wider, within the bound.
No kernel may reach another device: no remote copies, remote signals or barrier semaphores. Data moves between devices by JAX's collectives and lax.ppermute only.
A program may use at most 64 MiB of HBM per device.

v0:
```python
import jax
import jax.numpy as jnp
from jax import lax
from jax.sharding import PartitionSpec as P

HEADS = 64
HD = 128


def local_part(query_rows, key_rows, value_rows, first_weights):
    scores = jnp.einsum("bthd,bshd->bhts", query_rows, key_rows, preferred_element_type=jnp.float32)
    token_count = query_rows.shape[1]
    causal_mask = jnp.arange(token_count)[:, None] >= jnp.arange(token_count)[None, :]
    scores = jnp.where(causal_mask, scores, jnp.zeros_like(scores)).astype(jnp.bfloat16)
    result = jnp.einsum("bhts,bshd->bthd", scores, value_rows, preferred_element_type=jnp.float32)
    return result * jnp.transpose(first_weights, (0, 2, 1)).astype(jnp.float32)[..., None]


def read_prefix(query_rows, level_weights, node_states):
    level_count, head_count, inner, outer = node_states.shape
    merged = jnp.transpose(node_states, (1, 2, 0, 3)).reshape(
        head_count, inner, level_count * outer
    )
    projected = jnp.einsum("bthd,hdf->bthf", query_rows, merged, preferred_element_type=jnp.float32)
    projected = projected.reshape(projected.shape[:3] + (level_count, outer))
    scale_rows = jnp.transpose(level_weights, (0, 3, 2, 1)).astype(jnp.float32)[..., None]
    return jnp.sum(projected * scale_rows, axis=3)


def member_mask(target, positions, tree_depth):
    level_ids = jnp.arange(tree_depth, dtype=jnp.int32)[:, None]
    expanded = jnp.expand_dims(target, (-2, -1))
    column = positions[None, :]
    upper = jnp.bitwise_and(jnp.right_shift(expanded, level_ids), 1) == 1
    same_half = jnp.right_shift(column, level_ids + 1) == jnp.right_shift(expanded, level_ids + 1)
    lower_side = jnp.bitwise_and(jnp.right_shift(column, level_ids), 1) == 0
    return jnp.logical_and(upper, jnp.logical_and(same_half, lower_side)).astype(jnp.bfloat16)


def local(
    slab_query,
    slab_key,
    slab_value,
    slab_levels,
    norm_gain,
    user_query,
    user_key,
    user_value,
    user_levels,
    prefix_lengths,
):
    seq_count = lax.axis_size("seq")
    tree_depth = seq_count.bit_length() - 1
    position = lax.axis_index("seq")
    token_count, width = slab_query.shape
    head_count = width // HD
    user_count, suffix = (user_query.shape[0], user_query.shape[1])
    slab_queries = slab_query.reshape(1, token_count, head_count, HD)
    slab_keys = slab_key.reshape(1, token_count, head_count, HD)
    slab_values = slab_value.reshape(1, token_count, head_count, HD)
    user_queries = user_query.reshape(user_count, suffix, head_count, HD)
    user_keys = user_key.reshape(user_count, suffix, head_count, HD)
    user_values = user_value.reshape(user_count, suffix, head_count, HD)
    block_state = jnp.einsum(
        "thd,the->hde", slab_keys[0], slab_values[0], preferred_element_type=jnp.float32
    ).astype(jnp.bfloat16)
    slab_local = local_part(slab_queries, slab_keys, slab_values, slab_levels[0][None])
    user_local = local_part(user_queries, user_keys, user_values, user_levels[:, 0])
    slab_weights = slab_levels[1 : 1 + tree_depth][None]
    user_weights = user_levels[:, 1 : 1 + tree_depth]
    gathered = lax.all_gather(block_state[None], "seq", axis=0, tiled=True)
    positions = jnp.arange(gathered.shape[0], dtype=jnp.int32)
    own_mask = member_mask(position, positions, tree_depth)
    node_states = jnp.einsum(
        "kc,chde->khde", own_mask, gathered, preferred_element_type=jnp.float32
    ).astype(jnp.bfloat16)

    def user_read(packed):
        query_rows, weights, length = packed
        user_mask = member_mask(length, positions, tree_depth)
        nodes_here = jnp.einsum(
            "kc,chde->khde", user_mask, gathered, preferred_element_type=jnp.float32
        ).astype(jnp.bfloat16)
        return read_prefix(query_rows[None], weights[None], nodes_here)[0].astype(jnp.bfloat16)

    user_prefix = lax.map(user_read, (user_queries, user_weights, prefix_lengths))
    slab_total = slab_local + read_prefix(slab_queries, slab_weights, node_states)
    user_total = user_local + user_prefix.astype(jnp.float32)
    slab_square = jnp.sum(slab_total * slab_total, axis=(2, 3))
    user_square = jnp.sum(user_total * user_total, axis=(2, 3))
    slab_square, user_square = lax.psum((slab_square, user_square), "head")
    gain_rows = norm_gain.reshape(head_count, HD).astype(jnp.float32)
    slab_root = jnp.sqrt(slab_square / (HEADS * HD) + 1e-06)
    user_root = jnp.sqrt(user_square / (HEADS * HD) + 1e-06)
    slab_out = (
        (slab_total / slab_root[..., None, None] * gain_rows)
        .astype(jnp.bfloat16)
        .reshape(token_count, width)
    )
    user_out = (
        (user_total / user_root[..., None, None] * gain_rows)
        .astype(jnp.bfloat16)
        .reshape(user_count, suffix, width)
    )
    return (slab_out, user_out)


def solution(mesh):
    return jax.shard_map(
        local,
        mesh=mesh,
        in_specs=(
            P("seq", "head"),
            P("seq", "head"),
            P("seq", "head"),
            P(None, "head", "seq"),
            P("head"),
            P("seq", None, "head"),
            P("seq", None, "head"),
            P("seq", None, "head"),
            P("seq", None, "head", None),
            P("seq"),
        ),
        out_specs=(P("seq", "head"), P("seq", None, "head")),
        check_vma=False,
    )
```

profile of v0, /device:TPU:0, one launch (start us, length us, event | category | flops | bytes accessed | tf_op | source)
XLA Modules:
  0.0 164.9 jit_solution(867537397964718757)
XLA Ops:
  7.3 1.4 copy.88
  8.7 2.3 %convolution_convert_fusion = bf16[16,128,128]{2,1,0:T(8,128)(2,1)} fusion(bf16[128,16,128]{0,2,1:T(8,128)(2,1)S(1)} %bitcast.178, bf16[128,2048]{1,0:T(8,128)(2,1)} %param.14), kind=kOutput, calls=%fused_computation.40 | convolution fusion | flops 67371008 | bytes 1572864 | tf_op jit(solution)/shard_map/thd,the->hde/dot_general | solution.py:64
  14.1 1.3 copy_bitcast_fusion.1
  15.4 35.2 %all-gather.3.cloned.1.call-done = bf16[128,128,128]{2,1,0:T(8,128)(2,1)} async-done(((bf16[16,128,128]{2,1,0:T(8,128)(2,1)}), bf16[128,128,128]{2,1,0:T(8,128)(2,1)}) %all-gather.3.cloned.1.call-update) | async-done | bytes 4194320 | tf_op jit(solution)/shard_map/all_gather | solution.py:71
  50.6 7.8 %copy.68 = bf16[8,16,128,128]{3,0,2,1:T(8,128)(2,1)} copy(bf16[8,16,128,128]{3,2,1,0:T(8,128)(2,1)} %bitcast.174) | data formatting | bytes 8388608 | tf_op jit(solution)/shard_map/all_gather | solution.py:71
  58.4 2.8 %convert_bitcast_fusion.3 = bf16[16,128,3,128]{3,2,1,0:T(4,128)(2,1)S(1)} fusion(s32[3]{0:T(128)S(1)} %get-tuple-element.128, s32[3]{0:T(128)S(1)} %get-tuple-element.127, pred[3]{0:T(512)(128)(4,1)S(1)} %and_compare_fusion.2, bf16[8,16,128,128]{3,2,1,0:T(8,128)(2,1)S(1)} %bitcast.175), kind=kOutput, calls=%fused_computation.35 | convolution fusion | flops 13369512 | bytes 5767195 | tf_op jit(solution)/shard_map/kc,chde->khde/dot_general | solution.py:74
  61.3 2.4 %copy.69 = bf16[16,128,3,128]{1,3,2,0:T(8,128)(2,1)} copy(bf16[16,128,3,128]{3,2,1,0:T(4,128)(2,1)S(1)} %convert_bitcast_fusion.3) | data formatting | bytes 3145728 | tf_op jit(solution)/shard_map/convert_element_type | solution.py:76
  63.7 68.5 %while.12 = (s32[]{:T(128)}, bf16[4,64,16,128]{3,1,2,0:T(8,128)(2,1)}, s32[4]{0:T(128)S(1)}, bf16[8,16,128,128]{3,0,2,1:T(8,128)(2,1)}, bf16[4,64,16,128]{3,1,2,...) while((s32[]{:T(128)}, bf16[4,64,16,128]{3,1,2,0:T(8,128)(2,1)}, ...), condition=%wide.region_5.6_spmd.clone.clone, body=%wide.region_3.5_spmd.clone.clone.sunk | while | flops 114691256 | bytes 21027996 | solution.py:86
  64.3 0.6 iota_add_fusion.3
  65.0 0.7 and_compare_fusion.4
  65.6 3.5 %convert_bitcast_fusion.9 = bf16[16,128,3,128]{3,2,1,0:T(4,128)(2,1)S(1)} fusion(bf16[8,16,128,128]{3,0,2,1:T(8,128)(2,1)} %get-tuple-element.187, s32[3]{0:T(128)S(1)} %get-tuple-element.168, s32[3]{0:T(128)S(1)} %get-tuple-element.169, pred[3]{0:T(512)(128)(4,1)S(1)} %and_compare_fusion.4), kind=kOutput, calls=%fused_computation.2.clone.1 | convolution fusion | flops 13369512 | bytes 5767195 | tf_op jit(solution)/shard_map/while/body/eval_jaxpr/kc,chde->khde/dot_general | solution.py:81
  69.1 2.2 %copy.143 = bf16[16,128,3,128]{1,3,2,0:T(8,128)(2,1)} copy(bf16[16,128,3,128]{3,2,1,0:T(4,128)(2,1)S(1)} %convert_bitcast_fusion.9) | data formatting | bytes 3145728 | tf_op jit(solution)/shard_map/while/body/eval_jaxpr/convert_element_type | solution.py:83
  71.3 2.2 %convolution_bitcast_fusion.3 = f32[1,64,16,384]{3,1,2,0:T(8,128)S(1)} fusion(bf16[16,128,384]{1,2,0:T(8,128)(2,1)} %bitcast.172, bf16[4,64,16,128]{3,1,2,0:T(8,128)(2,1)} %get-tuple-element.188, s32[]{:T(128)} %get-tuple-element.177), kind=kOutput, calls=%fused_computation.3.clone.1 | convolution fusion | flops 100663296 | bytes 3408384 | tf_op jit(solution)/shard_map/while/body/eval_jaxpr/bthd,hdf->bthf/dot_general | solution.py:24
  73.6 2.1 %copy.144 = f32[1,64,16,384]{3,2,1,0:T(8,128)} copy(f32[1,64,16,384]{3,1,2,0:T(8,128)S(1)} %convolution_bitcast_fusion.3) | data formatting | bytes 3145728 | tf_op jit(solution)/shard_map/while/body/eval_jaxpr/bthd,hdf->bthf/transpose | solution.py:24
  75.7 2.5 %reshape.197 = f32[1,64,16,3,128]{4,3,2,1,0:T(4,128)S(1)} reshape(f32[1,64,16,384]{3,2,1,0:T(8,128)} %copy.144) | data formatting | bytes 3145728 | tf_op jit(solution)/shard_map/while/body/eval_jaxpr/reshape | solution.py:25
  78.5 1.5 multiply_reduce_fusion.5
  80.0 0.8 copy_dynamic-update-slice_fusion.2
  82.1 0.7 and_compare_fusion.4
  82.8 3.5 %convert_bitcast_fusion.9 = bf16[16,128,3,128]{3,2,1,0:T(4,128)(2,1)S(1)} fusion(bf16[8,16,128,128]{3,0,2,1:T(8,128)(2,1)} %get-tuple-element.187, s32[3]{0:T(128)S(1)} %get-tuple-element.168, s32[3]{0:T(128)S(1)} %get-tuple-element.169, pred[3]{0:T(512)(128)(4,1)S(1)} %and_compare_fusion.4), kind=kOutput, calls=%fused_computation.2.clone.1 | convolution fusion | flops 13369512 | bytes 5767195 | tf_op jit(solution)/shard_map/while/body/eval_jaxpr/kc,chde->khde/dot_general | solution.py:81
  86.3 2.2 %copy.143 = bf16[16,128,3,128]{1,3,2,0:T(8,128)(2,1)} copy(bf16[16,128,3,128]{3,2,1,0:T(4,128)(2,1)S(1)} %convert_bitcast_fusion.9) | data formatting | bytes 3145728 | tf_op jit(solution)/shard_map/while/body/eval_jaxpr/convert_element_type | solution.py:83
  88.5 2.2 %convolution_bitcast_fusion.3 = f32[1,64,16,384]{3,1,2,0:T(8,128)S(1)} fusion(bf16[16,128,384]{1,2,0:T(8,128)(2,1)} %bitcast.172, bf16[4,64,16,128]{3,1,2,0:T(8,128)(2,1)} %get-tuple-element.188, s32[]{:T(128)} %get-tuple-element.177), kind=kOutput, calls=%fused_computation.3.clone.1 | convolution fusion | flops 100663296 | bytes 3408384 | tf_op jit(solution)/shard_map/while/body/eval_jaxpr/bthd,hdf->bthf/dot_general | solution.py:24
  90.7 2.1 %copy.144 = f32[1,64,16,384]{3,2,1,0:T(8,128)} copy(f32[1,64,16,384]{3,1,2,0:T(8,128)S(1)} %convolution_bitcast_fusion.3) | data formatting | bytes 3145728 | tf_op jit(solution)/shard_map/while/body/eval_jaxpr/bthd,hdf->bthf/transpose | solution.py:24
  92.8 2.5 %reshape.197 = f32[1,64,16,3,128]{4,3,2,1,0:T(4,128)S(1)} reshape(f32[1,64,16,384]{3,2,1,0:T(8,128)} %copy.144) | data formatting | bytes 3145728 | tf_op jit(solution)/shard_map/while/body/eval_jaxpr/reshape | solution.py:25
  95.7 1.5 multiply_reduce_fusion.5
  97.2 0.8 copy_dynamic-update-slice_fusion.2
  99.2 0.7 and_compare_fusion.4
  99.9 3.5 %convert_bitcast_fusion.9 = bf16[16,128,3,128]{3,2,1,0:T(4,128)(2,1)S(1)} fusion(bf16[8,16,128,128]{3,0,2,1:T(8,128)(2,1)} %get-tuple-element.187, s32[3]{0:T(128)S(1)} %get-tuple-element.168, s32[3]{0:T(128)S(1)} %get-tuple-element.169, pred[3]{0:T(512)(128)(4,1)S(1)} %and_compare_fusion.4), kind=kOutput, calls=%fused_computation.2.clone.1 | convolution fusion | flops 13369512 | bytes 5767195 | tf_op jit(solution)/shard_map/while/body/eval_jaxpr/kc,chde->khde/dot_general | solution.py:81
  103.4 2.2 %copy.143 = bf16[16,128,3,128]{1,3,2,0:T(8,128)(2,1)} copy(bf16[16,128,3,128]{3,2,1,0:T(4,128)(2,1)S(1)} %convert_bitcast_fusion.9) | data formatting | bytes 3145728 | tf_op jit(solution)/shard_map/while/body/eval_jaxpr/convert_element_type | solution.py:83
  105.6 2.2 %convolution_bitcast_fusion.3 = f32[1,64,16,384]{3,1,2,0:T(8,128)S(1)} fusion(bf16[16,128,384]{1,2,0:T(8,128)(2,1)} %bitcast.172, bf16[4,64,16,128]{3,1,2,0:T(8,128)(2,1)} %get-tuple-element.188, s32[]{:T(128)} %get-tuple-element.177), kind=kOutput, calls=%fused_computation.3.clone.1 | convolution fusion | flops 100663296 | bytes 3408384 | tf_op jit(solution)/shard_map/while/body/eval_jaxpr/bthd,hdf->bthf/dot_general | solution.py:24
  107.8 2.1 %copy.144 = f32[1,64,16,384]{3,2,1,0:T(8,128)} copy(f32[1,64,16,384]{3,1,2,0:T(8,128)S(1)} %convolution_bitcast_fusion.3) | data formatting | bytes 3145728 | tf_op jit(solution)/shard_map/while/body/eval_jaxpr/bthd,hdf->bthf/transpose | solution.py:24
  109.9 2.5 %reshape.197 = f32[1,64,16,3,128]{4,3,2,1,0:T(4,128)S(1)} reshape(f32[1,64,16,384]{3,2,1,0:T(8,128)} %copy.144) | data formatting | bytes 3145728 | tf_op jit(solution)/shard_map/while/body/eval_jaxpr/reshape | solution.py:25
  112.8 1.5 multiply_reduce_fusion.5
  114.3 0.8 copy_dynamic-update-slice_fusion.2
  116.3 0.7 and_compare_fusion.4
  117.0 3.5 %convert_bitcast_fusion.9 = bf16[16,128,3,128]{3,2,1,0:T(4,128)(2,1)S(1)} fusion(bf16[8,16,128,128]{3,0,2,1:T(8,128)(2,1)} %get-tuple-element.187, s32[3]{0:T(128)S(1)} %get-tuple-element.168, s32[3]{0:T(128)S(1)} %get-tuple-element.169, pred[3]{0:T(512)(128)(4,1)S(1)} %and_compare_fusion.4), kind=kOutput, calls=%fused_computation.2.clone.1 | convolution fusion | flops 13369512 | bytes 5767195 | tf_op jit(solution)/shard_map/while/body/eval_jaxpr/kc,chde->khde/dot_general | solution.py:81
  120.5 2.2 %copy.143 = bf16[16,128,3,128]{1,3,2,0:T(8,128)(2,1)} copy(bf16[16,128,3,128]{3,2,1,0:T(4,128)(2,1)S(1)} %convert_bitcast_fusion.9) | data formatting | bytes 3145728 | tf_op jit(solution)/shard_map/while/body/eval_jaxpr/convert_element_type | solution.py:83
  122.7 2.2 %convolution_bitcast_fusion.3 = f32[1,64,16,384]{3,1,2,0:T(8,128)S(1)} fusion(bf16[16,128,384]{1,2,0:T(8,128)(2,1)} %bitcast.172, bf16[4,64,16,128]{3,1,2,0:T(8,128)(2,1)} %get-tuple-element.188, s32[]{:T(128)} %get-tuple-element.177), kind=kOutput, calls=%fused_computation.3.clone.1 | convolution fusion | flops 100663296 | bytes 3408384 | tf_op jit(solution)/shard_map/while/body/eval_jaxpr/bthd,hdf->bthf/dot_general | solution.py:24
  125.0 2.1 %copy.144 = f32[1,64,16,384]{3,2,1,0:T(8,128)} copy(f32[1,64,16,384]{3,1,2,0:T(8,128)S(1)} %convolution_bitcast_fusion.3) | data formatting | bytes 3145728 | tf_op jit(solution)/shard_map/while/body/eval_jaxpr/bthd,hdf->bthf/transpose | solution.py:24
  127.0 2.5 %reshape.197 = f32[1,64,16,3,128]{4,3,2,1,0:T(4,128)S(1)} reshape(f32[1,64,16,384]{3,2,1,0:T(8,128)} %copy.144) | data formatting | bytes 3145728 | tf_op jit(solution)/shard_map/while/body/eval_jaxpr/reshape | solution.py:25
  129.9 1.5 multiply_reduce_fusion.5
  131.4 0.8 copy_dynamic-update-slice_fusion.2
  132.2 2.1 %fusion.34 = f32[16,384,128]{2,1,0:T(8,128)S(1)} fusion(bf16[16,128,384]{1,2,0:T(8,128)(2,1)} %bitcast.177, bf16[128,2048]{1,0:T(8,128)(2,1)} %param.12), kind=kOutput, calls=%fused_computation.55 | convolution fusion | flops 201326592 | bytes 5242880 | tf_op jit(solution)/shard_map/bthd,hdf->bthf/dot_general | solution.py:24
  134.3 1.4 multiply_reduce_fusion.1
  135.8 2.0 %multiply_reduce_fusion.3 = (f32[128]{0:T(128)S(1)}, f32[1,128,16,128]{1,3,2,0:T(8,128)S(1)}) fusion(f32[128,16,128]{0,2,1:T(8,128)} %multiply_reduce_fusion.1, f32[128,16]{0,1:T(8,128)S(1)} %copy-done.8, bf16[128,16,128]{0,2,1:T(8,128)(2,1)S(1)} %bitcast.179, pred[128,128]{1,0:T(8,128)(4,1)S(1)} %copy-done.7, bf16[128,2048]{1,0:T(8,128)(2,1)S(1)} %copy-done.4, ...), kind=kOutput, calls=%fused_computation.50 | convolution fusion | flops 135790464 | bytes 3695104 | tf_op jit(solution)/shard_map/bhts,bshd->bthd/dot_general | solution.py:15
  137.8 4.3 %multiply_reduce_fusion.2 = (f32[4,64]{1,0:T(4,128)S(1)}, f32[4,64,16,128]{3,1,2,0:T(8,128)}) fusion(bf16[4,64,16,128]{3,1,2,0:T(8,128)(2,1)} %get-tuple-element.42, f32[4,64,16]{1,2,0:T(8,128)S(1)} %copy-done.9, pred[64,64]{1,0:T(8,128)(4,1)S(1)} %copy-done.11, bf16[4,64,2048]{2,1,0:T(8,128)(2,1)} %param.19, bf16[4,64,2048]{2,1,0:T(8,128)(2,1)} %param.18, ...), kind=kOutput, calls=%fused_computation.33 | convolution fusion | flops 137363200 | bytes 6312960 | tf_op jit(solution)/shard_map/bhts,bshd->bthd/dot_general | solution.py:15
  142.1 11.7 %all-reduce = (f32[1,128]{1,0:T(1,128)S(1)}, f32[4,64]{1,0:T(4,128)S(1)}) all-reduce(f32[1,128]{1,0:T(1,128)S(1)} %bitcast.181, f32[4,64]{1,0:T(4,128)S(1)} %get-tuple-element.125), channel_id=1, replica_groups=mesh['seq'=8,'head'=4] {'head'}, use_global_device_ids=true, to_apply=%region_2.3 | all-reduce | flops 384 | bytes 3072 | tf_op jit(solution)/shard_map/psum | solution.py:91
  154.2 1.0 copy.80
  155.2 2.9 %copy_bitcast_fusion = bf16[4,64,2048]{2,1,0:T(8,128)(2,1)} fusion(f32[16,128]{1,0:T(8,128)S(1)} %copy-done.6, f32[4,64,16,128]{3,1,2,0:T(8,128)} %get-tuple-element.126, f32[4,64]{1,0:T(4,128)S(1)} %add_sqrt_fusion), kind=kLoop, calls=%fused_computation.42 | loop fusion | flops 1572864 | bytes 3154944 | tf_op jit(solution)/shard_map/reshape | solution.py:103
  (64 shorter events, 9.2 us)
Async XLA Ops:
  7.2 7.0 %copy-start = (bf16[4,64,2048]{2,1,0:T(8,128)(2,1)S(1)}, bf16[4,64,2048]{2,1,0:T(8,128)(2,1)}, u32[]{:S(2)}) copy-start(bf16[4,64,2048]{2,1,0:T(8,128)(2,1)} %param.17) | copy-start | bytes 3145732
  7.2 3.9 %copy-start.10 = (bf16[6,16,128]{2,1,0:T(8,128)(2,1)S(1)}, bf16[6,16,128]{2,1,0:T(8,128)(2,1)}, u32[]{:S(2)}) copy-start(bf16[6,16,128]{2,1,0:T(8,128)(2,1)} %param.15) | copy-start | bytes 73732
  7.2 6.3 %copy-start.5 = (bf16[4,6,16,64]{3,2,1,0:T(8,128)(2,1)S(1)}, bf16[4,6,16,64]{3,2,1,0:T(8,128)(2,1)}, u32[]{:S(2)}) copy-start(bf16[4,6,16,64]{3,2,1,0:T(8,128)(2,1)} %param.20) | copy-start | bytes 147460
  7.2 5.7 %copy-start.12 = (bf16[2048]{0:T(1024)(128)(2,1)S(1)}, bf16[2048]{0:T(1024)(128)(2,1)}, u32[]{:S(2)}) copy-start(bf16[2048]{0:T(1024)(128)(2,1)} %param.16) | copy-start | bytes 12292
  7.2 43.4 %all-gather.3.cloned.1.call-start = ((), (), s32[]{:S(2)}) async-start(), calls=%async_computation | async-start | bytes 4718592 | tf_op jit(solution)/shard_map/all_gather | solution.py:71
  8.7 6.7 %copy-start.2 = (bf16[128,2048]{0,1:T(8,128)(2,1)}, bf16[128,2048]{0,1:T(8,128)(2,1)S(1)}, u32[]{:S(2)}) copy-start(bf16[128,2048]{0,1:T(8,128)(2,1)S(1)} %copy.88) | copy-start | bytes 1572868
  50.6 7.9 %copy-start.1 = (bf16[128,128,128]{2,1,0:T(8,128)(2,1)S(1)}, bf16[128,128,128]{2,1,0:T(8,128)(2,1)}, u32[]{:S(2)}) copy-start(bf16[128,128,128]{2,1,0:T(8,128)(2,1)} %all-gather.3.cloned.1.call-done) | copy-start | bytes 12582916
  61.2 2.5 %slice-start = ((bf16[4,6,16,64]{3,2,1,0:T(8,128)(2,1)}), bf16[4,3,16,64]{3,2,1,0:T(8,128)(2,1)S(1)}, s32[]{:S(2)}) async-start(bf16[4,6,16,64]{3,2,1,0:T(8,128)(2,1)} %param.20), calls=%async_computation.1 | async-start | bytes 98304 | tf_op jit(solution)/shard_map/slice | solution.py:70
  61.3 2.5 %copy-start.13 = (s32[4]{0:T(128)S(1)}, s32[4]{0:T(128)}, u32[]{:S(2)}) copy-start(s32[4]{0:T(128)} %param.21) | copy-start | bytes 52
  134.3 1.5 copy-start.3
  134.3 1.5 copy-start.4
  134.3 1.4 copy-start.7
  134.3 1.4 copy-start.8
  135.8 2.1 %copy-start.9 = (f32[4,64,16]{1,2,0:T(8,128)S(1)}, f32[4,64,16]{1,2,0:T(8,128)}, u32[]{:S(2)}) copy-start(f32[4,64,16]{1,2,0:T(8,128)} %convert_bitcast_fusion.4) | copy-start | bytes 49156
  135.8 2.1 %copy-start.11 = (pred[64,64]{1,0:T(8,128)(4,1)S(1)}, pred[64,64]{1,0:T(8,128)(4,1)}, u32[]{:S(2)}) copy-start(pred[64,64]{1,0:T(8,128)(4,1)} %iota_compare_fusion.1) | copy-start | bytes 12292
  137.8 16.0 %copy-start.6 = (f32[16,128]{1,0:T(8,128)S(1)}, f32[16,128]{1,0:T(8,128)}, u32[]{:S(2)}) copy-start(f32[16,128]{1,0:T(8,128)} %bitcast_convert_fusion) | copy-start | bytes 24580
Sparse Core Ops, SparseCore 0:
  11.1 39.4 all-gather.2
where the time goes:
time: 166 us; the launch traced here: 165 us
  local copies, waits for them, and re-layouts  47.9 us (29%)
  matrix products  36.4 us (22%)
  waiting for transfers between devices  35.2 us (21%)
  other arithmetic  19.1 us (12%)
  between operations  14.2 us (9%)
  blocking collectives  11.7 us (7%)
    all_gather x1, waiting for transfers between devices, local(): gathered = lax.all_gather(block_state[None], 'seq', axis=0, tiled=True)  35.2 us
    dot_general x4, matrix products, user_read(): jnp.einsum('kc,chde->khde', user_mask, gathered, preferred_element_type=j...  14 us
    psum x1, blocking collectives, local(): slab_square, user_square = lax.psum((slab_square, user_square), 'head')  11.7 us
    dot_general x5, matrix products, read_prefix(): jnp.einsum('bthd,hdf->bthf', query_rows, merged, preferred_element_type=j...  11 us
    reshape x4, local copies, waits for them, and re-layouts, read_prefix(): projected = projected.reshape(projected.shape[:3] + (level_count, outer))  9.97 us
    convert_element_type x4, local copies, waits for them, and re-layouts, user_read(): nodes_here = jnp.einsum('kc,chde->khde', user_mask, gathered, preferred_e...  8.87 us
    transpose x4, local copies, waits for them, and re-layouts, read_prefix(): jnp.einsum('bthd,hdf->bthf', query_rows, merged, preferred_element_type=j...  8.34 us
    all_gather x1, local copies, waits for them, and re-layouts, local(): gathered = lax.all_gather(block_state[None], 'seq', axis=0, tiled=True)  7.85 us
  transfers between devices with their start and end apart: 1, of which 1 were waited for; matrix products, arithmetic and copies ran while one was open for 3% of the time, Pallas kernels for 0%

commit v1 on v0

v1 whole, which is shorter than its diff:
```python
import functools

import jax
import jax.numpy as jnp
from jax import lax
from jax.experimental import pallas as pl
from jax.experimental.pallas import tpu as pltpu
from jax.sharding import PartitionSpec as P

HEADS = 64
HD = 128
ROWS = 128
VMEM_BYTES = 48 * 1024 * 1024


def matmul(a, b, contract):
    return lax.dot_general(a, b, (contract, ((), ())), preferred_element_type=jnp.float32)


def state_kernel(key_ref, value_ref, first_ref, second_ref):
    half = first_ref.shape[0]
    for head in range(2 * half):
        cols = slice(head * HD, (head + 1) * HD)
        state = matmul(key_ref[:, cols], value_ref[:, cols], ((0,), (0,)))
        target = first_ref if head < half else second_ref
        target[head % half] = state.astype(jnp.bfloat16)


def local_kernel(suffix, sq_ref, sk_ref, sv_ref, uq_ref, uk_ref, uv_ref, sw_ref, uw_ref, so_ref, uo_ref):
    head_count = sq_ref.shape[1] // HD
    row = lax.broadcasted_iota(jnp.int32, (ROWS, ROWS), 0)
    col = lax.broadcasted_iota(jnp.int32, (ROWS, ROWS), 1)
    causal = row >= col
    within = jnp.logical_and(causal, row // suffix == col // suffix)
    parts = [(sq_ref, sk_ref, sv_ref, sw_ref, so_ref, causal), (uq_ref, uk_ref, uv_ref, uw_ref, uo_ref, within)]
    for head in range(head_count):
        cols = slice(head * HD, (head + 1) * HD)
        for q_ref, k_ref, v_ref, w_ref, o_ref, mask in parts:
            for start in range(0, q_ref.shape[0], ROWS):
                rows = slice(start, start + ROWS)
                scores = matmul(q_ref[rows, cols], k_ref[rows, cols], ((1,), (1,)))
                scores = jnp.where(mask, scores, 0.0).astype(jnp.bfloat16)
                result = matmul(scores, v_ref[rows, cols], ((1,), (0,)))
                o_ref[rows, cols] = result * w_ref[rows, head : head + 1]


def prefix_kernel(depth, suffix, order_ref, length_ref, sq_ref, uq_ref, sw_ref, uw_ref, sl_ref, ul_ref, *rest):
    block_count = 1 << depth
    pieces = rest[: 2 * block_count]
    st_ref, ut_ref, square_ref, nodes, s_square, u_square, sems = rest[2 * block_count :]
    position = order_ref[0]
    head_count = nodes.shape[1]
    half = head_count // 2
    copies = []
    for offset in range(block_count):
        for side in range(2):
            copies.append(
                pltpu.make_async_copy(
                    pieces[2 * offset + side],
                    nodes.at[position ^ offset, pl.ds(side * half, half)],
                    sems.at[2 * offset + side],
                )
            )
    for copy in copies:
        copy.start()
    for copy in copies:
        copy.wait()
    for level in range(depth, 1, -1):
        for group in range(block_count >> level):
            base = group << level
            size = 1 << (level - 1)
            total = nodes[base].astype(jnp.float32)
            for extra in range(1, size):
                total = total + nodes[base + extra].astype(jnp.float32)
            nodes[base + size - 1] = total.astype(jnp.bfloat16)

    def slots(target):
        return [
            lax.shift_left(lax.shift_right_logical(target, level), level) + ((1 << (level - 1)) - 1)
            for level in range(1, depth + 1)
        ]

    slab_slots = slots(position)
    user_slots = [slots(length_ref[user]) for user in range(uq_ref.shape[0] // suffix)]
    for head in range(head_count):
        cols = slice(head * HD, (head + 1) * HD)

        def read(q_ref, w_ref, rows, node_slots):
            total = None
            for level, slot in enumerate(node_slots):
                column = (level + 1) * head_count + head
                part = matmul(q_ref[rows, cols], nodes[slot, head], ((1,), (0,)))
                part = part * w_ref[rows, column : column + 1]
                total = part if total is None else total + part
            return total

        def accumulate(acc_ref, rows, total):
            if head == 0:
                acc_ref[rows] = total * total
            else:
                acc_ref[rows] += total * total

        rows = slice(0, sq_ref.shape[0])
        total = sl_ref[:, cols] + read(sq_ref, sw_ref, rows, slab_slots)
        st_ref[:, cols] = total
        accumulate(s_square, rows, total)
        for user, node_slots in enumerate(user_slots):
            rows = slice(user * suffix, (user + 1) * suffix)
            prefix = read(uq_ref, uw_ref, rows, node_slots).astype(jnp.bfloat16)
            total = ul_ref[rows, cols] + prefix.astype(jnp.float32)
            ut_ref[rows, cols] = total
            accumulate(u_square, rows, total)
    line = 0
    for acc_ref in (s_square, u_square):
        for start in range(0, acc_ref.shape[0], ROWS):
            turned = jnp.transpose(acc_ref[start : start + ROWS])
            square_ref[line : line + 1] = jnp.sum(turned, axis=0, keepdims=True)
            line += 1


def norm_kernel(features, st_ref, ut_ref, gain_ref, *rest):
    squares = rest[:-3]
    so_ref, uo_ref, scale_ref = rest[-3:]

    @pl.when(pl.program_id(0) == 0)
    def _():
        total = squares[0][...]
        for part in squares[1:]:
            total = total + part[...]
        scale = lax.rsqrt(total / features + 1e-06)
        for line in range(scale.shape[0]):
            spread = jnp.broadcast_to(scale[line : line + 1], (ROWS, ROWS))
            scale_ref[line] = jnp.transpose(spread)

    gain = gain_ref[...].astype(jnp.float32)
    line = 0
    for t_ref, o_ref in ((st_ref, so_ref), (ut_ref, uo_ref)):
        for start in range(0, t_ref.shape[0], ROWS):
            rows = slice(start, start + ROWS)
            for low in range(0, t_ref.shape[1], HD):
                cols = slice(low, low + HD)
                o_ref[rows, cols] = (t_ref[rows, cols] * scale_ref[line] * gain[:, cols]).astype(jnp.bfloat16)
            line += 1


def exchange(first, second, depth):
    block_count = 1 << depth

    def swap(value, bit):
        return lax.ppermute(value, "seq", [(i, i ^ (1 << bit)) for i in range(block_count)])

    outer = list(range(1, depth))
    held = []
    for piece, bits in ((first, outer), (second, outer[::-1])):
        have = {0: piece}
        for bit in bits:
            have.update({key | (1 << bit): swap(value, bit) for key, value in list(have.items())})
        held.append(have)
    for have in held:
        have.update({key | 1: swap(value, 0) for key, value in list(have.items())})
    return [have[key] for key in range(block_count) for have in held]


def local(
    slab_query,
    slab_key,
    slab_value,
    slab_levels,
    norm_gain,
    user_query,
    user_key,
    user_value,
    user_levels,
    prefix_lengths,
):
    seq_count = lax.axis_size("seq")
    head_axis = lax.axis_size("head")
    depth = seq_count.bit_length() - 1
    position = lax.axis_index("seq").astype(jnp.int32)
    token_count, width = slab_query.shape
    head_count = width // HD
    user_count, suffix = user_query.shape[:2]
    user_rows = user_count * suffix
    lines = (token_count + user_rows) // ROWS
    params = pltpu.CompilerParams(vmem_limit_bytes=VMEM_BYTES)
    f32 = functools.partial(jax.ShapeDtypeStruct, dtype=jnp.float32)
    bf16 = functools.partial(jax.ShapeDtypeStruct, dtype=jnp.bfloat16)
    vmem = pl.BlockSpec(memory_space=pltpu.VMEM)
    smem = pl.BlockSpec(memory_space=pltpu.SMEM)
    whole = pl.BlockSpec(memory_space=pl.ANY)

    first, second = pl.pallas_call(
        state_kernel,
        out_shape=[bf16((head_count // 2, HD, HD))] * 2,
        in_specs=[vmem] * 2,
        out_specs=[vmem] * 2,
        compiler_params=params,
    )(slab_key, slab_value)
    pieces = exchange(first, second, depth)

    steps = jnp.arange(depth, dtype=jnp.int32)
    slab_bits = jnp.bitwise_and(jnp.right_shift(position, steps), 1)
    user_bits = jnp.bitwise_and(jnp.right_shift(prefix_lengths[:, None], steps), 1)
    slab_keep = jnp.concatenate([jnp.ones((1,), jnp.int32), slab_bits]).astype(jnp.float32)
    user_keep = jnp.concatenate([jnp.ones((user_count, 1), jnp.int32), user_bits], axis=1).astype(jnp.float32)
    slab_weights = slab_levels[: depth + 1].astype(jnp.float32) * slab_keep[:, None, None]
    user_weights = user_levels[:, : depth + 1].astype(jnp.float32) * user_keep[:, :, None, None]
    slab_weights = jnp.transpose(slab_weights, (2, 0, 1)).reshape(token_count, -1)
    user_weights = jnp.transpose(user_weights, (0, 3, 1, 2)).reshape(user_rows, -1)
    user_queries = user_query.reshape(user_rows, width)
    user_keys = user_key.reshape(user_rows, width)
    user_values = user_value.reshape(user_rows, width)

    slab_local, user_local = pl.pallas_call(
        functools.partial(local_kernel, suffix),
        out_shape=[f32((token_count, width)), f32((user_rows, width))],
        in_specs=[vmem] * 8,
        out_specs=[vmem] * 2,
        compiler_params=params,
        cost_estimate=pl.CostEstimate(
            flops=4 * ROWS * width * (token_count + user_rows),
            bytes_accessed=10 * width * (token_count + user_rows),
            transcendentals=0,
        ),
    )(slab_query, slab_key, slab_value, user_queries, user_keys, user_values, slab_weights, user_weights)

    slab_total, user_total, square = pl.pallas_call(
        functools.partial(prefix_kernel, depth, suffix),
        out_shape=[f32((token_count, width)), f32((user_rows, width)), f32((lines, ROWS))],
        in_specs=[smem] * 2 + [vmem] * 6 + [whole] * (2 * seq_count),
        out_specs=[vmem] * 3,
        scratch_shapes=[
            pltpu.VMEM((seq_count, head_count, HD, HD), jnp.bfloat16),
            pltpu.VMEM((token_count, HD), jnp.float32),
            pltpu.VMEM((user_rows, HD), jnp.float32),
            pltpu.SemaphoreType.DMA((2 * seq_count,)),
        ],
        compiler_params=params,
    )(
        position.reshape(1),
        prefix_lengths,
        slab_query,
        user_queries,
        slab_weights,
        user_weights,
        slab_local,
        user_local,
        *pieces,
    )

    squares = [square]
    for shift in range(1, head_axis):
        pairs = [(i, (i + shift) % head_axis) for i in range(head_axis)]
        squares.append(lax.ppermute(square, "head", pairs))

    chunk = width // 4
    slab_out, user_out = pl.pallas_call(
        functools.partial(norm_kernel, float(width * head_axis)),
        out_shape=[bf16((token_count, width)), bf16((user_rows, width))],
        grid=(width // chunk,),
        in_specs=[
            pl.BlockSpec((token_count, chunk), lambda i: (0, i)),
            pl.BlockSpec((user_rows, chunk), lambda i: (0, i)),
            pl.BlockSpec((1, chunk), lambda i: (0, i)),
        ]
        + [pl.BlockSpec((lines, ROWS), lambda i: (0, 0))] * head_axis,
        out_specs=[
            pl.BlockSpec((token_count, chunk), lambda i: (0, i)),
            pl.BlockSpec((user_rows, chunk), lambda i: (0, i)),
        ],
        scratch_shapes=[pltpu.VMEM((lines, ROWS, ROWS), jnp.float32)],
        compiler_params=params,
    )(slab_total, user_total, norm_gain.reshape(1, width), *squares)
    return slab_out, user_out.reshape(user_count, suffix, width)


def solution(mesh):
    return jax.shard_map(
        local,
        mesh=mesh,
        in_specs=(
            P("seq", "head"),
            P("seq", "head"),
            P("seq", "head"),
            P(None, "head", "seq"),
            P("head"),
            P("seq", None, "head"),
            P("seq", None, "head"),
            P("seq", None, "head"),
            P("seq", None, "head", None),
            P("seq"),
        ),
        out_specs=(P("seq", "head"), P("seq", None, "head")),
        check_vma=False,
    )
```

time: 166 us -> 67.3 us (0.41)
  local copies, waits for them, and re-layouts: 47.9 us -> 11.1 us
  matrix products: 36.4 us -> 0 us
  Pallas kernels: 0 us -> 20.7 us
  waiting for transfers between devices: 35.2 us -> 17.5 us
  other arithmetic: 19.1 us -> 2.59 us
  starting transfers between devices: 0.04 us -> 14.1 us
  between operations: 14.2 us -> 0.83 us
  blocking collectives: 11.7 us -> 0 us
    dot_general x13 -> x0, matrix products: 36.4 us -> none  [the longest x4 14 us: user_read(): jnp.einsum('kc,chde->khde', user_mask, gathered, preferred_element_type=j...]
    all_gather x1 -> x0, waiting for transfers between devices: 35.2 us -> none  [local(): gathered = lax.all_gather(block_state[None], 'seq', axis=0, tiled=True)]
    pallas_call x0 -> x4, Pallas kernels: none -> 20.7 us  [the longest x1 9.45 us: local(): pl.pallas_call(functools.partial(prefix_kernel, depth, suffix), out_shape...]
    ppermute x0 -> x17, waiting for transfers between devices: none -> 17.5 us  [the longest x14 15.3 us: swap(): lax.ppermute(value, 'seq', [(i, i ^ 1 << bit) for i in range(block_count)])]
    ppermute x0 -> x17, starting transfers between devices: none -> 14.1 us  [the longest x14 8.38 us: swap(): lax.ppermute(value, 'seq', [(i, i ^ 1 << bit) for i in range(block_count)])]
    psum x1 -> x0, blocking collectives: 11.7 us -> none  [local(): slab_square, user_square = lax.psum((slab_square, user_square), 'head')]
    convert_element_type x5 -> x0, local copies, waits for them, and re-layouts: 11.3 us -> none  [the longest x4 8.87 us: user_read(): nodes_here = jnp.einsum('kc,chde->khde', user_mask, gathered, preferred_e...]
    reshape x5 -> x4, local copies, waits for them, and re-layouts: 11.2 us -> 0.33 us  [the longest x2 0.23 us: local(): jnp.transpose(user_weights, (0, 3, 1, 2)).reshape(user_rows, -1)]
  transfers between devices with their start and end apart: 1 -> 17, of which waited for: 1 -> 5; matrix products, arithmetic and copies ran while one was open for 3% -> 5% of each run, Pallas kernels for 0% -> 13%
where the time goes in v1:
time: 67.3 us; the launch traced here: 66.8 us
  Pallas kernels  20.7 us (31%)
  waiting for transfers between devices  17.5 us (26%)
  starting transfers between devices  14.1 us (21%)
  local copies, waits for them, and re-layouts  11.1 us (16%)
  other arithmetic  2.59 us (4%)
  between operations  0.83 us (1%)
    ppermute x14, waiting for transfers between devices, swap(): lax.ppermute(value, 'seq', [(i, i ^ 1 << bit) for i in range(block_count)])  15.3 us
    unnamed x32, local copies, waits for them, and re-layouts  10.7 us
    pallas_call x1, Pallas kernels, local(): pl.pallas_call(functools.partial(prefix_kernel, depth, suffix), out_shape...  9.45 us
    pallas_call x1, Pallas kernels, local(): pl.pallas_call(functools.partial(local_kernel, suffix), out_shape=[f32((t...  8.81 us
    ppermute x14, starting transfers between devices, swap(): lax.ppermute(value, 'seq', [(i, i ^ 1 << bit) for i in range(block_count)])  8.38 us
    ppermute x3, starting transfers between devices, local(): squares.append(lax.ppermute(square, 'head', pairs))  5.71 us
    ppermute x3, waiting for transfers between devices, local(): squares.append(lax.ppermute(square, 'head', pairs))  2.22 us
    pallas_call x1, Pallas kernels, local(): pl.pallas_call(functools.partial(norm_kernel, float(width * head_axis)),...  2.07 us
  transfers between devices with their start and end apart: 17, of which 5 were waited for; matrix products, arithmetic and copies ran while one was open for 5% of the time, Pallas kernels for 13%

profile of v1, /device:TPU:0, one launch (start us, length us, event | category | flops | bytes accessed | tf_op | source)
XLA Modules:
  0.0 66.8 jit_solution(8937170328475803368)
XLA Ops:
  0.6 0.0 copy-start
  0.7 0.0 copy-start.2
  0.7 1.1 %copy-done.2 = bf16[128,2048]{1,0:T(8,128)(2,1)S(1)} copy-done((bf16[128,2048]{1,0:T(8,128)(2,1)S(1)}, bf16[128,2048]{1,0:T(8,128)(2,1)}, u32[]{:S(2)}) %copy-start.2) | copy-done | bytes 524312
  1.8 1.0 %copy-done.4 = bf16[128,2048]{1,0:T(8,128)(2,1)S(1)} copy-done((bf16[128,2048]{1,0:T(8,128)(2,1)S(1)}, bf16[128,2048]{1,0:T(8,128)(2,1)}, u32[]{:S(2)}) %copy-start.4) | copy-done | bytes 524312
  2.9 0.3 shard_map.114
  3.2 3.0 %collective-permute-start.7 = (bf16[8,128,128]{2,1,0:T(8,128)(2,1)S(1)}, bf16[8,128,128]{2,1,0:T(8,128)(2,1)S(1)}, u32[]{:S(2)}, u32[]{:S(2)}) collective-permute-start(bf16[8,128,128]{2,1,0:T(8,128)(2,1)S(1)} %get-tuple-element.14.rest_1_), channel_id=1, source_target_pairs={{0,16},{4,20},{8,24},{12,28},{16,0},{20,4},{24,8},{28,12},{1,17},{... | collective-permute-start | bytes 786440 | tf_op jit(solution)/shard_map/ppermute | solution.py:150
  6.2 1.5 %collective-permute-start.3 = (bf16[8,128,128]{2,1,0:T(8,128)(2,1)S(1)}, bf16[8,128,128]{2,1,0:T(8,128)(2,1)S(1)}, u32[]{:S(2)}, u32[]{:S(2)}) collective-permute-start(bf16[8,128,128]{2,1,0:T(8,128)(2,1)S(1)} %get-tuple-element.14.rest_1_), channel_id=1, source_target_pairs={{0,8},{4,12},{8,0},{12,4},{16,24},{20,28},{24,16},{28,20},{1,9},{5... | collective-permute-start | bytes 786440 | tf_op jit(solution)/shard_map/ppermute | solution.py:150
  7.7 0.5 collective-permute-start.2
  8.3 0.1 collective-permute-start.6
  8.3 0.1 add_convert_fusion
  8.4 0.8 %convert_multiply_fusion = f32[4,16,128]{2,1,0:T(8,128)S(1)} fusion(f32[4]{0:T(128)S(1)} %add_convert_fusion, bf16[6,16,128]{2,1,0:T(8,128)(2,1)} %param.13), kind=kLoop, calls=%fused_computation.1 | loop fusion | flops 16384 | bytes 49168 | tf_op jit(solution)/shard_map/mul | solution.py:206
  9.2 0.1 copy.17.sw_ref
  9.3 10.3 %collective-permute-done.2.rest_4_ = bf16[8,128,128]{2,1,0:T(8,128)(2,1)S(1)} collective-permute-done((bf16[8,128,128]{2,1,0:T(8,128)(2,1)S(1)}, bf16[8,128,128]{2,1,0:T(8,128)(2,1)S(1)}, u32[]{:S(2)}, u32[]{:S(2)}) %collective-permute-start.2) | collective-permute-done | bytes 262176 | tf_op jit(solution)/shard_map/ppermute | solution.py:150
  19.6 0.4 collective-permute-start.10
  20.0 0.2 collective-permute-start.4
  20.2 0.0 collective-permute-done.6.rest_8_
  20.2 1.6 %collective-permute-start.11 = (bf16[8,128,128]{2,1,0:T(8,128)(2,1)S(1)}, bf16[8,128,128]{2,1,0:T(8,128)(2,1)}, u32[]{:S(2)}, u32[]{:S(2)}) collective-permute-start(bf16[8,128,128]{2,1,0:T(8,128)(2,1)S(1)} %collective-permute-done.7.rest_9_), channel_id=1, source_target_pairs={{0,8},{4,12},{8,0},{12,4},{16,24},{20,28},{24,16},{28,20},{1,9},{5... | collective-permute-start | bytes 786440 | tf_op jit(solution)/shard_map/ppermute | solution.py:150
  21.9 0.7 %shift-right-arithmetic_and_fusion = s32[4,3]{1,0:T(4,128)S(1)} fusion(s32[4]{0:T(128)} %length_ref.1), kind=kLoop, calls=%fused_computation.3 | loop fusion | flops 24 | bytes 64 | tf_op jit(solution)/shard_map/and | solution.py:203
  22.6 0.1 pad_convert_fusion
  22.7 0.0 collective-permute-start.9
  22.7 0.0 copy-start.10
  22.7 0.7 %copy-done.10 = bf16[8,128,128]{2,1,0:T(8,128)(2,1)} copy-done((bf16[8,128,128]{2,1,0:T(8,128)(2,1)}, bf16[8,128,128]{2,1,0:T(8,128)(2,1)S(1)}, u32[]{:S(2)}) %copy-start.10) | copy-done | bytes 262168
  23.4 0.5 collective-permute-start.5
  23.9 4.6 %collective-permute-done.10.rest_12_ = bf16[8,128,128]{2,1,0:T(8,128)(2,1)} collective-permute-done((bf16[8,128,128]{2,1,0:T(8,128)(2,1)S(1)}, bf16[8,128,128]{2,1,0:T(8,128)(2,1)}, u32[]{:S(2)}, u32[]{:S(2)}) %collective-permute-start.10) | collective-permute-done | bytes 262176 | tf_op jit(solution)/shard_map/ppermute | solution.py:150
  28.5 0.4 collective-permute-done.11.rest_13_
  28.8 0.1 collective-permute-start.12
  29.0 0.7 %copy-done.12 = bf16[8,128,128]{2,1,0:T(8,128)(2,1)} copy-done((bf16[8,128,128]{2,1,0:T(8,128)(2,1)}, bf16[8,128,128]{2,1,0:T(8,128)(2,1)S(1)}, u32[]{:S(2)}) %copy-start.12) | copy-done | bytes 262168
  29.7 0.4 collective-permute-start.13
  30.0 0.9 %multiply_bitcast_fusion = f32[4,64,4,16]{1,3,2,0:T(8,128)S(1)} fusion(f32[4,4]{1,0:T(4,128)S(1)} %pad_convert_fusion, bf16[4,6,16,64]{3,2,1,0:T(8,128)(2,1)} %param.18), kind=kLoop, calls=%fused_computation | loop fusion | flops 32768 | bytes 98368 | tf_op jit(solution)/shard_map/transpose | solution.py:209
  31.0 0.1 copy.14
  31.1 0.1 reshape.46
  31.2 0.1 copy.18.uw_ref
  31.3 0.0 copy-start.3
  31.3 1.0 %copy-done.3 = bf16[128,2048]{1,0:T(8,128)(2,1)S(1)} copy-done((bf16[128,2048]{1,0:T(8,128)(2,1)S(1)}, bf16[128,2048]{1,0:T(8,128)(2,1)}, u32[]{:S(2)}) %copy-start.3) | copy-done | bytes 524312
  32.4 1.0 %copy-done.5 = bf16[128,2048]{1,0:T(8,128)(2,1)S(1)} copy-done((bf16[128,2048]{1,0:T(8,128)(2,1)S(1)}, bf16[128,2048]{1,0:T(8,128)(2,1)}, u32[]{:S(2)}) %copy-start.5) | copy-done | bytes 524312
  33.4 1.2 %copy-done.7 = bf16[4,64,2048]{2,1,0:T(8,128)(2,1)S(1)} copy-done((bf16[4,64,2048]{2,1,0:T(8,128)(2,1)S(1)}, bf16[4,64,2048]{2,1,0:T(8,128)(2,1)}, u32[]{:S(2)}) %copy-start.7) | copy-done | bytes 1048600
  34.6 1.2 %copy-done.8 = bf16[4,64,2048]{2,1,0:T(8,128)(2,1)S(1)} copy-done((bf16[4,64,2048]{2,1,0:T(8,128)(2,1)S(1)}, bf16[4,64,2048]{2,1,0:T(8,128)(2,1)}, u32[]{:S(2)}) %copy-start.8) | copy-done | bytes 1048600
  35.9 8.8 %shard_map.113 = (f32[128,2048]{1,0:T(8,128)S(1)}, f32[256,2048]{1,0:T(8,128)}) custom-call(bf16[128,2048]{1,0:T(8,128)(2,1)S(1)} %copy-done.1, bf16[128,2048]{1,0:T(8,128)(2,1)S(1)} %copy-done.3, bf16[128,2048]{1,0:T(8,128)(2,1)S(1)} %copy-done.5, bf16[256,2048]{1,0:T(8,128)(2,1)S(1)} %bitcast.13, bf16[256,2048]{1,0:T(8,128)(2,1)S(1)} %bitcast.14, ...), custom_call_target="tpu_custom_call" | custom-call | flops 402653184 | bytes 7864320 | tf_op jit(solution)/shard_map/pallas_call | solution.py:214
  44.7 1.0 %copy-done.9 = f32[128,2048]{1,0:T(8,128)} copy-done((f32[128,2048]{1,0:T(8,128)}, f32[128,2048]{1,0:T(8,128)S(1)}, u32[]{:S(2)}) %copy-start.9) | copy-done | bytes 1048600
  45.7 0.0 copy-start.15
  45.7 9.4 %shard_map.115 = (f32[128,2048]{1,0:T(8,128)S(1)}, f32[256,2048]{1,0:T(8,128)}, f32[3,128]{1,0:T(4,128)S(1)}) custom-call(s32[1]{0:T(128)} %bitcast.order_ref, s32[4]{0:T(128)S(1)} %copy-done.14, bf16[128,2048]{1,0:T(8,128)(2,1)S(1)} %copy-done.1, bf16[256,2048]{1,0:T(8,128)(2,1)} %bitcast.12, f32[128,64]{1,0:T(8,128)S(1)} %copy.17.sw_ref, ...), custom_call_target="tpu_custom_call" | custom-call | tf_op jit(solution)/shard_map/pallas_call | solution.py:227
  55.2 1.8 %collective-permute-start.14 = (f32[3,128]{1,0:T(4,128)S(1)}, f32[3,128]{1,0:T(4,128)S(1)}, u32[]{:S(2)}, u32[]{:S(2)}) collective-permute-start(f32[3,128]{1,0:T(4,128)S(1)} %get-tuple-element.17.rest_0_), channel_id=1, source_target_pairs={{0,1},{1,2},{2,3},{3,0},{4,5},{5,6},{6,7},{7,4},{8,9},{9,10},{10,1... | collective-permute-start | bytes 4616 | tf_op jit(solution)/shard_map/ppermute | solution.py:254
  56.9 2.6 %collective-permute-start.15 = (f32[3,128]{1,0:T(4,128)S(1)}, f32[3,128]{1,0:T(4,128)S(1)}, u32[]{:S(2)}, u32[]{:S(2)}) collective-permute-start(f32[3,128]{1,0:T(4,128)S(1)} %get-tuple-element.17.rest_0_), channel_id=1, source_target_pairs={{0,2},{1,3},{2,0},{3,1},{4,6},{5,7},{6,4},{7,5},{8,10},{9,11},{10,... | collective-permute-start | bytes 4616 | tf_op jit(solution)/shard_map/ppermute | solution.py:254
  59.5 1.3 %collective-permute-start.16 = (f32[3,128]{1,0:T(4,128)S(1)}, f32[3,128]{1,0:T(4,128)S(1)}, u32[]{:S(2)}, u32[]{:S(2)}) collective-permute-start(f32[3,128]{1,0:T(4,128)S(1)} %get-tuple-element.17.rest_0_), channel_id=1, source_target_pairs={{0,3},{1,0},{2,1},{3,2},{4,7},{5,4},{6,5},{7,6},{8,11},{9,8},{10,9... | collective-permute-start | bytes 4616 | tf_op jit(solution)/shard_map/ppermute | solution.py:254
  60.9 0.5 collective-permute-done.15.rest_2_
  61.4 1.7 %collective-permute-done.16.rest_3_ = f32[3,128]{1,0:T(4,128)S(1)} collective-permute-done((f32[3,128]{1,0:T(4,128)S(1)}, f32[3,128]{1,0:T(4,128)S(1)}, u32[]{:S(2)}, u32[]{:S(2)}) %collective-permute-start.16) | collective-permute-done | bytes 1568 | tf_op jit(solution)/shard_map/ppermute | solution.py:254
  63.1 1.6 %copy-done.6 = f32[256,2048]{1,0:T(8,128)S(1)} copy-done((f32[256,2048]{1,0:T(8,128)S(1)}, f32[256,2048]{1,0:T(8,128)}, u32[]{:S(2)}) %copy-start.6) | copy-done | bytes 2097176
  64.7 2.1 %shard_map.116 = (bf16[128,2048]{1,0:T(8,128)(2,1)}, bf16[256,2048]{1,0:T(8,128)(2,1)}) custom-call(f32[128,2048]{1,0:T(8,128)S(1)} %get-tuple-element.15.st_ref, f32[256,2048]{1,0:T(8,128)S(1)} %copy-done.6, bf16[1,2048]{1,0:T(2,128)(2,1)S(1)} %reshape.49.gain_ref, f32[3,128]{1,0:T(4,128)S(1)} %get-tuple-element.17.rest_0_, ...), custom_call_target="tpu_custom_call" | custom-call | tf_op jit(solution)/shard_map/pallas_call | solution.py:257
  (33 shorter events, 0.1 us)
Async XLA Ops:
  0.6 30.7 %copy-start = (bf16[4,64,2048]{2,1,0:T(8,128)(2,1)S(1)}, bf16[4,64,2048]{2,1,0:T(8,128)(2,1)}, u32[]{:S(2)}) copy-start(bf16[4,64,2048]{2,1,0:T(8,128)(2,1)} %param.15) | copy-start | bytes 3145732
  0.6 30.7 %copy-start.1 = (bf16[128,2048]{1,0:T(8,128)(2,1)S(1)}, bf16[128,2048]{1,0:T(8,128)(2,1)}, u32[]{:S(2)}) copy-start(bf16[128,2048]{1,0:T(8,128)(2,1)} %sq_ref.3) | copy-start | bytes 1572868
  0.7 1.2 %copy-start.2 = (bf16[128,2048]{1,0:T(8,128)(2,1)S(1)}, bf16[128,2048]{1,0:T(8,128)(2,1)}, u32[]{:S(2)}) copy-start(bf16[128,2048]{1,0:T(8,128)(2,1)} %key_ref.1) | copy-start | bytes 1572868
  1.8 1.0 %copy-start.4 = (bf16[128,2048]{1,0:T(8,128)(2,1)S(1)}, bf16[128,2048]{1,0:T(8,128)(2,1)}, u32[]{:S(2)}) copy-start(bf16[128,2048]{1,0:T(8,128)(2,1)} %value_ref.1) | copy-start | bytes 1572868
  3.2 16.4 %collective-permute-start.7 = (bf16[8,128,128]{2,1,0:T(8,128)(2,1)S(1)}, bf16[8,128,128]{2,1,0:T(8,128)(2,1)S(1)}, u32[]{:S(2)}, u32[]{:S(2)}) collective-permute-start(bf16[8,128,128]{2,1,0:T(8,128)(2,1)S(1)} %get-tuple-element.14.rest_1_), channel_id=1, source_target_pairs={{0,16},{4,20},{8,24},{12,28},{16,0},{20,4},{24,8},{28,12},{1,17},{... | collective-permute-start | bytes 786440 | tf_op jit(solution)/shard_map/ppermute | solution.py:150
  6.2 13.8 %collective-permute-start.3 = (bf16[8,128,128]{2,1,0:T(8,128)(2,1)S(1)}, bf16[8,128,128]{2,1,0:T(8,128)(2,1)S(1)}, u32[]{:S(2)}, u32[]{:S(2)}) collective-permute-start(bf16[8,128,128]{2,1,0:T(8,128)(2,1)S(1)} %get-tuple-element.14.rest_1_), channel_id=1, source_target_pairs={{0,8},{4,12},{8,0},{12,4},{16,24},{20,28},{24,16},{28,20},{1,9},{5... | collective-permute-start | bytes 786440 | tf_op jit(solution)/shard_map/ppermute | solution.py:150
  7.7 11.9 %collective-permute-start.2 = (bf16[8,128,128]{2,1,0:T(8,128)(2,1)S(1)}, bf16[8,128,128]{2,1,0:T(8,128)(2,1)S(1)}, u32[]{:S(2)}, u32[]{:S(2)}) collective-permute-start(bf16[8,128,128]{2,1,0:T(8,128)(2,1)S(1)} %get-tuple-element.13.rest_0_), channel_id=1, source_target_pairs={{0,8},{4,12},{8,0},{12,4},{16,24},{20,28},{24,16},{28,20},{1,9},{5... | collective-permute-start | bytes 786440 | tf_op jit(solution)/shard_map/ppermute | solution.py:150
  8.3 12.0 %collective-permute-start.6 = (bf16[8,128,128]{2,1,0:T(8,128)(2,1)S(1)}, bf16[8,128,128]{2,1,0:T(8,128)(2,1)S(1)}, u32[]{:S(2)}, u32[]{:S(2)}) collective-permute-start(bf16[8,128,128]{2,1,0:T(8,128)(2,1)S(1)} %get-tuple-element.13.rest_0_), channel_id=1, source_target_pairs={{0,16},{4,20},{8,24},{12,28},{16,0},{20,4},{24,8},{28,12},{1,17},{... | collective-permute-start | bytes 786440 | tf_op jit(solution)/shard_map/ppermute | solution.py:150
  8.3 14.3 %collective-permute-start = (bf16[8,128,128]{2,1,0:T(8,128)(2,1)S(1)}, bf16[8,128,128]{2,1,0:T(8,128)(2,1)}, u32[]{:S(2)}, u32[]{:S(2)}) collective-permute-start(bf16[8,128,128]{2,1,0:T(8,128)(2,1)S(1)} %get-tuple-element.13.rest_0_), channel_id=1, source_target_pairs={{0,4},{4,0},{8,12},{12,8},{16,20},{20,16},{24,28},{28,24},{1,5},{5... | collective-permute-start | bytes 786440 | tf_op jit(solution)/shard_map/ppermute | solution.py:150
  19.6 3.1 %collective-permute-start.1 = (bf16[8,128,128]{2,1,0:T(8,128)(2,1)S(1)}, bf16[8,128,128]{2,1,0:T(8,128)(2,1)S(1)}, u32[]{:S(2)}, u32[]{:S(2)}) collective-permute-start(bf16[8,128,128]{2,1,0:T(8,128)(2,1)S(1)} %get-tuple-element.14.rest_1_), channel_id=1, source_target_pairs={{0,4},{4,0},{8,12},{12,8},{16,20},{20,16},{24,28},{28,24},{1,5},{5... | collective-permute-start | bytes 786440 | tf_op jit(solution)/shard_map/ppermute | solution.py:150
  19.6 8.8 %collective-permute-start.10 = (bf16[8,128,128]{2,1,0:T(8,128)(2,1)S(1)}, bf16[8,128,128]{2,1,0:T(8,128)(2,1)}, u32[]{:S(2)}, u32[]{:S(2)}) collective-permute-start(bf16[8,128,128]{2,1,0:T(8,128)(2,1)S(1)} %collective-permute-done.2.rest_4_), channel_id=1, source_target_pairs={{0,16},{4,20},{8,24},{12,28},{16,0},{20,4},{24,8},{28,12},{1,17},{... | collective-permute-start | bytes 786440 | tf_op jit(solution)/shard_map/ppermute | solution.py:150
  20.0 9.0 %collective-permute-start.4 = (bf16[8,128,128]{2,1,0:T(8,128)(2,1)S(1)}, bf16[8,128,128]{2,1,0:T(8,128)(2,1)S(1)}, u32[]{:S(2)}, u32[]{:S(2)}) collective-permute-start(bf16[8,128,128]{2,1,0:T(8,128)(2,1)S(1)} %collective-permute-done.2.rest_4_), channel_id=1, source_target_pairs={{0,4},{4,0},{8,12},{12,8},{16,20},{20,16},{24,28},{28,24},{1,5},{5... | collective-permute-start | bytes 786440 | tf_op jit(solution)/shard_map/ppermute | solution.py:150
  20.2 8.6 %collective-permute-start.11 = (bf16[8,128,128]{2,1,0:T(8,128)(2,1)S(1)}, bf16[8,128,128]{2,1,0:T(8,128)(2,1)}, u32[]{:S(2)}, u32[]{:S(2)}) collective-permute-start(bf16[8,128,128]{2,1,0:T(8,128)(2,1)S(1)} %collective-permute-done.7.rest_9_), channel_id=1, source_target_pairs={{0,8},{4,12},{8,0},{12,4},{16,24},{20,28},{24,16},{28,20},{1,9},{5... | collective-permute-start | bytes 786440 | tf_op jit(solution)/shard_map/ppermute | solution.py:150
  22.7 23.0 %collective-permute-start.9 = (bf16[8,128,128]{2,1,0:T(8,128)(2,1)S(1)}, bf16[8,128,128]{2,1,0:T(8,128)(2,1)}, u32[]{:S(2)}, u32[]{:S(2)}) collective-permute-start(bf16[8,128,128]{2,1,0:T(8,128)(2,1)S(1)} %collective-permute-done.7.rest_9_), channel_id=1, source_target_pairs={{0,4},{4,0},{8,12},{12,8},{16,20},{20,16},{24,28},{28,24},{1,5},{5... | collective-permute-start | bytes 786440 | tf_op jit(solution)/shard_map/ppermute | solution.py:150
  22.7 0.7 %copy-start.10 = (bf16[8,128,128]{2,1,0:T(8,128)(2,1)}, bf16[8,128,128]{2,1,0:T(8,128)(2,1)S(1)}, u32[]{:S(2)}) copy-start(bf16[8,128,128]{2,1,0:T(8,128)(2,1)S(1)} %collective-permute-done.1.rest_3_) | copy-start | bytes 786436
  23.4 22.2 %collective-permute-start.5 = (bf16[8,128,128]{2,1,0:T(8,128)(2,1)S(1)}, bf16[8,128,128]{2,1,0:T(8,128)(2,1)}, u32[]{:S(2)}, u32[]{:S(2)}) collective-permute-start(bf16[8,128,128]{2,1,0:T(8,128)(2,1)S(1)} %collective-permute-done.3.rest_5_), channel_id=1, source_target_pairs={{0,4},{4,0},{8,12},{12,8},{16,20},{20,16},{24,28},{28,24},{1,5},{5... | collective-permute-start | bytes 786440 | tf_op jit(solution)/shard_map/ppermute | solution.py:150
  28.5 17.2 %collective-permute-start.8 = (bf16[8,128,128]{2,1,0:T(8,128)(2,1)S(1)}, bf16[8,128,128]{2,1,0:T(8,128)(2,1)}, u32[]{:S(2)}, u32[]{:S(2)}) collective-permute-start(bf16[8,128,128]{2,1,0:T(8,128)(2,1)S(1)} %collective-permute-done.6.rest_8_), channel_id=1, source_target_pairs={{0,4},{4,0},{8,12},{12,8},{16,20},{20,16},{24,28},{28,24},{1,5},{5... | collective-permute-start | bytes 786440 | tf_op jit(solution)/shard_map/ppermute | solution.py:150
  28.8 16.8 %collective-permute-start.12 = (bf16[8,128,128]{2,1,0:T(8,128)(2,1)}, bf16[8,128,128]{2,1,0:T(8,128)(2,1)}, u32[]{:S(2)}, u32[]{:S(2)}) collective-permute-start(bf16[8,128,128]{2,1,0:T(8,128)(2,1)} %collective-permute-done.10.rest_12_), channel_id=1, source_target_pairs={{0,4},{4,0},{8,12},{12,8},{16,20},{20,16},{24,28},{28,24},{1,5},{5... | collective-permute-start | bytes 786440 | tf_op jit(solution)/shard_map/ppermute | solution.py:150
  29.0 0.7 %copy-start.12 = (bf16[8,128,128]{2,1,0:T(8,128)(2,1)}, bf16[8,128,128]{2,1,0:T(8,128)(2,1)S(1)}, u32[]{:S(2)}) copy-start(bf16[8,128,128]{2,1,0:T(8,128)(2,1)S(1)} %collective-permute-done.4.rest_6_) | copy-start | bytes 786436
  29.7 16.0 %collective-permute-start.13 = (bf16[8,128,128]{2,1,0:T(8,128)(2,1)}, bf16[8,128,128]{2,1,0:T(8,128)(2,1)}, u32[]{:S(2)}, u32[]{:S(2)}) collective-permute-start(bf16[8,128,128]{2,1,0:T(8,128)(2,1)} %collective-permute-done.11.rest_13_), channel_id=1, source_target_pairs={{0,4},{4,0},{8,12},{12,8},{16,20},{20,16},{24,28},{28,24},{1,5},{5... | collective-permute-start | bytes 786440 | tf_op jit(solution)/shard_map/ppermute | solution.py:150
  31.3 1.0 %copy-start.3 = (bf16[128,2048]{1,0:T(8,128)(2,1)S(1)}, bf16[128,2048]{1,0:T(8,128)(2,1)}, u32[]{:S(2)}) copy-start(bf16[128,2048]{1,0:T(8,128)(2,1)} %key_ref.1) | copy-start | bytes 1572868
  32.4 1.0 %copy-start.5 = (bf16[128,2048]{1,0:T(8,128)(2,1)S(1)}, bf16[128,2048]{1,0:T(8,128)(2,1)}, u32[]{:S(2)}) copy-start(bf16[128,2048]{1,0:T(8,128)(2,1)} %value_ref.1) | copy-start | bytes 1572868
  33.4 1.2 %copy-start.7 = (bf16[4,64,2048]{2,1,0:T(8,128)(2,1)S(1)}, bf16[4,64,2048]{2,1,0:T(8,128)(2,1)}, u32[]{:S(2)}) copy-start(bf16[4,64,2048]{2,1,0:T(8,128)(2,1)} %param.16) | copy-start | bytes 3145732
  34.6 1.2 %copy-start.8 = (bf16[4,64,2048]{2,1,0:T(8,128)(2,1)S(1)}, bf16[4,64,2048]{2,1,0:T(8,128)(2,1)}, u32[]{:S(2)}) copy-start(bf16[4,64,2048]{2,1,0:T(8,128)(2,1)} %param.17) | copy-start | bytes 3145732
  35.8 9.8 %copy-start.11 = (bf16[8,128,128]{2,1,0:T(8,128)(2,1)S(1)}, bf16[8,128,128]{2,1,0:T(8,128)(2,1)}, u32[]{:S(2)}) copy-start(bf16[8,128,128]{2,1,0:T(8,128)(2,1)} %copy-done.10) | copy-start | bytes 786436
  35.8 9.8 %copy-start.13 = (bf16[8,128,128]{2,1,0:T(8,128)(2,1)S(1)}, bf16[8,128,128]{2,1,0:T(8,128)(2,1)}, u32[]{:S(2)}) copy-start(bf16[8,128,128]{2,1,0:T(8,128)(2,1)} %copy-done.12) | copy-start | bytes 786436
  35.8 9.8 %copy-start.14 = (s32[4]{0:T(128)S(1)}, s32[4]{0:T(128)}, u32[]{:S(2)}) copy-start(s32[4]{0:T(128)} %length_ref.1) | copy-start | bytes 52
  44.7 1.0 %copy-start.9 = (f32[128,2048]{1,0:T(8,128)}, f32[128,2048]{1,0:T(8,128)S(1)}, u32[]{:S(2)}) copy-start(f32[128,2048]{1,0:T(8,128)S(1)} %get-tuple-element.11.sl_ref) | copy-start | bytes 3145732
  45.7 15.2 %copy-start.15 = (bf16[2048]{0:T(1024)(128)(2,1)S(1)}, bf16[2048]{0:T(1024)(128)(2,1)}, u32[]{:S(2)}) copy-start(bf16[2048]{0:T(1024)(128)(2,1)} %param.14) | copy-start | bytes 12292
  55.2 5.7 %collective-permute-start.14 = (f32[3,128]{1,0:T(4,128)S(1)}, f32[3,128]{1,0:T(4,128)S(1)}, u32[]{:S(2)}, u32[]{:S(2)}) collective-permute-start(f32[3,128]{1,0:T(4,128)S(1)} %get-tuple-element.17.rest_0_), channel_id=1, source_target_pairs={{0,1},{1,2},{2,3},{3,0},{4,5},{5,6},{6,7},{7,4},{8,9},{9,10},{10,1... | collective-permute-start | bytes 4616 | tf_op jit(solution)/shard_map/ppermute | solution.py:254
  56.9 4.5 %collective-permute-start.15 = (f32[3,128]{1,0:T(4,128)S(1)}, f32[3,128]{1,0:T(4,128)S(1)}, u32[]{:S(2)}, u32[]{:S(2)}) collective-permute-start(f32[3,128]{1,0:T(4,128)S(1)} %get-tuple-element.17.rest_0_), channel_id=1, source_target_pairs={{0,2},{1,3},{2,0},{3,1},{4,6},{5,7},{6,4},{7,5},{8,10},{9,11},{10,... | collective-permute-start | bytes 4616 | tf_op jit(solution)/shard_map/ppermute | solution.py:254
  59.5 3.6 %collective-permute-start.16 = (f32[3,128]{1,0:T(4,128)S(1)}, f32[3,128]{1,0:T(4,128)S(1)}, u32[]{:S(2)}, u32[]{:S(2)}) collective-permute-start(f32[3,128]{1,0:T(4,128)S(1)} %get-tuple-element.17.rest_0_), channel_id=1, source_target_pairs={{0,3},{1,0},{2,1},{3,2},{4,7},{5,4},{6,5},{7,6},{8,11},{9,8},{10,9... | collective-permute-start | bytes 4616 | tf_op jit(solution)/shard_map/ppermute | solution.py:254
  63.1 1.6 %copy-start.6 = (f32[256,2048]{1,0:T(8,128)S(1)}, f32[256,2048]{1,0:T(8,128)}, u32[]{:S(2)}) copy-start(f32[256,2048]{1,0:T(8,128)} %get-tuple-element.16.ut_ref) | copy-start | bytes 6291460

commit v2 on v0

v2 whole, which is shorter than its diff:
```python
import functools

import jax
import jax.numpy as jnp
from jax import lax
from jax.experimental import pallas as pl
from jax.experimental.pallas import tpu as pltpu
from jax.sharding import PartitionSpec as P

HEADS = 64
HD = 128
ROWS = 128
VMEM_BYTES = 20 * 1024 * 1024
STATE_VMEM_BYTES = 62 * 1024 * 1024
LOCAL_VMEM_BYTES = 52 * 1024 * 1024


def matmul(a, b, contract):
    return lax.dot_general(a, b, (contract, ((), ())), preferred_element_type=jnp.float32)


def load_columns(sources, targets, sems, chunks):
    copies = []
    for chunk in range(chunks):
        group = []
        for i, (source, target) in enumerate(zip(sources, targets)):
            size = source.shape[1] // chunks
            cols = pl.ds(chunk * size, size)
            group.append(pltpu.make_async_copy(source.at[:, cols], target.at[:, cols], sems.at[i, chunk]))
            group[-1].start()
        copies.append(group)

    def wait(chunk):
        for copy in copies[chunk]:
            copy.wait()

    return wait


def state_kernel(chunks, key_hbm, value_hbm, out_ref, key_ref, value_ref, sems):
    head_count = out_ref.shape[0]
    wait = load_columns((key_hbm, value_hbm), (key_ref, value_ref), sems, chunks)
    for head in range(head_count):
        if head % (head_count // chunks) == 0:
            wait(head // (head_count // chunks))
        cols = slice(head * HD, (head + 1) * HD)
        state = matmul(key_ref[:, cols], value_ref[:, cols], ((0,), (0,)))
        out_ref[head] = state.astype(jnp.bfloat16)


def split_kernel(count, half, order_ref, *refs):
    for i in range(count):
        for head in range(half):
            refs[count + 2 * i][head] = refs[i][head]
            refs[count + 2 * i + 1][head] = refs[i][half + head]


def choose_levels(target, position, depth, level_count, head_count):
    block_count = 1 << depth
    shift = head_count.bit_length() - 1
    shape = (level_count * head_count, (block_count + 1) * head_count)
    row = lax.broadcasted_iota(jnp.int32, shape, 0)
    col = lax.broadcasted_iota(jnp.int32, shape, 1)
    level = row >> shift
    offset = col >> shift
    block = offset ^ position
    diff = block ^ target
    chosen = jnp.logical_and(level == 0, offset == block_count)
    below = jnp.logical_and(offset < block_count, block < target)
    for step in range(1, depth + 1):
        span = jnp.logical_and(diff >= (1 << (step - 1)), diff < (1 << step))
        chosen = jnp.logical_or(chosen, jnp.logical_and(below, jnp.logical_and(span, level == step)))
    same = (row & (head_count - 1)) == (col & (head_count - 1))
    return jnp.where(jnp.logical_and(chosen, same), 1.0, 0.0).astype(jnp.bfloat16)


def local_kernel(depth, suffix, chunks, length_ref, sw_ref, uw_ref, *rest):
    sources, (so_ref, uo_ref, sc_ref, uc_ref), loaded, sems = rest[:6], rest[6:10], rest[10:16], rest[16]
    sq_ref, sk_ref, sv_ref, uq_ref, uk_ref, uv_ref = loaded
    wait = load_columns(sources, loaded, sems, chunks)
    head_count = sq_ref.shape[1] // HD
    level_count = sw_ref.shape[0] // head_count
    position = lax.axis_index("seq").astype(jnp.int32)
    pick = functools.partial(
        choose_levels, position=position, depth=depth, level_count=level_count, head_count=head_count
    )
    sc_ref[...] = matmul(sw_ref[...], pick(position), ((0,), (0,)))
    for user in range(uw_ref.shape[0]):
        weights = matmul(uw_ref[user], pick(length_ref[user]), ((0,), (0,)))
        uc_ref[user * suffix : (user + 1) * suffix] = weights
    own = (1 << depth) * head_count
    row = lax.broadcasted_iota(jnp.int32, (ROWS, ROWS), 0)
    col = lax.broadcasted_iota(jnp.int32, (ROWS, ROWS), 1)
    causal = row >= col
    within = jnp.logical_and(causal, row // suffix == col // suffix)
    parts = [(sq_ref, sk_ref, sv_ref, sc_ref, so_ref, causal), (uq_ref, uk_ref, uv_ref, uc_ref, uo_ref, within)]
    for head in range(head_count):
        if head % (head_count // chunks) == 0:
            wait(head // (head_count // chunks))
        cols = slice(head * HD, (head + 1) * HD)
        for q_ref, k_ref, v_ref, c_ref, o_ref, mask in parts:
            for start in range(0, q_ref.shape[0], ROWS):
                rows = slice(start, start + ROWS)
                scores = matmul(q_ref[rows, cols], k_ref[rows, cols], ((1,), (1,)))
                scores = jnp.where(mask, scores, 0.0).astype(jnp.bfloat16)
                result = matmul(scores, v_ref[rows, cols], ((1,), (0,)))
                o_ref[rows, cols] = result * c_ref[rows, own + head : own + head + 1]


def add_blocks(groups, state_refs, head_count, head, q_ref, c_ref, base):
    cols = slice(head * HD, (head + 1) * HD)
    query = q_ref[:, cols]
    total = base
    for group in groups:
        scaled = []
        for offset in group:
            column = offset * head_count + head
            weight = jnp.broadcast_to(c_ref[:, column : column + 1], query.shape).astype(jnp.bfloat16)
            scaled.append(query * weight)
        states = []
        for offset in group:
            parts = state_refs[offset]
            share = head_count // len(parts)
            states.append(parts[head // share][head % share])
        total = total + matmul(jnp.concatenate(scaled, axis=1), jnp.concatenate(states, axis=0), ((1,), (0,)))
    return total


def read_kernel(groups, halves, last, sq_ref, uq_ref, sc_ref, uc_ref, sa_ref, ua_ref, *rest):
    head_count = sq_ref.shape[1] // HD
    state_refs = {}
    used = 0
    for offset in [offset for group in groups for offset in group]:
        state_refs[offset] = rest[used : used + halves]
        used += halves
    st_ref, ut_ref = rest[used : used + 2]
    squares = {}
    for head in range(head_count):
        cols = slice(head * HD, (head + 1) * HD)
        for side, (q_ref, c_ref, a_ref, t_ref) in enumerate(
            ((sq_ref, sc_ref, sa_ref, st_ref), (uq_ref, uc_ref, ua_ref, ut_ref))
        ):
            total = add_blocks(groups, state_refs, head_count, head, q_ref, c_ref, a_ref[:, cols])
            t_ref[:, cols] = total
            if last:
                acc_ref = rest[used + 3 + side]
                if head == 0:
                    acc_ref[...] = total * total
                else:
                    acc_ref[...] += total * total
    if last:
        square_ref = rest[used + 2]
        line = 0
        for acc_ref in rest[used + 3 : used + 5]:
            for start in range(0, acc_ref.shape[0], ROWS):
                turned = jnp.transpose(acc_ref[start : start + ROWS])
                value = jnp.sum(turned, axis=0, keepdims=True)
                for copy in range(square_ref.shape[0]):
                    square_ref[copy, line : line + 1] = value
                line += 1


def norm_kernel(features, st_ref, ut_ref, gain_ref, square_ref, so_ref, uo_ref, scale_ref):
    @pl.when(pl.program_id(0) == 0)
    def _():
        total = square_ref[0]
        for part in range(1, square_ref.shape[0]):
            total = total + square_ref[part]
        scale = lax.rsqrt(total / features + 1e-06)
        for line in range(scale.shape[0]):
            spread = jnp.broadcast_to(scale[line : line + 1], (ROWS, ROWS))
            scale_ref[line] = jnp.transpose(spread)

    gain = gain_ref[...].astype(jnp.float32)
    line = 0
    for t_ref, o_ref in ((st_ref, so_ref), (ut_ref, uo_ref)):
        for start in range(0, t_ref.shape[0], ROWS):
            rows = slice(start, start + ROWS)
            for low in range(0, t_ref.shape[1], HD):
                cols = slice(low, low + HD)
                o_ref[rows, cols] = (t_ref[rows, cols] * scale_ref[line] * gain[:, cols]).astype(jnp.bfloat16)
            line += 1


def local(
    slab_query,
    slab_key,
    slab_value,
    slab_levels,
    norm_gain,
    user_query,
    user_key,
    user_value,
    user_levels,
    prefix_lengths,
):
    seq_count = lax.axis_size("seq")
    head_axis = lax.axis_size("head")
    depth = seq_count.bit_length() - 1
    token_count, width = slab_query.shape
    head_count = width // HD
    half = head_count // 2
    user_count, suffix = user_query.shape[:2]
    user_rows = user_count * suffix
    lines = (token_count + user_rows) // ROWS
    params = pltpu.CompilerParams(vmem_limit_bytes=VMEM_BYTES)
    state_params = pltpu.CompilerParams(vmem_limit_bytes=STATE_VMEM_BYTES)
    local_params = pltpu.CompilerParams(vmem_limit_bytes=LOCAL_VMEM_BYTES)
    f32 = functools.partial(jax.ShapeDtypeStruct, dtype=jnp.float32)
    bf16 = functools.partial(jax.ShapeDtypeStruct, dtype=jnp.bfloat16)
    vmem = pl.BlockSpec(memory_space=pltpu.VMEM)
    smem = pl.BlockSpec(memory_space=pltpu.SMEM)
    anywhere = pl.BlockSpec(memory_space=pl.ANY)
    hbm = pl.BlockSpec(memory_space=pltpu.HBM)
    chunks = min(4, half)
    rows_cost = 2 * width * (token_count + user_rows)

    def cost(flops, moved):
        return pl.CostEstimate(flops=flops, bytes_accessed=moved, transcendentals=0)

    def swap(value, bit):
        return lax.ppermute(value, "seq", [(i, i ^ (1 << bit)) for i in range(seq_count)])

    state = pl.pallas_call(
        functools.partial(state_kernel, chunks),
        out_shape=bf16((head_count, HD, HD)),
        in_specs=[hbm] * 2,
        out_specs=vmem,
        scratch_shapes=[pltpu.VMEM((token_count, width), jnp.bfloat16)] * 2 + [pltpu.SemaphoreType.DMA((2, chunks))],
        compiler_params=state_params,
    )(slab_key, slab_value)

    outer = list(range(1, depth))
    whole = {0: state}
    for bit in outer:
        whole[1 << bit] = swap(state, bit)
    whole[1] = swap(state, 0)

    user_queries = user_query.reshape(user_rows, width)
    user_keys = user_key.reshape(user_rows, width)
    user_values = user_value.reshape(user_rows, width)
    columns = (seq_count + 1) * head_count
    slab_acc, user_acc, slab_coef, user_coef = pl.pallas_call(
        functools.partial(local_kernel, depth, suffix, chunks),
        out_shape=[
            f32((token_count, width)),
            f32((user_rows, width)),
            f32((token_count, columns)),
            f32((user_rows, columns)),
        ],
        in_specs=[smem] + [vmem] * 2 + [hbm] * 6,
        out_specs=[vmem] * 4,
        scratch_shapes=[pltpu.VMEM((token_count, width), jnp.bfloat16)] * 3
        + [pltpu.VMEM((user_rows, width), jnp.bfloat16)] * 3
        + [pltpu.SemaphoreType.DMA((6, chunks))],
        compiler_params=local_params,
        cost_estimate=cost(ROWS, ROWS),
    )(
        prefix_lengths,
        slab_levels.reshape(-1, token_count),
        user_levels.reshape(user_count, -1, suffix),
        slab_query,
        slab_key,
        slab_value,
        user_queries,
        user_keys,
        user_values,
    )

    sides = {}
    received = lax.optimization_barrier((slab_coef, *[whole[1 << bit] for bit in outer]))[1:]
    for bit, value in zip(outer, received):
        whole[1 << bit] = value
    if len(outer) > 1:
        split = pl.pallas_call(
            functools.partial(split_kernel, len(outer), half),
            out_shape=[bf16((half, HD, HD))] * (2 * len(outer)),
            in_specs=[anywhere] + [vmem] * len(outer),
            out_specs=[vmem] * (2 * len(outer)),
            compiler_params=params,
        )(slab_coef, *received)
        for i, bit in enumerate(outer):
            sides[1 << bit] = [split[2 * i], split[2 * i + 1]]
    later = sorted((m for m in range(0, seq_count, 2) if m.bit_count() > 1), key=lambda m: m.bit_count())
    for m in later:
        high, low = m.bit_length() - 1, (m & -m).bit_length() - 1
        sides[m] = [swap(sides[m ^ (1 << high)][0], high), swap(sides[m ^ (1 << low)][1], low)]
    def read(groups, states, halves, accs, last):
        outs = [f32((token_count, width)), f32((user_rows, width))]
        scratch = []
        if last:
            outs.append(f32((head_axis, lines, ROWS)))
            scratch = [pltpu.VMEM((token_count, HD), jnp.float32), pltpu.VMEM((user_rows, HD), jnp.float32)]
        return pl.pallas_call(
            functools.partial(read_kernel, groups, halves, last),
            out_shape=outs,
            in_specs=[vmem] * (6 + len(states)),
            out_specs=[vmem] * len(outs),
            scratch_shapes=scratch,
            compiler_params=params,
            cost_estimate=cost(ROWS, ROWS),
        )(slab_query, user_queries, slab_coef, user_coef, *accs, *states)

    def after(results, values):
        return list(lax.optimization_barrier((results, values))[1])

    def read_whole(offsets, accs):
        groups = [tuple(offsets[i : i + 2]) for i in range(0, len(offsets), 2)]
        return read(groups, [whole[m] for m in offsets], 1, accs, False)

    direct = [1 << bit for bit in outer]
    if later:
        for m, value in zip(direct, after(sides[direct[0]], [whole[m] for m in direct])):
            whole[m] = value
    accs = read_whole([0, 1] + direct, (slab_acc, user_acc))
    for m, value in zip(direct, after(accs[0], [whole[m] for m in direct])):
        whole[m | 1] = swap(value, 0)
    accs = read_whole([m | 1 for m in direct], accs)
    for m in later:
        sides[m | 1] = [swap(piece, 0) for piece in after(accs[0], sides[m])]
    late = [(m, m | 1) for m in later]
    late_states = [piece for group in late for m in group for piece in sides[m]]
    slab_total, user_total, square = read(late, late_states, 2, accs, True)

    squares = lax.all_to_all(square, "head", 0, 0)

    chunk = width // 4
    slab_out, user_out = pl.pallas_call(
        functools.partial(norm_kernel, float(width * head_axis)),
        out_shape=[bf16((token_count, width)), bf16((user_rows, width))],
        grid=(width // chunk,),
        in_specs=[
            pl.BlockSpec((token_count, chunk), lambda i: (0, i)),
            pl.BlockSpec((user_rows, chunk), lambda i: (0, i)),
            pl.BlockSpec((1, chunk), lambda i: (0, i)),
            pl.BlockSpec((head_axis, lines, ROWS), lambda i: (0, 0, 0)),
        ],
        out_specs=[
            pl.BlockSpec((token_count, chunk), lambda i: (0, i)),
            pl.BlockSpec((user_rows, chunk), lambda i: (0, i)),
        ],
        scratch_shapes=[pltpu.VMEM((lines, ROWS, ROWS), jnp.float32)],
        compiler_params=params,
    )(slab_total, user_total, norm_gain.reshape(1, width), squares)
    return slab_out, user_out.reshape(user_count, suffix, width)


def solution(mesh):
    return jax.shard_map(
        local,
        mesh=mesh,
        in_specs=(
            P("seq", "head"),
            P("seq", "head"),
            P("seq", "head"),
            P(None, "head", "seq"),
            P("head"),
            P("seq", None, "head"),
            P("seq", None, "head"),
            P("seq", None, "head"),
            P("seq", None, "head", None),
            P("seq"),
        ),
        out_specs=(P("seq", "head"), P("seq", None, "head")),
        check_vma=False,
    )
```

time: 166 us -> 60.1 us (0.36)
  local copies, waits for them, and re-layouts: 47.9 us -> 10.1 us
  matrix products: 36.4 us -> 0 us
  Pallas kernels: 0 us -> 23.8 us
  waiting for transfers between devices: 35.2 us -> 13.8 us
  other arithmetic: 19.1 us -> 0 us
  between operations: 14.2 us -> 0.71 us
  blocking collectives: 11.7 us -> 0 us
  starting transfers between devices: 0.04 us -> 11.2 us
    dot_general x13 -> x0, matrix products: 36.4 us -> none  [the longest x4 14 us: user_read(): jnp.einsum('kc,chde->khde', user_mask, gathered, preferred_element_type=j...]
    all_gather x1 -> x0, waiting for transfers between devices: 35.2 us -> none  [local(): gathered = lax.all_gather(block_state[None], 'seq', axis=0, tiled=True)]
    pallas_call x0 -> x7, Pallas kernels: none -> 23.8 us  [the longest x1 11.3 us: local(): pl.pallas_call(functools.partial(local_kernel, depth, suffix, chunks), ou...]
    psum x1 -> x0, blocking collectives: 11.7 us -> none  [local(): slab_square, user_square = lax.psum((slab_square, user_square), 'head')]
    convert_element_type x5 -> x0, local copies, waits for them, and re-layouts: 11.3 us -> none  [the longest x4 8.87 us: user_read(): nodes_here = jnp.einsum('kc,chde->khde', user_mask, gathered, preferred_e...]
    reshape x5 -> x1, local copies, waits for them, and re-layouts: 11.2 us -> 0.01 us  [local(): norm_gain.reshape(1, width)]
    unnamed x29 -> x24, local copies, waits for them, and re-layouts: 1.08 us -> 10.1 us
    transpose x4 -> x0, local copies, waits for them, and re-layouts: 8.34 us -> none  [read_prefix(): jnp.einsum('bthd,hdf->bthf', query_rows, merged, preferred_element_type=j...]
  transfers between devices with their start and end apart: 1 -> 10, of which waited for: 1 -> 7; matrix products, arithmetic and copies ran while one was open for 3% -> 0% of each run, Pallas kernels for 0% -> 23%
where the time goes in v2:
time: 60.1 us; the launch traced here: 59.6 us
  Pallas kernels  23.8 us (40%)
  waiting for transfers between devices  13.8 us (23%)
  starting transfers between devices  11.2 us (19%)
  local copies, waits for them, and re-layouts  10.1 us (17%)
  between operations  0.71 us (1%)
    pallas_call x1, Pallas kernels, local(): pl.pallas_call(functools.partial(local_kernel, depth, suffix, chunks), ou...  11.3 us
    unnamed x24, local copies, waits for them, and re-layouts  10.1 us
    ppermute x9, waiting for transfers between devices, swap(): lax.ppermute(value, 'seq', [(i, i ^ 1 << bit) for i in range(seq_count)])  8.24 us
    pallas_call x3, Pallas kernels, read(): pl.pallas_call(functools.partial(read_kernel, groups, halves, last), out_...  6.86 us
    ppermute x9, starting transfers between devices, swap(): lax.ppermute(value, 'seq', [(i, i ^ 1 << bit) for i in range(seq_count)])  6.29 us
    all_to_all x1, waiting for transfers between devices, local(): squares = lax.all_to_all(square, 'head', 0, 0)  5.58 us
    all_to_all x1, starting transfers between devices, local(): squares = lax.all_to_all(square, 'head', 0, 0)  4.87 us
    pallas_call x1, Pallas kernels, local(): pl.pallas_call(functools.partial(state_kernel, chunks), out_shape=bf16((h...  2.7 us
  transfers between devices with their start and end apart: 10, of which 7 were waited for; matrix products, arithmetic and copies ran while one was open for 0% of the time, Pallas kernels for 23%

profile of v2, /device:TPU:0, one launch (start us, length us, event | category | flops | bytes accessed | tf_op | source)
XLA Modules:
  0.0 59.6 jit_solution(16856703855272452938)
XLA Ops:
  0.6 2.7 %shard_map.114.rest_0_ = bf16[16,128,128]{2,1,0:T(8,128)(2,1)} custom-call(bf16[128,2048]{1,0:T(8,128)(2,1)} %key_hbm.1, bf16[128,2048]{1,0:T(8,128)(2,1)} %value_hbm.1), custom_call_target="tpu_custom_call" | custom-call | tf_op jit(solution)/shard_map/pallas_call | solution.py:224
  3.3 3.0 %collective-permute-start.1 = (bf16[16,128,128]{2,1,0:T(8,128)(2,1)}, bf16[16,128,128]{2,1,0:T(8,128)(2,1)S(1)}, u32[]{:S(2)}, u32[]{:S(2)}) collective-permute-start(bf16[16,128,128]{2,1,0:T(8,128)(2,1)} %shard_map.114.rest_0_), channel_id=1, source_target_pairs={{0,8},{4,12},{8,0},{12,4},{16,24},{20,28},{24,16},{28,20},{1,9},{5... | collective-permute-start | bytes 1572872 | tf_op jit(solution)/shard_map/ppermute | solution.py:222
  6.3 1.5 %collective-permute-start.2 = (bf16[16,128,128]{2,1,0:T(8,128)(2,1)}, bf16[16,128,128]{2,1,0:T(8,128)(2,1)S(1)}, u32[]{:S(2)}, u32[]{:S(2)}) collective-permute-start(bf16[16,128,128]{2,1,0:T(8,128)(2,1)} %shard_map.114.rest_0_), channel_id=1, source_target_pairs={{0,16},{4,20},{8,24},{12,28},{16,0},{20,4},{24,8},{28,12},{1,17},{... | collective-permute-start | bytes 1572872 | tf_op jit(solution)/shard_map/ppermute | solution.py:222
  7.9 0.0 collective-permute-start
  7.9 0.0 copy-start.1
  7.9 1.0 %copy-done.1 = bf16[128,2048]{1,0:T(8,128)(2,1)S(1)} copy-done((bf16[128,2048]{1,0:T(8,128)(2,1)S(1)}, bf16[128,2048]{1,0:T(8,128)(2,1)}, u32[]{:S(2)}) %copy-start.1) | copy-done | bytes 524312
  8.9 0.0 copy-start.3
  8.9 1.0 %copy-done.3 = bf16[128,2048]{1,0:T(8,128)(2,1)S(1)} copy-done((bf16[128,2048]{1,0:T(8,128)(2,1)S(1)}, bf16[128,2048]{1,0:T(8,128)(2,1)}, u32[]{:S(2)}) %copy-start.3) | copy-done | bytes 524312
  10.0 0.0 copy-start.8
  10.0 0.9 %copy-done.8 = bf16[4,6,16,64]{3,2,1,0:T(8,128)(2,1)S(1)} copy-done((bf16[4,6,16,64]{3,2,1,0:T(8,128)(2,1)S(1)}, bf16[4,6,16,64]{3,2,1,0:T(8,128)(2,1)}, u32[]{:S(2)}) %copy-start.8) | copy-done | bytes 49176
  10.8 0.0 copy-start.9
  10.8 0.7 %copy-done.9 = bf16[6,16,128]{2,1,0:T(8,128)(2,1)S(1)} copy-done((bf16[6,16,128]{2,1,0:T(8,128)(2,1)S(1)}, bf16[6,16,128]{2,1,0:T(8,128)(2,1)}, u32[]{:S(2)}) %copy-start.9) | copy-done | bytes 24600
  11.6 0.0 copy-start.10
  11.6 0.7 %copy-done.10 = s32[4]{0:T(128)S(1)} copy-done((s32[4]{0:T(128)S(1)}, s32[4]{0:T(128)}, u32[]{:S(2)}) %copy-start.10) | copy-done | bytes 40
  12.2 0.0 copy-start
  12.2 0.0 copy-start.4
  12.2 11.3 %shard_map.113 = (f32[128,2048]{1,0:T(8,128)}, f32[256,2048]{1,0:T(8,128)}, f32[128,144]{1,0:T(8,128)S(1)}, f32[256,144]{1,0:T(8,128)S(1)}) custom-call(s32[4]{0:T(128)S(1)} %copy-done.10, bf16[96,128]{1,0:T(8,128)(2,1)S(1)} %bitcast.11, bf16[4,96,64]{2,1,0:T(8,128)(2,1)S(1)} %bitcast.10, bf16[128,2048]{1,0:T(8,128)(2,1)S(1)} %copy-done.1, ...), custom_call_target="tpu_custom_call" | custom-call | flops 128 | bytes 128 | tf_op jit(solution)/shard_map/pallas_call | solution.py:243
  23.6 0.0 collective-permute-done.1.refs_0_.rest_2_
  23.6 0.0 collective-permute-done.2.refs_1_.rest_3_
  23.6 0.9 %shard_map.115 = (bf16[8,128,128]{2,1,0:T(8,128)(2,1)S(1)}, bf16[8,128,128]{2,1,0:T(8,128)(2,1)}, bf16[8,128,128]{2,1,0:T(8,128)(2,1)}, bf16[8,128,128]{2,1,0:T(8,128)(2,1)S(1)}) custom-call(f32[128,144]{1,0:T(8,128)S(1)} %get-tuple-element.25.order_ref.sc_ref, bf16[16,128,128]{2,1,0:T(8,128)(2,1)S(1)} %collective-permute-done.1.refs_0_.rest_2_, ...), custom_call_target="tpu_custom_call" | custom-call | tf_op jit(solution)/shard_map/pallas_call | solution.py:275
  24.5 0.0 collective-permute-done.rest_1_
  24.5 0.0 copy-done
  24.5 0.0 copy-done.4
  24.5 0.0 copy-start.2
  24.5 1.6 %copy-done.2 = f32[256,2048]{1,0:T(8,128)S(1)} copy-done((f32[256,2048]{1,0:T(8,128)S(1)}, f32[256,2048]{1,0:T(8,128)}, u32[]{:S(2)}) %copy-start.2) | copy-done | bytes 2097176
  26.1 0.0 copy-start.7
  26.1 1.2 %copy-done.7 = f32[128,2048]{1,0:T(8,128)S(1)} copy-done((f32[128,2048]{1,0:T(8,128)S(1)}, f32[128,2048]{1,0:T(8,128)}, u32[]{:S(2)}) %copy-start.7) | copy-done | bytes 1048600
  27.3 3.1 %shard_map.116 = (f32[128,2048]{1,0:T(8,128)S(1)}, f32[256,2048]{1,0:T(8,128)S(1)}) custom-call(bf16[128,2048]{1,0:T(8,128)(2,1)S(1)} %copy-done.1, bf16[256,2048]{1,0:T(8,128)(2,1)S(1)} %bitcast.7, f32[128,144]{1,0:T(8,128)S(1)} %get-tuple-element.25.order_ref.sc_ref, f32[256,144]{1,0:T(8,128)S(1)} %get-tuple-element.26.uc_ref, f32[128,2048]{1,0:T(8,128)S(1)} %copy-done.7, ...), custom_call_target="tpu_custom_call" | custom-call | flops 128 | bytes 128 | tf_op jit(solution)/shard_map/pallas_call | solution.py:294
  30.4 0.6 collective-permute-start.3
  30.9 0.1 collective-permute-start.4
  31.0 0.5 collective-permute-start.5
  31.5 0.1 collective-permute-start.6
  31.6 0.8 %collective-permute-done.3.rest_0_ = bf16[16,128,128]{2,1,0:T(8,128)(2,1)S(1)} collective-permute-done((bf16[16,128,128]{2,1,0:T(8,128)(2,1)S(1)}, bf16[16,128,128]{2,1,0:T(8,128)(2,1)S(1)}, u32[]{:S(2)}, u32[]{:S(2)}) %collective-permute-start.3) | collective-permute-done | bytes 524320 | tf_op jit(solution)/shard_map/ppermute | solution.py:222
  32.5 0.7 %collective-permute-done.4.rest_1_ = bf16[16,128,128]{2,1,0:T(8,128)(2,1)S(1)} collective-permute-done((bf16[16,128,128]{2,1,0:T(8,128)(2,1)S(1)}, bf16[16,128,128]{2,1,0:T(8,128)(2,1)S(1)}, u32[]{:S(2)}, u32[]{:S(2)}) %collective-permute-start.4) | collective-permute-done | bytes 524320 | tf_op jit(solution)/shard_map/ppermute | solution.py:222
  33.2 1.4 %shard_map.117 = (f32[128,2048]{1,0:T(8,128)S(1)}, f32[256,2048]{1,0:T(8,128)S(1)}) custom-call(bf16[128,2048]{1,0:T(8,128)(2,1)S(1)} %copy-done.1, bf16[256,2048]{1,0:T(8,128)(2,1)S(1)} %bitcast.8, f32[128,144]{1,0:T(8,128)S(1)} %get-tuple-element.25.order_ref.sc_ref, f32[256,144]{1,0:T(8,128)S(1)} %get-tuple-element.26.uc_ref, ...), custom_call_target="tpu_custom_call" | custom-call | flops 128 | bytes 128 | tf_op jit(solution)/shard_map/pallas_call | solution.py:294
  34.6 5.0 %collective-permute-done.5.rest_0_ = bf16[8,128,128]{2,1,0:T(8,128)(2,1)S(1)} collective-permute-done((bf16[8,128,128]{2,1,0:T(8,128)(2,1)S(1)}, bf16[8,128,128]{2,1,0:T(8,128)(2,1)S(1)}, u32[]{:S(2)}, u32[]{:S(2)}) %collective-permute-start.5) | collective-permute-done | bytes 262176 | tf_op jit(solution)/shard_map/ppermute | solution.py:222
  39.7 0.2 collective-permute-done.6.rest_1_
  39.9 0.0 collective-permute-start.7
  39.9 0.5 collective-permute-start.8
  40.4 1.0 %collective-permute-done.7.rest_2_ = bf16[8,128,128]{2,1,0:T(8,128)(2,1)S(1)} collective-permute-done((bf16[8,128,128]{2,1,0:T(8,128)(2,1)S(1)}, bf16[8,128,128]{2,1,0:T(8,128)(2,1)S(1)}, u32[]{:S(2)}, u32[]{:S(2)}) %collective-permute-start.7) | collective-permute-done | bytes 262176 | tf_op jit(solution)/shard_map/ppermute | solution.py:222
  41.4 0.4 collective-permute-done.8.rest_3_
  41.8 2.4 %shard_map.118 = (f32[128,2048]{1,0:T(8,128)S(1)}, f32[256,2048]{1,0:T(8,128)S(1)}, f32[4,3,128]{2,1,0:T(4,128)}) custom-call(bf16[128,2048]{1,0:T(8,128)(2,1)S(1)} %copy-done.1, bf16[256,2048]{1,0:T(8,128)(2,1)S(1)} %bitcast.9, f32[128,144]{1,0:T(8,128)S(1)} %get-tuple-element.25.order_ref.sc_ref, f32[256,144]{1,0:T(8,128)S(1)} %get-tuple-element.26.uc_ref, ...), custom_call_target="tpu_custom_call" | custom-call | flops 128 | bytes 128 | tf_op jit(solution)/shard_map/pallas_call | solution.py:294
  44.2 1.3 %copy-done.5 = f32[256,2048]{1,0:T(8,128)} copy-done((f32[256,2048]{1,0:T(8,128)}, f32[256,2048]{1,0:T(8,128)S(1)}, u32[]{:S(2)}) %copy-start.5) | copy-done | bytes 2097176
  45.5 4.9 %all-to-all-start = ((f32[4,3,128]{2,1,0:T(4,128)}), f32[4,3,128]{2,1,0:T(4,128)S(1)}, u32[]{:S(2)}, u32[]{:S(2)}) async-start(f32[4,3,128]{2,1,0:T(4,128)} %get-tuple-element.45), calls=%async_computation | async-start | bytes 16384 | tf_op jit(solution)/shard_map/all_to_all | solution.py:325
  50.4 0.0 copy-done.11
  50.4 5.6 %all-to-all-done.square_ref = f32[4,3,128]{2,1,0:T(4,128)S(1)} async-done(((f32[4,3,128]{2,1,0:T(4,128)}), f32[4,3,128]{2,1,0:T(4,128)S(1)}, u32[]{:S(2)}, u32[]{:S(2)}) %all-to-all-start) | async-done | bytes 6176 | tf_op jit(solution)/shard_map/all_to_all | solution.py:325
  56.0 1.6 %copy-done.6 = f32[256,2048]{1,0:T(8,128)S(1)} copy-done((f32[256,2048]{1,0:T(8,128)S(1)}, f32[256,2048]{1,0:T(8,128)}, u32[]{:S(2)}) %copy-start.6) | copy-done | bytes 2097176
  57.6 2.1 %shard_map.119 = (bf16[128,2048]{1,0:T(8,128)(2,1)}, bf16[256,2048]{1,0:T(8,128)(2,1)}) custom-call(f32[128,2048]{1,0:T(8,128)S(1)} %get-tuple-element.43.st_ref, f32[256,2048]{1,0:T(8,128)S(1)} %copy-done.6, bf16[1,2048]{1,0:T(2,128)(2,1)S(1)} %reshape.30.gain_ref, f32[4,3,128]{2,1,0:T(4,128)S(1)} %all-to-all-done.square_ref), custom_call_target="tpu_custom_call" | custom-call | tf_op jit(solution)/shard_map/pallas_call | solution.py:328
  (4 shorter events, 0.0 us)
Async XLA Ops:
  3.3 20.2 %collective-permute-start.1 = (bf16[16,128,128]{2,1,0:T(8,128)(2,1)}, bf16[16,128,128]{2,1,0:T(8,128)(2,1)S(1)}, u32[]{:S(2)}, u32[]{:S(2)}) collective-permute-start(bf16[16,128,128]{2,1,0:T(8,128)(2,1)} %shard_map.114.rest_0_), channel_id=1, source_target_pairs={{0,8},{4,12},{8,0},{12,4},{16,24},{20,28},{24,16},{28,20},{1,9},{5... | collective-permute-start | bytes 1572872 | tf_op jit(solution)/shard_map/ppermute | solution.py:222
  6.3 17.2 %collective-permute-start.2 = (bf16[16,128,128]{2,1,0:T(8,128)(2,1)}, bf16[16,128,128]{2,1,0:T(8,128)(2,1)S(1)}, u32[]{:S(2)}, u32[]{:S(2)}) collective-permute-start(bf16[16,128,128]{2,1,0:T(8,128)(2,1)} %shard_map.114.rest_0_), channel_id=1, source_target_pairs={{0,16},{4,20},{8,24},{12,28},{16,0},{20,4},{24,8},{28,12},{1,17},{... | collective-permute-start | bytes 1572872 | tf_op jit(solution)/shard_map/ppermute | solution.py:222
  7.9 16.6 %collective-permute-start = (bf16[16,128,128]{2,1,0:T(8,128)(2,1)}, bf16[16,128,128]{2,1,0:T(8,128)(2,1)S(1)}, u32[]{:S(2)}, u32[]{:S(2)}) collective-permute-start(bf16[16,128,128]{2,1,0:T(8,128)(2,1)} %shard_map.114.rest_0_), channel_id=1, source_target_pairs={{0,4},{4,0},{8,12},{12,8},{16,20},{20,16},{24,28},{28,24},{1,5},{5... | collective-permute-start | bytes 1572872 | tf_op jit(solution)/shard_map/ppermute | solution.py:222
  7.9 1.0 %copy-start.1 = (bf16[128,2048]{1,0:T(8,128)(2,1)S(1)}, bf16[128,2048]{1,0:T(8,128)(2,1)}, u32[]{:S(2)}) copy-start(bf16[128,2048]{1,0:T(8,128)(2,1)} %sq_ref.5) | copy-start | bytes 1572868
  8.9 1.0 %copy-start.3 = (bf16[128,2048]{1,0:T(8,128)(2,1)S(1)}, bf16[128,2048]{1,0:T(8,128)(2,1)}, u32[]{:S(2)}) copy-start(bf16[128,2048]{1,0:T(8,128)(2,1)} %key_hbm.1) | copy-start | bytes 1572868
  10.0 0.9 %copy-start.8 = (bf16[4,6,16,64]{3,2,1,0:T(8,128)(2,1)S(1)}, bf16[4,6,16,64]{3,2,1,0:T(8,128)(2,1)}, u32[]{:S(2)}) copy-start(bf16[4,6,16,64]{3,2,1,0:T(8,128)(2,1)} %param.18) | copy-start | bytes 147460
  10.8 0.7 %copy-start.9 = (bf16[6,16,128]{2,1,0:T(8,128)(2,1)S(1)}, bf16[6,16,128]{2,1,0:T(8,128)(2,1)}, u32[]{:S(2)}) copy-start(bf16[6,16,128]{2,1,0:T(8,128)(2,1)} %param.13) | copy-start | bytes 73732
  11.6 0.7 %copy-start.10 = (s32[4]{0:T(128)S(1)}, s32[4]{0:T(128)}, u32[]{:S(2)}) copy-start(s32[4]{0:T(128)} %length_ref.1) | copy-start | bytes 52
  12.2 12.2 %copy-start = (bf16[4,64,2048]{2,1,0:T(8,128)(2,1)S(1)}, bf16[4,64,2048]{2,1,0:T(8,128)(2,1)}, u32[]{:S(2)}) copy-start(bf16[4,64,2048]{2,1,0:T(8,128)(2,1)} %param.15) | copy-start | bytes 3145732
  12.2 12.2 %copy-start.4 = (bf16[16,128,128]{2,1,0:T(8,128)(2,1)S(1)}, bf16[16,128,128]{2,1,0:T(8,128)(2,1)}, u32[]{:S(2)}) copy-start(bf16[16,128,128]{2,1,0:T(8,128)(2,1)} %shard_map.114.rest_0_) | copy-start | bytes 1572868
  24.5 1.6 %copy-start.2 = (f32[256,2048]{1,0:T(8,128)S(1)}, f32[256,2048]{1,0:T(8,128)}, u32[]{:S(2)}) copy-start(f32[256,2048]{1,0:T(8,128)} %get-tuple-element.28.ua_ref) | copy-start | bytes 6291460
  26.1 1.2 %copy-start.7 = (f32[128,2048]{1,0:T(8,128)S(1)}, f32[128,2048]{1,0:T(8,128)}, u32[]{:S(2)}) copy-start(f32[128,2048]{1,0:T(8,128)} %get-tuple-element.27.sa_ref) | copy-start | bytes 3145732
  30.4 2.1 %collective-permute-start.3 = (bf16[16,128,128]{2,1,0:T(8,128)(2,1)S(1)}, bf16[16,128,128]{2,1,0:T(8,128)(2,1)S(1)}, u32[]{:S(2)}, u32[]{:S(2)}) collective-permute-start(bf16[16,128,128]{2,1,0:T(8,128)(2,1)S(1)} %collective-permute-done.1.refs_0_.rest_2_), channel_id=1, source_target_pairs={{0,4},{4,0},{8,12},{12,8},{16,20},{20,16},{24,28},{28,24},{1,5},{5... | collective-permute-start | bytes 1572872 | tf_op jit(solution)/shard_map/ppermute | solution.py:222
  30.9 2.3 %collective-permute-start.4 = (bf16[16,128,128]{2,1,0:T(8,128)(2,1)S(1)}, bf16[16,128,128]{2,1,0:T(8,128)(2,1)S(1)}, u32[]{:S(2)}, u32[]{:S(2)}) collective-permute-start(bf16[16,128,128]{2,1,0:T(8,128)(2,1)S(1)} %collective-permute-done.2.refs_1_.rest_3_), channel_id=1, source_target_pairs={{0,4},{4,0},{8,12},{12,8},{16,20},{20,16},{24,28},{28,24},{1,5},{5... | collective-permute-start | bytes 1572872 | tf_op jit(solution)/shard_map/ppermute | solution.py:222
  31.0 8.7 %collective-permute-start.5 = (bf16[8,128,128]{2,1,0:T(8,128)(2,1)S(1)}, bf16[8,128,128]{2,1,0:T(8,128)(2,1)S(1)}, u32[]{:S(2)}, u32[]{:S(2)}) collective-permute-start(bf16[8,128,128]{2,1,0:T(8,128)(2,1)S(1)} %get-tuple-element.31), channel_id=1, source_target_pairs={{0,16},{4,20},{8,24},{12,28},{16,0},{20,4},{24,8},{28,12},{1,17},{... | collective-permute-start | bytes 786440 | tf_op jit(solution)/shard_map/ppermute | solution.py:222
  31.5 8.4 %collective-permute-start.6 = (bf16[8,128,128]{2,1,0:T(8,128)(2,1)S(1)}, bf16[8,128,128]{2,1,0:T(8,128)(2,1)S(1)}, u32[]{:S(2)}, u32[]{:S(2)}) collective-permute-start(bf16[8,128,128]{2,1,0:T(8,128)(2,1)S(1)} %get-tuple-element.40), channel_id=1, source_target_pairs={{0,8},{4,12},{8,0},{12,4},{16,24},{20,28},{24,16},{28,20},{1,9},{5... | collective-permute-start | bytes 786440 | tf_op jit(solution)/shard_map/ppermute | solution.py:222
  39.9 1.5 %collective-permute-start.7 = (bf16[8,128,128]{2,1,0:T(8,128)(2,1)S(1)}, bf16[8,128,128]{2,1,0:T(8,128)(2,1)S(1)}, u32[]{:S(2)}, u32[]{:S(2)}) collective-permute-start(bf16[8,128,128]{2,1,0:T(8,128)(2,1)S(1)} %collective-permute-done.5.rest_0_), channel_id=1, source_target_pairs={{0,4},{4,0},{8,12},{12,8},{16,20},{20,16},{24,28},{28,24},{1,5},{5... | collective-permute-start | bytes 786440 | tf_op jit(solution)/shard_map/ppermute | solution.py:222
  39.9 1.9 %collective-permute-start.8 = (bf16[8,128,128]{2,1,0:T(8,128)(2,1)S(1)}, bf16[8,128,128]{2,1,0:T(8,128)(2,1)S(1)}, u32[]{:S(2)}, u32[]{:S(2)}) collective-permute-start(bf16[8,128,128]{2,1,0:T(8,128)(2,1)S(1)} %collective-permute-done.6.rest_1_), channel_id=1, source_target_pairs={{0,4},{4,0},{8,12},{12,8},{16,20},{20,16},{24,28},{28,24},{1,5},{5... | collective-permute-start | bytes 786440 | tf_op jit(solution)/shard_map/ppermute | solution.py:222
  41.8 8.6 %copy-start.11 = (bf16[2048]{0:T(1024)(128)(2,1)S(1)}, bf16[2048]{0:T(1024)(128)(2,1)}, u32[]{:S(2)}) copy-start(bf16[2048]{0:T(1024)(128)(2,1)} %param.14) | copy-start | bytes 12292
  44.2 1.3 %copy-start.5 = (f32[256,2048]{1,0:T(8,128)}, f32[256,2048]{1,0:T(8,128)S(1)}, u32[]{:S(2)}) copy-start(f32[256,2048]{1,0:T(8,128)S(1)} %get-tuple-element.44.ut_ref) | copy-start | bytes 6291460
  45.5 10.5 %all-to-all-start = ((f32[4,3,128]{2,1,0:T(4,128)}), f32[4,3,128]{2,1,0:T(4,128)S(1)}, u32[]{:S(2)}, u32[]{:S(2)}) async-start(f32[4,3,128]{2,1,0:T(4,128)} %get-tuple-element.45), calls=%async_computation | async-start | bytes 16384 | tf_op jit(solution)/shard_map/all_to_all | solution.py:325
  56.0 1.6 %copy-start.6 = (f32[256,2048]{1,0:T(8,128)S(1)}, f32[256,2048]{1,0:T(8,128)}, u32[]{:S(2)}) copy-start(f32[256,2048]{1,0:T(8,128)} %copy-done.5) | copy-start | bytes 6291460

commit v3 on v2

--- a/solution.py
+++ b/solution.py
@@ -11,8 +11,6 @@
 HD = 128
 ROWS = 128
 VMEM_BYTES = 20 * 1024 * 1024
-STATE_VMEM_BYTES = 62 * 1024 * 1024
-LOCAL_VMEM_BYTES = 52 * 1024 * 1024
 
 
 def matmul(a, b, contract):
@@ -48,11 +46,11 @@
         out_ref[head] = state.astype(jnp.bfloat16)
 
 
-def split_kernel(count, half, order_ref, *refs):
-    for i in range(count):
+def split_kernel(picks, order_ref, *refs):
+    for (i, side), out_ref in zip(picks, refs[len(refs) - len(picks) :]):
+        half = out_ref.shape[0]
         for head in range(half):
-            refs[count + 2 * i][head] = refs[i][head]
-            refs[count + 2 * i + 1][head] = refs[i][half + head]
+            out_ref[head] = refs[i][side * half + head]
 
 
 def choose_levels(target, position, depth, level_count, head_count):
@@ -74,10 +72,20 @@
     return jnp.where(jnp.logical_and(chosen, same), 1.0, 0.0).astype(jnp.bfloat16)
 
 
-def local_kernel(depth, suffix, chunks, length_ref, sw_ref, uw_ref, *rest):
-    sources, (so_ref, uo_ref, sc_ref, uc_ref), loaded, sems = rest[:6], rest[6:10], rest[10:16], rest[16]
+def local_kernel(depth, suffix, chunks, *refs):
+    small, sources, (so_ref, uo_ref, sc_ref, uc_ref) = refs[:3], refs[3:9], refs[9:13]
+    small_loaded, loaded, small_sems, sems = refs[13:16], refs[16:22], refs[22], refs[23]
+    length_ref, sw_ref, uw_ref = small_loaded
     sq_ref, sk_ref, sv_ref, uq_ref, uk_ref, uv_ref = loaded
+    small_copies = [
+        pltpu.make_async_copy(source, target, small_sems.at[i])
+        for i, (source, target) in enumerate(zip(small, small_loaded))
+    ]
+    for copy in small_copies:
+        copy.start()
     wait = load_columns(sources, loaded, sems, chunks)
+    for copy in small_copies:
+        copy.wait()
     head_count = sq_ref.shape[1] // HD
     level_count = sw_ref.shape[0] // head_count
     position = lax.axis_index("seq").astype(jnp.int32)
@@ -94,17 +102,23 @@
     causal = row >= col
     within = jnp.logical_and(causal, row // suffix == col // suffix)
     parts = [(sq_ref, sk_ref, sv_ref, sc_ref, so_ref, causal), (uq_ref, uk_ref, uv_ref, uc_ref, uo_ref, within)]
-    for head in range(head_count):
-        if head % (head_count // chunks) == 0:
-            wait(head // (head_count // chunks))
-        cols = slice(head * HD, (head + 1) * HD)
-        for q_ref, k_ref, v_ref, c_ref, o_ref, mask in parts:
-            for start in range(0, q_ref.shape[0], ROWS):
-                rows = slice(start, start + ROWS)
-                scores = matmul(q_ref[rows, cols], k_ref[rows, cols], ((1,), (1,)))
-                scores = jnp.where(mask, scores, 0.0).astype(jnp.bfloat16)
-                result = matmul(scores, v_ref[rows, cols], ((1,), (0,)))
-                o_ref[rows, cols] = result * c_ref[rows, own + head : own + head + 1]
+    step = 2
+    for first in range(0, head_count, step):
+        if first % (head_count // chunks) == 0:
+            wait(first // (head_count // chunks))
+        units = [
+            (head, slice(head * HD, (head + 1) * HD), slice(start, start + ROWS), part)
+            for head in range(first, first + step)
+            for part in parts
+            for start in range(0, part[0].shape[0], ROWS)
+        ]
+        scores = [matmul(part[0][rows, cols], part[1][rows, cols], ((1,), (1,))) for _, cols, rows, part in units]
+        scores = [jnp.where(unit[3][5], score, 0.0).astype(jnp.bfloat16) for unit, score in zip(units, scores)]
+        results = [
+            matmul(score, part[2][rows, cols], ((1,), (0,))) for score, (_, cols, rows, part) in zip(scores, units)
+        ]
+        for result, (head, cols, rows, part) in zip(results, units):
+            part[4][rows, cols] = result * part[3][rows, own + head : own + head + 1]
 
 
 def add_blocks(groups, state_refs, head_count, head, q_ref, c_ref, base):
@@ -154,32 +168,31 @@
         for acc_ref in rest[used + 3 : used + 5]:
             for start in range(0, acc_ref.shape[0], ROWS):
                 turned = jnp.transpose(acc_ref[start : start + ROWS])
-                value = jnp.sum(turned, axis=0, keepdims=True)
-                for copy in range(square_ref.shape[0]):
-                    square_ref[copy, line : line + 1] = value
+                square_ref[line : line + 1] = jnp.sum(turned, axis=0, keepdims=True)
                 line += 1
 
 
-def norm_kernel(features, st_ref, ut_ref, gain_ref, square_ref, so_ref, uo_ref, scale_ref):
-    @pl.when(pl.program_id(0) == 0)
-    def _():
-        total = square_ref[0]
-        for part in range(1, square_ref.shape[0]):
-            total = total + square_ref[part]
-        scale = lax.rsqrt(total / features + 1e-06)
-        for line in range(scale.shape[0]):
-            spread = jnp.broadcast_to(scale[line : line + 1], (ROWS, ROWS))
-            scale_ref[line] = jnp.transpose(spread)
-
-    gain = gain_ref[...].astype(jnp.float32)
-    line = 0
-    for t_ref, o_ref in ((st_ref, so_ref), (ut_ref, uo_ref)):
-        for start in range(0, t_ref.shape[0], ROWS):
-            rows = slice(start, start + ROWS)
-            for low in range(0, t_ref.shape[1], HD):
-                cols = slice(low, low + HD)
-                o_ref[rows, cols] = (t_ref[rows, cols] * scale_ref[line] * gain[:, cols]).astype(jnp.bfloat16)
-            line += 1
+def norm_kernel(features, chunks, st_ref, ut_ref, gain_ref, one_ref, two_ref, so_hbm, uo_hbm, so_ref, uo_ref, sems):
+    square = one_ref[...] + two_ref[...]
+    scale = lax.rsqrt(square / features + 1e-06)
+    scales = [jnp.transpose(jnp.broadcast_to(scale[line : line + 1], (ROWS, ROWS))) for line in range(scale.shape[0])]
+    size = st_ref.shape[1] // chunks
+    copies = []
+    for chunk in range(chunks):
+        line = 0
+        wide = pl.ds(chunk * size, size)
+        for side, (t_ref, o_ref, o_hbm) in enumerate(((st_ref, so_ref, so_hbm), (ut_ref, uo_ref, uo_hbm))):
+            for start in range(0, t_ref.shape[0], ROWS):
+                rows = slice(start, start + ROWS)
+                for low in range(chunk * size, (chunk + 1) * size, HD):
+                    cols = slice(low, low + HD)
+                    gain = gain_ref[:, cols].astype(jnp.float32)
+                    o_ref[rows, cols] = (t_ref[rows, cols] * scales[line] * gain).astype(jnp.bfloat16)
+                line += 1
+            copies.append(pltpu.make_async_copy(o_ref.at[:, wide], o_hbm.at[:, wide], sems.at[side, chunk]))
+            copies[-1].start()
+    for copy in copies:
+        copy.wait()
 
 
 def local(
@@ -204,17 +217,16 @@
     user_rows = user_count * suffix
     lines = (token_count + user_rows) // ROWS
     params = pltpu.CompilerParams(vmem_limit_bytes=VMEM_BYTES)
-    state_params = pltpu.CompilerParams(vmem_limit_bytes=STATE_VMEM_BYTES)
-    local_params = pltpu.CompilerParams(vmem_limit_bytes=LOCAL_VMEM_BYTES)
-    f32 = functools.partial(jax.ShapeDtypeStruct, dtype=jnp.float32)
     bf16 = functools.partial(jax.ShapeDtypeStruct, dtype=jnp.bfloat16)
     vmem = pl.BlockSpec(memory_space=pltpu.VMEM)
-    smem = pl.BlockSpec(memory_space=pltpu.SMEM)
     anywhere = pl.BlockSpec(memory_space=pl.ANY)
     hbm = pl.BlockSpec(memory_space=pltpu.HBM)
     chunks = min(4, half)
     rows_cost = 2 * width * (token_count + user_rows)
 
+    def pinned(*arrays):
+        return [pltpu.with_memory_space_constraint(array, pltpu.HBM) for array in arrays]
+
     def cost(flops, moved):
         return pl.CostEstimate(flops=flops, bytes_accessed=moved, transcendentals=0)
 
@@ -223,12 +235,12 @@
 
     state = pl.pallas_call(
         functools.partial(state_kernel, chunks),
-        out_shape=bf16((head_count, HD, HD)),
+        out_shape=pltpu.VMEM((head_count, HD, HD), jnp.bfloat16),
         in_specs=[hbm] * 2,
         out_specs=vmem,
         scratch_shapes=[pltpu.VMEM((token_count, width), jnp.bfloat16)] * 2 + [pltpu.SemaphoreType.DMA((2, chunks))],
-        compiler_params=state_params,
-    )(slab_key, slab_value)
+        compiler_params=params,
+    )(*pinned(slab_key, slab_value))
 
     outer = list(range(1, depth))
     whole = {0: state}
@@ -239,32 +251,32 @@
     user_queries = user_query.reshape(user_rows, width)
     user_keys = user_key.reshape(user_rows, width)
     user_values = user_value.reshape(user_rows, width)
+    slab_table = slab_levels.reshape(-1, token_count)
+    user_table = user_levels.reshape(user_count, -1, suffix)
     columns = (seq_count + 1) * head_count
     slab_acc, user_acc, slab_coef, user_coef = pl.pallas_call(
         functools.partial(local_kernel, depth, suffix, chunks),
         out_shape=[
-            f32((token_count, width)),
-            f32((user_rows, width)),
-            f32((token_count, columns)),
-            f32((user_rows, columns)),
+            pltpu.VMEM((token_count, width), jnp.float32),
+            pltpu.VMEM((user_rows, width), jnp.float32),
+            pltpu.VMEM((token_count, columns), jnp.float32),
+            pltpu.VMEM((user_rows, columns), jnp.float32),
         ],
-        in_specs=[smem] + [vmem] * 2 + [hbm] * 6,
+        in_specs=[hbm] * 9,
         out_specs=[vmem] * 4,
-        scratch_shapes=[pltpu.VMEM((token_count, width), jnp.bfloat16)] * 3
+        scratch_shapes=[
+            pltpu.SMEM((user_count,), jnp.int32),
+            pltpu.VMEM(slab_table.shape, jnp.bfloat16),
+            pltpu.VMEM(user_table.shape, jnp.bfloat16),
+        ]
+        + [pltpu.VMEM((token_count, width), jnp.bfloat16)] * 3
         + [pltpu.VMEM((user_rows, width), jnp.bfloat16)] * 3
-        + [pltpu.SemaphoreType.DMA((6, chunks))],
-        compiler_params=local_params,
+        + [pltpu.SemaphoreType.DMA((3,)), pltpu.SemaphoreType.DMA((6, chunks))],
+        compiler_params=params,
         cost_estimate=cost(ROWS, ROWS),
     )(
-        prefix_lengths,
-        slab_levels.reshape(-1, token_count),
-        user_levels.reshape(user_count, -1, suffix),
-        slab_query,
-        slab_key,
-        slab_value,
-        user_queries,
-        user_keys,
-        user_values,
+        *pinned(prefix_lengths, slab_table, user_table),
+        *pinned(slab_query, slab_key, slab_value, user_queries, user_keys, user_values),
     )
 
     sides = {}
@@ -272,24 +284,27 @@
     for bit, value in zip(outer, received):
         whole[1 << bit] = value
     if len(outer) > 1:
+        picks = [(i, 0) for i in range(len(outer) - 1)] + [(i, 1) for i in range(1, len(outer))]
         split = pl.pallas_call(
-            functools.partial(split_kernel, len(outer), half),
-            out_shape=[bf16((half, HD, HD))] * (2 * len(outer)),
+            functools.partial(split_kernel, picks),
+            out_shape=[pltpu.VMEM((half, HD, HD), jnp.bfloat16)] * len(picks),
             in_specs=[anywhere] + [vmem] * len(outer),
-            out_specs=[vmem] * (2 * len(outer)),
+            out_specs=[vmem] * len(picks),
             compiler_params=params,
         )(slab_coef, *received)
-        for i, bit in enumerate(outer):
-            sides[1 << bit] = [split[2 * i], split[2 * i + 1]]
+        for bit in outer:
+            sides[1 << bit] = [None, None]
+        for (i, side), value in zip(picks, split):
+            sides[1 << outer[i]][side] = value
     later = sorted((m for m in range(0, seq_count, 2) if m.bit_count() > 1), key=lambda m: m.bit_count())
     for m in later:
         high, low = m.bit_length() - 1, (m & -m).bit_length() - 1
         sides[m] = [swap(sides[m ^ (1 << high)][0], high), swap(sides[m ^ (1 << low)][1], low)]
     def read(groups, states, halves, accs, last):
-        outs = [f32((token_count, width)), f32((user_rows, width))]
+        outs = [pltpu.VMEM((token_count, width), jnp.float32), pltpu.VMEM((user_rows, width), jnp.float32)]
         scratch = []
         if last:
-            outs.append(f32((head_axis, lines, ROWS)))
+            outs.append(pltpu.VMEM((lines, ROWS), jnp.float32))
             scratch = [pltpu.VMEM((token_count, HD), jnp.float32), pltpu.VMEM((user_rows, HD), jnp.float32)]
         return pl.pallas_call(
             functools.partial(read_kernel, groups, halves, last),
@@ -310,11 +325,11 @@
 
     direct = [1 << bit for bit in outer]
     if later:
-        for m, value in zip(direct, after(sides[direct[0]], [whole[m] for m in direct])):
+        for m, value in zip(direct, after(split, [whole[m] for m in direct])):
             whole[m] = value
+    for m in direct:
+        whole[m | 1] = swap(whole[m], 0)
     accs = read_whole([0, 1] + direct, (slab_acc, user_acc))
-    for m, value in zip(direct, after(accs[0], [whole[m] for m in direct])):
-        whole[m | 1] = swap(value, 0)
     accs = read_whole([m | 1 for m in direct], accs)
     for m in later:
         sides[m | 1] = [swap(piece, 0) for piece in after(accs[0], sides[m])]
@@ -322,26 +337,23 @@
     late_states = [piece for group in late for m in group for piece in sides[m]]
     slab_total, user_total, square = read(late, late_states, 2, accs, True)
 
-    squares = lax.all_to_all(square, "head", 0, 0)
-
-    chunk = width // 4
+    mate = jnp.zeros_like(square)
+    for bit in range(head_axis.bit_length() - 1):
+        square = square + mate
+        mate = lax.ppermute(square, "head", [(i, i ^ (1 << bit)) for i in range(head_axis)])
+
     slab_out, user_out = pl.pallas_call(
-        functools.partial(norm_kernel, float(width * head_axis)),
+        functools.partial(norm_kernel, float(width * head_axis), chunks),
         out_shape=[bf16((token_count, width)), bf16((user_rows, width))],
-        grid=(width // chunk,),
-        in_specs=[
-            pl.BlockSpec((token_count, chunk), lambda i: (0, i)),
-            pl.BlockSpec((user_rows, chunk), lambda i: (0, i)),
-            pl.BlockSpec((1, chunk), lambda i: (0, i)),
-            pl.BlockSpec((head_axis, lines, ROWS), lambda i: (0, 0, 0)),
+        in_specs=[vmem] * 5,
+        out_specs=[hbm] * 2,
+        scratch_shapes=[
+            pltpu.VMEM((token_count, width), jnp.bfloat16),
+            pltpu.VMEM((user_rows, width), jnp.bfloat16),
+            pltpu.SemaphoreType.DMA((2, chunks)),
         ],
-        out_specs=[
-            pl.BlockSpec((token_count, chunk), lambda i: (0, i)),
-            pl.BlockSpec((user_rows, chunk), lambda i: (0, i)),
-        ],
-        scratch_shapes=[pltpu.VMEM((lines, ROWS, ROWS), jnp.float32)],
         compiler_params=params,
-    )(slab_total, user_total, norm_gain.reshape(1, width), squares)
+    )(slab_total, user_total, norm_gain.reshape(1, width), square, mate)
     return slab_out, user_out.reshape(user_count, suffix, width)
 
 

time: 60.1 us -> 42.6 us (0.71)
  local copies, waits for them, and re-layouts: 10.1 us -> 0.02 us
  Pallas kernels: 23.8 us -> 15.8 us
  starting transfers between devices: 11.2 us -> 11.9 us
    unnamed x24 -> x6, local copies, waits for them, and re-layouts: 10.1 us -> 0.01 us
    all_to_all x1 -> x0, waiting for transfers between devices: 5.58 us -> none  [local(): squares = lax.all_to_all(square, 'head', 0, 0)]
    pallas_call x1, Pallas kernels: 11.3 us -> 6.25 us  [local(): pl.pallas_call(functools.partial(local_kernel, depth, suffix, chunks), ou...]
    all_to_all x1 -> x0, starting transfers between devices: 4.87 us -> none  [local(): squares = lax.all_to_all(square, 'head', 0, 0)]
    ppermute x0 -> x2, starting transfers between devices: none -> 4.23 us  [local(): lax.ppermute(square, 'head', [(i, i ^ 1 << bit) for i in range(head_axis)])]
    ppermute x0 -> x2, waiting for transfers between devices: none -> 3.89 us  [local(): lax.ppermute(square, 'head', [(i, i ^ 1 << bit) for i in range(head_axis)])]
    pallas_call x3, Pallas kernels: 5.63 us -> 3.48 us  [the longest x1 1.91 us: local(): pl.pallas_call(functools.partial(state_kernel, chunks), out_shape=pltpu.V...]
    ppermute x9, waiting for transfers between devices: 8.24 us -> 10.1 us  [swap(): lax.ppermute(value, 'seq', [(i, i ^ 1 << bit) for i in range(seq_count)])]
  transfers between devices with their start and end apart: 10 -> 11, of which waited for: 7 -> 8; matrix products, arithmetic and copies ran while one was open for 0% -> 0% of each run, Pallas kernels for 23% -> 25%
where the time goes in v3:
time: 42.6 us; the launch traced here: 42.4 us
  Pallas kernels  15.8 us (37%)
  waiting for transfers between devices  14 us (33%)
  starting transfers between devices  11.9 us (28%)
  between operations  0.7 us (2%)
    ppermute x9, waiting for transfers between devices, swap(): lax.ppermute(value, 'seq', [(i, i ^ 1 << bit) for i in range(seq_count)])  10.1 us
    ppermute x9, starting transfers between devices, swap(): lax.ppermute(value, 'seq', [(i, i ^ 1 << bit) for i in range(seq_count)])  7.66 us
    pallas_call x1, Pallas kernels, local(): pl.pallas_call(functools.partial(local_kernel, depth, suffix, chunks), ou...  6.25 us
    pallas_call x3, Pallas kernels, read(): pl.pallas_call(functools.partial(read_kernel, groups, halves, last), out_...  6.07 us
    ppermute x2, starting transfers between devices, local(): lax.ppermute(square, 'head', [(i, i ^ 1 << bit) for i in range(head_axis)])  4.23 us
    ppermute x2, waiting for transfers between devices, local(): lax.ppermute(square, 'head', [(i, i ^ 1 << bit) for i in range(head_axis)])  3.89 us
    pallas_call x1, Pallas kernels, local(): pl.pallas_call(functools.partial(state_kernel, chunks), out_shape=pltpu.V...  1.91 us
    pallas_call x1, Pallas kernels, local(): pl.pallas_call(functools.partial(norm_kernel, float(width * head_axis), c...  1.53 us
  transfers between devices with their start and end apart: 11, of which 8 were waited for; matrix products, arithmetic and copies ran while one was open for 0% of the time, Pallas kernels for 25%

profile of v3, /device:TPU:0, one launch (start us, length us, event | category | flops | bytes accessed | tf_op | source)
XLA Modules:
  0.0 42.4 jit_solution(8980563231064846415)
XLA Ops:
  0.6 1.9 %shard_map.114.rest_0_ = bf16[16,128,128]{2,1,0:T(8,128)(2,1)S(1)} custom-call(bf16[128,2048]{1,0:T(8,128)(2,1)} %key_hbm.1, bf16[128,2048]{1,0:T(8,128)(2,1)} %value_hbm.1), custom_call_target="tpu_custom_call" | custom-call | tf_op jit(solution)/shard_map/pallas_call | solution.py:236
  2.5 3.0 %collective-permute-start.1 = (bf16[16,128,128]{2,1,0:T(8,128)(2,1)S(1)}, bf16[16,128,128]{2,1,0:T(8,128)(2,1)S(1)}, u32[]{:S(2)}, u32[]{:S(2)}) collective-permute-start(bf16[16,128,128]{2,1,0:T(8,128)(2,1)S(1)} %shard_map.114.rest_0_), channel_id=1, source_target_pairs={{0,8},{4,12},{8,0},{12,4},{16,24},{20,28},{24,16},{28,20},{1,9},{5... | collective-permute-start | bytes 1572872 | tf_op jit(solution)/shard_map/ppermute | solution.py:234
  5.6 1.5 %collective-permute-start.2 = (bf16[16,128,128]{2,1,0:T(8,128)(2,1)S(1)}, bf16[16,128,128]{2,1,0:T(8,128)(2,1)S(1)}, u32[]{:S(2)}, u32[]{:S(2)}) collective-permute-start(bf16[16,128,128]{2,1,0:T(8,128)(2,1)S(1)} %shard_map.114.rest_0_), channel_id=1, source_target_pairs={{0,16},{4,20},{8,24},{12,28},{16,0},{20,4},{24,8},{28,12},{1,17},{... | collective-permute-start | bytes 1572872 | tf_op jit(solution)/shard_map/ppermute | solution.py:234
  7.1 0.0 collective-permute-start
  7.1 0.0 copy-start
  7.1 0.0 copy-start.1
  7.1 6.3 %shard_map.113 = (f32[128,2048]{1,0:T(8,128)S(1)}, f32[256,2048]{1,0:T(8,128)S(1)}, f32[128,144]{1,0:T(8,128)S(1)}, f32[256,144]{1,0:T(8,128)S(1)}) custom-call(s32[4]{0:T(128)} %refs_0_.1, bf16[96,128]{1,0:T(8,128)(2,1)} %bitcast.13, bf16[4,96,64]{2,1,0:T(8,128)(2,1)} %bitcast.12, bf16[128,2048]{1,0:T(8,128)(2,1)} %sq_ref.5, bf16[128,2048]{1,0:T(8,128)(2,1)} %key_hbm.1, ...), custom_call_target="tpu_custom_call" | custom-call | flops 128 | bytes 128 | tf_op jit(solution)/shard_map/pallas_call | solution.py:257
  13.3 4.1 %collective-permute-done.1.refs_0_.rest_2_ = bf16[16,128,128]{2,1,0:T(8,128)(2,1)S(1)} collective-permute-done((bf16[16,128,128]{2,1,0:T(8,128)(2,1)S(1)}, bf16[16,128,128]{2,1,0:T(8,128)(2,1)S(1)}, u32[]{:S(2)}, u32[]{:S(2)}) %collective-permute-start.1) | collective-permute-done | bytes 524320 | tf_op jit(solution)/shard_map/ppermute | solution.py:234
  17.5 1.5 %collective-permute-done.2.refs_1_.rest_3_ = bf16[16,128,128]{2,1,0:T(8,128)(2,1)S(1)} collective-permute-done((bf16[16,128,128]{2,1,0:T(8,128)(2,1)S(1)}, bf16[16,128,128]{2,1,0:T(8,128)(2,1)S(1)}, u32[]{:S(2)}, u32[]{:S(2)}) %collective-permute-start.2) | collective-permute-done | bytes 524320 | tf_op jit(solution)/shard_map/ppermute | solution.py:234
  19.0 0.1 collective-permute-start.3
  19.1 0.5 %collective-permute-start.4 = (bf16[16,128,128]{2,1,0:T(8,128)(2,1)S(1)}, bf16[16,128,128]{2,1,0:T(8,128)(2,1)S(1)}, u32[]{:S(2)}, u32[]{:S(2)}) collective-permute-start(bf16[16,128,128]{2,1,0:T(8,128)(2,1)S(1)} %collective-permute-done.2.refs_1_.rest_3_), channel_id=1, source_target_pairs={{0,4},{4,0},{8,12},{12,8},{16,20},{20,16},{24,28},{28,24},{1,5},{5... | collective-permute-start | bytes 1572872 | tf_op jit(solution)/shard_map/ppermute | solution.py:234
  19.6 1.5 %collective-permute-start.5 = (bf16[8,128,128]{2,1,0:T(8,128)(2,1)S(1)}, bf16[8,128,128]{2,1,0:T(8,128)(2,1)S(1)}, u32[]{:S(2)}, u32[]{:S(2)}) collective-permute-start(bf16[8,128,128]{2,1,0:T(8,128)(2,1)S(1)} %get-tuple-element.29), channel_id=1, source_target_pairs={{0,16},{4,20},{8,24},{12,28},{16,0},{20,4},{24,8},{28,12},{1,17},{... | collective-permute-start | bytes 786440 | tf_op jit(solution)/shard_map/ppermute | solution.py:234
  21.1 0.5 %collective-permute-start.6 = (bf16[8,128,128]{2,1,0:T(8,128)(2,1)S(1)}, bf16[8,128,128]{2,1,0:T(8,128)(2,1)S(1)}, u32[]{:S(2)}, u32[]{:S(2)}) collective-permute-start(bf16[8,128,128]{2,1,0:T(8,128)(2,1)S(1)} %get-tuple-element.30), channel_id=1, source_target_pairs={{0,8},{4,12},{8,0},{12,4},{16,24},{20,28},{24,16},{28,20},{1,9},{5... | collective-permute-start | bytes 786440 | tf_op jit(solution)/shard_map/ppermute | solution.py:234
  21.6 0.0 collective-permute-done.rest_1_
  21.6 0.0 copy-done
  21.6 0.0 copy-done.1
  21.6 2.9 %shard_map.116 = (f32[128,2048]{1,0:T(8,128)S(1)}, f32[256,2048]{1,0:T(8,128)S(1)}) custom-call(bf16[128,2048]{1,0:T(8,128)(2,1)S(1)} %copy-done.1, bf16[256,2048]{1,0:T(8,128)(2,1)S(1)} %bitcast.7, f32[128,144]{1,0:T(8,128)S(1)} %get-tuple-element.23.order_ref.sc_ref, f32[256,144]{1,0:T(8,128)S(1)} %get-tuple-element.24.uc_ref, ...), custom_call_target="tpu_custom_call" | custom-call | flops 128 | bytes 128 | tf_op jit(solution)/shard_map/pallas_call | solution.py:309
  24.5 0.0 collective-permute-done.3.rest_0_
  24.5 0.0 collective-permute-done.4.rest_1_
  24.5 1.4 %shard_map.117 = (f32[128,2048]{1,0:T(8,128)S(1)}, f32[256,2048]{1,0:T(8,128)S(1)}) custom-call(bf16[128,2048]{1,0:T(8,128)(2,1)S(1)} %copy-done.1, bf16[256,2048]{1,0:T(8,128)(2,1)S(1)} %bitcast.8, f32[128,144]{1,0:T(8,128)S(1)} %get-tuple-element.23.order_ref.sc_ref, f32[256,144]{1,0:T(8,128)S(1)} %get-tuple-element.24.uc_ref, ...), custom_call_target="tpu_custom_call" | custom-call | flops 128 | bytes 128 | tf_op jit(solution)/shard_map/pallas_call | solution.py:309
  25.9 1.9 %collective-permute-done.5.rest_0_ = bf16[8,128,128]{2,1,0:T(8,128)(2,1)S(1)} collective-permute-done((bf16[8,128,128]{2,1,0:T(8,128)(2,1)S(1)}, bf16[8,128,128]{2,1,0:T(8,128)(2,1)S(1)}, u32[]{:S(2)}, u32[]{:S(2)}) %collective-permute-start.5) | collective-permute-done | bytes 262176 | tf_op jit(solution)/shard_map/ppermute | solution.py:234
  27.8 1.2 %collective-permute-done.6.rest_1_ = bf16[8,128,128]{2,1,0:T(8,128)(2,1)S(1)} collective-permute-done((bf16[8,128,128]{2,1,0:T(8,128)(2,1)S(1)}, bf16[8,128,128]{2,1,0:T(8,128)(2,1)S(1)}, u32[]{:S(2)}, u32[]{:S(2)}) %collective-permute-start.6) | collective-permute-done | bytes 262176 | tf_op jit(solution)/shard_map/ppermute | solution.py:234
  29.1 0.0 collective-permute-start.7
  29.1 0.5 %collective-permute-start.8 = (bf16[8,128,128]{2,1,0:T(8,128)(2,1)S(1)}, bf16[8,128,128]{2,1,0:T(8,128)(2,1)S(1)}, u32[]{:S(2)}, u32[]{:S(2)}) collective-permute-start(bf16[8,128,128]{2,1,0:T(8,128)(2,1)S(1)} %collective-permute-done.6.rest_1_), channel_id=1, source_target_pairs={{0,4},{4,0},{8,12},{12,8},{16,20},{20,16},{24,28},{28,24},{1,5},{5... | collective-permute-start | bytes 786440 | tf_op jit(solution)/shard_map/ppermute | solution.py:234
  29.6 1.0 %collective-permute-done.7.rest_2_ = bf16[8,128,128]{2,1,0:T(8,128)(2,1)S(1)} collective-permute-done((bf16[8,128,128]{2,1,0:T(8,128)(2,1)S(1)}, bf16[8,128,128]{2,1,0:T(8,128)(2,1)S(1)}, u32[]{:S(2)}, u32[]{:S(2)}) %collective-permute-start.7) | collective-permute-done | bytes 262176 | tf_op jit(solution)/shard_map/ppermute | solution.py:234
  30.6 0.4 collective-permute-done.8.rest_3_
  31.0 0.0 copy-start.2
  31.0 1.8 %shard_map.118 = (f32[128,2048]{1,0:T(8,128)S(1)}, f32[256,2048]{1,0:T(8,128)S(1)}, f32[3,128]{1,0:T(4,128)S(1)}) custom-call(bf16[128,2048]{1,0:T(8,128)(2,1)S(1)} %copy-done.1, bf16[256,2048]{1,0:T(8,128)(2,1)S(1)} %bitcast.9, f32[128,144]{1,0:T(8,128)S(1)} %get-tuple-element.23.order_ref.sc_ref, f32[256,144]{1,0:T(8,128)S(1)} %get-tuple-element.24.uc_ref, ...), custom_call_target="tpu_custom_call" | custom-call | flops 128 | bytes 128 | tf_op jit(solution)/shard_map/pallas_call | solution.py:309
  32.8 1.6 %collective-permute-start.9 = (f32[3,128]{1,0:T(4,128)S(1)}, f32[3,128]{1,0:T(4,128)S(1)}, u32[]{:S(2)}, u32[]{:S(2)}) collective-permute-start(f32[3,128]{1,0:T(4,128)S(1)} %get-tuple-element.41), channel_id=1, source_target_pairs={{0,1},{1,0},{2,3},{3,2},{4,5},{5,4},{6,7},{7,6},{8,9},{9,8},{10,11... | collective-permute-start | bytes 4616 | tf_op jit(solution)/shard_map/ppermute | solution.py:343
  34.4 2.0 %collective-permute-done.9 = f32[3,128]{1,0:T(4,128)S(1)} collective-permute-done((f32[3,128]{1,0:T(4,128)S(1)}, f32[3,128]{1,0:T(4,128)S(1)}, u32[]{:S(2)}, u32[]{:S(2)}) %collective-permute-start.9) | collective-permute-done | bytes 1568 | tf_op jit(solution)/shard_map/ppermute | solution.py:343
  36.4 2.6 %collective-permute-start.10 = (f32[3,128]{1,0:T(4,128)S(1)}, f32[3,128]{1,0:T(4,128)S(1)}, u32[]{:S(2)}, u32[]{:S(2)}) collective-permute-start(f32[3,128]{1,0:T(4,128)S(1)} %add.3.one_ref), channel_id=1, source_target_pairs={{0,2},{1,3},{2,0},{3,1},{4,6},{5,7},{6,4},{7,5},{8,10},{9,11},{10,... | collective-permute-start | bytes 4616 | tf_op jit(solution)/shard_map/ppermute | solution.py:343
  39.0 0.0 copy-done.2
  39.0 1.9 %collective-permute-done.10.two_ref = f32[3,128]{1,0:T(4,128)S(1)} collective-permute-done((f32[3,128]{1,0:T(4,128)S(1)}, f32[3,128]{1,0:T(4,128)S(1)}, u32[]{:S(2)}, u32[]{:S(2)}) %collective-permute-start.10) | collective-permute-done | bytes 1568 | tf_op jit(solution)/shard_map/ppermute | solution.py:343
  40.9 1.5 %shard_map.119 = (bf16[128,2048]{1,0:T(8,128)(2,1)}, bf16[256,2048]{1,0:T(8,128)(2,1)}) custom-call(f32[128,2048]{1,0:T(8,128)S(1)} %get-tuple-element.39.st_ref, f32[256,2048]{1,0:T(8,128)S(1)} %get-tuple-element.40.ut_ref, bf16[1,2048]{1,0:T(2,128)(2,1)S(1)} %reshape.30.gain_ref, f32[3,128]{1,0:T(4,128)S(1)} %add.3.one_ref, ...), custom_call_target="tpu_custom_call" | custom-call | tf_op jit(solution)/shard_map/pallas_call | solution.py:345
  (3 shorter events, 0.0 us)
Async XLA Ops:
  2.5 14.9 %collective-permute-start.1 = (bf16[16,128,128]{2,1,0:T(8,128)(2,1)S(1)}, bf16[16,128,128]{2,1,0:T(8,128)(2,1)S(1)}, u32[]{:S(2)}, u32[]{:S(2)}) collective-permute-start(bf16[16,128,128]{2,1,0:T(8,128)(2,1)S(1)} %shard_map.114.rest_0_), channel_id=1, source_target_pairs={{0,8},{4,12},{8,0},{12,4},{16,24},{20,28},{24,16},{28,20},{1,9},{5... | collective-permute-start | bytes 1572872 | tf_op jit(solution)/shard_map/ppermute | solution.py:234
  5.6 13.4 %collective-permute-start.2 = (bf16[16,128,128]{2,1,0:T(8,128)(2,1)S(1)}, bf16[16,128,128]{2,1,0:T(8,128)(2,1)S(1)}, u32[]{:S(2)}, u32[]{:S(2)}) collective-permute-start(bf16[16,128,128]{2,1,0:T(8,128)(2,1)S(1)} %shard_map.114.rest_0_), channel_id=1, source_target_pairs={{0,16},{4,20},{8,24},{12,28},{16,0},{20,4},{24,8},{28,12},{1,17},{... | collective-permute-start | bytes 1572872 | tf_op jit(solution)/shard_map/ppermute | solution.py:234
  7.1 14.5 %collective-permute-start = (bf16[16,128,128]{2,1,0:T(8,128)(2,1)S(1)}, bf16[16,128,128]{2,1,0:T(8,128)(2,1)S(1)}, u32[]{:S(2)}, u32[]{:S(2)}) collective-permute-start(bf16[16,128,128]{2,1,0:T(8,128)(2,1)S(1)} %shard_map.114.rest_0_), channel_id=1, source_target_pairs={{0,4},{4,0},{8,12},{12,8},{16,20},{20,16},{24,28},{28,24},{1,5},{5... | collective-permute-start | bytes 1572872 | tf_op jit(solution)/shard_map/ppermute | solution.py:234
  7.1 14.5 %copy-start = (bf16[4,64,2048]{2,1,0:T(8,128)(2,1)S(1)}, bf16[4,64,2048]{2,1,0:T(8,128)(2,1)}, u32[]{:S(2)}) copy-start(bf16[4,64,2048]{2,1,0:T(8,128)(2,1)} %param.15) | copy-start | bytes 3145732
  7.1 14.5 %copy-start.1 = (bf16[128,2048]{1,0:T(8,128)(2,1)S(1)}, bf16[128,2048]{1,0:T(8,128)(2,1)}, u32[]{:S(2)}) copy-start(bf16[128,2048]{1,0:T(8,128)(2,1)} %sq_ref.5) | copy-start | bytes 1572868
  19.0 5.5 %collective-permute-start.3 = (bf16[16,128,128]{2,1,0:T(8,128)(2,1)S(1)}, bf16[16,128,128]{2,1,0:T(8,128)(2,1)S(1)}, u32[]{:S(2)}, u32[]{:S(2)}) collective-permute-start(bf16[16,128,128]{2,1,0:T(8,128)(2,1)S(1)} %collective-permute-done.1.refs_0_.rest_2_), channel_id=1, source_target_pairs={{0,4},{4,0},{8,12},{12,8},{16,20},{20,16},{24,28},{28,24},{1,5},{5... | collective-permute-start | bytes 1572872 | tf_op jit(solution)/shard_map/ppermute | solution.py:234
  19.1 5.4 %collective-permute-start.4 = (bf16[16,128,128]{2,1,0:T(8,128)(2,1)S(1)}, bf16[16,128,128]{2,1,0:T(8,128)(2,1)S(1)}, u32[]{:S(2)}, u32[]{:S(2)}) collective-permute-start(bf16[16,128,128]{2,1,0:T(8,128)(2,1)S(1)} %collective-permute-done.2.refs_1_.rest_3_), channel_id=1, source_target_pairs={{0,4},{4,0},{8,12},{12,8},{16,20},{20,16},{24,28},{28,24},{1,5},{5... | collective-permute-start | bytes 1572872 | tf_op jit(solution)/shard_map/ppermute | solution.py:234
  19.6 8.3 %collective-permute-start.5 = (bf16[8,128,128]{2,1,0:T(8,128)(2,1)S(1)}, bf16[8,128,128]{2,1,0:T(8,128)(2,1)S(1)}, u32[]{:S(2)}, u32[]{:S(2)}) collective-permute-start(bf16[8,128,128]{2,1,0:T(8,128)(2,1)S(1)} %get-tuple-element.29), channel_id=1, source_target_pairs={{0,16},{4,20},{8,24},{12,28},{16,0},{20,4},{24,8},{28,12},{1,17},{... | collective-permute-start | bytes 786440 | tf_op jit(solution)/shard_map/ppermute | solution.py:234
  21.1 8.0 %collective-permute-start.6 = (bf16[8,128,128]{2,1,0:T(8,128)(2,1)S(1)}, bf16[8,128,128]{2,1,0:T(8,128)(2,1)S(1)}, u32[]{:S(2)}, u32[]{:S(2)}) collective-permute-start(bf16[8,128,128]{2,1,0:T(8,128)(2,1)S(1)} %get-tuple-element.30), channel_id=1, source_target_pairs={{0,8},{4,12},{8,0},{12,4},{16,24},{20,28},{24,16},{28,20},{1,9},{5... | collective-permute-start | bytes 786440 | tf_op jit(solution)/shard_map/ppermute | solution.py:234
  29.1 1.5 %collective-permute-start.7 = (bf16[8,128,128]{2,1,0:T(8,128)(2,1)S(1)}, bf16[8,128,128]{2,1,0:T(8,128)(2,1)S(1)}, u32[]{:S(2)}, u32[]{:S(2)}) collective-permute-start(bf16[8,128,128]{2,1,0:T(8,128)(2,1)S(1)} %collective-permute-done.5.rest_0_), channel_id=1, source_target_pairs={{0,4},{4,0},{8,12},{12,8},{16,20},{20,16},{24,28},{28,24},{1,5},{5... | collective-permute-start | bytes 786440 | tf_op jit(solution)/shard_map/ppermute | solution.py:234
  29.1 1.9 %collective-permute-start.8 = (bf16[8,128,128]{2,1,0:T(8,128)(2,1)S(1)}, bf16[8,128,128]{2,1,0:T(8,128)(2,1)S(1)}, u32[]{:S(2)}, u32[]{:S(2)}) collective-permute-start(bf16[8,128,128]{2,1,0:T(8,128)(2,1)S(1)} %collective-permute-done.6.rest_1_), channel_id=1, source_target_pairs={{0,4},{4,0},{8,12},{12,8},{16,20},{20,16},{24,28},{28,24},{1,5},{5... | collective-permute-start | bytes 786440 | tf_op jit(solution)/shard_map/ppermute | solution.py:234
  31.0 8.0 %copy-start.2 = (bf16[2048]{0:T(1024)(128)(2,1)S(1)}, bf16[2048]{0:T(1024)(128)(2,1)}, u32[]{:S(2)}) copy-start(bf16[2048]{0:T(1024)(128)(2,1)} %param.14) | copy-start | bytes 12292
  32.8 3.6 %collective-permute-start.9 = (f32[3,128]{1,0:T(4,128)S(1)}, f32[3,128]{1,0:T(4,128)S(1)}, u32[]{:S(2)}, u32[]{:S(2)}) collective-permute-start(f32[3,128]{1,0:T(4,128)S(1)} %get-tuple-element.41), channel_id=1, source_target_pairs={{0,1},{1,0},{2,3},{3,2},{4,5},{5,4},{6,7},{7,6},{8,9},{9,8},{10,11... | collective-permute-start | bytes 4616 | tf_op jit(solution)/shard_map/ppermute | solution.py:343
  36.4 4.5 %collective-permute-start.10 = (f32[3,128]{1,0:T(4,128)S(1)}, f32[3,128]{1,0:T(4,128)S(1)}, u32[]{:S(2)}, u32[]{:S(2)}) collective-permute-start(f32[3,128]{1,0:T(4,128)S(1)} %add.3.one_ref), channel_id=1, source_target_pairs={{0,2},{1,3},{2,0},{3,1},{4,6},{5,7},{6,4},{7,5},{8,10},{9,11},{10,... | collective-permute-start | bytes 4616 | tf_op jit(solution)/shard_map/ppermute | solution.py:343

commit v4 on v3

v4 whole, which is shorter than its diff:
```python
import functools

import jax
import jax.numpy as jnp
from jax import lax
from jax.experimental import pallas as pl
from jax.experimental.pallas import tpu as pltpu
from jax.sharding import PartitionSpec as P

HEADS = 64
HD = 128
ROWS = 128
VMEM_BYTES = 20 * 1024 * 1024


def matmul(a, b, contract):
    return lax.dot_general(a, b, (contract, ((), ())), preferred_element_type=jnp.float32)


def load_columns(sources, targets, sems, chunks):
    copies = []
    for chunk in range(chunks):
        group = []
        for i, (source, target) in enumerate(zip(sources, targets)):
            size = source.shape[1] // chunks
            cols = pl.ds(chunk * size, size)
            group.append(pltpu.make_async_copy(source.at[:, cols], target.at[:, cols], sems.at[i, chunk]))
            group[-1].start()
        copies.append(group)

    def wait(chunk):
        for copy in copies[chunk]:
            copy.wait()

    return wait


def state_kernel(chunks, key_hbm, value_hbm, first_ref, second_ref, whole_ref, key_ref, value_ref, sems):
    half = first_ref.shape[0]
    head_count = 2 * half
    wait = load_columns((key_hbm, value_hbm), (key_ref, value_ref), sems, chunks)
    for head in range(head_count):
        if head % (head_count // chunks) == 0:
            wait(head // (head_count // chunks))
        cols = slice(head * HD, (head + 1) * HD)
        state = matmul(key_ref[:, cols], value_ref[:, cols], ((0,), (0,))).astype(jnp.bfloat16)
        whole_ref[0, head] = state
        if head < half:
            first_ref[head] = state
        else:
            second_ref[head - half] = state


def join_kernel(order_ref, *refs):
    out_ref = refs[-1]
    half = out_ref.shape[1] // 2
    for i in range(out_ref.shape[0]):
        for side in range(2):
            for head in range(half):
                out_ref[i, side * half + head] = refs[2 * i + side][head]


def choose_levels(target, position, depth, level_count, head_count):
    block_count = 1 << depth
    shift = head_count.bit_length() - 1
    shape = (level_count * head_count, (block_count + 1) * head_count)
    row = lax.broadcasted_iota(jnp.int32, shape, 0)
    col = lax.broadcasted_iota(jnp.int32, shape, 1)
    level = row >> shift
    offset = col >> shift
    block = offset ^ position
    diff = block ^ target
    chosen = jnp.logical_and(level == 0, offset == block_count)
    below = jnp.logical_and(offset < block_count, block < target)
    for step in range(1, depth + 1):
        span = jnp.logical_and(diff >= (1 << (step - 1)), diff < (1 << step))
        chosen = jnp.logical_or(chosen, jnp.logical_and(below, jnp.logical_and(span, level == step)))
    same = (row & (head_count - 1)) == (col & (head_count - 1))
    return jnp.where(jnp.logical_and(chosen, same), 1.0, 0.0).astype(jnp.bfloat16)


def attend(mask, chunks, wait, q_ref, k_ref, v_ref, c_ref, o_ref, own):
    head_count = q_ref.shape[1] // HD
    step = 2
    for first in range(0, head_count, step):
        if first % (head_count // chunks) == 0:
            wait(first // (head_count // chunks))
        units = [
            (head, slice(head * HD, (head + 1) * HD), slice(start, start + ROWS))
            for head in range(first, first + step)
            for start in range(0, q_ref.shape[0], ROWS)
        ]
        scores = [matmul(q_ref[rows, cols], k_ref[rows, cols], ((1,), (1,))) for _, cols, rows in units]
        scores = [jnp.where(mask, score, 0.0).astype(jnp.bfloat16) for score in scores]
        results = [matmul(score, v_ref[rows, cols], ((1,), (0,))) for score, (_, cols, rows) in zip(scores, units)]
        for result, (head, cols, rows) in zip(results, units):
            o_ref[rows, cols] = result * c_ref[rows, own + head : own + head + 1]


def local_kernel(depth, suffix, chunks, *refs):
    small_count = 2 if suffix else 1
    refs = list(refs)
    take = lambda count: [refs.pop(0) for _ in range(count)]
    small, sources, (o_ref, c_ref), small_loaded, loaded = take(small_count), take(3), take(2), take(small_count), take(3)
    small_sems, sems = refs
    small_copies = [
        pltpu.make_async_copy(source, target, small_sems.at[i])
        for i, (source, target) in enumerate(zip(small, small_loaded))
    ]
    for copy in small_copies:
        copy.start()
    wait = load_columns(sources, loaded, sems, chunks)
    for copy in small_copies:
        copy.wait()
    weight_ref = small_loaded[-1]
    head_count = loaded[0].shape[1] // HD
    position = lax.axis_index("seq").astype(jnp.int32)
    pick = functools.partial(
        choose_levels,
        position=position,
        depth=depth,
        level_count=weight_ref.shape[-2] // head_count,
        head_count=head_count,
    )
    row = lax.broadcasted_iota(jnp.int32, (ROWS, ROWS), 0)
    col = lax.broadcasted_iota(jnp.int32, (ROWS, ROWS), 1)
    mask = row >= col
    if suffix:
        mask = jnp.logical_and(mask, row // suffix == col // suffix)
        for user in range(weight_ref.shape[0]):
            weights = matmul(weight_ref[user], pick(small_loaded[0][user]), ((0,), (0,)))
            c_ref[user * suffix : (user + 1) * suffix] = weights
    else:
        c_ref[...] = matmul(weight_ref[...], pick(position), ((0,), (0,)))
    attend(mask, chunks, wait, *loaded, c_ref, o_ref, (1 << depth) * head_count)


def add_blocks(groups, state_refs, head_count, head, q_ref, c_ref, base):
    cols = slice(head * HD, (head + 1) * HD)
    query = q_ref[:, cols]
    total = base
    for group in groups:
        scaled = []
        for offset in group:
            column = offset * head_count + head
            weight = jnp.broadcast_to(c_ref[:, column : column + 1], query.shape).astype(jnp.bfloat16)
            scaled.append(query * weight)
        states = [state_refs[offset][0][state_refs[offset][1], head] for offset in group]
        total = total + matmul(jnp.concatenate(scaled, axis=1), jnp.concatenate(states, axis=0), ((1,), (0,)))
    return total


def read_kernel(groups, places, last, sq_ref, uq_ref, sc_ref, uc_ref, sa_ref, ua_ref, *rest):
    head_count = sq_ref.shape[1] // HD
    used = 1 + max(which for which, _ in places.values())
    state_refs = {offset: (rest[which], index) for offset, (which, index) in places.items()}
    st_ref, ut_ref = rest[used : used + 2]
    for head in range(head_count):
        cols = slice(head * HD, (head + 1) * HD)
        for side, (q_ref, c_ref, a_ref, t_ref) in enumerate(
            ((sq_ref, sc_ref, sa_ref, st_ref), (uq_ref, uc_ref, ua_ref, ut_ref))
        ):
            total = add_blocks(groups, state_refs, head_count, head, q_ref, c_ref, a_ref[:, cols])
            t_ref[:, cols] = total
            if last:
                acc_ref = rest[used + 3 + side]
                if head == 0:
                    acc_ref[...] = total * total
                else:
                    acc_ref[...] += total * total
    if last:
        square_ref = rest[used + 2]
        line = 0
        for acc_ref in rest[used + 3 : used + 5]:
            for start in range(0, acc_ref.shape[0], ROWS):
                turned = jnp.transpose(acc_ref[start : start + ROWS])
                square_ref[line : line + 1] = jnp.sum(turned, axis=0, keepdims=True)
                line += 1


def norm_kernel(features, chunks, st_ref, ut_ref, gain_ref, one_ref, two_ref, so_hbm, uo_hbm, so_ref, uo_ref, sems):
    square = one_ref[...] + two_ref[...]
    scale = lax.rsqrt(square / features + 1e-06)
    scales = [jnp.transpose(jnp.broadcast_to(scale[line : line + 1], (ROWS, ROWS))) for line in range(scale.shape[0])]
    size = st_ref.shape[1] // chunks
    copies = []
    for chunk in range(chunks):
        line = 0
        wide = pl.ds(chunk * size, size)
        for side, (t_ref, o_ref, o_hbm) in enumerate(((st_ref, so_ref, so_hbm), (ut_ref, uo_ref, uo_hbm))):
            for start in range(0, t_ref.shape[0], ROWS):
                rows = slice(start, start + ROWS)
                for low in range(chunk * size, (chunk + 1) * size, HD):
                    cols = slice(low, low + HD)
                    gain = gain_ref[:, cols].astype(jnp.float32)
                    o_ref[rows, cols] = (t_ref[rows, cols] * scales[line] * gain).astype(jnp.bfloat16)
                line += 1
            copies.append(pltpu.make_async_copy(o_ref.at[:, wide], o_hbm.at[:, wide], sems.at[side, chunk]))
            copies[-1].start()
    for copy in copies:
        copy.wait()


def local(
    slab_query,
    slab_key,
    slab_value,
    slab_levels,
    norm_gain,
    user_query,
    user_key,
    user_value,
    user_levels,
    prefix_lengths,
):
    seq_count = lax.axis_size("seq")
    head_axis = lax.axis_size("head")
    depth = seq_count.bit_length() - 1
    token_count, width = slab_query.shape
    head_count = width // HD
    half = head_count // 2
    user_count, suffix = user_query.shape[:2]
    user_rows = user_count * suffix
    lines = (token_count + user_rows) // ROWS
    params = pltpu.CompilerParams(vmem_limit_bytes=VMEM_BYTES)
    bf16 = functools.partial(jax.ShapeDtypeStruct, dtype=jnp.bfloat16)
    vmem = pl.BlockSpec(memory_space=pltpu.VMEM)
    anywhere = pl.BlockSpec(memory_space=pl.ANY)
    hbm = pl.BlockSpec(memory_space=pltpu.HBM)
    chunks = min(4, half)
    rows_cost = 2 * width * (token_count + user_rows)

    def pinned(*arrays):
        return [pltpu.with_memory_space_constraint(array, pltpu.HBM) for array in arrays]

    def cost(flops, moved):
        return pl.CostEstimate(flops=flops, bytes_accessed=moved, transcendentals=0)

    def swap(value, bit):
        return lax.ppermute(value, "seq", [(i, i ^ (1 << bit)) for i in range(seq_count)])

    def after(results, values):
        return list(lax.optimization_barrier((results, values))[1])

    def join(order, halves):
        return pl.pallas_call(
            join_kernel,
            out_shape=pltpu.VMEM((len(halves) // 2, head_count, HD, HD), jnp.bfloat16),
            in_specs=[anywhere] + [vmem] * len(halves),
            out_specs=vmem,
            compiler_params=params,
        )(order, *halves)

    half_state = pltpu.VMEM((half, HD, HD), jnp.bfloat16)
    first, second, state = pl.pallas_call(
        functools.partial(state_kernel, chunks),
        out_shape=[half_state, half_state, pltpu.VMEM((1, head_count, HD, HD), jnp.bfloat16)],
        in_specs=[hbm] * 2,
        out_specs=[vmem] * 3,
        scratch_shapes=[pltpu.VMEM((token_count, width), jnp.bfloat16)] * 2 + [pltpu.SemaphoreType.DMA((2, chunks))],
        compiler_params=params,
    )(*pinned(slab_key, slab_value))
    halves = [first, second]

    columns = (seq_count + 1) * head_count

    def local_part(rows, suffix, small, scratch, arrays):
        return pl.pallas_call(
            functools.partial(local_kernel, depth, suffix, chunks),
            out_shape=[pltpu.VMEM((rows, width), jnp.float32), pltpu.VMEM((rows, columns), jnp.float32)],
            in_specs=[hbm] * (len(small) + 3),
            out_specs=[vmem] * 2,
            scratch_shapes=scratch
            + [pltpu.VMEM((rows, width), jnp.bfloat16)] * 3
            + [pltpu.SemaphoreType.DMA((len(small),)), pltpu.SemaphoreType.DMA((3, chunks))],
            compiler_params=params,
            cost_estimate=cost(0, 0),
        )(*pinned(*small), *pinned(*arrays))

    outer = list(range(1, depth))
    places = [(bit, side) for bit in outer for side in range(2)]
    ahead = [(bit, 0) for bit in outer[:-1]] + [(bit, 1) for bit in outer[1:]] or places
    sides = {1 << bit: [None, None] for bit in outer}
    for bit, side in ahead:
        sides[1 << bit][side] = swap(halves[side], bit)
    slab_table = slab_levels.reshape(-1, token_count)
    slab_acc, slab_coef = local_part(
        token_count,
        0,
        [slab_table],
        [pltpu.VMEM(slab_table.shape, jnp.bfloat16)],
        [slab_query, slab_key, slab_value],
    )
    state, *halves = after(slab_coef, [state] + halves)
    whole = {0: state, 1: swap(state, 0)}
    for bit, side in places:
        if (bit, side) not in ahead:
            sides[1 << bit][side] = swap(halves[side], bit)

    later = sorted((m for m in range(0, seq_count, 2) if m.bit_count() > 1), key=lambda m: m.bit_count())
    for m in later:
        high, low = m.bit_length() - 1, (m & -m).bit_length() - 1
        sides[m] = [swap(sides[m ^ (1 << high)][0], high), swap(sides[m ^ (1 << low)][1], low)]
    user_queries = user_query.reshape(user_rows, width)
    user_table = user_levels.reshape(user_count, -1, suffix)
    lengths = after([whole[1]] + [sides[1 << bit][side] for bit, side in ahead], [prefix_lengths])[0]
    user_acc, user_coef = local_part(
        user_rows,
        suffix,
        [lengths, user_table],
        [pltpu.SMEM((user_count,), jnp.int32), pltpu.VMEM(user_table.shape, jnp.bfloat16)],
        [user_queries, user_key.reshape(user_rows, width), user_value.reshape(user_rows, width)],
    )

    def read(groups, states, accs, last):
        found = {}
        for which, (offsets, _) in enumerate(states):
            found.update({offset: (which, index) for index, offset in enumerate(offsets)})
        outs = [pltpu.VMEM((token_count, width), jnp.float32), pltpu.VMEM((user_rows, width), jnp.float32)]
        scratch = []
        if last:
            outs.append(pltpu.VMEM((lines, ROWS), jnp.float32))
            scratch = [pltpu.VMEM((token_count, HD), jnp.float32), pltpu.VMEM((user_rows, HD), jnp.float32)]
        return pl.pallas_call(
            functools.partial(read_kernel, groups, found, last),
            out_shape=outs,
            in_specs=[vmem] * (6 + len(states)),
            out_specs=[vmem] * len(outs),
            scratch_shapes=scratch,
            compiler_params=params,
            cost_estimate=cost(0, 0),
        )(slab_query, user_queries, slab_coef, user_coef, *accs, *[array for _, array in states])

    def pairs(offsets):
        return [tuple(offsets[i : i + 2]) for i in range(0, len(offsets), 2)]

    direct = [1 << bit for bit in outer]
    mates = [m | 1 for m in direct]
    for m in direct:
        whole[m] = join(user_coef, sides[m])
    for m in direct:
        whole[m | 1] = swap(whole[m], 0)
    accs = read(pairs([0, 1] + direct), [([m], whole[m]) for m in [0, 1] + direct], (slab_acc, user_acc), False)
    late = join(accs[0], [piece for m in later for piece in sides[m]])
    accs = read(pairs(mates), [([m], whole[m]) for m in mates], accs, False)
    late_mates = swap(late, 0)
    slab_total, user_total, square = read(
        [(m, m | 1) for m in later], [(later, late), ([m | 1 for m in later], late_mates)], accs, True
    )

    mate = jnp.zeros_like(square)
    for bit in range(head_axis.bit_length() - 1):
        square = square + mate
        mate = lax.ppermute(square, "head", [(i, i ^ (1 << bit)) for i in range(head_axis)])

    slab_out, user_out = pl.pallas_call(
        functools.partial(norm_kernel, float(width * head_axis), chunks),
        out_shape=[bf16((token_count, width)), bf16((user_rows, width))],
        in_specs=[vmem] * 5,
        out_specs=[hbm] * 2,
        scratch_shapes=[
            pltpu.VMEM((token_count, width), jnp.bfloat16),
            pltpu.VMEM((user_rows, width), jnp.bfloat16),
            pltpu.SemaphoreType.DMA((2, chunks)),
        ],
        compiler_params=params,
    )(slab_total, user_total, norm_gain.reshape(1, width), square, mate)
    return slab_out, user_out.reshape(user_count, suffix, width)


def solution(mesh):
    return jax.shard_map(
        local,
        mesh=mesh,
        in_specs=(
            P("seq", "head"),
            P("seq", "head"),
            P("seq", "head"),
            P(None, "head", "seq"),
            P("head"),
            P("seq", None, "head"),
            P("seq", None, "head"),
            P("seq", None, "head"),
            P("seq", None, "head", None),
            P("seq"),
        ),
        out_specs=(P("seq", "head"), P("seq", None, "head")),
        check_vma=False,
    )
```

time: 42.6 us -> 42.5 us (level)
  waiting for transfers between devices: 14 us -> 9.42 us
  Pallas kernels: 15.8 us -> 17.9 us
  starting transfers between devices: 11.9 us -> 13.6 us
  local copies, waits for them, and re-layouts: 0.02 us -> 0.62 us
    ppermute x9 -> x10, waiting for transfers between devices: 10.1 us -> 5.52 us  [swap(): lax.ppermute(value, 'seq', [(i, i ^ 1 << bit) for i in range(seq_count)])]
    pallas_call x6 -> x9, Pallas kernels: 14.3 us -> 16.4 us  [the longest x2 8.38 us: local_part(): pl.pallas_call(functools.partial(local_kernel, depth, suffix, chunks), ou...]
    ppermute x9 -> x10, starting transfers between devices: 7.66 us -> 9.34 us  [swap(): lax.ppermute(value, 'seq', [(i, i ^ 1 << bit) for i in range(seq_count)])]
    unnamed x6, local copies, waits for them, and re-layouts: 0.01 us -> 0.61 us
  transfers between devices with their start and end apart: 11 -> 12, of which waited for: 8 -> 4; matrix products, arithmetic and copies ran while one was open for 0% -> 0% of each run, Pallas kernels for 25% -> 22%
where the time goes in v4:
time: 42.5 us; the launch traced here: 42.3 us
  Pallas kernels  17.9 us (42%)
  starting transfers between devices  13.6 us (32%)
  waiting for transfers between devices  9.42 us (22%)
  between operations  0.78 us (2%)
  local copies, waits for them, and re-layouts  0.62 us (1%)
    ppermute x10, starting transfers between devices, swap(): lax.ppermute(value, 'seq', [(i, i ^ 1 << bit) for i in range(seq_count)])  9.34 us
    pallas_call x2, Pallas kernels, local_part(): pl.pallas_call(functools.partial(local_kernel, depth, suffix, chunks), ou...  8.38 us
    pallas_call x3, Pallas kernels, read(): pl.pallas_call(functools.partial(read_kernel, groups, found, last), out_s...  6.02 us
    ppermute x10, waiting for transfers between devices, swap(): lax.ppermute(value, 'seq', [(i, i ^ 1 << bit) for i in range(seq_count)])  5.52 us
    ppermute x2, starting transfers between devices, local(): lax.ppermute(square, 'head', [(i, i ^ 1 << bit) for i in range(head_axis)])  4.22 us
    ppermute x2, waiting for transfers between devices, local(): lax.ppermute(square, 'head', [(i, i ^ 1 << bit) for i in range(head_axis)])  3.9 us
    pallas_call x1, Pallas kernels, local(): pl.pallas_call(functools.partial(state_kernel, chunks), out_shape=[half_s...  1.92 us
    pallas_call x1, Pallas kernels, local(): pl.pallas_call(functools.partial(norm_kernel, float(width * head_axis), c...  1.53 us
  transfers between devices with their start and end apart: 12, of which 4 were waited for; matrix products, arithmetic and copies ran while one was open for 0% of the time, Pallas kernels for 22%

profile of v4, /device:TPU:0, one launch (start us, length us, event | category | flops | bytes accessed | tf_op | source)
XLA Modules:
  0.0 42.3 jit_solution(5957924729510012689)
XLA Ops:
  0.6 1.9 %shard_map.114 = (bf16[8,128,128]{2,1,0:T(8,128)(2,1)S(1)}, bf16[8,128,128]{2,1,0:T(8,128)(2,1)S(1)}, bf16[1,16,128,128]{3,2,1,0:T(8,128)(2,1)S(1)}) custom-call(bf16[128,2048]{1,0:T(8,128)(2,1)} %key_hbm.1, bf16[128,2048]{1,0:T(8,128)(2,1)} %value_hbm.1), custom_call_target="tpu_custom_call" | custom-call | tf_op jit(solution)/shard_map/pallas_call | solution.py:255
  2.6 3.5 %shard_map.113 = (f32[128,2048]{1,0:T(8,128)S(1)}, f32[128,144]{1,0:T(8,128)S(1)}) custom-call(bf16[96,128]{1,0:T(8,128)(2,1)} %bitcast.13, bf16[128,2048]{1,0:T(8,128)(2,1)} %sq_ref.5, bf16[128,2048]{1,0:T(8,128)(2,1)} %key_hbm.1, bf16[128,2048]{1,0:T(8,128)(2,1)} %value_hbm.1), custom_call_target="tpu_custom_call" | custom-call | tf_op jit(solution)/shard_map/pallas_call | solution.py:268
  6.1 0.5 %collective-permute-start = (bf16[1,16,128,128]{3,2,1,0:T(8,128)(2,1)S(1)}, bf16[1,16,128,128]{3,2,1,0:T(8,128)(2,1)S(1)}, u32[]{:S(2)}, u32[]{:S(2)}) collective-permute-start(bf16[1,16,128,128]{3,2,1,0:T(8,128)(2,1)S(1)} %get-tuple-element.26.rest_0_), channel_id=1, source_target_pairs={{0,4},{4,0},{8,12},{12,8},{16,20},{20,16},{24,28},{28,24},{1,5},{5... | collective-permute-start | bytes 1572872 | tf_op jit(solution)/shard_map/ppermute | solution.py:240
  6.6 2.6 %collective-permute-start.1 = (bf16[8,128,128]{2,1,0:T(8,128)(2,1)S(1)}, bf16[8,128,128]{2,1,0:T(8,128)(2,1)S(1)}, u32[]{:S(2)}, u32[]{:S(2)}) collective-permute-start(bf16[8,128,128]{2,1,0:T(8,128)(2,1)S(1)} %get-tuple-element.32), channel_id=1, source_target_pairs={{0,8},{4,12},{8,0},{12,4},{16,24},{20,28},{24,16},{28,20},{1,9},{5... | collective-permute-start | bytes 786440 | tf_op jit(solution)/shard_map/ppermute | solution.py:240
  9.2 1.6 %collective-permute-start.2 = (bf16[8,128,128]{2,1,0:T(8,128)(2,1)S(1)}, bf16[8,128,128]{2,1,0:T(8,128)(2,1)S(1)}, u32[]{:S(2)}, u32[]{:S(2)}) collective-permute-start(bf16[8,128,128]{2,1,0:T(8,128)(2,1)S(1)} %get-tuple-element.31), channel_id=1, source_target_pairs={{0,16},{4,20},{8,24},{12,28},{16,0},{20,4},{24,8},{28,12},{1,17},{... | collective-permute-start | bytes 786440 | tf_op jit(solution)/shard_map/ppermute | solution.py:240
  10.7 0.5 %collective-permute-start.4 = (bf16[8,128,128]{2,1,0:T(8,128)(2,1)S(1)}, bf16[8,128,128]{2,1,0:T(8,128)(2,1)S(1)}, u32[]{:S(2)}, u32[]{:S(2)}) collective-permute-start(bf16[8,128,128]{2,1,0:T(8,128)(2,1)S(1)} %get-tuple-element.32), channel_id=1, source_target_pairs={{0,16},{4,20},{8,24},{12,28},{16,0},{20,4},{24,8},{28,12},{1,17},{... | collective-permute-start | bytes 786440 | tf_op jit(solution)/shard_map/ppermute | solution.py:240
  11.2 0.1 collective-permute-start.3
  11.3 5.1 %collective-permute-done.1.refs_0_ = bf16[8,128,128]{2,1,0:T(8,128)(2,1)S(1)} collective-permute-done((bf16[8,128,128]{2,1,0:T(8,128)(2,1)S(1)}, bf16[8,128,128]{2,1,0:T(8,128)(2,1)S(1)}, u32[]{:S(2)}, u32[]{:S(2)}) %collective-permute-start.1) | collective-permute-done | bytes 262176 | tf_op jit(solution)/shard_map/ppermute | solution.py:240
  16.3 2.0 %collective-permute-start.7 = (bf16[8,128,128]{2,1,0:T(8,128)(2,1)S(1)}, bf16[8,128,128]{2,1,0:T(8,128)(2,1)S(1)}, u32[]{:S(2)}, u32[]{:S(2)}) collective-permute-start(bf16[8,128,128]{2,1,0:T(8,128)(2,1)S(1)} %collective-permute-done.1.refs_0_), channel_id=1, source_target_pairs={{0,16},{4,20},{8,24},{12,28},{16,0},{20,4},{24,8},{28,12},{1,17},{... | collective-permute-start | bytes 786440 | tf_op jit(solution)/shard_map/ppermute | solution.py:240
  18.3 0.0 collective-permute-done.2.refs_1_
  18.3 1.5 %collective-permute-start.8 = (bf16[8,128,128]{2,1,0:T(8,128)(2,1)S(1)}, bf16[8,128,128]{2,1,0:T(8,128)(2,1)S(1)}, u32[]{:S(2)}, u32[]{:S(2)}) collective-permute-start(bf16[8,128,128]{2,1,0:T(8,128)(2,1)S(1)} %collective-permute-done.2.refs_1_), channel_id=1, source_target_pairs={{0,8},{4,12},{8,0},{12,4},{16,24},{20,28},{24,16},{28,20},{1,9},{5... | collective-permute-start | bytes 786440 | tf_op jit(solution)/shard_map/ppermute | solution.py:240
  19.8 0.0 collective-permute-done.rest_1_
  19.8 4.8 %shard_map.115 = (f32[256,2048]{1,0:T(8,128)S(1)}, f32[256,144]{1,0:T(8,128)S(1)}) custom-call(s32[4]{0:T(128)} %refs_0_, bf16[4,96,64]{2,1,0:T(8,128)(2,1)} %bitcast.12, bf16[256,2048]{1,0:T(8,128)(2,1)} %bitcast.6, bf16[256,2048]{1,0:T(8,128)(2,1)} %bitcast.10, bf16[256,2048]{1,0:T(8,128)(2,1)} %bitcast.11), custom_call_target="tpu_custom_call" | custom-call | tf_op jit(solution)/shard_map/pallas_call | solution.py:268
  24.7 0.0 copy-start
  24.7 0.0 copy-start.1
  24.7 0.0 collective-permute-done.4.refs_0_
  24.7 0.1 collective-permute-start.6
  24.8 0.0 collective-permute-done.3.refs_1_
  24.9 0.5 %collective-permute-start.5 = (bf16[1,16,128,128]{3,2,1,0:T(8,128)(2,1)S(1)}, bf16[1,16,128,128]{3,2,1,0:T(8,128)(2,1)S(1)}, u32[]{:S(2)}, u32[]{:S(2)}) collective-permute-start(bf16[1,16,128,128]{3,2,1,0:T(8,128)(2,1)S(1)} %shard_map.116.rest_2_), channel_id=1, source_target_pairs={{0,4},{4,0},{8,12},{12,8},{16,20},{20,16},{24,28},{28,24},{1,5},{5... | collective-permute-start | bytes 1572872 | tf_op jit(solution)/shard_map/ppermute | solution.py:240
  25.4 0.5 %copy-done = bf16[4,64,2048]{2,1,0:T(8,128)(2,1)S(1)} copy-done((bf16[4,64,2048]{2,1,0:T(8,128)(2,1)S(1)}, bf16[4,64,2048]{2,1,0:T(8,128)(2,1)}, u32[]{:S(2)}) %copy-start) | copy-done | bytes 1048600
  25.9 0.1 copy-done.1
  26.0 2.8 %shard_map.118 = (f32[128,2048]{1,0:T(8,128)S(1)}, f32[256,2048]{1,0:T(8,128)S(1)}) custom-call(bf16[128,2048]{1,0:T(8,128)(2,1)S(1)} %copy-done.1, bf16[256,2048]{1,0:T(8,128)(2,1)S(1)} %bitcast.7, f32[128,144]{1,0:T(8,128)S(1)} %get-tuple-element.22.sc_ref, f32[256,144]{1,0:T(8,128)S(1)} %get-tuple-element.28.order_ref.uc_ref, ...), custom_call_target="tpu_custom_call" | custom-call | tf_op jit(solution)/shard_map/pallas_call | solution.py:324
  28.9 0.0 collective-permute-done.7.refs_0_
  28.9 0.0 collective-permute-done.8.refs_1_
  28.9 0.1 collective-permute-start.9
  29.0 0.0 collective-permute-done.6.rest_1_
  29.0 0.0 collective-permute-done.5.rest_0_
  29.0 1.4 %shard_map.119 = (f32[128,2048]{1,0:T(8,128)S(1)}, f32[256,2048]{1,0:T(8,128)S(1)}) custom-call(bf16[128,2048]{1,0:T(8,128)(2,1)S(1)} %copy-done.1, bf16[256,2048]{1,0:T(8,128)(2,1)S(1)} %bitcast.8, f32[128,144]{1,0:T(8,128)S(1)} %get-tuple-element.22.sc_ref, f32[256,144]{1,0:T(8,128)S(1)} %get-tuple-element.28.order_ref.uc_ref, ...), custom_call_target="tpu_custom_call" | custom-call | tf_op jit(solution)/shard_map/pallas_call | solution.py:324
  30.5 0.4 %collective-permute-done.9.rest_1_ = bf16[1,16,128,128]{3,2,1,0:T(8,128)(2,1)S(1)} collective-permute-done((bf16[1,16,128,128]{3,2,1,0:T(8,128)(2,1)S(1)}, bf16[1,16,128,128]{3,2,1,0:T(8,128)(2,1)S(1)}, u32[]{:S(2)}, u32[]{:S(2)}) %collective-permute-start.9) | collective-permute-done | bytes 524320 | tf_op jit(solution)/shard_map/ppermute | solution.py:240
  30.9 0.0 copy-start.2
  30.9 1.7 %shard_map.121 = (f32[128,2048]{1,0:T(8,128)S(1)}, f32[256,2048]{1,0:T(8,128)S(1)}, f32[3,128]{1,0:T(4,128)S(1)}) custom-call(bf16[128,2048]{1,0:T(8,128)(2,1)S(1)} %copy-done.1, bf16[256,2048]{1,0:T(8,128)(2,1)S(1)} %bitcast.9, f32[128,144]{1,0:T(8,128)S(1)} %get-tuple-element.22.sc_ref, f32[256,144]{1,0:T(8,128)S(1)} %get-tuple-element.28.order_ref.uc_ref, ...), custom_call_target="tpu_custom_call" | custom-call | tf_op jit(solution)/shard_map/pallas_call | solution.py:324
  32.7 1.6 %collective-permute-start.10 = (f32[3,128]{1,0:T(4,128)S(1)}, f32[3,128]{1,0:T(4,128)S(1)}, u32[]{:S(2)}, u32[]{:S(2)}) collective-permute-start(f32[3,128]{1,0:T(4,128)S(1)} %get-tuple-element.39), channel_id=1, source_target_pairs={{0,1},{1,0},{2,3},{3,2},{4,5},{5,4},{6,7},{7,6},{8,9},{9,8},{10,11... | collective-permute-start | bytes 4616 | tf_op jit(solution)/shard_map/ppermute | solution.py:354
  34.3 2.0 %collective-permute-done.10 = f32[3,128]{1,0:T(4,128)S(1)} collective-permute-done((f32[3,128]{1,0:T(4,128)S(1)}, f32[3,128]{1,0:T(4,128)S(1)}, u32[]{:S(2)}, u32[]{:S(2)}) %collective-permute-start.10) | collective-permute-done | bytes 1568 | tf_op jit(solution)/shard_map/ppermute | solution.py:354
  36.3 2.6 %collective-permute-start.11 = (f32[3,128]{1,0:T(4,128)S(1)}, f32[3,128]{1,0:T(4,128)S(1)}, u32[]{:S(2)}, u32[]{:S(2)}) collective-permute-start(f32[3,128]{1,0:T(4,128)S(1)} %add.3.one_ref), channel_id=1, source_target_pairs={{0,2},{1,3},{2,0},{3,1},{4,6},{5,7},{6,4},{7,5},{8,10},{9,11},{10,... | collective-permute-start | bytes 4616 | tf_op jit(solution)/shard_map/ppermute | solution.py:354
  38.9 0.0 copy-done.2
  38.9 1.9 %collective-permute-done.11.two_ref = f32[3,128]{1,0:T(4,128)S(1)} collective-permute-done((f32[3,128]{1,0:T(4,128)S(1)}, f32[3,128]{1,0:T(4,128)S(1)}, u32[]{:S(2)}, u32[]{:S(2)}) %collective-permute-start.11) | collective-permute-done | bytes 1568 | tf_op jit(solution)/shard_map/ppermute | solution.py:354
  40.8 1.5 %shard_map.122 = (bf16[128,2048]{1,0:T(8,128)(2,1)}, bf16[256,2048]{1,0:T(8,128)(2,1)}) custom-call(f32[128,2048]{1,0:T(8,128)S(1)} %get-tuple-element.37.st_ref, f32[256,2048]{1,0:T(8,128)S(1)} %get-tuple-element.38.ut_ref, bf16[1,2048]{1,0:T(2,128)(2,1)S(1)} %reshape.30.gain_ref, f32[3,128]{1,0:T(4,128)S(1)} %add.3.one_ref, ...), custom_call_target="tpu_custom_call" | custom-call | tf_op jit(solution)/shard_map/pallas_call | solution.py:356
  (5 shorter events, 0.1 us)
Async XLA Ops:
  6.1 13.7 %collective-permute-start = (bf16[1,16,128,128]{3,2,1,0:T(8,128)(2,1)S(1)}, bf16[1,16,128,128]{3,2,1,0:T(8,128)(2,1)S(1)}, u32[]{:S(2)}, u32[]{:S(2)}) collective-permute-start(bf16[1,16,128,128]{3,2,1,0:T(8,128)(2,1)S(1)} %get-tuple-element.26.rest_0_), channel_id=1, source_target_pairs={{0,4},{4,0},{8,12},{12,8},{16,20},{20,16},{24,28},{28,24},{1,5},{5... | collective-permute-start | bytes 1572872 | tf_op jit(solution)/shard_map/ppermute | solution.py:240
  6.6 9.7 %collective-permute-start.1 = (bf16[8,128,128]{2,1,0:T(8,128)(2,1)S(1)}, bf16[8,128,128]{2,1,0:T(8,128)(2,1)S(1)}, u32[]{:S(2)}, u32[]{:S(2)}) collective-permute-start(bf16[8,128,128]{2,1,0:T(8,128)(2,1)S(1)} %get-tuple-element.32), channel_id=1, source_target_pairs={{0,8},{4,12},{8,0},{12,4},{16,24},{20,28},{24,16},{28,20},{1,9},{5... | collective-permute-start | bytes 786440 | tf_op jit(solution)/shard_map/ppermute | solution.py:240
  9.2 9.2 %collective-permute-start.2 = (bf16[8,128,128]{2,1,0:T(8,128)(2,1)S(1)}, bf16[8,128,128]{2,1,0:T(8,128)(2,1)S(1)}, u32[]{:S(2)}, u32[]{:S(2)}) collective-permute-start(bf16[8,128,128]{2,1,0:T(8,128)(2,1)S(1)} %get-tuple-element.31), channel_id=1, source_target_pairs={{0,16},{4,20},{8,24},{12,28},{16,0},{20,4},{24,8},{28,12},{1,17},{... | collective-permute-start | bytes 786440 | tf_op jit(solution)/shard_map/ppermute | solution.py:240
  10.7 14.0 %collective-permute-start.4 = (bf16[8,128,128]{2,1,0:T(8,128)(2,1)S(1)}, bf16[8,128,128]{2,1,0:T(8,128)(2,1)S(1)}, u32[]{:S(2)}, u32[]{:S(2)}) collective-permute-start(bf16[8,128,128]{2,1,0:T(8,128)(2,1)S(1)} %get-tuple-element.32), channel_id=1, source_target_pairs={{0,16},{4,20},{8,24},{12,28},{16,0},{20,4},{24,8},{28,12},{1,17},{... | collective-permute-start | bytes 786440 | tf_op jit(solution)/shard_map/ppermute | solution.py:240
  11.2 13.6 %collective-permute-start.3 = (bf16[8,128,128]{2,1,0:T(8,128)(2,1)S(1)}, bf16[8,128,128]{2,1,0:T(8,128)(2,1)S(1)}, u32[]{:S(2)}, u32[]{:S(2)}) collective-permute-start(bf16[8,128,128]{2,1,0:T(8,128)(2,1)S(1)} %get-tuple-element.31), channel_id=1, source_target_pairs={{0,8},{4,12},{8,0},{12,4},{16,24},{20,28},{24,16},{28,20},{1,9},{5... | collective-permute-start | bytes 786440 | tf_op jit(solution)/shard_map/ppermute | solution.py:240
  16.3 12.5 %collective-permute-start.7 = (bf16[8,128,128]{2,1,0:T(8,128)(2,1)S(1)}, bf16[8,128,128]{2,1,0:T(8,128)(2,1)S(1)}, u32[]{:S(2)}, u32[]{:S(2)}) collective-permute-start(bf16[8,128,128]{2,1,0:T(8,128)(2,1)S(1)} %collective-permute-done.1.refs_0_), channel_id=1, source_target_pairs={{0,16},{4,20},{8,24},{12,28},{16,0},{20,4},{24,8},{28,12},{1,17},{... | collective-permute-start | bytes 786440 | tf_op jit(solution)/shard_map/ppermute | solution.py:240
  18.3 10.6 %collective-permute-start.8 = (bf16[8,128,128]{2,1,0:T(8,128)(2,1)S(1)}, bf16[8,128,128]{2,1,0:T(8,128)(2,1)S(1)}, u32[]{:S(2)}, u32[]{:S(2)}) collective-permute-start(bf16[8,128,128]{2,1,0:T(8,128)(2,1)S(1)} %collective-permute-done.2.refs_1_), channel_id=1, source_target_pairs={{0,8},{4,12},{8,0},{12,4},{16,24},{20,28},{24,16},{28,20},{1,9},{5... | collective-permute-start | bytes 786440 | tf_op jit(solution)/shard_map/ppermute | solution.py:240
  24.7 1.2 %copy-start = (bf16[4,64,2048]{2,1,0:T(8,128)(2,1)S(1)}, bf16[4,64,2048]{2,1,0:T(8,128)(2,1)}, u32[]{:S(2)}) copy-start(bf16[4,64,2048]{2,1,0:T(8,128)(2,1)} %param.15) | copy-start | bytes 3145732
  24.7 1.3 %copy-start.1 = (bf16[128,2048]{1,0:T(8,128)(2,1)S(1)}, bf16[128,2048]{1,0:T(8,128)(2,1)}, u32[]{:S(2)}) copy-start(bf16[128,2048]{1,0:T(8,128)(2,1)} %sq_ref.5) | copy-start | bytes 1572868
  24.7 4.3 %collective-permute-start.6 = (bf16[1,16,128,128]{3,2,1,0:T(8,128)(2,1)S(1)}, bf16[1,16,128,128]{3,2,1,0:T(8,128)(2,1)S(1)}, u32[]{:S(2)}, u32[]{:S(2)}) collective-permute-start(bf16[1,16,128,128]{3,2,1,0:T(8,128)(2,1)S(1)} %shard_map.117.rest_3_), channel_id=1, source_target_pairs={{0,4},{4,0},{8,12},{12,8},{16,20},{20,16},{24,28},{28,24},{1,5},{5... | collective-permute-start | bytes 1572872 | tf_op jit(solution)/shard_map/ppermute | solution.py:240
  24.9 4.2 %collective-permute-start.5 = (bf16[1,16,128,128]{3,2,1,0:T(8,128)(2,1)S(1)}, bf16[1,16,128,128]{3,2,1,0:T(8,128)(2,1)S(1)}, u32[]{:S(2)}, u32[]{:S(2)}) collective-permute-start(bf16[1,16,128,128]{3,2,1,0:T(8,128)(2,1)S(1)} %shard_map.116.rest_2_), channel_id=1, source_target_pairs={{0,4},{4,0},{8,12},{12,8},{16,20},{20,16},{24,28},{28,24},{1,5},{5... | collective-permute-start | bytes 1572872 | tf_op jit(solution)/shard_map/ppermute | solution.py:240
  28.9 2.0 %collective-permute-start.9 = (bf16[1,16,128,128]{3,2,1,0:T(8,128)(2,1)S(1)}, bf16[1,16,128,128]{3,2,1,0:T(8,128)(2,1)S(1)}, u32[]{:S(2)}, u32[]{:S(2)}) collective-permute-start(bf16[1,16,128,128]{3,2,1,0:T(8,128)(2,1)S(1)} %shard_map.120.rest_0_), channel_id=1, source_target_pairs={{0,4},{4,0},{8,12},{12,8},{16,20},{20,16},{24,28},{28,24},{1,5},{5... | collective-permute-start | bytes 1572872 | tf_op jit(solution)/shard_map/ppermute | solution.py:240
  30.9 8.0 %copy-start.2 = (bf16[2048]{0:T(1024)(128)(2,1)S(1)}, bf16[2048]{0:T(1024)(128)(2,1)}, u32[]{:S(2)}) copy-start(bf16[2048]{0:T(1024)(128)(2,1)} %param.14) | copy-start | bytes 12292
  32.7 3.6 %collective-permute-start.10 = (f32[3,128]{1,0:T(4,128)S(1)}, f32[3,128]{1,0:T(4,128)S(1)}, u32[]{:S(2)}, u32[]{:S(2)}) collective-permute-start(f32[3,128]{1,0:T(4,128)S(1)} %get-tuple-element.39), channel_id=1, source_target_pairs={{0,1},{1,0},{2,3},{3,2},{4,5},{5,4},{6,7},{7,6},{8,9},{9,8},{10,11... | collective-permute-start | bytes 4616 | tf_op jit(solution)/shard_map/ppermute | solution.py:354
  36.3 4.5 %collective-permute-start.11 = (f32[3,128]{1,0:T(4,128)S(1)}, f32[3,128]{1,0:T(4,128)S(1)}, u32[]{:S(2)}, u32[]{:S(2)}) collective-permute-start(f32[3,128]{1,0:T(4,128)S(1)} %add.3.one_ref), channel_id=1, source_target_pairs={{0,2},{1,3},{2,0},{3,1},{4,6},{5,7},{6,4},{7,5},{8,10},{9,11},{10,... | collective-permute-start | bytes 4616 | tf_op jit(solution)/shard_map/ppermute | solution.py:354

commit v5 on v4

--- a/solution.py
+++ b/solution.py
@@ -79,12 +79,10 @@
     return jnp.where(jnp.logical_and(chosen, same), 1.0, 0.0).astype(jnp.bfloat16)
 
 
-def attend(mask, chunks, wait, q_ref, k_ref, v_ref, c_ref, o_ref, own):
+def attend(mask, q_ref, k_ref, v_ref, c_ref, o_ref, own):
     head_count = q_ref.shape[1] // HD
     step = 2
     for first in range(0, head_count, step):
-        if first % (head_count // chunks) == 0:
-            wait(first // (head_count // chunks))
         units = [
             (head, slice(head * HD, (head + 1) * HD), slice(start, start + ROWS))
             for head in range(first, first + step)
@@ -97,42 +95,45 @@
             o_ref[rows, cols] = result * c_ref[rows, own + head : own + head + 1]
 
 
-def local_kernel(depth, suffix, chunks, *refs):
-    small_count = 2 if suffix else 1
-    refs = list(refs)
-    take = lambda count: [refs.pop(0) for _ in range(count)]
-    small, sources, (o_ref, c_ref), small_loaded, loaded = take(small_count), take(3), take(2), take(small_count), take(3)
-    small_sems, sems = refs
-    small_copies = [
-        pltpu.make_async_copy(source, target, small_sems.at[i])
-        for i, (source, target) in enumerate(zip(small, small_loaded))
+def causal_mask(suffix=ROWS):
+    row = lax.broadcasted_iota(jnp.int32, (ROWS, ROWS), 0)
+    col = lax.broadcasted_iota(jnp.int32, (ROWS, ROWS), 1)
+    return jnp.logical_and(row >= col, row // suffix == col // suffix)
+
+
+def slab_kernel(depth, suffix, *refs):
+    sources, (k_ref, v_ref), (o_ref, sc_ref, uc_ref), rest = refs[:7], refs[7:9], refs[9:12], refs[12:]
+    q_ref, user_loaded, small_loaded, sems = rest[0], rest[1:4], rest[4:7], rest[7]
+    copies = [
+        pltpu.make_async_copy(source, target, sems.at[i])
+        for i, (source, target) in enumerate(zip(sources, (*small_loaded, q_ref, *user_loaded)))
     ]
-    for copy in small_copies:
+    for copy in copies:
         copy.start()
-    wait = load_columns(sources, loaded, sems, chunks)
-    for copy in small_copies:
+    for copy in copies[:3]:
         copy.wait()
-    weight_ref = small_loaded[-1]
-    head_count = loaded[0].shape[1] // HD
-    position = lax.axis_index("seq").astype(jnp.int32)
+    length_ref, slab_table, user_table = small_loaded
+    head_count = q_ref.shape[1] // HD
     pick = functools.partial(
         choose_levels,
-        position=position,
+        position=lax.axis_index("seq").astype(jnp.int32),
         depth=depth,
-        level_count=weight_ref.shape[-2] // head_count,
+        level_count=slab_table.shape[0] // head_count,
         head_count=head_count,
     )
-    row = lax.broadcasted_iota(jnp.int32, (ROWS, ROWS), 0)
-    col = lax.broadcasted_iota(jnp.int32, (ROWS, ROWS), 1)
-    mask = row >= col
-    if suffix:
-        mask = jnp.logical_and(mask, row // suffix == col // suffix)
-        for user in range(weight_ref.shape[0]):
-            weights = matmul(weight_ref[user], pick(small_loaded[0][user]), ((0,), (0,)))
-            c_ref[user * suffix : (user + 1) * suffix] = weights
-    else:
-        c_ref[...] = matmul(weight_ref[...], pick(position), ((0,), (0,)))
-    attend(mask, chunks, wait, *loaded, c_ref, o_ref, (1 << depth) * head_count)
+    sc_ref[...] = matmul(slab_table[...], pick(lax.axis_index("seq").astype(jnp.int32)), ((0,), (0,)))
+    for user in range(user_table.shape[0]):
+        weights = matmul(user_table[user], pick(length_ref[user]), ((0,), (0,)))
+        uc_ref[user * suffix : (user + 1) * suffix] = weights
+    copies[3].wait()
+    attend(causal_mask(), q_ref, k_ref, v_ref, sc_ref, o_ref, (1 << depth) * head_count)
+    for copy in copies[4:]:
+        copy.wait()
+
+
+def user_kernel(depth, suffix, c_ref, q_ref, k_ref, v_ref, o_ref):
+    own = (1 << depth) * (q_ref.shape[1] // HD)
+    attend(causal_mask(suffix), q_ref, k_ref, v_ref, c_ref, o_ref, own)
 
 
 def add_blocks(groups, state_refs, head_count, head, q_ref, c_ref, base):
@@ -252,30 +253,16 @@
         )(order, *halves)
 
     half_state = pltpu.VMEM((half, HD, HD), jnp.bfloat16)
-    first, second, state = pl.pallas_call(
+    slab_rows = pltpu.VMEM((token_count, width), jnp.bfloat16)
+    first, second, state, slab_keys, slab_values = pl.pallas_call(
         functools.partial(state_kernel, chunks),
-        out_shape=[half_state, half_state, pltpu.VMEM((1, head_count, HD, HD), jnp.bfloat16)],
+        out_shape=[half_state, half_state, pltpu.VMEM((1, head_count, HD, HD), jnp.bfloat16), slab_rows, slab_rows],
         in_specs=[hbm] * 2,
-        out_specs=[vmem] * 3,
-        scratch_shapes=[pltpu.VMEM((token_count, width), jnp.bfloat16)] * 2 + [pltpu.SemaphoreType.DMA((2, chunks))],
+        out_specs=[vmem] * 5,
+        scratch_shapes=[pltpu.SemaphoreType.DMA((2, chunks))],
         compiler_params=params,
     )(*pinned(slab_key, slab_value))
     halves = [first, second]
-
-    columns = (seq_count + 1) * head_count
-
-    def local_part(rows, suffix, small, scratch, arrays):
-        return pl.pallas_call(
-            functools.partial(local_kernel, depth, suffix, chunks),
-            out_shape=[pltpu.VMEM((rows, width), jnp.float32), pltpu.VMEM((rows, columns), jnp.float32)],
-            in_specs=[hbm] * (len(small) + 3),
-            out_specs=[vmem] * 2,
-            scratch_shapes=scratch
-            + [pltpu.VMEM((rows, width), jnp.bfloat16)] * 3
-            + [pltpu.SemaphoreType.DMA((len(small),)), pltpu.SemaphoreType.DMA((3, chunks))],
-            compiler_params=params,
-            cost_estimate=cost(0, 0),
-        )(*pinned(*small), *pinned(*arrays))
 
     outer = list(range(1, depth))
     places = [(bit, side) for bit in outer for side in range(2)]
@@ -284,14 +271,34 @@
     for bit, side in ahead:
         sides[1 << bit][side] = swap(halves[side], bit)
     slab_table = slab_levels.reshape(-1, token_count)
-    slab_acc, slab_coef = local_part(
-        token_count,
-        0,
-        [slab_table],
-        [pltpu.VMEM(slab_table.shape, jnp.bfloat16)],
-        [slab_query, slab_key, slab_value],
+    user_table = user_levels.reshape(user_count, -1, suffix)
+    columns = (seq_count + 1) * head_count
+    slab_acc, slab_coef, user_coef, slab_queries, user_queries, user_keys, user_values = pl.pallas_call(
+        functools.partial(slab_kernel, depth, suffix),
+        out_shape=[
+            pltpu.VMEM((token_count, width), jnp.float32),
+            pltpu.VMEM((token_count, columns), jnp.float32),
+            pltpu.VMEM((user_rows, columns), jnp.float32),
+            slab_rows,
+        ]
+        + [pltpu.VMEM((user_rows, width), jnp.bfloat16)] * 3,
+        in_specs=[hbm] * 7 + [vmem] * 2,
+        out_specs=[vmem] * 7,
+        scratch_shapes=[
+            pltpu.SMEM((user_count,), jnp.int32),
+            pltpu.VMEM(slab_table.shape, jnp.bfloat16),
+            pltpu.VMEM(user_table.shape, jnp.bfloat16),
+            pltpu.SemaphoreType.DMA((7,)),
+        ],
+        compiler_params=params,
+        cost_estimate=cost(0, 0),
+    )(
+        *pinned(prefix_lengths, slab_table, user_table, slab_query),
+        *pinned(*[array.reshape(user_rows, width) for array in (user_query, user_key, user_value)]),
+        slab_keys,
+        slab_values,
     )
-    state, *halves = after(slab_coef, [state] + halves)
+    halves = after(slab_coef, halves)
     whole = {0: state, 1: swap(state, 0)}
     for bit, side in places:
         if (bit, side) not in ahead:
@@ -301,16 +308,15 @@
     for m in later:
         high, low = m.bit_length() - 1, (m & -m).bit_length() - 1
         sides[m] = [swap(sides[m ^ (1 << high)][0], high), swap(sides[m ^ (1 << low)][1], low)]
-    user_queries = user_query.reshape(user_rows, width)
-    user_table = user_levels.reshape(user_count, -1, suffix)
-    lengths = after([whole[1]] + [sides[1 << bit][side] for bit, side in ahead], [prefix_lengths])[0]
-    user_acc, user_coef = local_part(
-        user_rows,
-        suffix,
-        [lengths, user_table],
-        [pltpu.SMEM((user_count,), jnp.int32), pltpu.VMEM(user_table.shape, jnp.bfloat16)],
-        [user_queries, user_key.reshape(user_rows, width), user_value.reshape(user_rows, width)],
-    )
+    user_coef = after([sides[1 << bit][side] for bit, side in ahead], [user_coef])[0]
+    user_acc = pl.pallas_call(
+        functools.partial(user_kernel, depth, suffix),
+        out_shape=pltpu.VMEM((user_rows, width), jnp.float32),
+        in_specs=[vmem] * 4,
+        out_specs=vmem,
+        compiler_params=params,
+        cost_estimate=cost(0, 0),
+    )(user_coef, user_queries, user_keys, user_values)
 
     def read(groups, states, accs, last):
         found = {}
@@ -329,7 +335,7 @@
             scratch_shapes=scratch,
             compiler_params=params,
             cost_estimate=cost(0, 0),
-        )(slab_query, user_queries, slab_coef, user_coef, *accs, *[array for _, array in states])
+        )(slab_queries, user_queries, slab_coef, user_coef, *accs, *[array for _, array in states])
 
     def pairs(offsets):
         return [tuple(offsets[i : i + 2]) for i in range(0, len(offsets), 2)]
@@ -337,7 +343,7 @@
     direct = [1 << bit for bit in outer]
     mates = [m | 1 for m in direct]
     for m in direct:
-        whole[m] = join(user_coef, sides[m])
+        whole[m] = join(user_acc, sides[m])
     for m in direct:
         whole[m | 1] = swap(whole[m], 0)
     accs = read(pairs([0, 1] + direct), [([m], whole[m]) for m in [0, 1] + direct], (slab_acc, user_acc), False)

time: 42.5 us -> 38.9 us (0.915)
  Pallas kernels: 17.9 us -> 14.8 us
  local copies, waits for them, and re-layouts: 0.62 us -> 0.01 us
    pallas_call x2, Pallas kernels: 8.38 us -> 5.12 us  [the longest x1 3.17 us: local(): pl.pallas_call(functools.partial(slab_kernel, depth, suffix), out_shape=[...]
    unnamed x6 -> x2, local copies, waits for them, and re-layouts: 0.61 us -> 0.01 us
  transfers between devices with their start and end apart: 12 -> 12, of which waited for: 4 -> 7; matrix products, arithmetic and copies ran while one was open for 0% -> 0% of each run, Pallas kernels for 22% -> 25%
where the time goes in v5:
time: 38.9 us; the launch traced here: 38.8 us
  Pallas kernels  14.8 us (38%)
  starting transfers between devices  13.5 us (35%)
  waiting for transfers between devices  9.77 us (25%)
  between operations  0.73 us (2%)
    ppermute x10, starting transfers between devices, swap(): lax.ppermute(value, 'seq', [(i, i ^ 1 << bit) for i in range(seq_count)])  9.24 us
    pallas_call x3, Pallas kernels, read(): pl.pallas_call(functools.partial(read_kernel, groups, found, last), out_s...  6.12 us
    ppermute x10, waiting for transfers between devices, swap(): lax.ppermute(value, 'seq', [(i, i ^ 1 << bit) for i in range(seq_count)])  5.88 us
    ppermute x2, starting transfers between devices, local(): lax.ppermute(square, 'head', [(i, i ^ 1 << bit) for i in range(head_axis)])  4.23 us
    ppermute x2, waiting for transfers between devices, local(): lax.ppermute(square, 'head', [(i, i ^ 1 << bit) for i in range(head_axis)])  3.89 us
    pallas_call x1, Pallas kernels, local(): pl.pallas_call(functools.partial(slab_kernel, depth, suffix), out_shape=[...  3.17 us
    pallas_call x1, Pallas kernels, local(): pl.pallas_call(functools.partial(user_kernel, depth, suffix), out_shape=p...  1.94 us
    pallas_call x1, Pallas kernels, local(): pl.pallas_call(functools.partial(state_kernel, chunks), out_shape=[half_s...  1.91 us
  transfers between devices with their start and end apart: 12, of which 7 were waited for; matrix products, arithmetic and copies ran while one was open for 0% of the time, Pallas kernels for 25%

profile of v5, /device:TPU:0, one launch (start us, length us, event | category | flops | bytes accessed | tf_op | source)
XLA Modules:
  0.0 38.8 jit_solution(9022288458434326861)
XLA Ops:
  0.6 1.9 %shard_map.113 = (bf16[8,128,128]{2,1,0:T(8,128)(2,1)S(1)}, bf16[8,128,128]{2,1,0:T(8,128)(2,1)S(1)}, bf16[1,16,128,128]{3,2,1,0:T(8,128)(2,1)S(1)}, bf16[128,2048]{1,0:T(8,128)(2,1)S(1)}, bf16[128,2048]{1,0:T(8,128)(2,1)S(1)}) custom-call(bf16[128,2048]{1,0:T(8,128)(2,1)} %key_hbm.1, bf16[128,2048]{1,0:T(8,128)(2,1)} %value_hbm.1), custom_call_target="tpu_custom_call" | custom-call | tf_op jit(solution)/shard_map/pallas_call | solution.py:257
  2.6 0.5 %collective-permute-start.2 = (bf16[1,16,128,128]{3,2,1,0:T(8,128)(2,1)S(1)}, bf16[1,16,128,128]{3,2,1,0:T(8,128)(2,1)S(1)}, u32[]{:S(2)}, u32[]{:S(2)}) collective-permute-start(bf16[1,16,128,128]{3,2,1,0:T(8,128)(2,1)S(1)} %get-tuple-element.38.rest_0_), channel_id=1, source_target_pairs={{0,4},{4,0},{8,12},{12,8},{16,20},{20,16},{24,28},{28,24},{1,5},{5... | collective-permute-start | bytes 1572872 | tf_op jit(solution)/shard_map/ppermute | solution.py:241
  3.1 2.6 %collective-permute-start = (bf16[8,128,128]{2,1,0:T(8,128)(2,1)S(1)}, bf16[8,128,128]{2,1,0:T(8,128)(2,1)S(1)}, u32[]{:S(2)}, u32[]{:S(2)}) collective-permute-start(bf16[8,128,128]{2,1,0:T(8,128)(2,1)S(1)} %get-tuple-element.40), channel_id=1, source_target_pairs={{0,8},{4,12},{8,0},{12,4},{16,24},{20,28},{24,16},{28,20},{1,9},{5... | collective-permute-start | bytes 786440 | tf_op jit(solution)/shard_map/ppermute | solution.py:241
  5.6 1.5 %collective-permute-start.1 = (bf16[8,128,128]{2,1,0:T(8,128)(2,1)S(1)}, bf16[8,128,128]{2,1,0:T(8,128)(2,1)S(1)}, u32[]{:S(2)}, u32[]{:S(2)}) collective-permute-start(bf16[8,128,128]{2,1,0:T(8,128)(2,1)S(1)} %get-tuple-element.39), channel_id=1, source_target_pairs={{0,16},{4,20},{8,24},{12,28},{16,0},{20,4},{24,8},{28,12},{1,17},{... | collective-permute-start | bytes 786440 | tf_op jit(solution)/shard_map/ppermute | solution.py:241
  7.2 3.2 %shard_map.114 = (f32[128,2048]{1,0:T(8,128)S(1)}, f32[128,144]{1,0:T(8,128)S(1)}, f32[256,144]{1,0:T(8,128)S(1)}, bf16[128,2048]{1,0:T(8,128)(2,1)S(1)}, bf16[2...) custom-call(s32[4]{0:T(128)} %refs_0_.1, bf16[96,128]{1,0:T(8,128)(2,1)} %bitcast.10, ...), custom_call_target="tpu_custom_call" | custom-call | tf_op jit(solution)/shard_map/pallas_call | solution.py:276
  10.3 0.6 %collective-permute-start.4 = (bf16[8,128,128]{2,1,0:T(8,128)(2,1)S(1)}, bf16[8,128,128]{2,1,0:T(8,128)(2,1)S(1)}, u32[]{:S(2)}, u32[]{:S(2)}) collective-permute-start(bf16[8,128,128]{2,1,0:T(8,128)(2,1)S(1)} %get-tuple-element.40), channel_id=1, source_target_pairs={{0,16},{4,20},{8,24},{12,28},{16,0},{20,4},{24,8},{28,12},{1,17},{... | collective-permute-start | bytes 786440 | tf_op jit(solution)/shard_map/ppermute | solution.py:241
  10.9 0.1 collective-permute-start.3
  11.0 1.5 %collective-permute-done.refs_0_ = bf16[8,128,128]{2,1,0:T(8,128)(2,1)S(1)} collective-permute-done((bf16[8,128,128]{2,1,0:T(8,128)(2,1)S(1)}, bf16[8,128,128]{2,1,0:T(8,128)(2,1)S(1)}, u32[]{:S(2)}, u32[]{:S(2)}) %collective-permute-start) | collective-permute-done | bytes 262176 | tf_op jit(solution)/shard_map/ppermute | solution.py:241
  12.5 1.8 %collective-permute-start.7 = (bf16[8,128,128]{2,1,0:T(8,128)(2,1)S(1)}, bf16[8,128,128]{2,1,0:T(8,128)(2,1)S(1)}, u32[]{:S(2)}, u32[]{:S(2)}) collective-permute-start(bf16[8,128,128]{2,1,0:T(8,128)(2,1)S(1)} %collective-permute-done.refs_0_), channel_id=1, source_target_pairs={{0,16},{4,20},{8,24},{12,28},{16,0},{20,4},{24,8},{28,12},{1,17},{... | collective-permute-start | bytes 786440 | tf_op jit(solution)/shard_map/ppermute | solution.py:241
  14.3 0.5 %collective-permute-done.1.refs_1_ = bf16[8,128,128]{2,1,0:T(8,128)(2,1)S(1)} collective-permute-done((bf16[8,128,128]{2,1,0:T(8,128)(2,1)S(1)}, bf16[8,128,128]{2,1,0:T(8,128)(2,1)S(1)}, u32[]{:S(2)}, u32[]{:S(2)}) %collective-permute-start.1) | collective-permute-done | bytes 262176 | tf_op jit(solution)/shard_map/ppermute | solution.py:241
  14.8 1.5 %collective-permute-start.8 = (bf16[8,128,128]{2,1,0:T(8,128)(2,1)S(1)}, bf16[8,128,128]{2,1,0:T(8,128)(2,1)S(1)}, u32[]{:S(2)}, u32[]{:S(2)}) collective-permute-start(bf16[8,128,128]{2,1,0:T(8,128)(2,1)S(1)} %collective-permute-done.1.refs_1_), channel_id=1, source_target_pairs={{0,8},{4,12},{8,0},{12,4},{16,24},{20,28},{24,16},{28,20},{1,9},{5... | collective-permute-start | bytes 786440 | tf_op jit(solution)/shard_map/ppermute | solution.py:241
  16.3 1.9 %shard_map.115.order_ref.ua_ref = f32[256,2048]{1,0:T(8,128)S(1)} custom-call(f32[256,144]{1,0:T(8,128)S(1)} %get-tuple-element.34.c_ref.uc_ref, bf16[256,2048]{1,0:T(8,128)(2,1)S(1)} %get-tuple-element.29.q_ref.uq_ref, bf16[256,2048]{1,0:T(8,128)(2,1)S(1)} %get-tuple-element.36.k_ref, bf16[256,2048]{1,0:T(8,128)(2,1)S(1)} %get-tuple-element.37.v_ref), custom_call_target="tpu_custom_call" | custom-call | tf_op jit(solution)/shard_map/pallas_call | solution.py:312
  18.2 2.2 %collective-permute-done.4.refs_0_ = bf16[8,128,128]{2,1,0:T(8,128)(2,1)S(1)} collective-permute-done((bf16[8,128,128]{2,1,0:T(8,128)(2,1)S(1)}, bf16[8,128,128]{2,1,0:T(8,128)(2,1)S(1)}, u32[]{:S(2)}, u32[]{:S(2)}) %collective-permute-start.4) | collective-permute-done | bytes 262176 | tf_op jit(solution)/shard_map/ppermute | solution.py:241
  20.4 0.1 collective-permute-start.6
  20.5 0.0 collective-permute-done.3.refs_1_
  20.6 0.5 %collective-permute-start.5 = (bf16[1,16,128,128]{3,2,1,0:T(8,128)(2,1)S(1)}, bf16[1,16,128,128]{3,2,1,0:T(8,128)(2,1)S(1)}, u32[]{:S(2)}, u32[]{:S(2)}) collective-permute-start(bf16[1,16,128,128]{3,2,1,0:T(8,128)(2,1)S(1)} %shard_map.116.rest_2_), channel_id=1, source_target_pairs={{0,4},{4,0},{8,12},{12,8},{16,20},{20,16},{24,28},{28,24},{1,5},{5... | collective-permute-start | bytes 1572872 | tf_op jit(solution)/shard_map/ppermute | solution.py:241
  21.1 0.0 collective-permute-done.2.rest_1_
  21.1 2.8 %shard_map.118 = (f32[128,2048]{1,0:T(8,128)S(1)}, f32[256,2048]{1,0:T(8,128)S(1)}) custom-call(bf16[128,2048]{1,0:T(8,128)(2,1)S(1)} %get-tuple-element.28.sq_ref, bf16[256,2048]{1,0:T(8,128)(2,1)S(1)} %get-tuple-element.29.q_ref.uq_ref, f32[128,144]{1,0:T(8,128)S(1)} %get-tuple-element.30.sc_ref, f32[256,144]{1,0:T(8,128)S(1)} %get-tuple-element.34.c_ref.uc_ref, ...), custom_call_target="tpu_custom_call" | custom-call | tf_op jit(solution)/shard_map/pallas_call | solution.py:330
  24.0 1.3 %collective-permute-done.7.refs_0_ = bf16[8,128,128]{2,1,0:T(8,128)(2,1)S(1)} collective-permute-done((bf16[8,128,128]{2,1,0:T(8,128)(2,1)S(1)}, bf16[8,128,128]{2,1,0:T(8,128)(2,1)S(1)}, u32[]{:S(2)}, u32[]{:S(2)}) %collective-permute-start.7) | collective-permute-done | bytes 262176 | tf_op jit(solution)/shard_map/ppermute | solution.py:241
  25.2 0.0 collective-permute-done.8.refs_1_
  25.3 0.1 collective-permute-start.9
  25.4 0.0 collective-permute-done.6.rest_1_
  25.4 0.0 collective-permute-done.5.rest_0_
  25.4 1.4 %shard_map.119 = (f32[128,2048]{1,0:T(8,128)S(1)}, f32[256,2048]{1,0:T(8,128)S(1)}) custom-call(bf16[128,2048]{1,0:T(8,128)(2,1)S(1)} %get-tuple-element.28.sq_ref, bf16[256,2048]{1,0:T(8,128)(2,1)S(1)} %get-tuple-element.29.q_ref.uq_ref, f32[128,144]{1,0:T(8,128)S(1)} %get-tuple-element.30.sc_ref, f32[256,144]{1,0:T(8,128)S(1)} %get-tuple-element.34.c_ref.uc_ref, ...), custom_call_target="tpu_custom_call" | custom-call | tf_op jit(solution)/shard_map/pallas_call | solution.py:330
  26.8 0.4 %collective-permute-done.9.rest_1_ = bf16[1,16,128,128]{3,2,1,0:T(8,128)(2,1)S(1)} collective-permute-done((bf16[1,16,128,128]{3,2,1,0:T(8,128)(2,1)S(1)}, bf16[1,16,128,128]{3,2,1,0:T(8,128)(2,1)S(1)}, u32[]{:S(2)}, u32[]{:S(2)}) %collective-permute-start.9) | collective-permute-done | bytes 524320 | tf_op jit(solution)/shard_map/ppermute | solution.py:241
  27.3 0.0 copy-start
  27.3 1.8 %shard_map.121 = (f32[128,2048]{1,0:T(8,128)S(1)}, f32[256,2048]{1,0:T(8,128)S(1)}, f32[3,128]{1,0:T(4,128)S(1)}) custom-call(bf16[128,2048]{1,0:T(8,128)(2,1)S(1)} %get-tuple-element.28.sq_ref, bf16[256,2048]{1,0:T(8,128)(2,1)S(1)} %get-tuple-element.29.q_ref.uq_ref, f32[128,144]{1,0:T(8,128)S(1)} %get-tuple-element.30.sc_ref, ...), custom_call_target="tpu_custom_call" | custom-call | tf_op jit(solution)/shard_map/pallas_call | solution.py:330
  29.1 1.6 %collective-permute-start.10 = (f32[3,128]{1,0:T(4,128)S(1)}, f32[3,128]{1,0:T(4,128)S(1)}, u32[]{:S(2)}, u32[]{:S(2)}) collective-permute-start(f32[3,128]{1,0:T(4,128)S(1)} %get-tuple-element.47), channel_id=1, source_target_pairs={{0,1},{1,0},{2,3},{3,2},{4,5},{5,4},{6,7},{7,6},{8,9},{9,8},{10,11... | collective-permute-start | bytes 4616 | tf_op jit(solution)/shard_map/ppermute | solution.py:360
  30.7 2.0 %collective-permute-done.10 = f32[3,128]{1,0:T(4,128)S(1)} collective-permute-done((f32[3,128]{1,0:T(4,128)S(1)}, f32[3,128]{1,0:T(4,128)S(1)}, u32[]{:S(2)}, u32[]{:S(2)}) %collective-permute-start.10) | collective-permute-done | bytes 1568 | tf_op jit(solution)/shard_map/ppermute | solution.py:360
  32.8 2.6 %collective-permute-start.11 = (f32[3,128]{1,0:T(4,128)S(1)}, f32[3,128]{1,0:T(4,128)S(1)}, u32[]{:S(2)}, u32[]{:S(2)}) collective-permute-start(f32[3,128]{1,0:T(4,128)S(1)} %add.3.one_ref), channel_id=1, source_target_pairs={{0,2},{1,3},{2,0},{3,1},{4,6},{5,7},{6,4},{7,5},{8,10},{9,11},{10,... | collective-permute-start | bytes 4616 | tf_op jit(solution)/shard_map/ppermute | solution.py:360
  35.3 0.0 copy-done
  35.4 1.9 %collective-permute-done.11.two_ref = f32[3,128]{1,0:T(4,128)S(1)} collective-permute-done((f32[3,128]{1,0:T(4,128)S(1)}, f32[3,128]{1,0:T(4,128)S(1)}, u32[]{:S(2)}, u32[]{:S(2)}) %collective-permute-start.11) | collective-permute-done | bytes 1568 | tf_op jit(solution)/shard_map/ppermute | solution.py:360
  37.2 1.5 %shard_map.122 = (bf16[128,2048]{1,0:T(8,128)(2,1)}, bf16[256,2048]{1,0:T(8,128)(2,1)}) custom-call(f32[128,2048]{1,0:T(8,128)S(1)} %get-tuple-element.45.st_ref, f32[256,2048]{1,0:T(8,128)S(1)} %get-tuple-element.46.ut_ref, bf16[1,2048]{1,0:T(2,128)(2,1)S(1)} %reshape.30.gain_ref, f32[3,128]{1,0:T(4,128)S(1)} %add.3.one_ref, ...), custom_call_target="tpu_custom_call" | custom-call | tf_op jit(solution)/shard_map/pallas_call | solution.py:362
  (5 shorter events, 0.1 us)
Async XLA Ops:
  2.6 18.6 %collective-permute-start.2 = (bf16[1,16,128,128]{3,2,1,0:T(8,128)(2,1)S(1)}, bf16[1,16,128,128]{3,2,1,0:T(8,128)(2,1)S(1)}, u32[]{:S(2)}, u32[]{:S(2)}) collective-permute-start(bf16[1,16,128,128]{3,2,1,0:T(8,128)(2,1)S(1)} %get-tuple-element.38.rest_0_), channel_id=1, source_target_pairs={{0,4},{4,0},{8,12},{12,8},{16,20},{20,16},{24,28},{28,24},{1,5},{5... | collective-permute-start | bytes 1572872 | tf_op jit(solution)/shard_map/ppermute | solution.py:241
  3.1 9.5 %collective-permute-start = (bf16[8,128,128]{2,1,0:T(8,128)(2,1)S(1)}, bf16[8,128,128]{2,1,0:T(8,128)(2,1)S(1)}, u32[]{:S(2)}, u32[]{:S(2)}) collective-permute-start(bf16[8,128,128]{2,1,0:T(8,128)(2,1)S(1)} %get-tuple-element.40), channel_id=1, source_target_pairs={{0,8},{4,12},{8,0},{12,4},{16,24},{20,28},{24,16},{28,20},{1,9},{5... | collective-permute-start | bytes 786440 | tf_op jit(solution)/shard_map/ppermute | solution.py:241
  5.6 9.2 %collective-permute-start.1 = (bf16[8,128,128]{2,1,0:T(8,128)(2,1)S(1)}, bf16[8,128,128]{2,1,0:T(8,128)(2,1)S(1)}, u32[]{:S(2)}, u32[]{:S(2)}) collective-permute-start(bf16[8,128,128]{2,1,0:T(8,128)(2,1)S(1)} %get-tuple-element.39), channel_id=1, source_target_pairs={{0,16},{4,20},{8,24},{12,28},{16,0},{20,4},{24,8},{28,12},{1,17},{... | collective-permute-start | bytes 786440 | tf_op jit(solution)/shard_map/ppermute | solution.py:241
  10.3 10.1 %collective-permute-start.4 = (bf16[8,128,128]{2,1,0:T(8,128)(2,1)S(1)}, bf16[8,128,128]{2,1,0:T(8,128)(2,1)S(1)}, u32[]{:S(2)}, u32[]{:S(2)}) collective-permute-start(bf16[8,128,128]{2,1,0:T(8,128)(2,1)S(1)} %get-tuple-element.40), channel_id=1, source_target_pairs={{0,16},{4,20},{8,24},{12,28},{16,0},{20,4},{24,8},{28,12},{1,17},{... | collective-permute-start | bytes 786440 | tf_op jit(solution)/shard_map/ppermute | solution.py:241
  10.9 9.6 %collective-permute-start.3 = (bf16[8,128,128]{2,1,0:T(8,128)(2,1)S(1)}, bf16[8,128,128]{2,1,0:T(8,128)(2,1)S(1)}, u32[]{:S(2)}, u32[]{:S(2)}) collective-permute-start(bf16[8,128,128]{2,1,0:T(8,128)(2,1)S(1)} %get-tuple-element.39), channel_id=1, source_target_pairs={{0,8},{4,12},{8,0},{12,4},{16,24},{20,28},{24,16},{28,20},{1,9},{5... | collective-permute-start | bytes 786440 | tf_op jit(solution)/shard_map/ppermute | solution.py:241
  12.5 12.7 %collective-permute-start.7 = (bf16[8,128,128]{2,1,0:T(8,128)(2,1)S(1)}, bf16[8,128,128]{2,1,0:T(8,128)(2,1)S(1)}, u32[]{:S(2)}, u32[]{:S(2)}) collective-permute-start(bf16[8,128,128]{2,1,0:T(8,128)(2,1)S(1)} %collective-permute-done.refs_0_), channel_id=1, source_target_pairs={{0,16},{4,20},{8,24},{12,28},{16,0},{20,4},{24,8},{28,12},{1,17},{... | collective-permute-start | bytes 786440 | tf_op jit(solution)/shard_map/ppermute | solution.py:241
  14.8 10.5 %collective-permute-start.8 = (bf16[8,128,128]{2,1,0:T(8,128)(2,1)S(1)}, bf16[8,128,128]{2,1,0:T(8,128)(2,1)S(1)}, u32[]{:S(2)}, u32[]{:S(2)}) collective-permute-start(bf16[8,128,128]{2,1,0:T(8,128)(2,1)S(1)} %collective-permute-done.1.refs_1_), channel_id=1, source_target_pairs={{0,8},{4,12},{8,0},{12,4},{16,24},{20,28},{24,16},{28,20},{1,9},{5... | collective-permute-start | bytes 786440 | tf_op jit(solution)/shard_map/ppermute | solution.py:241
  20.4 4.9 %collective-permute-start.6 = (bf16[1,16,128,128]{3,2,1,0:T(8,128)(2,1)S(1)}, bf16[1,16,128,128]{3,2,1,0:T(8,128)(2,1)S(1)}, u32[]{:S(2)}, u32[]{:S(2)}) collective-permute-start(bf16[1,16,128,128]{3,2,1,0:T(8,128)(2,1)S(1)} %shard_map.117.rest_3_), channel_id=1, source_target_pairs={{0,4},{4,0},{8,12},{12,8},{16,20},{20,16},{24,28},{28,24},{1,5},{5... | collective-permute-start | bytes 1572872 | tf_op jit(solution)/shard_map/ppermute | solution.py:241
  20.6 4.8 %collective-permute-start.5 = (bf16[1,16,128,128]{3,2,1,0:T(8,128)(2,1)S(1)}, bf16[1,16,128,128]{3,2,1,0:T(8,128)(2,1)S(1)}, u32[]{:S(2)}, u32[]{:S(2)}) collective-permute-start(bf16[1,16,128,128]{3,2,1,0:T(8,128)(2,1)S(1)} %shard_map.116.rest_2_), channel_id=1, source_target_pairs={{0,4},{4,0},{8,12},{12,8},{16,20},{20,16},{24,28},{28,24},{1,5},{5... | collective-permute-start | bytes 1572872 | tf_op jit(solution)/shard_map/ppermute | solution.py:241
  25.3 2.0 %collective-permute-start.9 = (bf16[1,16,128,128]{3,2,1,0:T(8,128)(2,1)S(1)}, bf16[1,16,128,128]{3,2,1,0:T(8,128)(2,1)S(1)}, u32[]{:S(2)}, u32[]{:S(2)}) collective-permute-start(bf16[1,16,128,128]{3,2,1,0:T(8,128)(2,1)S(1)} %shard_map.120.rest_0_), channel_id=1, source_target_pairs={{0,4},{4,0},{8,12},{12,8},{16,20},{20,16},{24,28},{28,24},{1,5},{5... | collective-permute-start | bytes 1572872 | tf_op jit(solution)/shard_map/ppermute | solution.py:241
  27.3 8.1 %copy-start = (bf16[2048]{0:T(1024)(128)(2,1)S(1)}, bf16[2048]{0:T(1024)(128)(2,1)}, u32[]{:S(2)}) copy-start(bf16[2048]{0:T(1024)(128)(2,1)} %param.14) | copy-start | bytes 12292
  29.1 3.6 %collective-permute-start.10 = (f32[3,128]{1,0:T(4,128)S(1)}, f32[3,128]{1,0:T(4,128)S(1)}, u32[]{:S(2)}, u32[]{:S(2)}) collective-permute-start(f32[3,128]{1,0:T(4,128)S(1)} %get-tuple-element.47), channel_id=1, source_target_pairs={{0,1},{1,0},{2,3},{3,2},{4,5},{5,4},{6,7},{7,6},{8,9},{9,8},{10,11... | collective-permute-start | bytes 4616 | tf_op jit(solution)/shard_map/ppermute | solution.py:360
  32.8 4.5 %collective-permute-start.11 = (f32[3,128]{1,0:T(4,128)S(1)}, f32[3,128]{1,0:T(4,128)S(1)}, u32[]{:S(2)}, u32[]{:S(2)}) collective-permute-start(f32[3,128]{1,0:T(4,128)S(1)} %add.3.one_ref), channel_id=1, source_target_pairs={{0,2},{1,3},{2,0},{3,1},{4,6},{5,7},{6,4},{7,5},{8,10},{9,11},{10,... | collective-permute-start | bytes 4616 | tf_op jit(solution)/shard_map/ppermute | solution.py:360

commit v6 on v5

--- a/solution.py
+++ b/solution.py
@@ -43,21 +43,29 @@
         if head % (head_count // chunks) == 0:
             wait(head // (head_count // chunks))
         cols = slice(head * HD, (head + 1) * HD)
-        state = matmul(key_ref[:, cols], value_ref[:, cols], ((0,), (0,))).astype(jnp.bfloat16)
-        whole_ref[0, head] = state
-        if head < half:
-            first_ref[head] = state
-        else:
-            second_ref[head - half] = state
+        state = matmul(key_ref[:, cols], value_ref[:, cols], ((0,), (0,)))
+        whole_ref[0, head] = state.astype(jnp.bfloat16)
+    parity = lax.axis_index("seq") & 1
+    for head in range(half):
+        first_ref[head] = whole_ref[0, parity * half + head]
+        second_ref[head] = whole_ref[0, (1 - parity) * half + head]
 
 
 def join_kernel(order_ref, *refs):
     out_ref = refs[-1]
+    parity = lax.axis_index("seq") & 1
     half = out_ref.shape[1] // 2
     for i in range(out_ref.shape[0]):
         for side in range(2):
             for head in range(half):
-                out_ref[i, side * half + head] = refs[2 * i + side][head]
+                out_ref[i, (side ^ parity) * half + head] = refs[2 * i + side][head]
+
+
+def turned(offset, depth):
+    result = jnp.zeros_like(offset)
+    for bit in range(1, depth):
+        result = result | (((offset >> bit) & 1) << (depth - bit))
+    return result
 
 
 def choose_levels(target, position, depth, level_count, head_count):
@@ -68,7 +76,8 @@
     col = lax.broadcasted_iota(jnp.int32, shape, 1)
     level = row >> shift
     offset = col >> shift
-    block = offset ^ position
+    low = offset & 1
+    block = position ^ low ^ jnp.where((low ^ position) & 1 == 1, turned(offset, depth), offset - low)
     diff = block ^ target
     chosen = jnp.logical_and(level == 0, offset == block_count)
     below = jnp.logical_and(offset < block_count, block < target)
@@ -92,7 +101,8 @@
         scores = [jnp.where(mask, score, 0.0).astype(jnp.bfloat16) for score in scores]
         results = [matmul(score, v_ref[rows, cols], ((1,), (0,))) for score, (_, cols, rows) in zip(scores, units)]
         for result, (head, cols, rows) in zip(results, units):
-            o_ref[rows, cols] = result * c_ref[rows, own + head : own + head + 1]
+            weight = jnp.broadcast_to(c_ref[rows, own + head : own + head + 1], (ROWS, HD))
+            o_ref[rows, cols] = result * weight.astype(jnp.float32)
 
 
 def causal_mask(suffix=ROWS):
@@ -101,82 +111,90 @@
     return jnp.logical_and(row >= col, row // suffix == col // suffix)
 
 
-def slab_kernel(depth, suffix, *refs):
-    sources, (k_ref, v_ref), (o_ref, sc_ref, uc_ref), rest = refs[:7], refs[7:9], refs[9:12], refs[12:]
-    q_ref, user_loaded, small_loaded, sems = rest[0], rest[1:4], rest[4:7], rest[7]
+def load_kernel(depth, suffix, *refs):
+    sources, (sc_ref, uc_ref), loaded, small_loaded, sems = refs[:7], refs[7:9], refs[9:13], refs[13:16], refs[16]
     copies = [
         pltpu.make_async_copy(source, target, sems.at[i])
-        for i, (source, target) in enumerate(zip(sources, (*small_loaded, q_ref, *user_loaded)))
+        for i, (source, target) in enumerate(zip(sources, (*small_loaded, *loaded)))
     ]
     for copy in copies:
         copy.start()
     for copy in copies[:3]:
         copy.wait()
     length_ref, slab_table, user_table = small_loaded
-    head_count = q_ref.shape[1] // HD
+    head_count = loaded[0].shape[1] // HD
+    position = lax.axis_index("seq").astype(jnp.int32)
     pick = functools.partial(
         choose_levels,
-        position=lax.axis_index("seq").astype(jnp.int32),
+        position=position,
         depth=depth,
         level_count=slab_table.shape[0] // head_count,
         head_count=head_count,
     )
-    sc_ref[...] = matmul(slab_table[...], pick(lax.axis_index("seq").astype(jnp.int32)), ((0,), (0,)))
+    sc_ref[...] = matmul(slab_table[...], pick(position), ((0,), (0,))).astype(jnp.bfloat16)
     for user in range(user_table.shape[0]):
         weights = matmul(user_table[user], pick(length_ref[user]), ((0,), (0,)))
-        uc_ref[user * suffix : (user + 1) * suffix] = weights
-    copies[3].wait()
-    attend(causal_mask(), q_ref, k_ref, v_ref, sc_ref, o_ref, (1 << depth) * head_count)
-    for copy in copies[4:]:
+        uc_ref[user * suffix : (user + 1) * suffix] = weights.astype(jnp.bfloat16)
+    for copy in copies[3:]:
         copy.wait()
 
 
-def user_kernel(depth, suffix, c_ref, q_ref, k_ref, v_ref, o_ref):
-    own = (1 << depth) * (q_ref.shape[1] // HD)
-    attend(causal_mask(suffix), q_ref, k_ref, v_ref, c_ref, o_ref, own)
-
-
-def add_blocks(groups, state_refs, head_count, head, q_ref, c_ref, base):
-    cols = slice(head * HD, (head + 1) * HD)
-    query = q_ref[:, cols]
-    total = base
-    for group in groups:
-        scaled = []
-        for offset in group:
-            column = offset * head_count + head
-            weight = jnp.broadcast_to(c_ref[:, column : column + 1], query.shape).astype(jnp.bfloat16)
-            scaled.append(query * weight)
-        states = [state_refs[offset][0][state_refs[offset][1], head] for offset in group]
-        total = total + matmul(jnp.concatenate(scaled, axis=1), jnp.concatenate(states, axis=0), ((1,), (0,)))
-    return total
-
-
-def read_kernel(groups, places, last, sq_ref, uq_ref, sc_ref, uc_ref, sa_ref, ua_ref, *rest):
+def slab_kernel(depth, c_ref, q_ref, k_ref, v_ref, o_ref):
+    attend(causal_mask(), q_ref, k_ref, v_ref, c_ref, o_ref, (1 << depth) * (q_ref.shape[1] // HD))
+
+
+def spread(c_ref, column, width):
+    return jnp.broadcast_to(c_ref[:, column : column + 1], (c_ref.shape[0], width))
+
+
+def user_kernel(depth, suffix, group, c_ref, q_ref, k_ref, v_ref, sc_ref, sq_ref, o_ref, *scaled_refs):
+    head_count = q_ref.shape[1] // HD
+    attend(causal_mask(suffix), q_ref, k_ref, v_ref, c_ref, o_ref, (1 << depth) * head_count)
+    for scaled_ref, query_ref, weight_ref in zip(scaled_refs, (sq_ref, q_ref), (sc_ref, c_ref)):
+        for head in range(head_count):
+            query = query_ref[:, head * HD : (head + 1) * HD]
+            for i, offset in enumerate(group):
+                start = (head * len(group) + i) * HD
+                weight = spread(weight_ref, offset * head_count + head, HD)
+                scaled_ref[:, start : start + HD] = query * weight
+
+
+def read_kernel(groups, places, sq_ref, uq_ref, sc_ref, uc_ref, sa_ref, ua_ref, *rest):
     head_count = sq_ref.shape[1] // HD
-    used = 1 + max(which for which, _ in places.values())
-    state_refs = {offset: (rest[which], index) for offset, (which, index) in places.items()}
-    st_ref, ut_ref = rest[used : used + 2]
+    st_ref, ut_ref = rest[-2:]
     for head in range(head_count):
         cols = slice(head * HD, (head + 1) * HD)
-        for side, (q_ref, c_ref, a_ref, t_ref) in enumerate(
-            ((sq_ref, sc_ref, sa_ref, st_ref), (uq_ref, uc_ref, ua_ref, ut_ref))
-        ):
-            total = add_blocks(groups, state_refs, head_count, head, q_ref, c_ref, a_ref[:, cols])
+        for q_ref, c_ref, a_ref, t_ref in ((sq_ref, sc_ref, sa_ref, st_ref), (uq_ref, uc_ref, ua_ref, ut_ref)):
+            query = q_ref[:, cols]
+            total = a_ref[:, cols]
+            for group in groups:
+                scaled = [query * spread(c_ref, offset * head_count + head, HD) for offset in group]
+                states = [rest[places[offset][0]][places[offset][1], head] for offset in group]
+                total = total + matmul(
+                    jnp.concatenate(scaled, axis=1), jnp.concatenate(states, axis=0), ((1,), (0,))
+                )
             t_ref[:, cols] = total
-            if last:
-                acc_ref = rest[used + 3 + side]
-                if head == 0:
-                    acc_ref[...] = total * total
-                else:
-                    acc_ref[...] += total * total
-    if last:
-        square_ref = rest[used + 2]
-        line = 0
-        for acc_ref in rest[used + 3 : used + 5]:
-            for start in range(0, acc_ref.shape[0], ROWS):
-                turned = jnp.transpose(acc_ref[start : start + ROWS])
-                square_ref[line : line + 1] = jnp.sum(turned, axis=0, keepdims=True)
-                line += 1
+
+
+def last_kernel(ss_ref, us_ref, sa_ref, ua_ref, state_ref, mate_ref, st_ref, ut_ref, square_ref, s_square, u_square):
+    head_count = sa_ref.shape[1] // HD
+    for head in range(head_count):
+        cols = slice(head * HD, (head + 1) * HD)
+        wide = slice(2 * head * HD, 2 * (head + 1) * HD)
+        states = jnp.concatenate([state_ref[0, head], mate_ref[0, head]], axis=0)
+        for q_ref, a_ref, t_ref, acc_ref in ((ss_ref, sa_ref, st_ref, s_square), (us_ref, ua_ref, ut_ref, u_square)):
+            total = a_ref[:, cols] + matmul(q_ref[:, wide], states, ((1,), (0,)))
+            t_ref[:, cols] = total
+            if head == 0:
+                acc_ref[...] = total * total
+            else:
+                acc_ref[...] += total * total
+    line = 0
+    for acc_ref in (s_square, u_square):
+        for start in range(0, acc_ref.shape[0], ROWS):
+            turned_part = jnp.transpose(acc_ref[start : start + ROWS])
+            square_ref[line : line + 1] = jnp.sum(turned_part, axis=0, keepdims=True)
+            line += 1
 
 
 def norm_kernel(features, chunks, st_ref, ut_ref, gain_ref, one_ref, two_ref, so_hbm, uo_hbm, so_ref, uo_ref, sems):
@@ -238,7 +256,8 @@
         return pl.CostEstimate(flops=flops, bytes_accessed=moved, transcendentals=0)
 
     def swap(value, bit):
-        return lax.ppermute(value, "seq", [(i, i ^ (1 << bit)) for i in range(seq_count)])
+        other = depth - bit if bit else 0
+        return lax.ppermute(value, "seq", [(i, i ^ (1 << (other if i & 1 else bit))) for i in range(seq_count)])
 
     def after(results, values):
         return list(lax.optimization_barrier((results, values))[1])
@@ -273,17 +292,16 @@
     slab_table = slab_levels.reshape(-1, token_count)
     user_table = user_levels.reshape(user_count, -1, suffix)
     columns = (seq_count + 1) * head_count
-    slab_acc, slab_coef, user_coef, slab_queries, user_queries, user_keys, user_values = pl.pallas_call(
-        functools.partial(slab_kernel, depth, suffix),
+    slab_coef, user_coef, slab_queries, user_queries, user_keys, user_values = pl.pallas_call(
+        functools.partial(load_kernel, depth, suffix),
         out_shape=[
-            pltpu.VMEM((token_count, width), jnp.float32),
-            pltpu.VMEM((token_count, columns), jnp.float32),
-            pltpu.VMEM((user_rows, columns), jnp.float32),
+            pltpu.VMEM((token_count, columns), jnp.bfloat16),
+            pltpu.VMEM((user_rows, columns), jnp.bfloat16),
             slab_rows,
         ]
         + [pltpu.VMEM((user_rows, width), jnp.bfloat16)] * 3,
-        in_specs=[hbm] * 7 + [vmem] * 2,
-        out_specs=[vmem] * 7,
+        in_specs=[hbm] * 7,
+        out_specs=[vmem] * 6,
         scratch_shapes=[
             pltpu.SMEM((user_count,), jnp.int32),
             pltpu.VMEM(slab_table.shape, jnp.bfloat16),
@@ -295,64 +313,77 @@
     )(
         *pinned(prefix_lengths, slab_table, user_table, slab_query),
         *pinned(*[array.reshape(user_rows, width) for array in (user_query, user_key, user_value)]),
-        slab_keys,
-        slab_values,
     )
     halves = after(slab_coef, halves)
-    whole = {0: state, 1: swap(state, 0)}
     for bit, side in places:
         if (bit, side) not in ahead:
             sides[1 << bit][side] = swap(halves[side], bit)
+    slab_acc = pl.pallas_call(
+        functools.partial(slab_kernel, depth),
+        out_shape=pltpu.VMEM((token_count, width), jnp.float32),
+        in_specs=[vmem] * 4,
+        out_specs=vmem,
+        compiler_params=params,
+        cost_estimate=cost(0, 0),
+    )(slab_coef, slab_queries, slab_keys, slab_values)
 
     later = sorted((m for m in range(0, seq_count, 2) if m.bit_count() > 1), key=lambda m: m.bit_count())
+    for (bit, side), value in zip(ahead, after(slab_acc, [sides[1 << bit][side] for bit, side in ahead])):
+        sides[1 << bit][side] = value
     for m in later:
         high, low = m.bit_length() - 1, (m & -m).bit_length() - 1
         sides[m] = [swap(sides[m ^ (1 << high)][0], high), swap(sides[m ^ (1 << low)][1], low)]
     user_coef = after([sides[1 << bit][side] for bit, side in ahead], [user_coef])[0]
-    user_acc = pl.pallas_call(
-        functools.partial(user_kernel, depth, suffix),
-        out_shape=pltpu.VMEM((user_rows, width), jnp.float32),
-        in_specs=[vmem] * 4,
-        out_specs=vmem,
+    last = later[-1]
+    user_acc, slab_scaled, user_scaled = pl.pallas_call(
+        functools.partial(user_kernel, depth, suffix, (last, last | 1)),
+        out_shape=[
+            pltpu.VMEM((user_rows, width), jnp.float32),
+            pltpu.VMEM((token_count, 2 * width), jnp.bfloat16),
+            pltpu.VMEM((user_rows, 2 * width), jnp.bfloat16),
+        ],
+        in_specs=[vmem] * 6,
+        out_specs=[vmem] * 3,
         compiler_params=params,
         cost_estimate=cost(0, 0),
-    )(user_coef, user_queries, user_keys, user_values)
-
-    def read(groups, states, accs, last):
-        found = {}
-        for which, (offsets, _) in enumerate(states):
-            found.update({offset: (which, index) for index, offset in enumerate(offsets)})
-        outs = [pltpu.VMEM((token_count, width), jnp.float32), pltpu.VMEM((user_rows, width), jnp.float32)]
-        scratch = []
-        if last:
-            outs.append(pltpu.VMEM((lines, ROWS), jnp.float32))
-            scratch = [pltpu.VMEM((token_count, HD), jnp.float32), pltpu.VMEM((user_rows, HD), jnp.float32)]
+    )(user_coef, user_queries, user_keys, user_values, slab_coef, slab_queries)
+
+    totals = [pltpu.VMEM((token_count, width), jnp.float32), pltpu.VMEM((user_rows, width), jnp.float32)]
+
+    def read(offsets, accs):
+        found = {offset: (which, 0) for which, offset in enumerate(offsets)}
+        groups = [tuple(offsets[i : i + 2]) for i in range(0, len(offsets), 2)]
         return pl.pallas_call(
-            functools.partial(read_kernel, groups, found, last),
-            out_shape=outs,
-            in_specs=[vmem] * (6 + len(states)),
-            out_specs=[vmem] * len(outs),
-            scratch_shapes=scratch,
+            functools.partial(read_kernel, groups, found),
+            out_shape=totals,
+            in_specs=[vmem] * (6 + len(offsets)),
+            out_specs=[vmem] * 2,
             compiler_params=params,
             cost_estimate=cost(0, 0),
-        )(slab_queries, user_queries, slab_coef, user_coef, *accs, *[array for _, array in states])
-
-    def pairs(offsets):
-        return [tuple(offsets[i : i + 2]) for i in range(0, len(offsets), 2)]
-
+        )(slab_queries, user_queries, slab_coef, user_coef, *accs, *[whole[m] for m in offsets])
+
+    whole = {0: after(user_acc, [state])[0]}
     direct = [1 << bit for bit in outer]
-    mates = [m | 1 for m in direct]
     for m in direct:
         whole[m] = join(user_acc, sides[m])
-    for m in direct:
+    for m in [0] + direct:
         whole[m | 1] = swap(whole[m], 0)
-    accs = read(pairs([0, 1] + direct), [([m], whole[m]) for m in [0, 1] + direct], (slab_acc, user_acc), False)
-    late = join(accs[0], [piece for m in later for piece in sides[m]])
-    accs = read(pairs(mates), [([m], whole[m]) for m in mates], accs, False)
-    late_mates = swap(late, 0)
-    slab_total, user_total, square = read(
-        [(m, m | 1) for m in later], [(later, late), ([m | 1 for m in later], late_mates)], accs, True
-    )
+    accs = read([0] + direct, (slab_acc, user_acc))
+    for m in later:
+        whole[m] = join(accs[0], sides[m])
+        whole[m | 1] = swap(whole[m], 0)
+    accs = read([m | 1 for m in [0] + direct], accs)
+    if later[:-1]:
+        accs = read([n for m in later[:-1] for n in (m, m | 1)], accs)
+    slab_total, user_total, square = pl.pallas_call(
+        last_kernel,
+        out_shape=totals + [pltpu.VMEM((lines, ROWS), jnp.float32)],
+        in_specs=[vmem] * 6,
+        out_specs=[vmem] * 3,
+        scratch_shapes=[pltpu.VMEM((token_count, HD), jnp.float32), pltpu.VMEM((user_rows, HD), jnp.float32)],
+        compiler_params=params,
+        cost_estimate=cost(0, 0),
+    )(slab_scaled, user_scaled, *accs, whole[last], whole[last | 1])
 
     mate = jnp.zeros_like(square)
     for bit in range(head_axis.bit_length() - 1):

time: 38.9 us -> 39.5 us (1.015)
  waiting for transfers between devices: 9.77 us -> 7.33 us
  Pallas kernels: 14.8 us -> 17.2 us
  starting transfers between devices: 13.5 us -> 14.1 us
    ppermute x10, waiting for transfers between devices: 5.88 us -> 3.45 us  [swap(): lax.ppermute(value, 'seq', [(i, i ^ 1 << (other if i & 1 else bit)) for i...]
    pallas_call x5 -> x6, Pallas kernels: 11.2 us -> 13.6 us  [the longest x2 6.15 us: read(): pl.pallas_call(functools.partial(read_kernel, groups, found), out_shape=t...]
    ppermute x10, starting transfers between devices: 9.24 us -> 9.82 us  [swap(): lax.ppermute(value, 'seq', [(i, i ^ 1 << (other if i & 1 else bit)) for i...]
  transfers between devices with their start and end apart: 12 -> 12, of which waited for: 7 -> 6; matrix products, arithmetic and copies ran while one was open for 0% -> 0% of each run, Pallas kernels for 25% -> 32%
where the time goes in v6:
time: 39.5 us; the launch traced here: 39.4 us
  Pallas kernels  17.2 us (44%)
  starting transfers between devices  14.1 us (36%)
  waiting for transfers between devices  7.33 us (19%)
  between operations  0.73 us (2%)
    ppermute x10, starting transfers between devices, swap(): lax.ppermute(value, 'seq', [(i, i ^ 1 << (other if i & 1 else bit)) for i...  9.82 us
    pallas_call x2, Pallas kernels, read(): pl.pallas_call(functools.partial(read_kernel, groups, found), out_shape=t...  6.15 us
    ppermute x2, starting transfers between devices, local(): lax.ppermute(square, 'head', [(i, i ^ 1 << bit) for i in range(head_axis)])  4.23 us
    ppermute x2, waiting for transfers between devices, local(): lax.ppermute(square, 'head', [(i, i ^ 1 << bit) for i in range(head_axis)])  3.89 us
    ppermute x10, waiting for transfers between devices, swap(): lax.ppermute(value, 'seq', [(i, i ^ 1 << (other if i & 1 else bit)) for i...  3.45 us
    pallas_call x1, Pallas kernels, local(): pl.pallas_call(functools.partial(user_kernel, depth, suffix, (last, last...  2.79 us
    pallas_call x1, Pallas kernels, local(): pl.pallas_call(functools.partial(load_kernel, depth, suffix), out_shape=[...  2.15 us
    pallas_call x1, Pallas kernels, local(): pl.pallas_call(functools.partial(state_kernel, chunks), out_shape=[half_s...  1.95 us
  transfers between devices with their start and end apart: 12, of which 6 were waited for; matrix products, arithmetic and copies ran while one was open for 0% of the time, Pallas kernels for 32%

profile of v6, /device:TPU:0, one launch (start us, length us, event | category | flops | bytes accessed | tf_op | source)
XLA Modules:
  0.0 39.4 jit_solution(17255042953003746968)
XLA Ops:
  0.6 2.0 %shard_map.114 = (bf16[8,128,128]{2,1,0:T(8,128)(2,1)S(1)}, bf16[8,128,128]{2,1,0:T(8,128)(2,1)S(1)}, bf16[1,16,128,128]{3,2,1,0:T(8,128)(2,1)S(1)}, bf16[128,2048]{1,0:T(8,128)(2,1)S(1)}, bf16[128,2048]{1,0:T(8,128)(2,1)S(1)}) custom-call(bf16[128,2048]{1,0:T(8,128)(2,1)} %key_hbm.1, bf16[128,2048]{1,0:T(8,128)(2,1)} %value_hbm.1), custom_call_target="tpu_custom_call" | custom-call | tf_op jit(solution)/shard_map/pallas_call | solution.py:276
  2.6 3.0 %collective-permute-start = (bf16[8,128,128]{2,1,0:T(8,128)(2,1)S(1)}, bf16[8,128,128]{2,1,0:T(8,128)(2,1)S(1)}, u32[]{:S(2)}, u32[]{:S(2)}) collective-permute-start(bf16[8,128,128]{2,1,0:T(8,128)(2,1)S(1)} %get-tuple-element.50), channel_id=1, source_target_pairs={{0,8},{4,20},{8,0},{12,28},{16,24},{20,4},{24,16},{28,12},{1,9},{5... | collective-permute-start | bytes 786440 | tf_op jit(solution)/shard_map/ppermute | solution.py:260
  5.6 1.5 %collective-permute-start.1 = (bf16[8,128,128]{2,1,0:T(8,128)(2,1)S(1)}, bf16[8,128,128]{2,1,0:T(8,128)(2,1)S(1)}, u32[]{:S(2)}, u32[]{:S(2)}) collective-permute-start(bf16[8,128,128]{2,1,0:T(8,128)(2,1)S(1)} %get-tuple-element.49), channel_id=1, source_target_pairs={{0,16},{4,12},{8,24},{12,4},{16,0},{20,28},{24,8},{28,20},{1,17},{... | collective-permute-start | bytes 786440 | tf_op jit(solution)/shard_map/ppermute | solution.py:260
  7.1 2.1 %shard_map.113 = (bf16[128,144]{1,0:T(8,128)(2,1)S(1)}, bf16[256,144]{1,0:T(8,128)(2,1)S(1)}, bf16[128,2048]{1,0:T(8,128)(2,1)S(1)}, bf16[256,2048]{1,0:T(8,128)...) custom-call(s32[4]{0:T(128)} %refs_0_.1, bf16[96,128]{1,0:T(8,128)(2,1)} %bitcast.10, ...), custom_call_target="tpu_custom_call" | custom-call | tf_op jit(solution)/shard_map/pallas_call | solution.py:295
  9.3 0.6 %collective-permute-start.2 = (bf16[8,128,128]{2,1,0:T(8,128)(2,1)S(1)}, bf16[8,128,128]{2,1,0:T(8,128)(2,1)S(1)}, u32[]{:S(2)}, u32[]{:S(2)}) collective-permute-start(bf16[8,128,128]{2,1,0:T(8,128)(2,1)S(1)} %get-tuple-element.49), channel_id=1, source_target_pairs={{0,8},{4,20},{8,0},{12,28},{16,24},{20,4},{24,16},{28,12},{1,9},{5... | collective-permute-start | bytes 786440 | tf_op jit(solution)/shard_map/ppermute | solution.py:260
  9.9 0.0 collective-permute-start.3
  9.9 1.4 %shard_map.115.sa_ref = f32[128,2048]{1,0:T(8,128)S(1)} custom-call(bf16[128,144]{1,0:T(8,128)(2,1)S(1)} %get-tuple-element.31.c_ref.sc_ref, bf16[128,2048]{1,0:T(8,128)(2,1)S(1)} %get-tuple-element.32.q_ref.sq_ref, bf16[128,2048]{1,0:T(8,128)(2,1)S(1)} %get-tuple-element.33.k_ref, bf16[128,2048]{1,0:T(8,128)(2,1)S(1)} %get-tuple-element.34.v_ref), custom_call_target="tpu_custom_call" | custom-call | tf_op jit(solution)/shard_map/pallas_call | solution.py:321
  11.3 0.8 %collective-permute-done.refs_0_ = bf16[8,128,128]{2,1,0:T(8,128)(2,1)S(1)} collective-permute-done((bf16[8,128,128]{2,1,0:T(8,128)(2,1)S(1)}, bf16[8,128,128]{2,1,0:T(8,128)(2,1)S(1)}, u32[]{:S(2)}, u32[]{:S(2)}) %collective-permute-start) | collective-permute-done | bytes 262176 | tf_op jit(solution)/shard_map/ppermute | solution.py:260
  12.2 1.0 %collective-permute-done.1.refs_1_ = bf16[8,128,128]{2,1,0:T(8,128)(2,1)S(1)} collective-permute-done((bf16[8,128,128]{2,1,0:T(8,128)(2,1)S(1)}, bf16[8,128,128]{2,1,0:T(8,128)(2,1)S(1)}, u32[]{:S(2)}, u32[]{:S(2)}) %collective-permute-start.1) | collective-permute-done | bytes 262176 | tf_op jit(solution)/shard_map/ppermute | solution.py:260
  13.1 2.5 %collective-permute-start.7 = (bf16[8,128,128]{2,1,0:T(8,128)(2,1)S(1)}, bf16[8,128,128]{2,1,0:T(8,128)(2,1)S(1)}, u32[]{:S(2)}, u32[]{:S(2)}) collective-permute-start(bf16[8,128,128]{2,1,0:T(8,128)(2,1)S(1)} %collective-permute-done.refs_0_), channel_id=1, source_target_pairs={{0,16},{4,12},{8,24},{12,4},{16,0},{20,28},{24,8},{28,20},{1,17},{... | collective-permute-start | bytes 786440 | tf_op jit(solution)/shard_map/ppermute | solution.py:260
  15.6 1.3 %collective-permute-start.8 = (bf16[8,128,128]{2,1,0:T(8,128)(2,1)S(1)}, bf16[8,128,128]{2,1,0:T(8,128)(2,1)S(1)}, u32[]{:S(2)}, u32[]{:S(2)}) collective-permute-start(bf16[8,128,128]{2,1,0:T(8,128)(2,1)S(1)} %collective-permute-done.1.refs_1_), channel_id=1, source_target_pairs={{0,8},{4,20},{8,0},{12,28},{16,24},{20,4},{24,16},{28,12},{1,9},{5... | collective-permute-start | bytes 786440 | tf_op jit(solution)/shard_map/ppermute | solution.py:260
  16.9 2.8 %shard_map.116 = (f32[256,2048]{1,0:T(8,128)S(1)}, bf16[128,4096]{1,0:T(8,128)(2,1)S(1)}, bf16[256,4096]{1,0:T(8,128)(2,1)S(1)}) custom-call(bf16[256,144]{1,0:T(8,128)(2,1)S(1)} %get-tuple-element.40.c_ref.uc_ref, bf16[256,2048]{1,0:T(8,128)(2,1)S(1)} %get-tuple-element.41.q_ref.uq_ref, bf16[256,2048]{1,0:T(8,128)(2,1)S(1)} %get-tuple-element.42.k_ref, ...), custom_call_target="tpu_custom_call" | custom-call | tf_op jit(solution)/shard_map/pallas_call | solution.py:338
  19.7 0.1 collective-permute-start.4
  19.8 0.0 collective-permute-done.2.refs_1_
  19.8 0.6 %collective-permute-start.5 = (bf16[1,16,128,128]{3,2,1,0:T(8,128)(2,1)S(1)}, bf16[1,16,128,128]{3,2,1,0:T(8,128)(2,1)S(1)}, u32[]{:S(2)}, u32[]{:S(2)}) collective-permute-start(bf16[1,16,128,128]{3,2,1,0:T(8,128)(2,1)S(1)} %shard_map.117.rest_1_), channel_id=1, source_target_pairs={{0,4},{4,0},{8,12},{12,8},{16,20},{20,16},{24,28},{28,24},{1,5},{5... | collective-permute-start | bytes 1572872 | tf_op jit(solution)/shard_map/ppermute | solution.py:260
  20.4 0.0 collective-permute-done.3.refs_0_
  20.4 3.1 %shard_map.119 = (f32[128,2048]{1,0:T(8,128)S(1)}, f32[256,2048]{1,0:T(8,128)S(1)}) custom-call(bf16[128,2048]{1,0:T(8,128)(2,1)S(1)} %get-tuple-element.32.q_ref.sq_ref, bf16[256,2048]{1,0:T(8,128)(2,1)S(1)} %get-tuple-element.41.q_ref.uq_ref, bf16[128,144]{1,0:T(8,128)(2,1)S(1)} %get-tuple-element.31.c_ref.sc_ref, ...), custom_call_target="tpu_custom_call" | custom-call | tf_op jit(solution)/shard_map/pallas_call | solution.py:356
  23.5 0.1 collective-permute-start.6
  23.6 0.0 collective-permute-done.7.refs_0_
  23.6 0.4 collective-permute-done.8.refs_1_
  24.0 0.2 collective-permute-start.9
  24.2 0.0 collective-permute-done.4.rest_0_
  24.2 0.0 collective-permute-done.5.rest_1_
  24.2 1.3 %collective-permute-done.6.rest_2_ = bf16[1,16,128,128]{3,2,1,0:T(8,128)(2,1)S(1)} collective-permute-done((bf16[1,16,128,128]{3,2,1,0:T(8,128)(2,1)S(1)}, bf16[1,16,128,128]{3,2,1,0:T(8,128)(2,1)S(1)}, u32[]{:S(2)}, u32[]{:S(2)}) %collective-permute-start.6) | collective-permute-done | bytes 524320 | tf_op jit(solution)/shard_map/ppermute | solution.py:260
  25.5 3.1 %shard_map.120 = (f32[128,2048]{1,0:T(8,128)S(1)}, f32[256,2048]{1,0:T(8,128)S(1)}) custom-call(bf16[128,2048]{1,0:T(8,128)(2,1)S(1)} %get-tuple-element.32.q_ref.sq_ref, bf16[256,2048]{1,0:T(8,128)(2,1)S(1)} %get-tuple-element.41.q_ref.uq_ref, bf16[128,144]{1,0:T(8,128)(2,1)S(1)} %get-tuple-element.31.c_ref.sc_ref, ...), custom_call_target="tpu_custom_call" | custom-call | tf_op jit(solution)/shard_map/pallas_call | solution.py:356
  28.6 0.0 collective-permute-done.9.mate_ref
  28.6 0.0 copy-start
  28.6 1.1 %shard_map.122 = (f32[128,2048]{1,0:T(8,128)S(1)}, f32[256,2048]{1,0:T(8,128)S(1)}, f32[3,128]{1,0:T(4,128)S(1)}) custom-call(bf16[128,4096]{1,0:T(8,128)(2,1)S(1)} %get-tuple-element.44.ss_ref, bf16[256,4096]{1,0:T(8,128)(2,1)S(1)} %get-tuple-element.45.us_ref, f32[128,2048]{1,0:T(8,128)S(1)} %get-tuple-element.53.sa_ref, ...), custom_call_target="tpu_custom_call" | custom-call | tf_op jit(solution)/shard_map/pallas_call | solution.py:378
  29.7 1.6 %collective-permute-start.10 = (f32[3,128]{1,0:T(4,128)S(1)}, f32[3,128]{1,0:T(4,128)S(1)}, u32[]{:S(2)}, u32[]{:S(2)}) collective-permute-start(f32[3,128]{1,0:T(4,128)S(1)} %get-tuple-element.57), channel_id=1, source_target_pairs={{0,1},{1,0},{2,3},{3,2},{4,5},{5,4},{6,7},{7,6},{8,9},{9,8},{10,11... | collective-permute-start | bytes 4616 | tf_op jit(solution)/shard_map/ppermute | solution.py:391
  31.3 2.0 %collective-permute-done.10 = f32[3,128]{1,0:T(4,128)S(1)} collective-permute-done((f32[3,128]{1,0:T(4,128)S(1)}, f32[3,128]{1,0:T(4,128)S(1)}, u32[]{:S(2)}, u32[]{:S(2)}) %collective-permute-start.10) | collective-permute-done | bytes 1568 | tf_op jit(solution)/shard_map/ppermute | solution.py:391
  33.4 2.6 %collective-permute-start.11 = (f32[3,128]{1,0:T(4,128)S(1)}, f32[3,128]{1,0:T(4,128)S(1)}, u32[]{:S(2)}, u32[]{:S(2)}) collective-permute-start(f32[3,128]{1,0:T(4,128)S(1)} %add.3.one_ref), channel_id=1, source_target_pairs={{0,2},{1,3},{2,0},{3,1},{4,6},{5,7},{6,4},{7,5},{8,10},{9,11},{10,... | collective-permute-start | bytes 4616 | tf_op jit(solution)/shard_map/ppermute | solution.py:391
  35.9 0.0 copy-done
  36.0 1.9 %collective-permute-done.11.two_ref = f32[3,128]{1,0:T(4,128)S(1)} collective-permute-done((f32[3,128]{1,0:T(4,128)S(1)}, f32[3,128]{1,0:T(4,128)S(1)}, u32[]{:S(2)}, u32[]{:S(2)}) %collective-permute-start.11) | collective-permute-done | bytes 1568 | tf_op jit(solution)/shard_map/ppermute | solution.py:391
  37.8 1.5 %shard_map.123 = (bf16[128,2048]{1,0:T(8,128)(2,1)}, bf16[256,2048]{1,0:T(8,128)(2,1)}) custom-call(f32[128,2048]{1,0:T(8,128)S(1)} %get-tuple-element.55.st_ref, f32[256,2048]{1,0:T(8,128)S(1)} %get-tuple-element.56.ut_ref, bf16[1,2048]{1,0:T(2,128)(2,1)S(1)} %reshape.30.gain_ref, f32[3,128]{1,0:T(4,128)S(1)} %add.3.one_ref, ...), custom_call_target="tpu_custom_call" | custom-call | tf_op jit(solution)/shard_map/pallas_call | solution.py:393
  (5 shorter events, 0.2 us)
Async XLA Ops:
  2.6 9.6 %collective-permute-start = (bf16[8,128,128]{2,1,0:T(8,128)(2,1)S(1)}, bf16[8,128,128]{2,1,0:T(8,128)(2,1)S(1)}, u32[]{:S(2)}, u32[]{:S(2)}) collective-permute-start(bf16[8,128,128]{2,1,0:T(8,128)(2,1)S(1)} %get-tuple-element.50), channel_id=1, source_target_pairs={{0,8},{4,20},{8,0},{12,28},{16,24},{20,4},{24,16},{28,12},{1,9},{5... | collective-permute-start | bytes 786440 | tf_op jit(solution)/shard_map/ppermute | solution.py:260
  5.6 7.5 %collective-permute-start.1 = (bf16[8,128,128]{2,1,0:T(8,128)(2,1)S(1)}, bf16[8,128,128]{2,1,0:T(8,128)(2,1)S(1)}, u32[]{:S(2)}, u32[]{:S(2)}) collective-permute-start(bf16[8,128,128]{2,1,0:T(8,128)(2,1)S(1)} %get-tuple-element.49), channel_id=1, source_target_pairs={{0,16},{4,12},{8,24},{12,4},{16,0},{20,28},{24,8},{28,20},{1,17},{... | collective-permute-start | bytes 786440 | tf_op jit(solution)/shard_map/ppermute | solution.py:260
  9.3 10.5 %collective-permute-start.2 = (bf16[8,128,128]{2,1,0:T(8,128)(2,1)S(1)}, bf16[8,128,128]{2,1,0:T(8,128)(2,1)S(1)}, u32[]{:S(2)}, u32[]{:S(2)}) collective-permute-start(bf16[8,128,128]{2,1,0:T(8,128)(2,1)S(1)} %get-tuple-element.49), channel_id=1, source_target_pairs={{0,8},{4,20},{8,0},{12,28},{16,24},{20,4},{24,16},{28,12},{1,9},{5... | collective-permute-start | bytes 786440 | tf_op jit(solution)/shard_map/ppermute | solution.py:260
  9.9 10.5 %collective-permute-start.3 = (bf16[8,128,128]{2,1,0:T(8,128)(2,1)S(1)}, bf16[8,128,128]{2,1,0:T(8,128)(2,1)S(1)}, u32[]{:S(2)}, u32[]{:S(2)}) collective-permute-start(bf16[8,128,128]{2,1,0:T(8,128)(2,1)S(1)} %get-tuple-element.50), channel_id=1, source_target_pairs={{0,16},{4,12},{8,24},{12,4},{16,0},{20,28},{24,8},{28,20},{1,17},{... | collective-permute-start | bytes 786440 | tf_op jit(solution)/shard_map/ppermute | solution.py:260
  13.1 10.5 %collective-permute-start.7 = (bf16[8,128,128]{2,1,0:T(8,128)(2,1)S(1)}, bf16[8,128,128]{2,1,0:T(8,128)(2,1)S(1)}, u32[]{:S(2)}, u32[]{:S(2)}) collective-permute-start(bf16[8,128,128]{2,1,0:T(8,128)(2,1)S(1)} %collective-permute-done.refs_0_), channel_id=1, source_target_pairs={{0,16},{4,12},{8,24},{12,4},{16,0},{20,28},{24,8},{28,20},{1,17},{... | collective-permute-start | bytes 786440 | tf_op jit(solution)/shard_map/ppermute | solution.py:260
  15.6 8.4 %collective-permute-start.8 = (bf16[8,128,128]{2,1,0:T(8,128)(2,1)S(1)}, bf16[8,128,128]{2,1,0:T(8,128)(2,1)S(1)}, u32[]{:S(2)}, u32[]{:S(2)}) collective-permute-start(bf16[8,128,128]{2,1,0:T(8,128)(2,1)S(1)} %collective-permute-done.1.refs_1_), channel_id=1, source_target_pairs={{0,8},{4,20},{8,0},{12,28},{16,24},{20,4},{24,16},{28,12},{1,9},{5... | collective-permute-start | bytes 786440 | tf_op jit(solution)/shard_map/ppermute | solution.py:260
  19.7 4.5 %collective-permute-start.4 = (bf16[1,16,128,128]{3,2,1,0:T(8,128)(2,1)S(1)}, bf16[1,16,128,128]{3,2,1,0:T(8,128)(2,1)S(1)}, u32[]{:S(2)}, u32[]{:S(2)}) collective-permute-start(bf16[1,16,128,128]{3,2,1,0:T(8,128)(2,1)S(1)} %get-tuple-element.48.rest_0_), channel_id=1, source_target_pairs={{0,4},{4,0},{8,12},{12,8},{16,20},{20,16},{24,28},{28,24},{1,5},{5... | collective-permute-start | bytes 1572872 | tf_op jit(solution)/shard_map/ppermute | solution.py:260
  19.8 4.4 %collective-permute-start.5 = (bf16[1,16,128,128]{3,2,1,0:T(8,128)(2,1)S(1)}, bf16[1,16,128,128]{3,2,1,0:T(8,128)(2,1)S(1)}, u32[]{:S(2)}, u32[]{:S(2)}) collective-permute-start(bf16[1,16,128,128]{3,2,1,0:T(8,128)(2,1)S(1)} %shard_map.117.rest_1_), channel_id=1, source_target_pairs={{0,4},{4,0},{8,12},{12,8},{16,20},{20,16},{24,28},{28,24},{1,5},{5... | collective-permute-start | bytes 1572872 | tf_op jit(solution)/shard_map/ppermute | solution.py:260
  23.5 2.0 %collective-permute-start.6 = (bf16[1,16,128,128]{3,2,1,0:T(8,128)(2,1)S(1)}, bf16[1,16,128,128]{3,2,1,0:T(8,128)(2,1)S(1)}, u32[]{:S(2)}, u32[]{:S(2)}) collective-permute-start(bf16[1,16,128,128]{3,2,1,0:T(8,128)(2,1)S(1)} %shard_map.118.rest_2_), channel_id=1, source_target_pairs={{0,4},{4,0},{8,12},{12,8},{16,20},{20,16},{24,28},{28,24},{1,5},{5... | collective-permute-start | bytes 1572872 | tf_op jit(solution)/shard_map/ppermute | solution.py:260
  24.0 4.5 %collective-permute-start.9 = (bf16[1,16,128,128]{3,2,1,0:T(8,128)(2,1)S(1)}, bf16[1,16,128,128]{3,2,1,0:T(8,128)(2,1)S(1)}, u32[]{:S(2)}, u32[]{:S(2)}) collective-permute-start(bf16[1,16,128,128]{3,2,1,0:T(8,128)(2,1)S(1)} %shard_map.121.state_ref), channel_id=1, source_target_pairs={{0,4},{4,0},{8,12},{12,8},{16,20},{20,16},{24,28},{28,24},{1,5},{5... | collective-permute-start | bytes 1572872 | tf_op jit(solution)/shard_map/ppermute | solution.py:260
  28.6 7.4 %copy-start = (bf16[2048]{0:T(1024)(128)(2,1)S(1)}, bf16[2048]{0:T(1024)(128)(2,1)}, u32[]{:S(2)}) copy-start(bf16[2048]{0:T(1024)(128)(2,1)} %param.14) | copy-start | bytes 12292
  29.7 3.6 %collective-permute-start.10 = (f32[3,128]{1,0:T(4,128)S(1)}, f32[3,128]{1,0:T(4,128)S(1)}, u32[]{:S(2)}, u32[]{:S(2)}) collective-permute-start(f32[3,128]{1,0:T(4,128)S(1)} %get-tuple-element.57), channel_id=1, source_target_pairs={{0,1},{1,0},{2,3},{3,2},{4,5},{5,4},{6,7},{7,6},{8,9},{9,8},{10,11... | collective-permute-start | bytes 4616 | tf_op jit(solution)/shard_map/ppermute | solution.py:391
  33.4 4.5 %collective-permute-start.11 = (f32[3,128]{1,0:T(4,128)S(1)}, f32[3,128]{1,0:T(4,128)S(1)}, u32[]{:S(2)}, u32[]{:S(2)}) collective-permute-start(f32[3,128]{1,0:T(4,128)S(1)} %add.3.one_ref), channel_id=1, source_target_pairs={{0,2},{1,3},{2,0},{3,1},{4,6},{5,7},{6,4},{7,5},{8,10},{9,11},{10,... | collective-permute-start | bytes 4616 | tf_op jit(solution)/shard_map/ppermute | solution.py:391

commit v7 on v6

v7 whole, which is shorter than its diff:
```python
import functools

import jax
import jax.numpy as jnp
from jax import lax
from jax.experimental import pallas as pl
from jax.experimental.pallas import tpu as pltpu
from jax.sharding import PartitionSpec as P

HEADS = 64
HD = 128
ROWS = 128
VMEM_BYTES = 20 * 1024 * 1024


def matmul(a, b, contract):
    return lax.dot_general(a, b, (contract, ((), ())), preferred_element_type=jnp.float32)


def load_columns(sources, targets, sems, chunks):
    copies = []
    for chunk in range(chunks):
        group = []
        for i, (source, target) in enumerate(zip(sources, targets)):
            size = source.shape[1] // chunks
            cols = pl.ds(chunk * size, size)
            group.append(pltpu.make_async_copy(source.at[:, cols], target.at[:, cols], sems.at[i, chunk]))
            group[-1].start()
        copies.append(group)

    def wait(chunk):
        for copy in copies[chunk]:
            copy.wait()

    return wait


def state_kernel(chunks, key_hbm, value_hbm, first_ref, second_ref, whole_ref, key_ref, value_ref, sems):
    half = first_ref.shape[0]
    head_count = 2 * half
    wait = load_columns((key_hbm, value_hbm), (key_ref, value_ref), sems, chunks)
    for head in range(head_count):
        if head % (head_count // chunks) == 0:
            wait(head // (head_count // chunks))
        cols = slice(head * HD, (head + 1) * HD)
        state = matmul(key_ref[:, cols], value_ref[:, cols], ((0,), (0,)))
        whole_ref[0, head] = state.astype(jnp.bfloat16)
    parity = lax.axis_index("seq") & 1
    for head in range(half):
        first_ref[head] = whole_ref[0, parity * half + head]
        second_ref[head] = whole_ref[0, (1 - parity) * half + head]


def join_kernel(order_ref, *refs):
    out_ref = refs[-1]
    parity = lax.axis_index("seq") & 1
    half = out_ref.shape[1] // 2
    for i in range(out_ref.shape[0]):
        for side in range(2):
            for head in range(half):
                out_ref[i, (side ^ parity) * half + head] = refs[2 * i + side][head]


def turned(offset, depth):
    return sum(((offset >> bit) & 1) << (depth - bit) for bit in range(1, depth))


def level_of(offset, target, position, depth):
    low = offset & 1
    block = position ^ low ^ jnp.where(((position ^ low) & 1) == 1, turned(offset, depth), offset - low)
    diff = block ^ target
    level = sum((diff >= (1 << step)).astype(jnp.int32) for step in range(depth))
    return jnp.where(block < target, level, 0)


def attend(mask, q_ref, k_ref, v_ref, w_ref, o_ref):
    head_count = q_ref.shape[1] // HD
    step = 2
    for first in range(0, head_count, step):
        units = [
            (head, slice(head * HD, (head + 1) * HD), slice(start, start + ROWS))
            for head in range(first, first + step)
            for start in range(0, q_ref.shape[0], ROWS)
        ]
        scores = [matmul(q_ref[rows, cols], k_ref[rows, cols], ((1,), (1,))) for _, cols, rows in units]
        scores = [jnp.where(mask, score, 0.0).astype(jnp.bfloat16) for score in scores]
        results = [matmul(score, v_ref[rows, cols], ((1,), (0,))) for score, (_, cols, rows) in zip(scores, units)]
        for result, (head, cols, rows) in zip(results, units):
            o_ref[rows, cols] = result * w_ref[rows, head : head + 1]


def causal_mask(suffix=ROWS):
    row = lax.broadcasted_iota(jnp.int32, (ROWS, ROWS), 0)
    col = lax.broadcasted_iota(jnp.int32, (ROWS, ROWS), 1)
    return jnp.logical_and(row >= col, row // suffix == col // suffix)


def start_copies(sources, targets, sems):
    copies = [
        pltpu.make_async_copy(source, target, sems.at[i]) for i, (source, target) in enumerate(zip(sources, targets))
    ]
    for copy in copies:
        copy.start()
    return copies


def load_kernel(suffix, *refs):
    sources, (sw_ref, uw_ref), loaded, tables, sems = refs[:4], refs[4:6], refs[6:8], refs[8:10], refs[10]
    copies = start_copies(sources, (*tables, *loaded), sems)
    slab_table, user_table = tables
    for copy in copies[:2]:
        copy.wait()
    columns = sw_ref.shape[1]
    row = lax.broadcasted_iota(jnp.int32, (slab_table.shape[0], columns), 0)
    col = lax.broadcasted_iota(jnp.int32, (slab_table.shape[0], columns), 1)
    same = jnp.where(row == col, 1.0, 0.0).astype(jnp.bfloat16)
    sw_ref[...] = matmul(slab_table[...], same, ((0,), (0,)))
    for user in range(user_table.shape[0]):
        uw_ref[user * suffix : (user + 1) * suffix] = matmul(user_table[user], same, ((0,), (0,)))
    for copy in copies[2:]:
        copy.wait()


def scale_queries(q_ref, w_ref, scaled_ref):
    head_count = q_ref.shape[1] // HD
    scaled_ref[0] = jnp.zeros_like(scaled_ref[0])
    for head in range(head_count):
        cols = slice(head * HD, (head + 1) * HD)
        query = q_ref[:, cols]
        for level in range(1, scaled_ref.shape[0]):
            column = level * head_count + head
            weight = jnp.broadcast_to(w_ref[:, column : column + 1], query.shape).astype(jnp.bfloat16)
            scaled_ref[level, :, cols] = query * weight


def slab_kernel(*refs):
    sources, (w_ref, q_ref, k_ref, v_ref), (o_ref, scaled_ref), loaded, sems = (
        refs[:3],
        refs[3:7],
        refs[7:9],
        refs[9:12],
        refs[12],
    )
    copies = start_copies(sources, loaded, sems)
    attend(causal_mask(), q_ref, k_ref, v_ref, w_ref, o_ref)
    scale_queries(q_ref, w_ref, scaled_ref)
    for copy in copies:
        copy.wait()


def user_kernel(suffix, w_ref, q_ref, k_ref, v_ref, o_ref, scaled_ref):
    attend(causal_mask(suffix), q_ref, k_ref, v_ref, w_ref, o_ref)
    scale_queries(q_ref, w_ref, scaled_ref)


def read_kernel(depth, suffix, groups, ahead, length_ref, ss_ref, us_ref, sa_ref, ua_ref, *rest):
    offsets = [offset for group in groups for offset in group]
    states, outs, (lengths, sem) = rest[: len(offsets)], rest[len(offsets) : -2], rest[-2:]
    copy = pltpu.make_async_copy(length_ref, lengths, sem)
    copy.start()
    copy.wait()
    position = lax.axis_index("seq").astype(jnp.int32)
    head_count = sa_ref.shape[1] // HD
    users = range(ua_ref.shape[0] // suffix)
    targets = [lengths[user] for user in users]
    slab_level = {o: level_of(o, position, position, depth) for o in (*offsets, *ahead)}
    user_level = {o: [level_of(o, target, position, depth) for target in targets] for o in (*offsets, *ahead)}

    def slab_rows(offset, cols):
        return ss_ref[slab_level[offset], :, cols]

    def user_rows(offset, cols):
        parts = [us_ref[user_level[offset][user], user * suffix : (user + 1) * suffix, cols] for user in users]
        return jnp.concatenate(parts, axis=0)

    for head in range(head_count):
        cols = slice(head * HD, (head + 1) * HD)
        for pick, a_ref, t_ref in ((slab_rows, sa_ref, outs[0]), (user_rows, ua_ref, outs[1])):
            total = a_ref[:, cols]
            for group in groups:
                queries = jnp.concatenate([pick(offset, cols) for offset in group], axis=1)
                blocks = jnp.concatenate([states[offsets.index(offset)][0, head] for offset in group], axis=0)
                total = total + matmul(queries, blocks, ((1,), (0,)))
            t_ref[:, cols] = total
        for pick, out_ref in zip((slab_rows, user_rows), outs[2:]):
            for i, offset in enumerate(ahead):
                start = (head * len(ahead) + i) * HD
                out_ref[:, start : start + HD] = pick(offset, cols)


def last_kernel(ss_ref, us_ref, sa_ref, ua_ref, state_ref, mate_ref, st_ref, ut_ref, square_ref):
    head_count = sa_ref.shape[1] // HD
    line = 0
    for q_ref, a_ref, t_ref in ((ss_ref, sa_ref, st_ref), (us_ref, ua_ref, ut_ref)):
        for start in range(0, a_ref.shape[0], ROWS):
            rows = slice(start, start + ROWS)
            squares = None
            for head in range(head_count):
                cols = slice(head * HD, (head + 1) * HD)
                wide = slice(2 * head * HD, 2 * (head + 1) * HD)
                states = jnp.concatenate([state_ref[0, head], mate_ref[0, head]], axis=0)
                total = a_ref[rows, cols] + matmul(q_ref[rows, wide], states, ((1,), (0,)))
                t_ref[rows, cols] = total
                squares = total * total if squares is None else squares + total * total
            square_ref[line : line + 1] = jnp.sum(jnp.transpose(squares), axis=0, keepdims=True)
            line += 1


def norm_kernel(features, chunks, st_ref, ut_ref, gain_ref, one_ref, two_ref, so_hbm, uo_hbm, so_ref, uo_ref, sems):
    square = one_ref[...] + two_ref[...]
    scale = lax.rsqrt(square / features + 1e-06)
    scales = [jnp.transpose(jnp.broadcast_to(scale[line : line + 1], (ROWS, ROWS))) for line in range(scale.shape[0])]
    size = st_ref.shape[1] // chunks
    copies = []
    for chunk in range(chunks):
        line = 0
        wide = pl.ds(chunk * size, size)
        for side, (t_ref, o_ref, o_hbm) in enumerate(((st_ref, so_ref, so_hbm), (ut_ref, uo_ref, uo_hbm))):
            for start in range(0, t_ref.shape[0], ROWS):
                rows = slice(start, start + ROWS)
                for low in range(chunk * size, (chunk + 1) * size, HD):
                    cols = slice(low, low + HD)
                    gain = gain_ref[:, cols].astype(jnp.float32)
                    o_ref[rows, cols] = (t_ref[rows, cols] * scales[line] * gain).astype(jnp.bfloat16)
                line += 1
            copies.append(pltpu.make_async_copy(o_ref.at[:, wide], o_hbm.at[:, wide], sems.at[side, chunk]))
            copies[-1].start()
    for copy in copies:
        copy.wait()


def local(
    slab_query,
    slab_key,
    slab_value,
    slab_levels,
    norm_gain,
    user_query,
    user_key,
    user_value,
    user_levels,
    prefix_lengths,
):
    seq_count = lax.axis_size("seq")
    head_axis = lax.axis_size("head")
    depth = seq_count.bit_length() - 1
    token_count, width = slab_query.shape
    head_count = width // HD
    half = head_count // 2
    user_count, suffix = user_query.shape[:2]
    user_rows = user_count * suffix
    lines = (token_count + user_rows) // ROWS
    params = pltpu.CompilerParams(vmem_limit_bytes=VMEM_BYTES)
    bf16 = functools.partial(jax.ShapeDtypeStruct, dtype=jnp.bfloat16)
    vmem = pl.BlockSpec(memory_space=pltpu.VMEM)
    anywhere = pl.BlockSpec(memory_space=pl.ANY)
    hbm = pl.BlockSpec(memory_space=pltpu.HBM)
    chunks = min(4, half)
    rows_cost = 2 * width * (token_count + user_rows)

    def pinned(*arrays):
        return [pltpu.with_memory_space_constraint(array, pltpu.HBM) for array in arrays]

    def cost(flops, moved):
        return pl.CostEstimate(flops=flops, bytes_accessed=moved, transcendentals=0)

    def swap(value, bit):
        other = depth - bit if bit else 0
        return lax.ppermute(value, "seq", [(i, i ^ (1 << (other if i & 1 else bit))) for i in range(seq_count)])

    def after(results, values):
        return list(lax.optimization_barrier((results, values))[1])

    def join(order, halves):
        return pl.pallas_call(
            join_kernel,
            out_shape=pltpu.VMEM((len(halves) // 2, head_count, HD, HD), jnp.bfloat16),
            in_specs=[anywhere] + [vmem] * len(halves),
            out_specs=vmem,
            compiler_params=params,
        )(order, *halves)

    half_state = pltpu.VMEM((half, HD, HD), jnp.bfloat16)
    slab_rows = pltpu.VMEM((token_count, width), jnp.bfloat16)
    first, second, state, slab_keys, slab_values = pl.pallas_call(
        functools.partial(state_kernel, chunks),
        out_shape=[half_state, half_state, pltpu.VMEM((1, head_count, HD, HD), jnp.bfloat16), slab_rows, slab_rows],
        in_specs=[hbm] * 2,
        out_specs=[vmem] * 5,
        scratch_shapes=[pltpu.SemaphoreType.DMA((2, chunks))],
        compiler_params=params,
    )(*pinned(slab_key, slab_value))
    halves = [first, second]

    outer = list(range(1, depth))
    places = [(bit, side) for bit in outer for side in range(2)]
    ahead = [(bit, 0) for bit in outer[:-1]] + [(bit, 1) for bit in outer[1:]] or places
    sides = {1 << bit: [None, None] for bit in outer}
    for bit, side in ahead:
        sides[1 << bit][side] = swap(halves[side], bit)
    levels = depth + 1
    slab_table = slab_levels.reshape(-1, token_count)
    user_table = user_levels.reshape(user_count, -1, suffix)
    user_array = pltpu.VMEM((user_rows, width), jnp.bfloat16)
    slab_weights, user_weights, slab_queries, lengths = pl.pallas_call(
        functools.partial(load_kernel, suffix),
        out_shape=[
            pltpu.VMEM((token_count, levels * head_count), jnp.float32),
            pltpu.VMEM((user_rows, levels * head_count), jnp.float32),
            slab_rows,
            pltpu.VMEM((user_count,), jnp.int32),
        ],
        in_specs=[hbm] * 4,
        out_specs=[vmem] * 4,
        scratch_shapes=[
            pltpu.VMEM(slab_table.shape, jnp.bfloat16),
            pltpu.VMEM(user_table.shape, jnp.bfloat16),
            pltpu.SemaphoreType.DMA((4,)),
        ],
        compiler_params=params,
        cost_estimate=cost(0, 0),
    )(*pinned(slab_table, user_table, slab_query, prefix_lengths))
    halves = after(slab_weights, halves)
    for bit, side in places:
        if (bit, side) not in ahead:
            sides[1 << bit][side] = swap(halves[side], bit)
    slab_acc, slab_scaled, user_queries, user_keys, user_values = pl.pallas_call(
        slab_kernel,
        out_shape=[
            pltpu.VMEM((token_count, width), jnp.float32),
            pltpu.VMEM((levels, token_count, width), jnp.bfloat16),
        ]
        + [user_array] * 3,
        in_specs=[hbm] * 3 + [vmem] * 4,
        out_specs=[vmem] * 5,
        scratch_shapes=[pltpu.SemaphoreType.DMA((3,))],
        compiler_params=params,
        cost_estimate=cost(0, 0),
    )(
        *pinned(*[array.reshape(user_rows, width) for array in (user_query, user_key, user_value)]),
        slab_weights,
        slab_queries,
        slab_keys,
        slab_values,
    )

    later = sorted((m for m in range(0, seq_count, 2) if m.bit_count() > 1), key=lambda m: m.bit_count())
    for (bit, side), value in zip(ahead, after(slab_acc, [sides[1 << bit][side] for bit, side in ahead])):
        sides[1 << bit][side] = value
    for m in later:
        high, low = m.bit_length() - 1, (m & -m).bit_length() - 1
        sides[m] = [swap(sides[m ^ (1 << high)][0], high), swap(sides[m ^ (1 << low)][1], low)]
    user_weights = after([sides[1 << bit][side] for bit, side in ahead], [user_weights])[0]
    user_acc, user_scaled = pl.pallas_call(
        functools.partial(user_kernel, suffix),
        out_shape=[
            pltpu.VMEM((user_rows, width), jnp.float32),
            pltpu.VMEM((levels, user_rows, width), jnp.bfloat16),
        ],
        in_specs=[vmem] * 4,
        out_specs=[vmem] * 2,
        compiler_params=params,
        cost_estimate=cost(0, 0),
    )(user_weights, user_queries, user_keys, user_values)

    totals = [pltpu.VMEM((token_count, width), jnp.float32), pltpu.VMEM((user_rows, width), jnp.float32)]

    def read(offsets, accs, ahead=()):
        groups = [tuple(offsets[i : i + 2]) for i in range(0, len(offsets), 2)]
        wide = len(ahead) * width
        extra = [pltpu.VMEM((rows, wide), jnp.bfloat16) for rows in (token_count, user_rows) if ahead]
        return pl.pallas_call(
            functools.partial(read_kernel, depth, suffix, groups, ahead),
            out_shape=totals + extra,
            in_specs=[vmem] * (5 + len(offsets)),
            out_specs=[vmem] * (2 + len(extra)),
            scratch_shapes=[pltpu.SMEM((user_count,), jnp.int32), pltpu.SemaphoreType.DMA(())],
            compiler_params=params,
            cost_estimate=cost(0, 0),
        )(lengths, slab_scaled, user_scaled, *accs, *[whole[m] for m in offsets])

    state = after(slab_weights, [state])[0]
    whole = {0: state, 1: swap(state, 0)}
    direct = [1 << bit for bit in outer]
    for m in direct:
        whole[m] = join(user_acc, sides[m])
        whole[m | 1] = swap(whole[m], 0)
    accs = read([0, 1] + direct, (slab_acc, user_acc))
    for m in later:
        whole[m] = join(accs[0], sides[m])
        whole[m | 1] = swap(whole[m], 0)
    last = later[-1]
    if later[:-1]:
        accs = read([n for m in later[:-1] for n in (m, m | 1)], accs)
    *accs, slab_ahead, user_ahead = read([m | 1 for m in direct], accs, (last, last | 1))
    slab_total, user_total, square = pl.pallas_call(
        last_kernel,
        out_shape=totals + [pltpu.VMEM((lines, ROWS), jnp.float32)],
        in_specs=[vmem] * 6,
        out_specs=[vmem] * 3,
        compiler_params=params,
        cost_estimate=cost(0, 0),
    )(slab_ahead, user_ahead, *accs, whole[last], whole[last | 1])

    mate = jnp.zeros_like(square)
    for bit in range(head_axis.bit_length() - 1):
        square = square + mate
        mate = lax.ppermute(square, "head", [(i, i ^ (1 << bit)) for i in range(head_axis)])

    slab_out, user_out = pl.pallas_call(
        functools.partial(norm_kernel, float(width * head_axis), chunks),
        out_shape=[bf16((token_count, width)), bf16((user_rows, width))],
        in_specs=[vmem] * 5,
        out_specs=[hbm] * 2,
        scratch_shapes=[
            pltpu.VMEM((token_count, width), jnp.bfloat16),
            pltpu.VMEM((user_rows, width), jnp.bfloat16),
            pltpu.SemaphoreType.DMA((2, chunks)),
        ],
        compiler_params=params,
    )(slab_total, user_total, norm_gain.reshape(1, width), square, mate)
    return slab_out, user_out.reshape(user_count, suffix, width)


def solution(mesh):
    return jax.shard_map(
        local,
        mesh=mesh,
        in_specs=(
            P("seq", "head"),
            P("seq", "head"),
            P("seq", "head"),
            P(None, "head", "seq"),
            P("head"),
            P("seq", None, "head"),
            P("seq", None, "head"),
            P("seq", None, "head"),
            P("seq", None, "head", None),
            P("seq"),
        ),
        out_specs=(P("seq", "head"), P("seq", None, "head")),
        check_vma=False,
    )
```

time: 39.5 us -> 37.6 us (0.952)
  waiting for transfers between devices: 7.33 us -> 5.65 us
  Pallas kernels: 17.2 us -> 15.8 us
  starting transfers between devices: 14.1 us -> 15.2 us
    pallas_call x5, Pallas kernels: 12.5 us -> 11 us  [the longest x2 4.73 us: read(): pl.pallas_call(functools.partial(read_kernel, depth, suffix, groups, ahea...]
    ppermute x2, starting transfers between devices: 4.23 us -> 5.22 us  [local(): lax.ppermute(square, 'head', [(i, i ^ 1 << bit) for i in range(head_axis)])]
    ppermute x10, waiting for transfers between devices: 3.45 us -> 2.54 us  [swap(): lax.ppermute(value, 'seq', [(i, i ^ 1 << (other if i & 1 else bit)) for i...]
    ppermute x2, waiting for transfers between devices: 3.89 us -> 3.11 us  [local(): lax.ppermute(square, 'head', [(i, i ^ 1 << bit) for i in range(head_axis)])]
  transfers between devices with their start and end apart: 12 -> 12, of which waited for: 6 -> 6; matrix products, arithmetic and copies ran while one was open for 0% -> 0% of each run, Pallas kernels for 32% -> 30%
where the time goes in v7:
time: 37.6 us; the launch traced here: 37.4 us
  Pallas kernels  15.8 us (42%)
  starting transfers between devices  15.2 us (40%)
  waiting for transfers between devices  5.65 us (15%)
  between operations  0.78 us (2%)
    ppermute x10, starting transfers between devices, swap(): lax.ppermute(value, 'seq', [(i, i ^ 1 << (other if i & 1 else bit)) for i...  9.97 us
    ppermute x2, starting transfers between devices, local(): lax.ppermute(square, 'head', [(i, i ^ 1 << bit) for i in range(head_axis)])  5.22 us
    pallas_call x2, Pallas kernels, read(): pl.pallas_call(functools.partial(read_kernel, depth, suffix, groups, ahea...  4.73 us
    ppermute x2, waiting for transfers between devices, local(): lax.ppermute(square, 'head', [(i, i ^ 1 << bit) for i in range(head_axis)])  3.11 us
    pallas_call x1, Pallas kernels, local(): pl.pallas_call(slab_kernel, out_shape=[pltpu.VMEM((token_count, width), j...  2.9 us
    ppermute x10, waiting for transfers between devices, swap(): lax.ppermute(value, 'seq', [(i, i ^ 1 << (other if i & 1 else bit)) for i...  2.54 us
    pallas_call x1, Pallas kernels, local(): pl.pallas_call(functools.partial(user_kernel, suffix), out_shape=[pltpu.V...  2.22 us
    pallas_call x1, Pallas kernels, local(): pl.pallas_call(functools.partial(state_kernel, chunks), out_shape=[half_s...  1.97 us
  transfers between devices with their start and end apart: 12, of which 6 were waited for; matrix products, arithmetic and copies ran while one was open for 0% of the time, Pallas kernels for 30%

profile of v7, /device:TPU:0, one launch (start us, length us, event | category | flops | bytes accessed | tf_op | source)
XLA Modules:
  0.0 37.4 jit_solution(10346152959018847912)
XLA Ops:
  0.6 2.0 %shard_map.114 = (bf16[8,128,128]{2,1,0:T(8,128)(2,1)S(1)}, bf16[8,128,128]{2,1,0:T(8,128)(2,1)S(1)}, bf16[1,16,128,128]{3,2,1,0:T(8,128)(2,1)S(1)}, bf16[128,2048]{1,0:T(8,128)(2,1)S(1)}, bf16[128,2048]{1,0:T(8,128)(2,1)S(1)}) custom-call(bf16[128,2048]{1,0:T(8,128)(2,1)} %key_hbm.1, bf16[128,2048]{1,0:T(8,128)(2,1)} %value_hbm.1), custom_call_target="tpu_custom_call" | custom-call | tf_op jit(solution)/shard_map/pallas_call | solution.py:285
  2.6 3.0 %collective-permute-start = (bf16[8,128,128]{2,1,0:T(8,128)(2,1)S(1)}, bf16[8,128,128]{2,1,0:T(8,128)(2,1)S(1)}, u32[]{:S(2)}, u32[]{:S(2)}) collective-permute-start(bf16[8,128,128]{2,1,0:T(8,128)(2,1)S(1)} %get-tuple-element.56), channel_id=1, source_target_pairs={{0,8},{4,20},{8,0},{12,28},{16,24},{20,4},{24,16},{28,12},{1,9},{5... | collective-permute-start | bytes 786440 | tf_op jit(solution)/shard_map/ppermute | solution.py:269
  5.6 1.5 %collective-permute-start.1 = (bf16[8,128,128]{2,1,0:T(8,128)(2,1)S(1)}, bf16[8,128,128]{2,1,0:T(8,128)(2,1)S(1)}, u32[]{:S(2)}, u32[]{:S(2)}) collective-permute-start(bf16[8,128,128]{2,1,0:T(8,128)(2,1)S(1)} %get-tuple-element.55), channel_id=1, source_target_pairs={{0,16},{4,12},{8,24},{12,4},{16,0},{20,28},{24,8},{28,20},{1,17},{... | collective-permute-start | bytes 786440 | tf_op jit(solution)/shard_map/ppermute | solution.py:269
  7.1 1.2 %shard_map.113 = (f32[128,64]{1,0:T(8,128)S(1)}, f32[256,64]{1,0:T(8,128)S(1)}, bf16[128,2048]{1,0:T(8,128)(2,1)S(1)}, s32[4]{0:T(128)S(1)}) custom-call(bf16[96,128]{1,0:T(8,128)(2,1)} %bitcast.10, bf16[4,96,64]{2,1,0:T(8,128)(2,1)} %bitcast.9, bf16[128,2048]{1,0:T(8,128)(2,1)} %refs_2_.1, s32[4]{0:T(128)} %refs_3_.1), custom_call_target="tpu_custom_call" | custom-call | tf_op jit(solution)/shard_map/pallas_call | solution.py:305
  8.3 0.1 collective-permute-start.2
  8.4 0.6 %collective-permute-start.3 = (bf16[8,128,128]{2,1,0:T(8,128)(2,1)S(1)}, bf16[8,128,128]{2,1,0:T(8,128)(2,1)S(1)}, u32[]{:S(2)}, u32[]{:S(2)}) collective-permute-start(bf16[8,128,128]{2,1,0:T(8,128)(2,1)S(1)} %get-tuple-element.55), channel_id=1, source_target_pairs={{0,8},{4,20},{8,0},{12,28},{16,24},{20,4},{24,16},{28,12},{1,9},{5... | collective-permute-start | bytes 786440 | tf_op jit(solution)/shard_map/ppermute | solution.py:269
  9.0 0.1 collective-permute-start.4
  9.0 2.9 %shard_map.115 = (f32[128,2048]{1,0:T(8,128)S(1)}, bf16[4,128,2048]{2,1,0:T(8,128)(2,1)S(1)}, bf16[256,2048]{1,0:T(8,128)(2,1)S(1)}, bf16[256,2048]{1,0:T(8,128)(2,1)S(1)}, bf16[256,2048]{1,0:T(8,128)(2,1)S(1)}) custom-call(bf16[256,2048]{1,0:T(8,128)(2,1)} %bitcast.6, bf16[256,2048]{1,0:T(8,128)(2,1)} %bitcast.7, bf16[256,2048]{1,0:T(8,128)(2,1)} %bitcast.8, ...), custom_call_target="tpu_custom_call" | custom-call | tf_op jit(solution)/shard_map/pallas_call | solution.py:327
  11.9 0.3 collective-permute-done.refs_0_
  12.2 0.7 %collective-permute-done.1.refs_1_ = bf16[8,128,128]{2,1,0:T(8,128)(2,1)S(1)} collective-permute-done((bf16[8,128,128]{2,1,0:T(8,128)(2,1)S(1)}, bf16[8,128,128]{2,1,0:T(8,128)(2,1)S(1)}, u32[]{:S(2)}, u32[]{:S(2)}) %collective-permute-start.1) | collective-permute-done | bytes 262176 | tf_op jit(solution)/shard_map/ppermute | solution.py:269
  12.9 2.5 %collective-permute-start.7 = (bf16[8,128,128]{2,1,0:T(8,128)(2,1)S(1)}, bf16[8,128,128]{2,1,0:T(8,128)(2,1)S(1)}, u32[]{:S(2)}, u32[]{:S(2)}) collective-permute-start(bf16[8,128,128]{2,1,0:T(8,128)(2,1)S(1)} %collective-permute-done.refs_0_), channel_id=1, source_target_pairs={{0,16},{4,12},{8,24},{12,4},{16,0},{20,28},{24,8},{28,20},{1,17},{... | collective-permute-start | bytes 786440 | tf_op jit(solution)/shard_map/ppermute | solution.py:269
  15.4 1.5 %collective-permute-start.8 = (bf16[8,128,128]{2,1,0:T(8,128)(2,1)S(1)}, bf16[8,128,128]{2,1,0:T(8,128)(2,1)S(1)}, u32[]{:S(2)}, u32[]{:S(2)}) collective-permute-start(bf16[8,128,128]{2,1,0:T(8,128)(2,1)S(1)} %collective-permute-done.1.refs_1_), channel_id=1, source_target_pairs={{0,8},{4,20},{8,0},{12,28},{16,24},{20,4},{24,16},{28,12},{1,9},{5... | collective-permute-start | bytes 786440 | tf_op jit(solution)/shard_map/ppermute | solution.py:269
  16.9 2.2 %shard_map.116 = (f32[256,2048]{1,0:T(8,128)S(1)}, bf16[4,256,2048]{2,1,0:T(8,128)(2,1)S(1)}) custom-call(f32[256,64]{1,0:T(8,128)S(1)} %get-tuple-element.47.w_ref, bf16[256,2048]{1,0:T(8,128)(2,1)S(1)} %get-tuple-element.48.q_ref, bf16[256,2048]{1,0:T(8,128)(2,1)S(1)} %get-tuple-element.49.k_ref, bf16[256,2048]{1,0:T(8,128)(2,1)S(1)} %get-tuple-element.50.v_ref), custom_call_target="tpu_custom_call" | custom-call | tf_op jit(solution)/shard_map/pallas_call | solution.py:354
  19.1 0.0 collective-permute-done.3.refs_1_
  19.2 0.1 collective-permute-start.5
  19.3 0.0 collective-permute-done.4.refs_0_
  19.4 0.6 %collective-permute-start.6 = (bf16[1,16,128,128]{3,2,1,0:T(8,128)(2,1)S(1)}, bf16[1,16,128,128]{3,2,1,0:T(8,128)(2,1)S(1)}, u32[]{:S(2)}, u32[]{:S(2)}) collective-permute-start(bf16[1,16,128,128]{3,2,1,0:T(8,128)(2,1)S(1)} %shard_map.118.rest_3_), channel_id=1, source_target_pairs={{0,4},{4,0},{8,12},{12,8},{16,20},{20,16},{24,28},{28,24},{1,5},{5... | collective-permute-start | bytes 1572872 | tf_op jit(solution)/shard_map/ppermute | solution.py:269
  19.9 0.0 collective-permute-done.2.rest_1_
  19.9 2.5 %shard_map.119 = (f32[128,2048]{1,0:T(8,128)S(1)}, f32[256,2048]{1,0:T(8,128)S(1)}) custom-call(s32[4]{0:T(128)S(1)} %get-tuple-element.35.length_ref, bf16[4,128,2048]{2,1,0:T(8,128)(2,1)S(1)} %get-tuple-element.40.ss_ref, bf16[4,256,2048]{2,1,0:T(8,128)(2,1)S(1)} %get-tuple-element.51.us_ref, f32[128,2048]{1,0:T(8,128)S(1)} %get-tuple-element.41.sa_ref, ...), custom_call_target="tpu_custom_call" | custom-call | tf_op jit(solution)/shard_map/pallas_call | solution.py:372
  22.4 0.8 %collective-permute-done.7.refs_0_ = bf16[8,128,128]{2,1,0:T(8,128)(2,1)S(1)} collective-permute-done((bf16[8,128,128]{2,1,0:T(8,128)(2,1)S(1)}, bf16[8,128,128]{2,1,0:T(8,128)(2,1)S(1)}, u32[]{:S(2)}, u32[]{:S(2)}) %collective-permute-start.7) | collective-permute-done | bytes 262176 | tf_op jit(solution)/shard_map/ppermute | solution.py:269
  23.2 0.8 %collective-permute-done.8.refs_1_ = bf16[8,128,128]{2,1,0:T(8,128)(2,1)S(1)} collective-permute-done((bf16[8,128,128]{2,1,0:T(8,128)(2,1)S(1)}, bf16[8,128,128]{2,1,0:T(8,128)(2,1)S(1)}, u32[]{:S(2)}, u32[]{:S(2)}) %collective-permute-start.8) | collective-permute-done | bytes 262176 | tf_op jit(solution)/shard_map/ppermute | solution.py:269
  24.1 0.1 collective-permute-start.9
  24.1 0.0 collective-permute-done.5.rest_0_
  24.2 0.0 collective-permute-done.6.rest_1_
  24.2 2.2 %shard_map.120 = (f32[128,2048]{1,0:T(8,128)S(1)}, f32[256,2048]{1,0:T(8,128)S(1)}, bf16[128,4096]{1,0:T(8,128)(2,1)S(1)}, bf16[256,4096]{1,0:T(8,128)(2,1)S(1)}) custom-call(s32[4]{0:T(128)S(1)} %get-tuple-element.35.length_ref, bf16[4,128,2048]{2,1,0:T(8,128)(2,1)S(1)} %get-tuple-element.40.ss_ref, bf16[4,256,2048]{2,1,0:T(8,128)(2,1)S(1)} %get-tuple-element.51.us_ref, ...), custom_call_target="tpu_custom_call" | custom-call | tf_op jit(solution)/shard_map/pallas_call | solution.py:372
  26.4 0.0 collective-permute-done.9.mate_ref
  26.4 0.0 copy-start
  26.4 1.1 %shard_map.122 = (f32[128,2048]{1,0:T(8,128)S(1)}, f32[256,2048]{1,0:T(8,128)S(1)}, f32[3,128]{1,0:T(4,128)S(1)}) custom-call(bf16[128,4096]{1,0:T(8,128)(2,1)S(1)} %get-tuple-element.59.ss_ref, bf16[256,4096]{1,0:T(8,128)(2,1)S(1)} %get-tuple-element.60.us_ref, f32[128,2048]{1,0:T(8,128)S(1)} %get-tuple-element.61.sa_ref, ...), custom_call_target="tpu_custom_call" | custom-call | tf_op jit(solution)/shard_map/pallas_call | solution.py:396
  27.5 2.2 %collective-permute-start.10 = (f32[3,128]{1,0:T(4,128)S(1)}, f32[3,128]{1,0:T(4,128)S(1)}, u32[]{:S(2)}, u32[]{:S(2)}) collective-permute-start(f32[3,128]{1,0:T(4,128)S(1)} %get-tuple-element.65), channel_id=1, source_target_pairs={{0,1},{1,0},{2,3},{3,2},{4,5},{5,4},{6,7},{7,6},{8,9},{9,8},{10,11... | collective-permute-start | bytes 4616 | tf_op jit(solution)/shard_map/ppermute | solution.py:408
  29.7 1.6 %collective-permute-done.10 = f32[3,128]{1,0:T(4,128)S(1)} collective-permute-done((f32[3,128]{1,0:T(4,128)S(1)}, f32[3,128]{1,0:T(4,128)S(1)}, u32[]{:S(2)}, u32[]{:S(2)}) %collective-permute-start.10) | collective-permute-done | bytes 1568 | tf_op jit(solution)/shard_map/ppermute | solution.py:408
  31.3 3.0 %collective-permute-start.11 = (f32[3,128]{1,0:T(4,128)S(1)}, f32[3,128]{1,0:T(4,128)S(1)}, u32[]{:S(2)}, u32[]{:S(2)}) collective-permute-start(f32[3,128]{1,0:T(4,128)S(1)} %add.3.one_ref), channel_id=1, source_target_pairs={{0,2},{1,3},{2,0},{3,1},{4,6},{5,7},{6,4},{7,5},{8,10},{9,11},{10,... | collective-permute-start | bytes 4616 | tf_op jit(solution)/shard_map/ppermute | solution.py:408
  34.3 0.0 copy-done
  34.3 1.5 %collective-permute-done.11.two_ref = f32[3,128]{1,0:T(4,128)S(1)} collective-permute-done((f32[3,128]{1,0:T(4,128)S(1)}, f32[3,128]{1,0:T(4,128)S(1)}, u32[]{:S(2)}, u32[]{:S(2)}) %collective-permute-start.11) | collective-permute-done | bytes 1568 | tf_op jit(solution)/shard_map/ppermute | solution.py:408
  35.9 1.5 %shard_map.123 = (bf16[128,2048]{1,0:T(8,128)(2,1)}, bf16[256,2048]{1,0:T(8,128)(2,1)}) custom-call(f32[128,2048]{1,0:T(8,128)S(1)} %get-tuple-element.63.st_ref, f32[256,2048]{1,0:T(8,128)S(1)} %get-tuple-element.64.ut_ref, bf16[1,2048]{1,0:T(2,128)(2,1)S(1)} %reshape.30.gain_ref, f32[3,128]{1,0:T(4,128)S(1)} %add.3.one_ref, ...), custom_call_target="tpu_custom_call" | custom-call | tf_op jit(solution)/shard_map/pallas_call | solution.py:410
  (5 shorter events, 0.2 us)
Async XLA Ops:
  2.6 9.6 %collective-permute-start = (bf16[8,128,128]{2,1,0:T(8,128)(2,1)S(1)}, bf16[8,128,128]{2,1,0:T(8,128)(2,1)S(1)}, u32[]{:S(2)}, u32[]{:S(2)}) collective-permute-start(bf16[8,128,128]{2,1,0:T(8,128)(2,1)S(1)} %get-tuple-element.56), channel_id=1, source_target_pairs={{0,8},{4,20},{8,0},{12,28},{16,24},{20,4},{24,16},{28,12},{1,9},{5... | collective-permute-start | bytes 786440 | tf_op jit(solution)/shard_map/ppermute | solution.py:269
  5.6 7.3 %collective-permute-start.1 = (bf16[8,128,128]{2,1,0:T(8,128)(2,1)S(1)}, bf16[8,128,128]{2,1,0:T(8,128)(2,1)S(1)}, u32[]{:S(2)}, u32[]{:S(2)}) collective-permute-start(bf16[8,128,128]{2,1,0:T(8,128)(2,1)S(1)} %get-tuple-element.55), channel_id=1, source_target_pairs={{0,16},{4,12},{8,24},{12,4},{16,0},{20,28},{24,8},{28,20},{1,17},{... | collective-permute-start | bytes 786440 | tf_op jit(solution)/shard_map/ppermute | solution.py:269
  8.3 11.6 %collective-permute-start.2 = (bf16[1,16,128,128]{3,2,1,0:T(8,128)(2,1)S(1)}, bf16[1,16,128,128]{3,2,1,0:T(8,128)(2,1)S(1)}, u32[]{:S(2)}, u32[]{:S(2)}) collective-permute-start(bf16[1,16,128,128]{3,2,1,0:T(8,128)(2,1)S(1)} %get-tuple-element.54.rest_0_), channel_id=1, source_target_pairs={{0,4},{4,0},{8,12},{12,8},{16,20},{20,16},{24,28},{28,24},{1,5},{5... | collective-permute-start | bytes 1572872 | tf_op jit(solution)/shard_map/ppermute | solution.py:269
  8.4 10.8 %collective-permute-start.3 = (bf16[8,128,128]{2,1,0:T(8,128)(2,1)S(1)}, bf16[8,128,128]{2,1,0:T(8,128)(2,1)S(1)}, u32[]{:S(2)}, u32[]{:S(2)}) collective-permute-start(bf16[8,128,128]{2,1,0:T(8,128)(2,1)S(1)} %get-tuple-element.55), channel_id=1, source_target_pairs={{0,8},{4,20},{8,0},{12,28},{16,24},{20,4},{24,16},{28,12},{1,9},{5... | collective-permute-start | bytes 786440 | tf_op jit(solution)/shard_map/ppermute | solution.py:269
  9.0 10.3 %collective-permute-start.4 = (bf16[8,128,128]{2,1,0:T(8,128)(2,1)S(1)}, bf16[8,128,128]{2,1,0:T(8,128)(2,1)S(1)}, u32[]{:S(2)}, u32[]{:S(2)}) collective-permute-start(bf16[8,128,128]{2,1,0:T(8,128)(2,1)S(1)} %get-tuple-element.56), channel_id=1, source_target_pairs={{0,16},{4,12},{8,24},{12,4},{16,0},{20,28},{24,8},{28,20},{1,17},{... | collective-permute-start | bytes 786440 | tf_op jit(solution)/shard_map/ppermute | solution.py:269
  12.9 10.3 %collective-permute-start.7 = (bf16[8,128,128]{2,1,0:T(8,128)(2,1)S(1)}, bf16[8,128,128]{2,1,0:T(8,128)(2,1)S(1)}, u32[]{:S(2)}, u32[]{:S(2)}) collective-permute-start(bf16[8,128,128]{2,1,0:T(8,128)(2,1)S(1)} %collective-permute-done.refs_0_), channel_id=1, source_target_pairs={{0,16},{4,12},{8,24},{12,4},{16,0},{20,28},{24,8},{28,20},{1,17},{... | collective-permute-start | bytes 786440 | tf_op jit(solution)/shard_map/ppermute | solution.py:269
  15.4 8.6 %collective-permute-start.8 = (bf16[8,128,128]{2,1,0:T(8,128)(2,1)S(1)}, bf16[8,128,128]{2,1,0:T(8,128)(2,1)S(1)}, u32[]{:S(2)}, u32[]{:S(2)}) collective-permute-start(bf16[8,128,128]{2,1,0:T(8,128)(2,1)S(1)} %collective-permute-done.1.refs_1_), channel_id=1, source_target_pairs={{0,8},{4,20},{8,0},{12,28},{16,24},{20,4},{24,16},{28,12},{1,9},{5... | collective-permute-start | bytes 786440 | tf_op jit(solution)/shard_map/ppermute | solution.py:269
  19.2 4.9 %collective-permute-start.5 = (bf16[1,16,128,128]{3,2,1,0:T(8,128)(2,1)S(1)}, bf16[1,16,128,128]{3,2,1,0:T(8,128)(2,1)S(1)}, u32[]{:S(2)}, u32[]{:S(2)}) collective-permute-start(bf16[1,16,128,128]{3,2,1,0:T(8,128)(2,1)S(1)} %shard_map.117.rest_2_), channel_id=1, source_target_pairs={{0,4},{4,0},{8,12},{12,8},{16,20},{20,16},{24,28},{28,24},{1,5},{5... | collective-permute-start | bytes 1572872 | tf_op jit(solution)/shard_map/ppermute | solution.py:269
  19.4 4.8 %collective-permute-start.6 = (bf16[1,16,128,128]{3,2,1,0:T(8,128)(2,1)S(1)}, bf16[1,16,128,128]{3,2,1,0:T(8,128)(2,1)S(1)}, u32[]{:S(2)}, u32[]{:S(2)}) collective-permute-start(bf16[1,16,128,128]{3,2,1,0:T(8,128)(2,1)S(1)} %shard_map.118.rest_3_), channel_id=1, source_target_pairs={{0,4},{4,0},{8,12},{12,8},{16,20},{20,16},{24,28},{28,24},{1,5},{5... | collective-permute-start | bytes 1572872 | tf_op jit(solution)/shard_map/ppermute | solution.py:269
  24.1 2.3 %collective-permute-start.9 = (bf16[1,16,128,128]{3,2,1,0:T(8,128)(2,1)S(1)}, bf16[1,16,128,128]{3,2,1,0:T(8,128)(2,1)S(1)}, u32[]{:S(2)}, u32[]{:S(2)}) collective-permute-start(bf16[1,16,128,128]{3,2,1,0:T(8,128)(2,1)S(1)} %shard_map.121.state_ref), channel_id=1, source_target_pairs={{0,4},{4,0},{8,12},{12,8},{16,20},{20,16},{24,28},{28,24},{1,5},{5... | collective-permute-start | bytes 1572872 | tf_op jit(solution)/shard_map/ppermute | solution.py:269
  26.4 7.9 %copy-start = (bf16[2048]{0:T(1024)(128)(2,1)S(1)}, bf16[2048]{0:T(1024)(128)(2,1)}, u32[]{:S(2)}) copy-start(bf16[2048]{0:T(1024)(128)(2,1)} %param.14) | copy-start | bytes 12292
  27.5 3.8 %collective-permute-start.10 = (f32[3,128]{1,0:T(4,128)S(1)}, f32[3,128]{1,0:T(4,128)S(1)}, u32[]{:S(2)}, u32[]{:S(2)}) collective-permute-start(f32[3,128]{1,0:T(4,128)S(1)} %get-tuple-element.65), channel_id=1, source_target_pairs={{0,1},{1,0},{2,3},{3,2},{4,5},{5,4},{6,7},{7,6},{8,9},{9,8},{10,11... | collective-permute-start | bytes 4616 | tf_op jit(solution)/shard_map/ppermute | solution.py:408
  31.3 4.6 %collective-permute-start.11 = (f32[3,128]{1,0:T(4,128)S(1)}, f32[3,128]{1,0:T(4,128)S(1)}, u32[]{:S(2)}, u32[]{:S(2)}) collective-permute-start(f32[3,128]{1,0:T(4,128)S(1)} %add.3.one_ref), channel_id=1, source_target_pairs={{0,2},{1,3},{2,0},{3,1},{4,6},{5,7},{6,4},{7,5},{8,10},{9,11},{10,... | collective-permute-start | bytes 4616 | tf_op jit(solution)/shard_map/ppermute | solution.py:408

commit v8 on v7

--- a/solution.py
+++ b/solution.py
@@ -209,22 +209,22 @@
 def norm_kernel(features, chunks, st_ref, ut_ref, gain_ref, one_ref, two_ref, so_hbm, uo_hbm, so_ref, uo_ref, sems):
     square = one_ref[...] + two_ref[...]
     scale = lax.rsqrt(square / features + 1e-06)
-    scales = [jnp.transpose(jnp.broadcast_to(scale[line : line + 1], (ROWS, ROWS))) for line in range(scale.shape[0])]
     size = st_ref.shape[1] // chunks
     copies = []
-    for chunk in range(chunks):
-        line = 0
-        wide = pl.ds(chunk * size, size)
-        for side, (t_ref, o_ref, o_hbm) in enumerate(((st_ref, so_ref, so_hbm), (ut_ref, uo_ref, uo_hbm))):
-            for start in range(0, t_ref.shape[0], ROWS):
-                rows = slice(start, start + ROWS)
+    line = 0
+    for t_ref, o_ref, o_hbm in ((st_ref, so_ref, so_hbm), (ut_ref, uo_ref, uo_hbm)):
+        for start in range(0, t_ref.shape[0], ROWS):
+            rows = slice(start, start + ROWS)
+            factor = jnp.transpose(jnp.broadcast_to(scale[line : line + 1], (ROWS, ROWS)))
+            for chunk in range(chunks):
                 for low in range(chunk * size, (chunk + 1) * size, HD):
                     cols = slice(low, low + HD)
                     gain = gain_ref[:, cols].astype(jnp.float32)
-                    o_ref[rows, cols] = (t_ref[rows, cols] * scales[line] * gain).astype(jnp.bfloat16)
-                line += 1
-            copies.append(pltpu.make_async_copy(o_ref.at[:, wide], o_hbm.at[:, wide], sems.at[side, chunk]))
-            copies[-1].start()
+                    o_ref[rows, cols] = (t_ref[rows, cols] * factor * gain).astype(jnp.bfloat16)
+                part = (pl.ds(start, ROWS), pl.ds(chunk * size, size))
+                copies.append(pltpu.make_async_copy(o_ref.at[part], o_hbm.at[part], sems.at[line, chunk]))
+                copies[-1].start()
+            line += 1
     for copy in copies:
         copy.wait()
 
@@ -264,9 +264,15 @@
     def cost(flops, moved):
         return pl.CostEstimate(flops=flops, bytes_accessed=moved, transcendentals=0)
 
-    def swap(value, bit):
+    held = {0: list(range(seq_count))}
+
+    def swap(value, bit, offset):
         other = depth - bit if bit else 0
-        return lax.ppermute(value, "seq", [(i, i ^ (1 << (other if i & 1 else bit))) for i in range(seq_count)])
+        pairs = [(i, i ^ (1 << (other if i & 1 else bit))) for i in range(seq_count)]
+        pairs = [(i, j) for i, j in pairs if held[offset][i] not in (None, seq_count - 1)]
+        came = {j: held[offset][i] for i, j in pairs}
+        held[offset | (1 << bit)] = [came.get(i) for i in range(seq_count)]
+        return lax.ppermute(value, "seq", pairs)
 
     def after(results, values):
         return list(lax.optimization_barrier((results, values))[1])
@@ -297,7 +303,7 @@
     ahead = [(bit, 0) for bit in outer[:-1]] + [(bit, 1) for bit in outer[1:]] or places
     sides = {1 << bit: [None, None] for bit in outer}
     for bit, side in ahead:
-        sides[1 << bit][side] = swap(halves[side], bit)
+        sides[1 << bit][side] = swap(halves[side], bit, 0)
     levels = depth + 1
     slab_table = slab_levels.reshape(-1, token_count)
     user_table = user_levels.reshape(user_count, -1, suffix)
@@ -323,7 +329,7 @@
     halves = after(slab_weights, halves)
     for bit, side in places:
         if (bit, side) not in ahead:
-            sides[1 << bit][side] = swap(halves[side], bit)
+            sides[1 << bit][side] = swap(halves[side], bit, 0)
     slab_acc, slab_scaled, user_queries, user_keys, user_values = pl.pallas_call(
         slab_kernel,
         out_shape=[
@@ -349,7 +355,10 @@
         sides[1 << bit][side] = value
     for m in later:
         high, low = m.bit_length() - 1, (m & -m).bit_length() - 1
-        sides[m] = [swap(sides[m ^ (1 << high)][0], high), swap(sides[m ^ (1 << low)][1], low)]
+        sides[m] = [
+            swap(sides[m ^ (1 << high)][0], high, m ^ (1 << high)),
+            swap(sides[m ^ (1 << low)][1], low, m ^ (1 << low)),
+        ]
     user_weights = after([sides[1 << bit][side] for bit, side in ahead], [user_weights])[0]
     user_acc, user_scaled = pl.pallas_call(
         functools.partial(user_kernel, suffix),
@@ -380,19 +389,19 @@
         )(lengths, slab_scaled, user_scaled, *accs, *[whole[m] for m in offsets])
 
     state = after(slab_weights, [state])[0]
-    whole = {0: state, 1: swap(state, 0)}
+    whole = {0: state, 1: swap(state, 0, 0)}
     direct = [1 << bit for bit in outer]
     for m in direct:
         whole[m] = join(user_acc, sides[m])
-        whole[m | 1] = swap(whole[m], 0)
-    accs = read([0, 1] + direct, (slab_acc, user_acc))
+        whole[m | 1] = swap(whole[m], 0, m)
+    last = later[-1]
+    *accs, slab_ahead, user_ahead = read([0, 1] + direct, (slab_acc, user_acc), (last, last | 1))
     for m in later:
         whole[m] = join(accs[0], sides[m])
-        whole[m | 1] = swap(whole[m], 0)
-    last = later[-1]
+        whole[m | 1] = swap(whole[m], 0, m)
     if later[:-1]:
         accs = read([n for m in later[:-1] for n in (m, m | 1)], accs)
-    *accs, slab_ahead, user_ahead = read([m | 1 for m in direct], accs, (last, last | 1))
+    accs = read([m | 1 for m in direct], accs)
     slab_total, user_total, square = pl.pallas_call(
         last_kernel,
         out_shape=totals + [pltpu.VMEM((lines, ROWS), jnp.float32)],
@@ -415,7 +424,7 @@
         scratch_shapes=[
             pltpu.VMEM((token_count, width), jnp.bfloat16),
             pltpu.VMEM((user_rows, width), jnp.bfloat16),
-            pltpu.SemaphoreType.DMA((2, chunks)),
+            pltpu.SemaphoreType.DMA((lines, chunks)),
         ],
         compiler_params=params,
     )(slab_total, user_total, norm_gain.reshape(1, width), square, mate)

time: 37.6 us -> 53.4 us (1.42)
  starting transfers between devices: 15.2 us -> 32.4 us
  waiting for transfers between devices: 5.65 us -> 3.92 us
    ppermute x10, starting transfers between devices: 9.97 us -> 28.2 us  [swap(): return lax.ppermute(value, 'seq', pairs)]
    ppermute x10, waiting for transfers between devices: 2.54 us -> 0.03 us  [swap(): return lax.ppermute(value, 'seq', pairs)]
    ppermute x2, starting transfers between devices: 5.22 us -> 4.23 us  [local(): lax.ppermute(square, 'head', [(i, i ^ 1 << bit) for i in range(head_axis)])]
    ppermute x2, waiting for transfers between devices: 3.11 us -> 3.89 us  [local(): lax.ppermute(square, 'head', [(i, i ^ 1 << bit) for i in range(head_axis)])]
  transfers between devices with their start and end apart: 12 -> 12, of which waited for: 6 -> 2; matrix products, arithmetic and copies ran while one was open for 0% -> 0% of each run, Pallas kernels for 30% -> 21%
where the time goes in v8:
time: 53.4 us; the launch traced here: 53 us
  starting transfers between devices  32.4 us (61%)
  Pallas kernels  15.8 us (30%)
  waiting for transfers between devices  3.92 us (7%)
  between operations  0.87 us (2%)
    ppermute x10, starting transfers between devices, swap(): return lax.ppermute(value, 'seq', pairs)  28.2 us
    pallas_call x2, Pallas kernels, read(): pl.pallas_call(functools.partial(read_kernel, depth, suffix, groups, ahea...  4.83 us
    ppermute x2, starting transfers between devices, local(): lax.ppermute(square, 'head', [(i, i ^ 1 << bit) for i in range(head_axis)])  4.23 us
    ppermute x2, waiting for transfers between devices, local(): lax.ppermute(square, 'head', [(i, i ^ 1 << bit) for i in range(head_axis)])  3.89 us
    pallas_call x1, Pallas kernels, local(): pl.pallas_call(slab_kernel, out_shape=[pltpu.VMEM((token_count, width), j...  2.9 us
    pallas_call x1, Pallas kernels, local(): pl.pallas_call(functools.partial(user_kernel, suffix), out_shape=[pltpu.V...  2.13 us
    pallas_call x1, Pallas kernels, local(): pl.pallas_call(functools.partial(state_kernel, chunks), out_shape=[half_s...  1.97 us
    pallas_call x1, Pallas kernels, local(): pl.pallas_call(functools.partial(norm_kernel, float(width * head_axis), c...  1.48 us
  transfers between devices with their start and end apart: 12, of which 2 were waited for; matrix products, arithmetic and copies ran while one was open for 0% of the time, Pallas kernels for 21%

profile of v8, /device:TPU:0, one launch (start us, length us, event | category | flops | bytes accessed | tf_op | source)
XLA Modules:
  0.0 53.0 jit_solution(13188927682398053192)
XLA Ops:
  0.6 2.0 %shard_map.114 = (bf16[8,128,128]{2,1,0:T(8,128)(2,1)S(1)}, bf16[8,128,128]{2,1,0:T(8,128)(2,1)S(1)}, bf16[1,16,128,128]{3,2,1,0:T(8,128)(2,1)S(1)}, bf16[128,2048]{1,0:T(8,128)(2,1)S(1)}, bf16[128,2048]{1,0:T(8,128)(2,1)S(1)}) custom-call(bf16[128,2048]{1,0:T(8,128)(2,1)} %key_hbm.1, bf16[128,2048]{1,0:T(8,128)(2,1)} %value_hbm.1), custom_call_target="tpu_custom_call" | custom-call | tf_op jit(solution)/shard_map/pallas_call | solution.py:291
  2.6 4.8 %collective-permute-start = (bf16[8,128,128]{2,1,0:T(8,128)(2,1)S(1)}, bf16[8,128,128]{2,1,0:T(8,128)(2,1)S(1)}, u32[]{:S(2)}, u32[]{:S(2)}) collective-permute-start(bf16[8,128,128]{2,1,0:T(8,128)(2,1)S(1)} %get-tuple-element.56), channel_id=1, source_target_pairs={{0,8},{4,20},{8,0},{12,28},{16,24},{20,4},{24,16},{1,9},{5,21},{9,... | collective-permute-start | bytes 786440 | tf_op jit(solution)/shard_map/ppermute | solution.py:275
  7.5 3.4 %collective-permute-start.1 = (bf16[8,128,128]{2,1,0:T(8,128)(2,1)S(1)}, bf16[8,128,128]{2,1,0:T(8,128)(2,1)S(1)}, u32[]{:S(2)}, u32[]{:S(2)}) collective-permute-start(bf16[8,128,128]{2,1,0:T(8,128)(2,1)S(1)} %get-tuple-element.55), channel_id=1, source_target_pairs={{0,16},{4,12},{8,24},{12,4},{16,0},{20,28},{24,8},{1,17},{5,13},{9... | collective-permute-start | bytes 786440 | tf_op jit(solution)/shard_map/ppermute | solution.py:275
  10.9 1.2 %shard_map.113 = (f32[128,64]{1,0:T(8,128)S(1)}, f32[256,64]{1,0:T(8,128)S(1)}, bf16[128,2048]{1,0:T(8,128)(2,1)S(1)}, s32[4]{0:T(128)S(1)}) custom-call(bf16[96,128]{1,0:T(8,128)(2,1)} %bitcast.10, bf16[4,96,64]{2,1,0:T(8,128)(2,1)} %bitcast.9, bf16[128,2048]{1,0:T(8,128)(2,1)} %refs_2_.1, s32[4]{0:T(128)} %refs_3_.1), custom_call_target="tpu_custom_call" | custom-call | tf_op jit(solution)/shard_map/pallas_call | solution.py:311
  12.1 1.9 %collective-permute-start.2 = (bf16[1,16,128,128]{3,2,1,0:T(8,128)(2,1)S(1)}, bf16[1,16,128,128]{3,2,1,0:T(8,128)(2,1)S(1)}, u32[]{:S(2)}, u32[]{:S(2)}) collective-permute-start(bf16[1,16,128,128]{3,2,1,0:T(8,128)(2,1)S(1)} %get-tuple-element.54.rest_0_), channel_id=1, source_target_pairs={{0,4},{4,0},{8,12},{12,8},{16,20},{20,16},{24,28},{1,5},{5,1},{9,1... | collective-permute-start | bytes 1572872 | tf_op jit(solution)/shard_map/ppermute | solution.py:275
  14.0 2.4 %collective-permute-start.4 = (bf16[8,128,128]{2,1,0:T(8,128)(2,1)S(1)}, bf16[8,128,128]{2,1,0:T(8,128)(2,1)S(1)}, u32[]{:S(2)}, u32[]{:S(2)}) collective-permute-start(bf16[8,128,128]{2,1,0:T(8,128)(2,1)S(1)} %get-tuple-element.56), channel_id=1, source_target_pairs={{0,16},{4,12},{8,24},{12,4},{16,0},{20,28},{24,8},{1,17},{5,13},{9... | collective-permute-start | bytes 786440 | tf_op jit(solution)/shard_map/ppermute | solution.py:275
  16.4 1.9 %collective-permute-start.3 = (bf16[8,128,128]{2,1,0:T(8,128)(2,1)S(1)}, bf16[8,128,128]{2,1,0:T(8,128)(2,1)S(1)}, u32[]{:S(2)}, u32[]{:S(2)}) collective-permute-start(bf16[8,128,128]{2,1,0:T(8,128)(2,1)S(1)} %get-tuple-element.55), channel_id=1, source_target_pairs={{0,8},{4,20},{8,0},{12,28},{16,24},{20,4},{24,16},{1,9},{5,21},{9,... | collective-permute-start | bytes 786440 | tf_op jit(solution)/shard_map/ppermute | solution.py:275
  18.4 2.9 %shard_map.115 = (f32[128,2048]{1,0:T(8,128)S(1)}, bf16[4,128,2048]{2,1,0:T(8,128)(2,1)S(1)}, bf16[256,2048]{1,0:T(8,128)(2,1)S(1)}, bf16[256,2048]{1,0:T(8,128)(2,1)S(1)}, bf16[256,2048]{1,0:T(8,128)(2,1)S(1)}) custom-call(bf16[256,2048]{1,0:T(8,128)(2,1)} %bitcast.6, bf16[256,2048]{1,0:T(8,128)(2,1)} %bitcast.7, bf16[256,2048]{1,0:T(8,128)(2,1)} %bitcast.8, ...), custom_call_target="tpu_custom_call" | custom-call | tf_op jit(solution)/shard_map/pallas_call | solution.py:333
  21.3 0.0 collective-permute-done.refs_0_
  21.3 0.0 collective-permute-done.1.refs_1_
  21.3 3.9 %collective-permute-start.7 = (bf16[8,128,128]{2,1,0:T(8,128)(2,1)S(1)}, bf16[8,128,128]{2,1,0:T(8,128)(2,1)S(1)}, u32[]{:S(2)}, u32[]{:S(2)}) collective-permute-start(bf16[8,128,128]{2,1,0:T(8,128)(2,1)S(1)} %collective-permute-done.refs_0_), channel_id=1, source_target_pairs={{0,16},{4,12},{8,24},{16,0},{20,28},{24,8},{28,20},{1,17},{5,13},{... | collective-permute-start | bytes 786440 | tf_op jit(solution)/shard_map/ppermute | solution.py:275
  25.2 3.4 %collective-permute-start.8 = (bf16[8,128,128]{2,1,0:T(8,128)(2,1)S(1)}, bf16[8,128,128]{2,1,0:T(8,128)(2,1)S(1)}, u32[]{:S(2)}, u32[]{:S(2)}) collective-permute-start(bf16[8,128,128]{2,1,0:T(8,128)(2,1)S(1)} %collective-permute-done.1.refs_1_), channel_id=1, source_target_pairs={{0,8},{4,20},{8,0},{12,28},{16,24},{24,16},{28,12},{1,9},{5,21},{9... | collective-permute-start | bytes 786440 | tf_op jit(solution)/shard_map/ppermute | solution.py:275
  28.7 2.1 %shard_map.116 = (f32[256,2048]{1,0:T(8,128)S(1)}, bf16[4,256,2048]{2,1,0:T(8,128)(2,1)S(1)}) custom-call(f32[256,64]{1,0:T(8,128)S(1)} %get-tuple-element.47.w_ref, bf16[256,2048]{1,0:T(8,128)(2,1)S(1)} %get-tuple-element.48.q_ref, bf16[256,2048]{1,0:T(8,128)(2,1)S(1)} %get-tuple-element.49.k_ref, bf16[256,2048]{1,0:T(8,128)(2,1)S(1)} %get-tuple-element.50.v_ref), custom_call_target="tpu_custom_call" | custom-call | tf_op jit(solution)/shard_map/pallas_call | solution.py:363
  30.8 0.0 collective-permute-done.4.refs_0_
  30.9 1.9 %collective-permute-start.6 = (bf16[1,16,128,128]{3,2,1,0:T(8,128)(2,1)S(1)}, bf16[1,16,128,128]{3,2,1,0:T(8,128)(2,1)S(1)}, u32[]{:S(2)}, u32[]{:S(2)}) collective-permute-start(bf16[1,16,128,128]{3,2,1,0:T(8,128)(2,1)S(1)} %shard_map.118.rest_3_), channel_id=1, source_target_pairs={{0,4},{4,0},{8,12},{12,8},{16,20},{24,28},{28,24},{1,5},{5,1},{9,1... | collective-permute-start | bytes 1572872 | tf_op jit(solution)/shard_map/ppermute | solution.py:275
  32.8 0.0 collective-permute-done.3.refs_1_
  32.9 2.4 %collective-permute-start.5 = (bf16[1,16,128,128]{3,2,1,0:T(8,128)(2,1)S(1)}, bf16[1,16,128,128]{3,2,1,0:T(8,128)(2,1)S(1)}, u32[]{:S(2)}, u32[]{:S(2)}) collective-permute-start(bf16[1,16,128,128]{3,2,1,0:T(8,128)(2,1)S(1)} %shard_map.117.rest_2_), channel_id=1, source_target_pairs={{0,4},{4,0},{8,12},{16,20},{20,16},{24,28},{28,24},{1,5},{5,1},{9,... | collective-permute-start | bytes 1572872 | tf_op jit(solution)/shard_map/ppermute | solution.py:275
  35.3 0.0 collective-permute-done.2.rest_1_
  35.3 3.2 %shard_map.119 = (f32[128,2048]{1,0:T(8,128)S(1)}, f32[256,2048]{1,0:T(8,128)S(1)}, bf16[128,4096]{1,0:T(8,128)(2,1)S(1)}, bf16[256,4096]{1,0:T(8,128)(2,1)S(1)}) custom-call(s32[4]{0:T(128)S(1)} %get-tuple-element.35.length_ref, bf16[4,128,2048]{2,1,0:T(8,128)(2,1)S(1)} %get-tuple-element.40.ss_ref, bf16[4,256,2048]{2,1,0:T(8,128)(2,1)S(1)} %get-tuple-element.51.us_ref, ...), custom_call_target="tpu_custom_call" | custom-call | tf_op jit(solution)/shard_map/pallas_call | solution.py:381
  38.5 0.0 collective-permute-done.7.refs_0_
  38.5 0.0 collective-permute-done.8.refs_1_
  38.6 1.9 %collective-permute-start.9 = (bf16[1,16,128,128]{3,2,1,0:T(8,128)(2,1)S(1)}, bf16[1,16,128,128]{3,2,1,0:T(8,128)(2,1)S(1)}, u32[]{:S(2)}, u32[]{:S(2)}) collective-permute-start(bf16[1,16,128,128]{3,2,1,0:T(8,128)(2,1)S(1)} %shard_map.121.state_ref), channel_id=1, source_target_pairs={{0,4},{8,12},{12,8},{16,20},{20,16},{24,28},{28,24},{1,5},{9,13},{... | collective-permute-start | bytes 1572872 | tf_op jit(solution)/shard_map/ppermute | solution.py:275
  40.5 0.0 collective-permute-done.6.rest_1_
  40.5 0.0 collective-permute-done.5.rest_0_
  40.5 1.6 %shard_map.120 = (f32[128,2048]{1,0:T(8,128)S(1)}, f32[256,2048]{1,0:T(8,128)S(1)}) custom-call(s32[4]{0:T(128)S(1)} %get-tuple-element.35.length_ref, bf16[4,128,2048]{2,1,0:T(8,128)(2,1)S(1)} %get-tuple-element.40.ss_ref, bf16[4,256,2048]{2,1,0:T(8,128)(2,1)S(1)} %get-tuple-element.51.us_ref, f32[128,2048]{1,0:T(8,128)S(1)} %get-tuple-element.59.sa_ref.order_ref, ...), custom_call_target="tpu_custom_call" | custom-call | tf_op jit(solution)/shard_map/pallas_call | solution.py:381
  42.2 0.0 collective-permute-done.9.mate_ref
  42.2 0.0 copy-start
  42.2 1.1 %shard_map.122 = (f32[128,2048]{1,0:T(8,128)S(1)}, f32[256,2048]{1,0:T(8,128)S(1)}, f32[3,128]{1,0:T(4,128)S(1)}) custom-call(bf16[128,4096]{1,0:T(8,128)(2,1)S(1)} %get-tuple-element.57.ss_ref, bf16[256,4096]{1,0:T(8,128)(2,1)S(1)} %get-tuple-element.58.us_ref, f32[128,2048]{1,0:T(8,128)S(1)} %get-tuple-element.61.sa_ref, ...), custom_call_target="tpu_custom_call" | custom-call | tf_op jit(solution)/shard_map/pallas_call | solution.py:405
  43.3 1.6 %collective-permute-start.10 = (f32[3,128]{1,0:T(4,128)S(1)}, f32[3,128]{1,0:T(4,128)S(1)}, u32[]{:S(2)}, u32[]{:S(2)}) collective-permute-start(f32[3,128]{1,0:T(4,128)S(1)} %get-tuple-element.65), channel_id=1, source_target_pairs={{0,1},{1,0},{2,3},{3,2},{4,5},{5,4},{6,7},{7,6},{8,9},{9,8},{10,11... | collective-permute-start | bytes 4616 | tf_op jit(solution)/shard_map/ppermute | solution.py:417
  45.0 2.0 %collective-permute-done.10 = f32[3,128]{1,0:T(4,128)S(1)} collective-permute-done((f32[3,128]{1,0:T(4,128)S(1)}, f32[3,128]{1,0:T(4,128)S(1)}, u32[]{:S(2)}, u32[]{:S(2)}) %collective-permute-start.10) | collective-permute-done | bytes 1568 | tf_op jit(solution)/shard_map/ppermute | solution.py:417
  47.0 2.6 %collective-permute-start.11 = (f32[3,128]{1,0:T(4,128)S(1)}, f32[3,128]{1,0:T(4,128)S(1)}, u32[]{:S(2)}, u32[]{:S(2)}) collective-permute-start(f32[3,128]{1,0:T(4,128)S(1)} %add.3.one_ref), channel_id=1, source_target_pairs={{0,2},{1,3},{2,0},{3,1},{4,6},{5,7},{6,4},{7,5},{8,10},{9,11},{10,... | collective-permute-start | bytes 4616 | tf_op jit(solution)/shard_map/ppermute | solution.py:417
  49.6 0.0 copy-done
  49.6 1.9 %collective-permute-done.11.two_ref = f32[3,128]{1,0:T(4,128)S(1)} collective-permute-done((f32[3,128]{1,0:T(4,128)S(1)}, f32[3,128]{1,0:T(4,128)S(1)}, u32[]{:S(2)}, u32[]{:S(2)}) %collective-permute-start.11) | collective-permute-done | bytes 1568 | tf_op jit(solution)/shard_map/ppermute | solution.py:417
  51.5 1.5 %shard_map.123 = (bf16[128,2048]{1,0:T(8,128)(2,1)}, bf16[256,2048]{1,0:T(8,128)(2,1)}) custom-call(f32[128,2048]{1,0:T(8,128)S(1)} %get-tuple-element.63.st_ref, f32[256,2048]{1,0:T(8,128)S(1)} %get-tuple-element.64.ut_ref, bf16[1,2048]{1,0:T(2,128)(2,1)S(1)} %reshape.30.gain_ref, f32[3,128]{1,0:T(4,128)S(1)} %add.3.one_ref, ...), custom_call_target="tpu_custom_call" | custom-call | tf_op jit(solution)/shard_map/pallas_call | solution.py:419
  (5 shorter events, 0.2 us)
Async XLA Ops:
  2.6 18.7 %collective-permute-start = (bf16[8,128,128]{2,1,0:T(8,128)(2,1)S(1)}, bf16[8,128,128]{2,1,0:T(8,128)(2,1)S(1)}, u32[]{:S(2)}, u32[]{:S(2)}) collective-permute-start(bf16[8,128,128]{2,1,0:T(8,128)(2,1)S(1)} %get-tuple-element.56), channel_id=1, source_target_pairs={{0,8},{4,20},{8,0},{12,28},{16,24},{20,4},{24,16},{1,9},{5,21},{9,... | collective-permute-start | bytes 786440 | tf_op jit(solution)/shard_map/ppermute | solution.py:275
  7.5 13.8 %collective-permute-start.1 = (bf16[8,128,128]{2,1,0:T(8,128)(2,1)S(1)}, bf16[8,128,128]{2,1,0:T(8,128)(2,1)S(1)}, u32[]{:S(2)}, u32[]{:S(2)}) collective-permute-start(bf16[8,128,128]{2,1,0:T(8,128)(2,1)S(1)} %get-tuple-element.55), channel_id=1, source_target_pairs={{0,16},{4,12},{8,24},{12,4},{16,0},{20,28},{24,8},{1,17},{5,13},{9... | collective-permute-start | bytes 786440 | tf_op jit(solution)/shard_map/ppermute | solution.py:275
  12.1 23.2 %collective-permute-start.2 = (bf16[1,16,128,128]{3,2,1,0:T(8,128)(2,1)S(1)}, bf16[1,16,128,128]{3,2,1,0:T(8,128)(2,1)S(1)}, u32[]{:S(2)}, u32[]{:S(2)}) collective-permute-start(bf16[1,16,128,128]{3,2,1,0:T(8,128)(2,1)S(1)} %get-tuple-element.54.rest_0_), channel_id=1, source_target_pairs={{0,4},{4,0},{8,12},{12,8},{16,20},{20,16},{24,28},{1,5},{5,1},{9,1... | collective-permute-start | bytes 1572872 | tf_op jit(solution)/shard_map/ppermute | solution.py:275
  14.0 16.8 %collective-permute-start.4 = (bf16[8,128,128]{2,1,0:T(8,128)(2,1)S(1)}, bf16[8,128,128]{2,1,0:T(8,128)(2,1)S(1)}, u32[]{:S(2)}, u32[]{:S(2)}) collective-permute-start(bf16[8,128,128]{2,1,0:T(8,128)(2,1)S(1)} %get-tuple-element.56), channel_id=1, source_target_pairs={{0,16},{4,12},{8,24},{12,4},{16,0},{20,28},{24,8},{1,17},{5,13},{9... | collective-permute-start | bytes 786440 | tf_op jit(solution)/shard_map/ppermute | solution.py:275
  16.4 16.4 %collective-permute-start.3 = (bf16[8,128,128]{2,1,0:T(8,128)(2,1)S(1)}, bf16[8,128,128]{2,1,0:T(8,128)(2,1)S(1)}, u32[]{:S(2)}, u32[]{:S(2)}) collective-permute-start(bf16[8,128,128]{2,1,0:T(8,128)(2,1)S(1)} %get-tuple-element.55), channel_id=1, source_target_pairs={{0,8},{4,20},{8,0},{12,28},{16,24},{20,4},{24,16},{1,9},{5,21},{9,... | collective-permute-start | bytes 786440 | tf_op jit(solution)/shard_map/ppermute | solution.py:275
  21.3 17.2 %collective-permute-start.7 = (bf16[8,128,128]{2,1,0:T(8,128)(2,1)S(1)}, bf16[8,128,128]{2,1,0:T(8,128)(2,1)S(1)}, u32[]{:S(2)}, u32[]{:S(2)}) collective-permute-start(bf16[8,128,128]{2,1,0:T(8,128)(2,1)S(1)} %collective-permute-done.refs_0_), channel_id=1, source_target_pairs={{0,16},{4,12},{8,24},{16,0},{20,28},{24,8},{28,20},{1,17},{5,13},{... | collective-permute-start | bytes 786440 | tf_op jit(solution)/shard_map/ppermute | solution.py:275
  25.2 13.3 %collective-permute-start.8 = (bf16[8,128,128]{2,1,0:T(8,128)(2,1)S(1)}, bf16[8,128,128]{2,1,0:T(8,128)(2,1)S(1)}, u32[]{:S(2)}, u32[]{:S(2)}) collective-permute-start(bf16[8,128,128]{2,1,0:T(8,128)(2,1)S(1)} %collective-permute-done.1.refs_1_), channel_id=1, source_target_pairs={{0,8},{4,20},{8,0},{12,28},{16,24},{24,16},{28,12},{1,9},{5,21},{9... | collective-permute-start | bytes 786440 | tf_op jit(solution)/shard_map/ppermute | solution.py:275
  30.9 9.7 %collective-permute-start.6 = (bf16[1,16,128,128]{3,2,1,0:T(8,128)(2,1)S(1)}, bf16[1,16,128,128]{3,2,1,0:T(8,128)(2,1)S(1)}, u32[]{:S(2)}, u32[]{:S(2)}) collective-permute-start(bf16[1,16,128,128]{3,2,1,0:T(8,128)(2,1)S(1)} %shard_map.118.rest_3_), channel_id=1, source_target_pairs={{0,4},{4,0},{8,12},{12,8},{16,20},{24,28},{28,24},{1,5},{5,1},{9,1... | collective-permute-start | bytes 1572872 | tf_op jit(solution)/shard_map/ppermute | solution.py:275
  32.9 7.7 %collective-permute-start.5 = (bf16[1,16,128,128]{3,2,1,0:T(8,128)(2,1)S(1)}, bf16[1,16,128,128]{3,2,1,0:T(8,128)(2,1)S(1)}, u32[]{:S(2)}, u32[]{:S(2)}) collective-permute-start(bf16[1,16,128,128]{3,2,1,0:T(8,128)(2,1)S(1)} %shard_map.117.rest_2_), channel_id=1, source_target_pairs={{0,4},{4,0},{8,12},{16,20},{20,16},{24,28},{28,24},{1,5},{5,1},{9,... | collective-permute-start | bytes 1572872 | tf_op jit(solution)/shard_map/ppermute | solution.py:275
  38.6 3.6 %collective-permute-start.9 = (bf16[1,16,128,128]{3,2,1,0:T(8,128)(2,1)S(1)}, bf16[1,16,128,128]{3,2,1,0:T(8,128)(2,1)S(1)}, u32[]{:S(2)}, u32[]{:S(2)}) collective-permute-start(bf16[1,16,128,128]{3,2,1,0:T(8,128)(2,1)S(1)} %shard_map.121.state_ref), channel_id=1, source_target_pairs={{0,4},{8,12},{12,8},{16,20},{20,16},{24,28},{28,24},{1,5},{9,13},{... | collective-permute-start | bytes 1572872 | tf_op jit(solution)/shard_map/ppermute | solution.py:275
  42.2 7.4 %copy-start = (bf16[2048]{0:T(1024)(128)(2,1)S(1)}, bf16[2048]{0:T(1024)(128)(2,1)}, u32[]{:S(2)}) copy-start(bf16[2048]{0:T(1024)(128)(2,1)} %param.14) | copy-start | bytes 12292
  43.3 3.7 %collective-permute-start.10 = (f32[3,128]{1,0:T(4,128)S(1)}, f32[3,128]{1,0:T(4,128)S(1)}, u32[]{:S(2)}, u32[]{:S(2)}) collective-permute-start(f32[3,128]{1,0:T(4,128)S(1)} %get-tuple-element.65), channel_id=1, source_target_pairs={{0,1},{1,0},{2,3},{3,2},{4,5},{5,4},{6,7},{7,6},{8,9},{9,8},{10,11... | collective-permute-start | bytes 4616 | tf_op jit(solution)/shard_map/ppermute | solution.py:417
  47.0 4.5 %collective-permute-start.11 = (f32[3,128]{1,0:T(4,128)S(1)}, f32[3,128]{1,0:T(4,128)S(1)}, u32[]{:S(2)}, u32[]{:S(2)}) collective-permute-start(f32[3,128]{1,0:T(4,128)S(1)} %add.3.one_ref), channel_id=1, source_target_pairs={{0,2},{1,3},{2,0},{3,1},{4,6},{5,7},{6,4},{7,5},{8,10},{9,11},{10,... | collective-permute-start | bytes 4616 | tf_op jit(solution)/shard_map/ppermute | solution.py:417

commit v9 on v8

--- a/solution.py
+++ b/solution.py
@@ -17,38 +17,30 @@
     return lax.dot_general(a, b, (contract, ((), ())), preferred_element_type=jnp.float32)
 
 
-def load_columns(sources, targets, sems, chunks):
-    copies = []
-    for chunk in range(chunks):
-        group = []
-        for i, (source, target) in enumerate(zip(sources, targets)):
-            size = source.shape[1] // chunks
-            cols = pl.ds(chunk * size, size)
-            group.append(pltpu.make_async_copy(source.at[:, cols], target.at[:, cols], sems.at[i, chunk]))
-            group[-1].start()
-        copies.append(group)
-
-    def wait(chunk):
-        for copy in copies[chunk]:
-            copy.wait()
-
-    return wait
-
-
-def state_kernel(chunks, key_hbm, value_hbm, first_ref, second_ref, whole_ref, key_ref, value_ref, sems):
-    half = first_ref.shape[0]
-    head_count = 2 * half
-    wait = load_columns((key_hbm, value_hbm), (key_ref, value_ref), sems, chunks)
-    for head in range(head_count):
-        if head % (head_count // chunks) == 0:
-            wait(head // (head_count // chunks))
-        cols = slice(head * HD, (head + 1) * HD)
-        state = matmul(key_ref[:, cols], value_ref[:, cols], ((0,), (0,)))
-        whole_ref[0, head] = state.astype(jnp.bfloat16)
+def start_copies(sources, targets, sems):
+    copies = [
+        pltpu.make_async_copy(source, target, sems.at[i]) for i, (source, target) in enumerate(zip(sources, targets))
+    ]
+    for copy in copies:
+        copy.start()
+    return copies
+
+
+def block_states(key_ref, value_ref, base, out_ref):
+    for head in range(out_ref.shape[0]):
+        start = head * HD if isinstance(base, int) else pl.multiple_of(base + head * HD, HD)
+        cols = pl.ds(start, HD)
+        out_ref[head] = matmul(key_ref[:, cols], value_ref[:, cols], ((0,), (0,))).astype(jnp.bfloat16)
+
+
+def first_kernel(key_hbm, value_hbm, out_ref, key_ref, value_ref, sems):
+    width = key_ref.shape[1]
     parity = lax.axis_index("seq") & 1
-    for head in range(half):
-        first_ref[head] = whole_ref[0, parity * half + head]
-        second_ref[head] = whole_ref[0, (1 - parity) * half + head]
+    cols = pl.ds(pl.multiple_of(parity * width, width), width)
+    copies = start_copies((key_hbm.at[:, cols], value_hbm.at[:, cols]), (key_ref, value_ref), sems)
+    for copy in copies:
+        copy.wait()
+    block_states(key_ref, value_ref, 0, out_ref)
 
 
 def join_kernel(order_ref, *refs):
@@ -95,20 +87,21 @@
     return jnp.logical_and(row >= col, row // suffix == col // suffix)
 
 
-def start_copies(sources, targets, sems):
-    copies = [
-        pltpu.make_async_copy(source, target, sems.at[i]) for i, (source, target) in enumerate(zip(sources, targets))
-    ]
-    for copy in copies:
-        copy.start()
-    return copies
-
-
 def load_kernel(suffix, *refs):
-    sources, (sw_ref, uw_ref), loaded, tables, sems = refs[:4], refs[4:6], refs[6:8], refs[8:10], refs[10]
-    copies = start_copies(sources, (*tables, *loaded), sems)
+    first_ref, sources, (second_ref, whole_ref, sw_ref, uw_ref), rest = refs[0], refs[1:7], refs[7:11], refs[11:]
+    loaded, tables, sems = rest[:4], rest[4:6], rest[6]
+    key_ref, value_ref = loaded[:2]
+    copies = start_copies(sources, (*loaded[:2], *tables, *loaded[2:]), sems)
     slab_table, user_table = tables
+    half = first_ref.shape[0]
+    parity = lax.axis_index("seq") & 1
     for copy in copies[:2]:
+        copy.wait()
+    block_states(key_ref, value_ref, (1 - parity) * (half * HD), second_ref)
+    for head in range(half):
+        whole_ref[0, parity * half + head] = first_ref[head]
+        whole_ref[0, (1 - parity) * half + head] = second_ref[head]
+    for copy in copies[2:4]:
         copy.wait()
     columns = sw_ref.shape[1]
     row = lax.broadcasted_iota(jnp.int32, (slab_table.shape[0], columns), 0)
@@ -117,7 +110,7 @@
     sw_ref[...] = matmul(slab_table[...], same, ((0,), (0,)))
     for user in range(user_table.shape[0]):
         uw_ref[user * suffix : (user + 1) * suffix] = matmul(user_table[user], same, ((0,), (0,)))
-    for copy in copies[2:]:
+    for copy in copies[4:]:
         copy.wait()
 
 
@@ -264,15 +257,9 @@
     def cost(flops, moved):
         return pl.CostEstimate(flops=flops, bytes_accessed=moved, transcendentals=0)
 
-    held = {0: list(range(seq_count))}
-
-    def swap(value, bit, offset):
+    def swap(value, bit):
         other = depth - bit if bit else 0
-        pairs = [(i, i ^ (1 << (other if i & 1 else bit))) for i in range(seq_count)]
-        pairs = [(i, j) for i, j in pairs if held[offset][i] not in (None, seq_count - 1)]
-        came = {j: held[offset][i] for i, j in pairs}
-        held[offset | (1 << bit)] = [came.get(i) for i in range(seq_count)]
-        return lax.ppermute(value, "seq", pairs)
+        return lax.ppermute(value, "seq", [(i, i ^ (1 << (other if i & 1 else bit))) for i in range(seq_count)])
 
     def after(results, values):
         return list(lax.optimization_barrier((results, values))[1])
@@ -288,48 +275,52 @@
 
     half_state = pltpu.VMEM((half, HD, HD), jnp.bfloat16)
     slab_rows = pltpu.VMEM((token_count, width), jnp.bfloat16)
-    first, second, state, slab_keys, slab_values = pl.pallas_call(
-        functools.partial(state_kernel, chunks),
-        out_shape=[half_state, half_state, pltpu.VMEM((1, head_count, HD, HD), jnp.bfloat16), slab_rows, slab_rows],
+    first = pl.pallas_call(
+        first_kernel,
+        out_shape=half_state,
         in_specs=[hbm] * 2,
-        out_specs=[vmem] * 5,
-        scratch_shapes=[pltpu.SemaphoreType.DMA((2, chunks))],
+        out_specs=vmem,
+        scratch_shapes=[pltpu.VMEM((token_count, width // 2), jnp.bfloat16)] * 2 + [pltpu.SemaphoreType.DMA((2,))],
         compiler_params=params,
     )(*pinned(slab_key, slab_value))
-    halves = [first, second]
 
     outer = list(range(1, depth))
     places = [(bit, side) for bit in outer for side in range(2)]
-    ahead = [(bit, 0) for bit in outer[:-1]] + [(bit, 1) for bit in outer[1:]] or places
+    ahead = [(bit, 0) for bit in outer[:-1]] + [(bit, 1) for bit in outer[1:]]
     sides = {1 << bit: [None, None] for bit in outer}
-    for bit, side in ahead:
-        sides[1 << bit][side] = swap(halves[side], bit, 0)
     levels = depth + 1
     slab_table = slab_levels.reshape(-1, token_count)
     user_table = user_levels.reshape(user_count, -1, suffix)
     user_array = pltpu.VMEM((user_rows, width), jnp.bfloat16)
-    slab_weights, user_weights, slab_queries, lengths = pl.pallas_call(
+    second, state, slab_weights, user_weights, slab_keys, slab_values, slab_queries, lengths = pl.pallas_call(
         functools.partial(load_kernel, suffix),
         out_shape=[
+            half_state,
+            pltpu.VMEM((1, head_count, HD, HD), jnp.bfloat16),
             pltpu.VMEM((token_count, levels * head_count), jnp.float32),
             pltpu.VMEM((user_rows, levels * head_count), jnp.float32),
             slab_rows,
+            slab_rows,
+            slab_rows,
             pltpu.VMEM((user_count,), jnp.int32),
         ],
-        in_specs=[hbm] * 4,
-        out_specs=[vmem] * 4,
+        in_specs=[vmem] + [hbm] * 6,
+        out_specs=[vmem] * 8,
         scratch_shapes=[
             pltpu.VMEM(slab_table.shape, jnp.bfloat16),
             pltpu.VMEM(user_table.shape, jnp.bfloat16),
-            pltpu.SemaphoreType.DMA((4,)),
+            pltpu.SemaphoreType.DMA((6,)),
         ],
         compiler_params=params,
         cost_estimate=cost(0, 0),
-    )(*pinned(slab_table, user_table, slab_query, prefix_lengths))
+    )(first, *pinned(slab_key, slab_value, slab_table, user_table, slab_query, prefix_lengths))
+    halves = [first, second]
+    for bit, side in ahead:
+        sides[1 << bit][side] = swap(halves[side], bit)
     halves = after(slab_weights, halves)
     for bit, side in places:
         if (bit, side) not in ahead:
-            sides[1 << bit][side] = swap(halves[side], bit, 0)
+            sides[1 << bit][side] = swap(halves[side], bit)
     slab_acc, slab_scaled, user_queries, user_keys, user_values = pl.pallas_call(
         slab_kernel,
         out_shape=[
@@ -355,10 +346,7 @@
         sides[1 << bit][side] = value
     for m in later:
         high, low = m.bit_length() - 1, (m & -m).bit_length() - 1
-        sides[m] = [
-            swap(sides[m ^ (1 << high)][0], high, m ^ (1 << high)),
-            swap(sides[m ^ (1 << low)][1], low, m ^ (1 << low)),
-        ]
+        sides[m] = [swap(sides[m ^ (1 << high)][0], high), swap(sides[m ^ (1 << low)][1], low)]
     user_weights = after([sides[1 << bit][side] for bit, side in ahead], [user_weights])[0]
     user_acc, user_scaled = pl.pallas_call(
         functools.partial(user_kernel, suffix),
@@ -388,17 +376,16 @@
             cost_estimate=cost(0, 0),
         )(lengths, slab_scaled, user_scaled, *accs, *[whole[m] for m in offsets])
 
-    state = after(slab_weights, [state])[0]
-    whole = {0: state, 1: swap(state, 0, 0)}
+    whole = {0: state, 1: swap(state, 0)}
     direct = [1 << bit for bit in outer]
     for m in direct:
         whole[m] = join(user_acc, sides[m])
-        whole[m | 1] = swap(whole[m], 0, m)
+        whole[m | 1] = swap(whole[m], 0)
     last = later[-1]
     *accs, slab_ahead, user_ahead = read([0, 1] + direct, (slab_acc, user_acc), (last, last | 1))
     for m in later:
         whole[m] = join(accs[0], sides[m])
-        whole[m | 1] = swap(whole[m], 0, m)
+        whole[m | 1] = swap(whole[m], 0)
     if later[:-1]:
         accs = read([n for m in later[:-1] for n in (m, m | 1)], accs)
     accs = read([m | 1 for m in direct], accs)

time: 53.4 us -> 37.4 us (0.70)
  starting transfers between devices: 32.4 us -> 12.7 us
  waiting for transfers between devices: 3.92 us -> 8.07 us
    ppermute x10, starting transfers between devices: 28.2 us -> 8.46 us  [swap(): lax.ppermute(value, 'seq', [(i, i ^ 1 << (other if i & 1 else bit)) for i...]
    ppermute x10, waiting for transfers between devices: 0.03 us -> 4.18 us  [swap(): lax.ppermute(value, 'seq', [(i, i ^ 1 << (other if i & 1 else bit)) for i...]
  transfers between devices with their start and end apart: 12 -> 12, of which waited for: 2 -> 5; matrix products, arithmetic and copies ran while one was open for 0% -> 0% of each run, Pallas kernels for 21% -> 32%
where the time goes in v9:
time: 37.4 us; the launch traced here: 37.2 us
  Pallas kernels  15.7 us (42%)
  starting transfers between devices  12.7 us (34%)
  waiting for transfers between devices  8.07 us (22%)
  between operations  0.76 us (2%)
    ppermute x10, starting transfers between devices, swap(): lax.ppermute(value, 'seq', [(i, i ^ 1 << (other if i & 1 else bit)) for i...  8.46 us
    pallas_call x2, Pallas kernels, read(): pl.pallas_call(functools.partial(read_kernel, depth, suffix, groups, ahea...  4.8 us
    ppermute x2, starting transfers between devices, local(): lax.ppermute(square, 'head', [(i, i ^ 1 << bit) for i in range(head_axis)])  4.23 us
    ppermute x10, waiting for transfers between devices, swap(): lax.ppermute(value, 'seq', [(i, i ^ 1 << (other if i & 1 else bit)) for i...  4.18 us
    ppermute x2, waiting for transfers between devices, local(): lax.ppermute(square, 'head', [(i, i ^ 1 << bit) for i in range(head_axis)])  3.89 us
    pallas_call x1, Pallas kernels, local(): pl.pallas_call(slab_kernel, out_shape=[pltpu.VMEM((token_count, width), j...  2.89 us
    pallas_call x1, Pallas kernels, local(): pl.pallas_call(functools.partial(user_kernel, suffix), out_shape=[pltpu.V...  2.13 us
    pallas_call x1, Pallas kernels, local(): pl.pallas_call(functools.partial(load_kernel, suffix), out_shape=[half_st...  1.77 us
  transfers between devices with their start and end apart: 12, of which 5 were waited for; matrix products, arithmetic and copies ran while one was open for 0% of the time, Pallas kernels for 32%

profile of v9, /device:TPU:0, one launch (start us, length us, event | category | flops | bytes accessed | tf_op | source)
XLA Modules:
  0.0 37.2 jit_solution(42095984915849213)
XLA Ops:
  0.6 1.3 %shard_map.113.refs_0_ = bf16[8,128,128]{2,1,0:T(8,128)(2,1)S(1)} custom-call(bf16[128,2048]{1,0:T(8,128)(2,1)} %refs_1_.1, bf16[128,2048]{1,0:T(8,128)(2,1)} %refs_2_.1), custom_call_target="tpu_custom_call" | custom-call | tf_op jit(solution)/shard_map/pallas_call | solution.py:278
  2.0 3.0 %collective-permute-start = (bf16[8,128,128]{2,1,0:T(8,128)(2,1)S(1)}, bf16[8,128,128]{2,1,0:T(8,128)(2,1)S(1)}, u32[]{:S(2)}, u32[]{:S(2)}) collective-permute-start(bf16[8,128,128]{2,1,0:T(8,128)(2,1)S(1)} %shard_map.113.refs_0_), channel_id=1, source_target_pairs={{0,8},{4,20},{8,0},{12,28},{16,24},{20,4},{24,16},{28,12},{1,9},{5... | collective-permute-start | bytes 786440 | tf_op jit(solution)/shard_map/ppermute | solution.py:262
  5.0 1.8 %shard_map.114 = (bf16[8,128,128]{2,1,0:T(8,128)(2,1)S(1)}, bf16[1,16,128,128]{3,2,1,0:T(8,128)(2,1)S(1)}, f32[128,64]{1,0:T(8,128)S(1)}, f32[256,64]{1,0:T(8,12...) custom-call(bf16[8,128,128]{2,1,0:T(8,128)(2,1)S(1)} %shard_map.113., ...), custom_call_target="tpu_custom_call" | custom-call | tf_op jit(solution)/shard_map/pallas_call | solution.py:295
  6.7 1.6 %collective-permute-start.1 = (bf16[8,128,128]{2,1,0:T(8,128)(2,1)S(1)}, bf16[8,128,128]{2,1,0:T(8,128)(2,1)S(1)}, u32[]{:S(2)}, u32[]{:S(2)}) collective-permute-start(bf16[8,128,128]{2,1,0:T(8,128)(2,1)S(1)} %get-tuple-element.51), channel_id=1, source_target_pairs={{0,16},{4,12},{8,24},{12,4},{16,0},{20,28},{24,8},{28,20},{1,17},{... | collective-permute-start | bytes 786440 | tf_op jit(solution)/shard_map/ppermute | solution.py:262
  8.3 0.0 collective-permute-start.2
  8.3 0.5 %collective-permute-start.4 = (bf16[8,128,128]{2,1,0:T(8,128)(2,1)S(1)}, bf16[8,128,128]{2,1,0:T(8,128)(2,1)S(1)}, u32[]{:S(2)}, u32[]{:S(2)}) collective-permute-start(bf16[8,128,128]{2,1,0:T(8,128)(2,1)S(1)} %shard_map.113.refs_0_), channel_id=1, source_target_pairs={{0,16},{4,12},{8,24},{12,4},{16,0},{20,28},{24,8},{28,20},{1,17},{... | collective-permute-start | bytes 786440 | tf_op jit(solution)/shard_map/ppermute | solution.py:262
  8.8 0.2 collective-permute-start.3
  9.0 2.9 %shard_map.115 = (f32[128,2048]{1,0:T(8,128)S(1)}, bf16[4,128,2048]{2,1,0:T(8,128)(2,1)S(1)}, bf16[256,2048]{1,0:T(8,128)(2,1)S(1)}, bf16[256,2048]{1,0:T(8,128)(2,1)S(1)}, bf16[256,2048]{1,0:T(8,128)(2,1)S(1)}) custom-call(bf16[256,2048]{1,0:T(8,128)(2,1)} %bitcast.6, bf16[256,2048]{1,0:T(8,128)(2,1)} %bitcast.7, bf16[256,2048]{1,0:T(8,128)(2,1)} %bitcast.8, ...), custom_call_target="tpu_custom_call" | custom-call | tf_op jit(solution)/shard_map/pallas_call | solution.py:324
  11.9 3.0 %collective-permute-done.1.refs_1_ = bf16[8,128,128]{2,1,0:T(8,128)(2,1)S(1)} collective-permute-done((bf16[8,128,128]{2,1,0:T(8,128)(2,1)S(1)}, bf16[8,128,128]{2,1,0:T(8,128)(2,1)S(1)}, u32[]{:S(2)}, u32[]{:S(2)}) %collective-permute-start.1) | collective-permute-done | bytes 262176 | tf_op jit(solution)/shard_map/ppermute | solution.py:262
  14.9 0.0 collective-permute-done.refs_0_
  14.9 2.5 %collective-permute-start.7 = (bf16[8,128,128]{2,1,0:T(8,128)(2,1)S(1)}, bf16[8,128,128]{2,1,0:T(8,128)(2,1)S(1)}, u32[]{:S(2)}, u32[]{:S(2)}) collective-permute-start(bf16[8,128,128]{2,1,0:T(8,128)(2,1)S(1)} %collective-permute-done.refs_0_), channel_id=1, source_target_pairs={{0,16},{4,12},{8,24},{12,4},{16,0},{20,28},{24,8},{28,20},{1,17},{... | collective-permute-start | bytes 786440 | tf_op jit(solution)/shard_map/ppermute | solution.py:262
  17.4 0.0 collective-permute-start.8
  17.4 2.1 %shard_map.116 = (f32[256,2048]{1,0:T(8,128)S(1)}, bf16[4,256,2048]{2,1,0:T(8,128)(2,1)S(1)}) custom-call(f32[256,64]{1,0:T(8,128)S(1)} %get-tuple-element.44.w_ref, bf16[256,2048]{1,0:T(8,128)(2,1)S(1)} %get-tuple-element.45.q_ref, bf16[256,2048]{1,0:T(8,128)(2,1)S(1)} %get-tuple-element.46.k_ref, bf16[256,2048]{1,0:T(8,128)(2,1)S(1)} %get-tuple-element.47.v_ref), custom_call_target="tpu_custom_call" | custom-call | tf_op jit(solution)/shard_map/pallas_call | solution.py:351
  19.6 0.0 collective-permute-done.4.refs_0_
  19.6 0.1 collective-permute-start.6
  19.7 0.0 collective-permute-done.3.refs_1_
  19.8 0.6 %collective-permute-start.5 = (bf16[1,16,128,128]{3,2,1,0:T(8,128)(2,1)S(1)}, bf16[1,16,128,128]{3,2,1,0:T(8,128)(2,1)S(1)}, u32[]{:S(2)}, u32[]{:S(2)}) collective-permute-start(bf16[1,16,128,128]{3,2,1,0:T(8,128)(2,1)S(1)} %shard_map.117.rest_2_), channel_id=1, source_target_pairs={{0,4},{4,0},{8,12},{12,8},{16,20},{20,16},{24,28},{28,24},{1,5},{5... | collective-permute-start | bytes 1572872 | tf_op jit(solution)/shard_map/ppermute | solution.py:262
  20.3 0.0 collective-permute-done.2.rest_1_
  20.3 3.2 %shard_map.119 = (f32[128,2048]{1,0:T(8,128)S(1)}, f32[256,2048]{1,0:T(8,128)S(1)}, bf16[128,4096]{1,0:T(8,128)(2,1)S(1)}, bf16[256,4096]{1,0:T(8,128)(2,1)S(1)}) custom-call(s32[4]{0:T(128)S(1)} %get-tuple-element.33.length_ref, bf16[4,128,2048]{2,1,0:T(8,128)(2,1)S(1)} %get-tuple-element.38.ss_ref, bf16[4,256,2048]{2,1,0:T(8,128)(2,1)S(1)} %get-tuple-element.48.us_ref, ...), custom_call_target="tpu_custom_call" | custom-call | tf_op jit(solution)/shard_map/pallas_call | solution.py:369
  23.5 0.9 %collective-permute-done.7.refs_0_ = bf16[8,128,128]{2,1,0:T(8,128)(2,1)S(1)} collective-permute-done((bf16[8,128,128]{2,1,0:T(8,128)(2,1)S(1)}, bf16[8,128,128]{2,1,0:T(8,128)(2,1)S(1)}, u32[]{:S(2)}, u32[]{:S(2)}) %collective-permute-start.7) | collective-permute-done | bytes 262176 | tf_op jit(solution)/shard_map/ppermute | solution.py:262
  24.4 0.0 collective-permute-done.8.refs_1_
  24.5 0.1 collective-permute-start.9
  24.5 0.0 collective-permute-done.6.rest_1_
  24.6 0.0 collective-permute-done.5.rest_0_
  24.6 1.6 %shard_map.120 = (f32[128,2048]{1,0:T(8,128)S(1)}, f32[256,2048]{1,0:T(8,128)S(1)}) custom-call(s32[4]{0:T(128)S(1)} %get-tuple-element.33.length_ref, bf16[4,128,2048]{2,1,0:T(8,128)(2,1)S(1)} %get-tuple-element.38.ss_ref, bf16[4,256,2048]{2,1,0:T(8,128)(2,1)S(1)} %get-tuple-element.48.us_ref, f32[128,2048]{1,0:T(8,128)S(1)} %get-tuple-element.55.sa_ref.order_ref, ...), custom_call_target="tpu_custom_call" | custom-call | tf_op jit(solution)/shard_map/pallas_call | solution.py:369
  26.2 0.3 collective-permute-done.9.mate_ref
  26.4 0.0 copy-start
  26.4 1.1 %shard_map.122 = (f32[128,2048]{1,0:T(8,128)S(1)}, f32[256,2048]{1,0:T(8,128)S(1)}, f32[3,128]{1,0:T(4,128)S(1)}) custom-call(bf16[128,4096]{1,0:T(8,128)(2,1)S(1)} %get-tuple-element.53.ss_ref, bf16[256,4096]{1,0:T(8,128)(2,1)S(1)} %get-tuple-element.54.us_ref, f32[128,2048]{1,0:T(8,128)S(1)} %get-tuple-element.57.sa_ref, ...), custom_call_target="tpu_custom_call" | custom-call | tf_op jit(solution)/shard_map/pallas_call | solution.py:392
  27.6 1.6 %collective-permute-start.10 = (f32[3,128]{1,0:T(4,128)S(1)}, f32[3,128]{1,0:T(4,128)S(1)}, u32[]{:S(2)}, u32[]{:S(2)}) collective-permute-start(f32[3,128]{1,0:T(4,128)S(1)} %get-tuple-element.61), channel_id=1, source_target_pairs={{0,1},{1,0},{2,3},{3,2},{4,5},{5,4},{6,7},{7,6},{8,9},{9,8},{10,11... | collective-permute-start | bytes 4616 | tf_op jit(solution)/shard_map/ppermute | solution.py:404
  29.2 2.0 %collective-permute-done.10 = f32[3,128]{1,0:T(4,128)S(1)} collective-permute-done((f32[3,128]{1,0:T(4,128)S(1)}, f32[3,128]{1,0:T(4,128)S(1)}, u32[]{:S(2)}, u32[]{:S(2)}) %collective-permute-start.10) | collective-permute-done | bytes 1568 | tf_op jit(solution)/shard_map/ppermute | solution.py:404
  31.2 2.6 %collective-permute-start.11 = (f32[3,128]{1,0:T(4,128)S(1)}, f32[3,128]{1,0:T(4,128)S(1)}, u32[]{:S(2)}, u32[]{:S(2)}) collective-permute-start(f32[3,128]{1,0:T(4,128)S(1)} %add.3.one_ref), channel_id=1, source_target_pairs={{0,2},{1,3},{2,0},{3,1},{4,6},{5,7},{6,4},{7,5},{8,10},{9,11},{10,... | collective-permute-start | bytes 4616 | tf_op jit(solution)/shard_map/ppermute | solution.py:404
  33.8 0.0 copy-done
  33.8 1.9 %collective-permute-done.11.two_ref = f32[3,128]{1,0:T(4,128)S(1)} collective-permute-done((f32[3,128]{1,0:T(4,128)S(1)}, f32[3,128]{1,0:T(4,128)S(1)}, u32[]{:S(2)}, u32[]{:S(2)}) %collective-permute-start.11) | collective-permute-done | bytes 1568 | tf_op jit(solution)/shard_map/ppermute | solution.py:404
  35.7 1.5 %shard_map.123 = (bf16[128,2048]{1,0:T(8,128)(2,1)}, bf16[256,2048]{1,0:T(8,128)(2,1)}) custom-call(f32[128,2048]{1,0:T(8,128)S(1)} %get-tuple-element.59.st_ref, f32[256,2048]{1,0:T(8,128)S(1)} %get-tuple-element.60.ut_ref, bf16[1,2048]{1,0:T(2,128)(2,1)S(1)} %reshape.30.gain_ref, f32[3,128]{1,0:T(4,128)S(1)} %add.3.one_ref, ...), custom_call_target="tpu_custom_call" | custom-call | tf_op jit(solution)/shard_map/pallas_call | solution.py:406
  (5 shorter events, 0.2 us)
Async XLA Ops:
  2.0 13.0 %collective-permute-start = (bf16[8,128,128]{2,1,0:T(8,128)(2,1)S(1)}, bf16[8,128,128]{2,1,0:T(8,128)(2,1)S(1)}, u32[]{:S(2)}, u32[]{:S(2)}) collective-permute-start(bf16[8,128,128]{2,1,0:T(8,128)(2,1)S(1)} %shard_map.113.refs_0_), channel_id=1, source_target_pairs={{0,8},{4,20},{8,0},{12,28},{16,24},{20,4},{24,16},{28,12},{1,9},{5... | collective-permute-start | bytes 786440 | tf_op jit(solution)/shard_map/ppermute | solution.py:262
  6.7 8.2 %collective-permute-start.1 = (bf16[8,128,128]{2,1,0:T(8,128)(2,1)S(1)}, bf16[8,128,128]{2,1,0:T(8,128)(2,1)S(1)}, u32[]{:S(2)}, u32[]{:S(2)}) collective-permute-start(bf16[8,128,128]{2,1,0:T(8,128)(2,1)S(1)} %get-tuple-element.51), channel_id=1, source_target_pairs={{0,16},{4,12},{8,24},{12,4},{16,0},{20,28},{24,8},{28,20},{1,17},{... | collective-permute-start | bytes 786440 | tf_op jit(solution)/shard_map/ppermute | solution.py:262
  8.3 12.0 %collective-permute-start.2 = (bf16[1,16,128,128]{3,2,1,0:T(8,128)(2,1)S(1)}, bf16[1,16,128,128]{3,2,1,0:T(8,128)(2,1)S(1)}, u32[]{:S(2)}, u32[]{:S(2)}) collective-permute-start(bf16[1,16,128,128]{3,2,1,0:T(8,128)(2,1)S(1)} %get-tuple-element.50.rest_0_), channel_id=1, source_target_pairs={{0,4},{4,0},{8,12},{12,8},{16,20},{20,16},{24,28},{28,24},{1,5},{5... | collective-permute-start | bytes 1572872 | tf_op jit(solution)/shard_map/ppermute | solution.py:262
  8.3 11.2 %collective-permute-start.4 = (bf16[8,128,128]{2,1,0:T(8,128)(2,1)S(1)}, bf16[8,128,128]{2,1,0:T(8,128)(2,1)S(1)}, u32[]{:S(2)}, u32[]{:S(2)}) collective-permute-start(bf16[8,128,128]{2,1,0:T(8,128)(2,1)S(1)} %shard_map.113.refs_0_), channel_id=1, source_target_pairs={{0,16},{4,12},{8,24},{12,4},{16,0},{20,28},{24,8},{28,20},{1,17},{... | collective-permute-start | bytes 786440 | tf_op jit(solution)/shard_map/ppermute | solution.py:262
  8.8 10.9 %collective-permute-start.3 = (bf16[8,128,128]{2,1,0:T(8,128)(2,1)S(1)}, bf16[8,128,128]{2,1,0:T(8,128)(2,1)S(1)}, u32[]{:S(2)}, u32[]{:S(2)}) collective-permute-start(bf16[8,128,128]{2,1,0:T(8,128)(2,1)S(1)} %get-tuple-element.51), channel_id=1, source_target_pairs={{0,8},{4,20},{8,0},{12,28},{16,24},{20,4},{24,16},{28,12},{1,9},{5... | collective-permute-start | bytes 786440 | tf_op jit(solution)/shard_map/ppermute | solution.py:262
  14.9 9.5 %collective-permute-start.7 = (bf16[8,128,128]{2,1,0:T(8,128)(2,1)S(1)}, bf16[8,128,128]{2,1,0:T(8,128)(2,1)S(1)}, u32[]{:S(2)}, u32[]{:S(2)}) collective-permute-start(bf16[8,128,128]{2,1,0:T(8,128)(2,1)S(1)} %collective-permute-done.refs_0_), channel_id=1, source_target_pairs={{0,16},{4,12},{8,24},{12,4},{16,0},{20,28},{24,8},{28,20},{1,17},{... | collective-permute-start | bytes 786440 | tf_op jit(solution)/shard_map/ppermute | solution.py:262
  17.4 7.0 %collective-permute-start.8 = (bf16[8,128,128]{2,1,0:T(8,128)(2,1)S(1)}, bf16[8,128,128]{2,1,0:T(8,128)(2,1)S(1)}, u32[]{:S(2)}, u32[]{:S(2)}) collective-permute-start(bf16[8,128,128]{2,1,0:T(8,128)(2,1)S(1)} %collective-permute-done.1.refs_1_), channel_id=1, source_target_pairs={{0,8},{4,20},{8,0},{12,28},{16,24},{20,4},{24,16},{28,12},{1,9},{5... | collective-permute-start | bytes 786440 | tf_op jit(solution)/shard_map/ppermute | solution.py:262
  19.6 4.9 %collective-permute-start.6 = (bf16[1,16,128,128]{3,2,1,0:T(8,128)(2,1)S(1)}, bf16[1,16,128,128]{3,2,1,0:T(8,128)(2,1)S(1)}, u32[]{:S(2)}, u32[]{:S(2)}) collective-permute-start(bf16[1,16,128,128]{3,2,1,0:T(8,128)(2,1)S(1)} %shard_map.118.rest_3_), channel_id=1, source_target_pairs={{0,4},{4,0},{8,12},{12,8},{16,20},{20,16},{24,28},{28,24},{1,5},{5... | collective-permute-start | bytes 1572872 | tf_op jit(solution)/shard_map/ppermute | solution.py:262
  19.8 4.8 %collective-permute-start.5 = (bf16[1,16,128,128]{3,2,1,0:T(8,128)(2,1)S(1)}, bf16[1,16,128,128]{3,2,1,0:T(8,128)(2,1)S(1)}, u32[]{:S(2)}, u32[]{:S(2)}) collective-permute-start(bf16[1,16,128,128]{3,2,1,0:T(8,128)(2,1)S(1)} %shard_map.117.rest_2_), channel_id=1, source_target_pairs={{0,4},{4,0},{8,12},{12,8},{16,20},{20,16},{24,28},{28,24},{1,5},{5... | collective-permute-start | bytes 1572872 | tf_op jit(solution)/shard_map/ppermute | solution.py:262
  24.5 2.0 %collective-permute-start.9 = (bf16[1,16,128,128]{3,2,1,0:T(8,128)(2,1)S(1)}, bf16[1,16,128,128]{3,2,1,0:T(8,128)(2,1)S(1)}, u32[]{:S(2)}, u32[]{:S(2)}) collective-permute-start(bf16[1,16,128,128]{3,2,1,0:T(8,128)(2,1)S(1)} %shard_map.121.state_ref), channel_id=1, source_target_pairs={{0,4},{4,0},{8,12},{12,8},{16,20},{20,16},{24,28},{28,24},{1,5},{5... | collective-permute-start | bytes 1572872 | tf_op jit(solution)/shard_map/ppermute | solution.py:262
  26.4 7.4 %copy-start = (bf16[2048]{0:T(1024)(128)(2,1)S(1)}, bf16[2048]{0:T(1024)(128)(2,1)}, u32[]{:S(2)}) copy-start(bf16[2048]{0:T(1024)(128)(2,1)} %param.14) | copy-start | bytes 12292
  27.6 3.7 %collective-permute-start.10 = (f32[3,128]{1,0:T(4,128)S(1)}, f32[3,128]{1,0:T(4,128)S(1)}, u32[]{:S(2)}, u32[]{:S(2)}) collective-permute-start(f32[3,128]{1,0:T(4,128)S(1)} %get-tuple-element.61), channel_id=1, source_target_pairs={{0,1},{1,0},{2,3},{3,2},{4,5},{5,4},{6,7},{7,6},{8,9},{9,8},{10,11... | collective-permute-start | bytes 4616 | tf_op jit(solution)/shard_map/ppermute | solution.py:404
  31.2 4.5 %collective-permute-start.11 = (f32[3,128]{1,0:T(4,128)S(1)}, f32[3,128]{1,0:T(4,128)S(1)}, u32[]{:S(2)}, u32[]{:S(2)}) collective-permute-start(f32[3,128]{1,0:T(4,128)S(1)} %add.3.one_ref), channel_id=1, source_target_pairs={{0,2},{1,3},{2,0},{3,1},{4,6},{5,7},{6,4},{7,5},{8,10},{9,11},{10,... | collective-permute-start | bytes 4616 | tf_op jit(solution)/shard_map/ppermute | solution.py:404

commit v10 on v9

--- a/solution.py
+++ b/solution.py
@@ -65,10 +65,11 @@
     return jnp.where(block < target, level, 0)
 
 
-def attend(mask, q_ref, k_ref, v_ref, w_ref, o_ref):
+def attend(mask, q_ref, k_ref, v_ref, w_ref, o_ref, wait=lambda head: None):
     head_count = q_ref.shape[1] // HD
     step = 2
     for first in range(0, head_count, step):
+        wait(first)
         units = [
             (head, slice(head * HD, (head + 1) * HD), slice(start, start + ROWS))
             for head in range(first, first + step)
@@ -126,24 +127,39 @@
             scaled_ref[level, :, cols] = query * weight
 
 
-def slab_kernel(*refs):
-    sources, (w_ref, q_ref, k_ref, v_ref), (o_ref, scaled_ref), loaded, sems = (
+def slab_kernel(w_ref, q_ref, k_ref, v_ref, o_ref):
+    attend(causal_mask(), q_ref, k_ref, v_ref, w_ref, o_ref)
+
+
+def user_kernel(suffix, *refs):
+    sources, (sw_ref, sq_ref, uw_ref), (ss_ref, o_ref, us_ref), loaded, sems = (
         refs[:3],
-        refs[3:7],
-        refs[7:9],
+        refs[3:6],
+        refs[6:9],
         refs[9:12],
         refs[12],
     )
-    copies = start_copies(sources, loaded, sems)
-    attend(causal_mask(), q_ref, k_ref, v_ref, w_ref, o_ref)
-    scale_queries(q_ref, w_ref, scaled_ref)
-    for copy in copies:
-        copy.wait()
-
-
-def user_kernel(suffix, w_ref, q_ref, k_ref, v_ref, o_ref, scaled_ref):
-    attend(causal_mask(suffix), q_ref, k_ref, v_ref, w_ref, o_ref)
-    scale_queries(q_ref, w_ref, scaled_ref)
+    chunks = sems.shape[1]
+    size = loaded[0].shape[1] // chunks
+    copies = []
+    for chunk in range(chunks):
+        cols = pl.ds(chunk * size, size)
+        group = [
+            pltpu.make_async_copy(source.at[:, cols], target.at[:, cols], sems.at[i, chunk])
+            for i, (source, target) in enumerate(zip(sources, loaded))
+        ]
+        for copy in group:
+            copy.start()
+        copies.append(group)
+    scale_queries(sq_ref, sw_ref, ss_ref)
+
+    def wait(head):
+        if head * HD % size == 0:
+            for copy in copies[head * HD // size]:
+                copy.wait()
+
+    attend(causal_mask(suffix), *loaded, uw_ref, o_ref, wait)
+    scale_queries(loaded[0], uw_ref, us_ref)
 
 
 def read_kernel(depth, suffix, groups, ahead, length_ref, ss_ref, us_ref, sa_ref, ua_ref, *rest):
@@ -291,7 +307,6 @@
     levels = depth + 1
     slab_table = slab_levels.reshape(-1, token_count)
     user_table = user_levels.reshape(user_count, -1, suffix)
-    user_array = pltpu.VMEM((user_rows, width), jnp.bfloat16)
     second, state, slab_weights, user_weights, slab_keys, slab_values, slab_queries, lengths = pl.pallas_call(
         functools.partial(load_kernel, suffix),
         out_shape=[
@@ -317,30 +332,18 @@
     halves = [first, second]
     for bit, side in ahead:
         sides[1 << bit][side] = swap(halves[side], bit)
-    halves = after(slab_weights, halves)
+    slab_acc = pl.pallas_call(
+        slab_kernel,
+        out_shape=pltpu.VMEM((token_count, width), jnp.float32),
+        in_specs=[vmem] * 4,
+        out_specs=vmem,
+        compiler_params=params,
+        cost_estimate=cost(0, 0),
+    )(slab_weights, slab_queries, slab_keys, slab_values)
+    halves = after(slab_acc, halves)
     for bit, side in places:
         if (bit, side) not in ahead:
             sides[1 << bit][side] = swap(halves[side], bit)
-    slab_acc, slab_scaled, user_queries, user_keys, user_values = pl.pallas_call(
-        slab_kernel,
-        out_shape=[
-            pltpu.VMEM((token_count, width), jnp.float32),
-            pltpu.VMEM((levels, token_count, width), jnp.bfloat16),
-        ]
-        + [user_array] * 3,
-        in_specs=[hbm] * 3 + [vmem] * 4,
-        out_specs=[vmem] * 5,
-        scratch_shapes=[pltpu.SemaphoreType.DMA((3,))],
-        compiler_params=params,
-        cost_estimate=cost(0, 0),
-    )(
-        *pinned(*[array.reshape(user_rows, width) for array in (user_query, user_key, user_value)]),
-        slab_weights,
-        slab_queries,
-        slab_keys,
-        slab_values,
-    )
-
     later = sorted((m for m in range(0, seq_count, 2) if m.bit_count() > 1), key=lambda m: m.bit_count())
     for (bit, side), value in zip(ahead, after(slab_acc, [sides[1 << bit][side] for bit, side in ahead])):
         sides[1 << bit][side] = value
@@ -348,17 +351,24 @@
         high, low = m.bit_length() - 1, (m & -m).bit_length() - 1
         sides[m] = [swap(sides[m ^ (1 << high)][0], high), swap(sides[m ^ (1 << low)][1], low)]
     user_weights = after([sides[1 << bit][side] for bit, side in ahead], [user_weights])[0]
-    user_acc, user_scaled = pl.pallas_call(
+    slab_scaled, user_acc, user_scaled = pl.pallas_call(
         functools.partial(user_kernel, suffix),
         out_shape=[
+            pltpu.VMEM((levels, token_count, width), jnp.bfloat16),
             pltpu.VMEM((user_rows, width), jnp.float32),
             pltpu.VMEM((levels, user_rows, width), jnp.bfloat16),
         ],
-        in_specs=[vmem] * 4,
-        out_specs=[vmem] * 2,
+        in_specs=[hbm] * 3 + [vmem] * 3,
+        out_specs=[vmem] * 3,
+        scratch_shapes=[pltpu.VMEM((user_rows, width), jnp.bfloat16)] * 3 + [pltpu.SemaphoreType.DMA((3, chunks))],
         compiler_params=params,
         cost_estimate=cost(0, 0),
-    )(user_weights, user_queries, user_keys, user_values)
+    )(
+        *pinned(*[array.reshape(user_rows, width) for array in (user_query, user_key, user_value)]),
+        slab_weights,
+        slab_queries,
+        user_weights,
+    )
 
     totals = [pltpu.VMEM((token_count, width), jnp.float32), pltpu.VMEM((user_rows, width), jnp.float32)]
 

time: 37.4 us -> 37.3 us (level)
  waiting for transfers between devices: 8.07 us -> 7.43 us
  Pallas kernels: 15.7 us -> 16.3 us
    pallas_call x1, Pallas kernels: 2.13 us -> 4.27 us  [local(): pl.pallas_call(functools.partial(user_kernel, suffix), out_shape=[pltpu.V...]
    pallas_call x1, Pallas kernels: 2.89 us -> 1.42 us  [local(): pl.pallas_call(slab_kernel, out_shape=pltpu.VMEM((token_count, width), jn...]
    ppermute x10, waiting for transfers between devices: 4.18 us -> 3.52 us  [swap(): lax.ppermute(value, 'seq', [(i, i ^ 1 << (other if i & 1 else bit)) for i...]
  transfers between devices with their start and end apart: 12 -> 12, of which waited for: 5 -> 5; matrix products, arithmetic and copies ran while one was open for 0% -> 0% of each run, Pallas kernels for 32% -> 33%
where the time goes in v10:
time: 37.3 us; the launch traced here: 37.1 us
  Pallas kernels  16.3 us (44%)
  starting transfers between devices  12.7 us (34%)
  waiting for transfers between devices  7.43 us (20%)
  between operations  0.75 us (2%)
    ppermute x10, starting transfers between devices, swap(): lax.ppermute(value, 'seq', [(i, i ^ 1 << (other if i & 1 else bit)) for i...  8.46 us
    pallas_call x2, Pallas kernels, read(): pl.pallas_call(functools.partial(read_kernel, depth, suffix, groups, ahea...  4.8 us
    pallas_call x1, Pallas kernels, local(): pl.pallas_call(functools.partial(user_kernel, suffix), out_shape=[pltpu.V...  4.27 us
    ppermute x2, starting transfers between devices, local(): lax.ppermute(square, 'head', [(i, i ^ 1 << bit) for i in range(head_axis)])  4.22 us
    ppermute x2, waiting for transfers between devices, local(): lax.ppermute(square, 'head', [(i, i ^ 1 << bit) for i in range(head_axis)])  3.9 us
    ppermute x10, waiting for transfers between devices, swap(): lax.ppermute(value, 'seq', [(i, i ^ 1 << (other if i & 1 else bit)) for i...  3.52 us
    pallas_call x1, Pallas kernels, local(): pl.pallas_call(functools.partial(load_kernel, suffix), out_shape=[half_st...  1.77 us
    pallas_call x1, Pallas kernels, local(): pl.pallas_call(functools.partial(norm_kernel, float(width * head_axis), c...  1.48 us
  transfers between devices with their start and end apart: 12, of which 5 were waited for; matrix products, arithmetic and copies ran while one was open for 0% of the time, Pallas kernels for 33%

profile of v10, /device:TPU:0, one launch (start us, length us, event | category | flops | bytes accessed | tf_op | source)
XLA Modules:
  0.0 37.1 jit_solution(11205691866108118639)
XLA Ops:
  0.6 1.3 %shard_map.113.refs_0_ = bf16[8,128,128]{2,1,0:T(8,128)(2,1)S(1)} custom-call(bf16[128,2048]{1,0:T(8,128)(2,1)} %refs_1_.1, bf16[128,2048]{1,0:T(8,128)(2,1)} %refs_2_.1), custom_call_target="tpu_custom_call" | custom-call | tf_op jit(solution)/shard_map/pallas_call | solution.py:294
  2.0 3.0 %collective-permute-start = (bf16[8,128,128]{2,1,0:T(8,128)(2,1)S(1)}, bf16[8,128,128]{2,1,0:T(8,128)(2,1)S(1)}, u32[]{:S(2)}, u32[]{:S(2)}) collective-permute-start(bf16[8,128,128]{2,1,0:T(8,128)(2,1)S(1)} %shard_map.113.refs_0_), channel_id=1, source_target_pairs={{0,8},{4,20},{8,0},{12,28},{16,24},{20,4},{24,16},{28,12},{1,9},{5... | collective-permute-start | bytes 786440 | tf_op jit(solution)/shard_map/ppermute | solution.py:278
  5.0 1.8 %shard_map.114 = (bf16[8,128,128]{2,1,0:T(8,128)(2,1)S(1)}, bf16[1,16,128,128]{3,2,1,0:T(8,128)(2,1)S(1)}, f32[128,64]{1,0:T(8,128)S(1)}, f32[256,64]{1,0:T(8,12...) custom-call(bf16[8,128,128]{2,1,0:T(8,128)(2,1)S(1)} %shard_map.113., ...), custom_call_target="tpu_custom_call" | custom-call | tf_op jit(solution)/shard_map/pallas_call | solution.py:310
  6.7 1.6 %collective-permute-start.1 = (bf16[8,128,128]{2,1,0:T(8,128)(2,1)S(1)}, bf16[8,128,128]{2,1,0:T(8,128)(2,1)S(1)}, u32[]{:S(2)}, u32[]{:S(2)}) collective-permute-start(bf16[8,128,128]{2,1,0:T(8,128)(2,1)S(1)} %get-tuple-element.43), channel_id=1, source_target_pairs={{0,16},{4,12},{8,24},{12,4},{16,0},{20,28},{24,8},{28,20},{1,17},{... | collective-permute-start | bytes 786440 | tf_op jit(solution)/shard_map/ppermute | solution.py:278
  8.3 0.0 collective-permute-start.2
  8.3 1.4 %shard_map.115.sa_ref = f32[128,2048]{1,0:T(8,128)S(1)} custom-call(f32[128,64]{1,0:T(8,128)S(1)} %get-tuple-element.30.w_ref.refs_3_, bf16[128,2048]{1,0:T(8,128)(2,1)S(1)} %get-tuple-element.31.q_ref.refs_4_, bf16[128,2048]{1,0:T(8,128)(2,1)S(1)} %get-tuple-element.32.k_ref, bf16[128,2048]{1,0:T(8,128)(2,1)S(1)} %get-tuple-element.33.v_ref), custom_call_target="tpu_custom_call" | custom-call | tf_op jit(solution)/shard_map/pallas_call | solution.py:335
  9.8 0.6 %collective-permute-start.4 = (bf16[8,128,128]{2,1,0:T(8,128)(2,1)S(1)}, bf16[8,128,128]{2,1,0:T(8,128)(2,1)S(1)}, u32[]{:S(2)}, u32[]{:S(2)}) collective-permute-start(bf16[8,128,128]{2,1,0:T(8,128)(2,1)S(1)} %shard_map.113.refs_0_), channel_id=1, source_target_pairs={{0,16},{4,12},{8,24},{12,4},{16,0},{20,28},{24,8},{28,20},{1,17},{... | collective-permute-start | bytes 786440 | tf_op jit(solution)/shard_map/ppermute | solution.py:278
  10.3 0.1 collective-permute-start.3
  10.4 2.9 %collective-permute-done.1.refs_1_ = bf16[8,128,128]{2,1,0:T(8,128)(2,1)S(1)} collective-permute-done((bf16[8,128,128]{2,1,0:T(8,128)(2,1)S(1)}, bf16[8,128,128]{2,1,0:T(8,128)(2,1)S(1)}, u32[]{:S(2)}, u32[]{:S(2)}) %collective-permute-start.1) | collective-permute-done | bytes 262176 | tf_op jit(solution)/shard_map/ppermute | solution.py:278
  13.3 0.0 collective-permute-done.refs_0_
  13.4 2.5 %collective-permute-start.7 = (bf16[8,128,128]{2,1,0:T(8,128)(2,1)S(1)}, bf16[8,128,128]{2,1,0:T(8,128)(2,1)S(1)}, u32[]{:S(2)}, u32[]{:S(2)}) collective-permute-start(bf16[8,128,128]{2,1,0:T(8,128)(2,1)S(1)} %collective-permute-done.refs_0_), channel_id=1, source_target_pairs={{0,16},{4,12},{8,24},{12,4},{16,0},{20,28},{24,8},{28,20},{1,17},{... | collective-permute-start | bytes 786440 | tf_op jit(solution)/shard_map/ppermute | solution.py:278
  15.8 0.0 collective-permute-start.8
  15.8 4.3 %shard_map.116 = (bf16[4,128,2048]{2,1,0:T(8,128)(2,1)S(1)}, f32[256,2048]{1,0:T(8,128)S(1)}, bf16[4,256,2048]{2,1,0:T(8,128)(2,1)S(1)}) custom-call(bf16[256,2048]{1,0:T(8,128)(2,1)} %bitcast.6, bf16[256,2048]{1,0:T(8,128)(2,1)} %bitcast.7, bf16[256,2048]{1,0:T(8,128)(2,1)} %bitcast.8, f32[128,64]{1,0:T(8,128)S(1)} %get-tuple-element.30.w_ref.refs_3_, ...), custom_call_target="tpu_custom_call" | custom-call | tf_op jit(solution)/shard_map/pallas_call | solution.py:354
  20.1 0.0 collective-permute-done.4.refs_0_
  20.2 0.1 collective-permute-start.6
  20.3 0.0 collective-permute-done.3.refs_1_
  20.3 0.6 %collective-permute-start.5 = (bf16[1,16,128,128]{3,2,1,0:T(8,128)(2,1)S(1)}, bf16[1,16,128,128]{3,2,1,0:T(8,128)(2,1)S(1)}, u32[]{:S(2)}, u32[]{:S(2)}) collective-permute-start(bf16[1,16,128,128]{3,2,1,0:T(8,128)(2,1)S(1)} %shard_map.117.rest_2_), channel_id=1, source_target_pairs={{0,4},{4,0},{8,12},{12,8},{16,20},{20,16},{24,28},{28,24},{1,5},{5... | collective-permute-start | bytes 1572872 | tf_op jit(solution)/shard_map/ppermute | solution.py:278
  20.9 0.0 collective-permute-done.2.rest_1_
  20.9 3.2 %shard_map.119 = (f32[128,2048]{1,0:T(8,128)S(1)}, f32[256,2048]{1,0:T(8,128)S(1)}, bf16[128,4096]{1,0:T(8,128)(2,1)S(1)}, bf16[256,4096]{1,0:T(8,128)(2,1)S(1)}) custom-call(s32[4]{0:T(128)S(1)} %get-tuple-element.29.length_ref, bf16[4,128,2048]{2,1,0:T(8,128)(2,1)S(1)} %get-tuple-element.39.ss_ref, bf16[4,256,2048]{2,1,0:T(8,128)(2,1)S(1)} %get-tuple-element.40.us_ref, ...), custom_call_target="tpu_custom_call" | custom-call | tf_op jit(solution)/shard_map/pallas_call | solution.py:379
  24.1 0.4 collective-permute-done.7.refs_0_
  24.4 0.0 collective-permute-done.8.refs_1_
  24.5 0.1 collective-permute-start.9
  24.6 0.0 collective-permute-done.6.rest_1_
  24.6 0.0 collective-permute-done.5.rest_0_
  24.6 1.6 %shard_map.120 = (f32[128,2048]{1,0:T(8,128)S(1)}, f32[256,2048]{1,0:T(8,128)S(1)}) custom-call(s32[4]{0:T(128)S(1)} %get-tuple-element.29.length_ref, bf16[4,128,2048]{2,1,0:T(8,128)(2,1)S(1)} %get-tuple-element.39.ss_ref, bf16[4,256,2048]{2,1,0:T(8,128)(2,1)S(1)} %get-tuple-element.40.us_ref, f32[128,2048]{1,0:T(8,128)S(1)} %get-tuple-element.47.sa_ref.order_ref, ...), custom_call_target="tpu_custom_call" | custom-call | tf_op jit(solution)/shard_map/pallas_call | solution.py:379
  26.2 0.2 collective-permute-done.9.mate_ref
  26.5 0.0 copy-start
  26.5 1.1 %shard_map.122 = (f32[128,2048]{1,0:T(8,128)S(1)}, f32[256,2048]{1,0:T(8,128)S(1)}, f32[3,128]{1,0:T(4,128)S(1)}) custom-call(bf16[128,4096]{1,0:T(8,128)(2,1)S(1)} %get-tuple-element.45.ss_ref, bf16[256,4096]{1,0:T(8,128)(2,1)S(1)} %get-tuple-element.46.us_ref, f32[128,2048]{1,0:T(8,128)S(1)} %get-tuple-element.49.sa_ref, ...), custom_call_target="tpu_custom_call" | custom-call | tf_op jit(solution)/shard_map/pallas_call | solution.py:402
  27.5 1.6 %collective-permute-start.10 = (f32[3,128]{1,0:T(4,128)S(1)}, f32[3,128]{1,0:T(4,128)S(1)}, u32[]{:S(2)}, u32[]{:S(2)}) collective-permute-start(f32[3,128]{1,0:T(4,128)S(1)} %get-tuple-element.53), channel_id=1, source_target_pairs={{0,1},{1,0},{2,3},{3,2},{4,5},{5,4},{6,7},{7,6},{8,9},{9,8},{10,11... | collective-permute-start | bytes 4616 | tf_op jit(solution)/shard_map/ppermute | solution.py:414
  29.2 2.0 %collective-permute-done.10 = f32[3,128]{1,0:T(4,128)S(1)} collective-permute-done((f32[3,128]{1,0:T(4,128)S(1)}, f32[3,128]{1,0:T(4,128)S(1)}, u32[]{:S(2)}, u32[]{:S(2)}) %collective-permute-start.10) | collective-permute-done | bytes 1568 | tf_op jit(solution)/shard_map/ppermute | solution.py:414
  31.2 2.6 %collective-permute-start.11 = (f32[3,128]{1,0:T(4,128)S(1)}, f32[3,128]{1,0:T(4,128)S(1)}, u32[]{:S(2)}, u32[]{:S(2)}) collective-permute-start(f32[3,128]{1,0:T(4,128)S(1)} %add.3.one_ref), channel_id=1, source_target_pairs={{0,2},{1,3},{2,0},{3,1},{4,6},{5,7},{6,4},{7,5},{8,10},{9,11},{10,... | collective-permute-start | bytes 4616 | tf_op jit(solution)/shard_map/ppermute | solution.py:414
  33.8 0.0 copy-done
  33.8 1.9 %collective-permute-done.11.two_ref = f32[3,128]{1,0:T(4,128)S(1)} collective-permute-done((f32[3,128]{1,0:T(4,128)S(1)}, f32[3,128]{1,0:T(4,128)S(1)}, u32[]{:S(2)}, u32[]{:S(2)}) %collective-permute-start.11) | collective-permute-done | bytes 1568 | tf_op jit(solution)/shard_map/ppermute | solution.py:414
  35.7 1.5 %shard_map.123 = (bf16[128,2048]{1,0:T(8,128)(2,1)}, bf16[256,2048]{1,0:T(8,128)(2,1)}) custom-call(f32[128,2048]{1,0:T(8,128)S(1)} %get-tuple-element.51.st_ref, f32[256,2048]{1,0:T(8,128)S(1)} %get-tuple-element.52.ut_ref, bf16[1,2048]{1,0:T(2,128)(2,1)S(1)} %reshape.30.gain_ref, f32[3,128]{1,0:T(4,128)S(1)} %add.3.one_ref, ...), custom_call_target="tpu_custom_call" | custom-call | tf_op jit(solution)/shard_map/pallas_call | solution.py:416
  (5 shorter events, 0.2 us)
Async XLA Ops:
  2.0 11.4 %collective-permute-start = (bf16[8,128,128]{2,1,0:T(8,128)(2,1)S(1)}, bf16[8,128,128]{2,1,0:T(8,128)(2,1)S(1)}, u32[]{:S(2)}, u32[]{:S(2)}) collective-permute-start(bf16[8,128,128]{2,1,0:T(8,128)(2,1)S(1)} %shard_map.113.refs_0_), channel_id=1, source_target_pairs={{0,8},{4,20},{8,0},{12,28},{16,24},{20,4},{24,16},{28,12},{1,9},{5... | collective-permute-start | bytes 786440 | tf_op jit(solution)/shard_map/ppermute | solution.py:278
  6.7 6.6 %collective-permute-start.1 = (bf16[8,128,128]{2,1,0:T(8,128)(2,1)S(1)}, bf16[8,128,128]{2,1,0:T(8,128)(2,1)S(1)}, u32[]{:S(2)}, u32[]{:S(2)}) collective-permute-start(bf16[8,128,128]{2,1,0:T(8,128)(2,1)S(1)} %get-tuple-element.43), channel_id=1, source_target_pairs={{0,16},{4,12},{8,24},{12,4},{16,0},{20,28},{24,8},{28,20},{1,17},{... | collective-permute-start | bytes 786440 | tf_op jit(solution)/shard_map/ppermute | solution.py:278
  8.3 12.6 %collective-permute-start.2 = (bf16[1,16,128,128]{3,2,1,0:T(8,128)(2,1)S(1)}, bf16[1,16,128,128]{3,2,1,0:T(8,128)(2,1)S(1)}, u32[]{:S(2)}, u32[]{:S(2)}) collective-permute-start(bf16[1,16,128,128]{3,2,1,0:T(8,128)(2,1)S(1)} %get-tuple-element.42.rest_0_), channel_id=1, source_target_pairs={{0,4},{4,0},{8,12},{12,8},{16,20},{20,16},{24,28},{28,24},{1,5},{5... | collective-permute-start | bytes 1572872 | tf_op jit(solution)/shard_map/ppermute | solution.py:278
  9.8 10.4 %collective-permute-start.4 = (bf16[8,128,128]{2,1,0:T(8,128)(2,1)S(1)}, bf16[8,128,128]{2,1,0:T(8,128)(2,1)S(1)}, u32[]{:S(2)}, u32[]{:S(2)}) collective-permute-start(bf16[8,128,128]{2,1,0:T(8,128)(2,1)S(1)} %shard_map.113.refs_0_), channel_id=1, source_target_pairs={{0,16},{4,12},{8,24},{12,4},{16,0},{20,28},{24,8},{28,20},{1,17},{... | collective-permute-start | bytes 786440 | tf_op jit(solution)/shard_map/ppermute | solution.py:278
  10.3 9.9 %collective-permute-start.3 = (bf16[8,128,128]{2,1,0:T(8,128)(2,1)S(1)}, bf16[8,128,128]{2,1,0:T(8,128)(2,1)S(1)}, u32[]{:S(2)}, u32[]{:S(2)}) collective-permute-start(bf16[8,128,128]{2,1,0:T(8,128)(2,1)S(1)} %get-tuple-element.43), channel_id=1, source_target_pairs={{0,8},{4,20},{8,0},{12,28},{16,24},{20,4},{24,16},{28,12},{1,9},{5... | collective-permute-start | bytes 786440 | tf_op jit(solution)/shard_map/ppermute | solution.py:278
  13.4 11.1 %collective-permute-start.7 = (bf16[8,128,128]{2,1,0:T(8,128)(2,1)S(1)}, bf16[8,128,128]{2,1,0:T(8,128)(2,1)S(1)}, u32[]{:S(2)}, u32[]{:S(2)}) collective-permute-start(bf16[8,128,128]{2,1,0:T(8,128)(2,1)S(1)} %collective-permute-done.refs_0_), channel_id=1, source_target_pairs={{0,16},{4,12},{8,24},{12,4},{16,0},{20,28},{24,8},{28,20},{1,17},{... | collective-permute-start | bytes 786440 | tf_op jit(solution)/shard_map/ppermute | solution.py:278
  15.8 8.6 %collective-permute-start.8 = (bf16[8,128,128]{2,1,0:T(8,128)(2,1)S(1)}, bf16[8,128,128]{2,1,0:T(8,128)(2,1)S(1)}, u32[]{:S(2)}, u32[]{:S(2)}) collective-permute-start(bf16[8,128,128]{2,1,0:T(8,128)(2,1)S(1)} %collective-permute-done.1.refs_1_), channel_id=1, source_target_pairs={{0,8},{4,20},{8,0},{12,28},{16,24},{20,4},{24,16},{28,12},{1,9},{5... | collective-permute-start | bytes 786440 | tf_op jit(solution)/shard_map/ppermute | solution.py:278
  20.2 4.4 %collective-permute-start.6 = (bf16[1,16,128,128]{3,2,1,0:T(8,128)(2,1)S(1)}, bf16[1,16,128,128]{3,2,1,0:T(8,128)(2,1)S(1)}, u32[]{:S(2)}, u32[]{:S(2)}) collective-permute-start(bf16[1,16,128,128]{3,2,1,0:T(8,128)(2,1)S(1)} %shard_map.118.rest_3_), channel_id=1, source_target_pairs={{0,4},{4,0},{8,12},{12,8},{16,20},{20,16},{24,28},{28,24},{1,5},{5... | collective-permute-start | bytes 1572872 | tf_op jit(solution)/shard_map/ppermute | solution.py:278
  20.3 4.2 %collective-permute-start.5 = (bf16[1,16,128,128]{3,2,1,0:T(8,128)(2,1)S(1)}, bf16[1,16,128,128]{3,2,1,0:T(8,128)(2,1)S(1)}, u32[]{:S(2)}, u32[]{:S(2)}) collective-permute-start(bf16[1,16,128,128]{3,2,1,0:T(8,128)(2,1)S(1)} %shard_map.117.rest_2_), channel_id=1, source_target_pairs={{0,4},{4,0},{8,12},{12,8},{16,20},{20,16},{24,28},{28,24},{1,5},{5... | collective-permute-start | bytes 1572872 | tf_op jit(solution)/shard_map/ppermute | solution.py:278
  24.5 2.0 %collective-permute-start.9 = (bf16[1,16,128,128]{3,2,1,0:T(8,128)(2,1)S(1)}, bf16[1,16,128,128]{3,2,1,0:T(8,128)(2,1)S(1)}, u32[]{:S(2)}, u32[]{:S(2)}) collective-permute-start(bf16[1,16,128,128]{3,2,1,0:T(8,128)(2,1)S(1)} %shard_map.121.state_ref), channel_id=1, source_target_pairs={{0,4},{4,0},{8,12},{12,8},{16,20},{20,16},{24,28},{28,24},{1,5},{5... | collective-permute-start | bytes 1572872 | tf_op jit(solution)/shard_map/ppermute | solution.py:278
  26.5 7.3 %copy-start = (bf16[2048]{0:T(1024)(128)(2,1)S(1)}, bf16[2048]{0:T(1024)(128)(2,1)}, u32[]{:S(2)}) copy-start(bf16[2048]{0:T(1024)(128)(2,1)} %param.14) | copy-start | bytes 12292
  27.5 3.7 %collective-permute-start.10 = (f32[3,128]{1,0:T(4,128)S(1)}, f32[3,128]{1,0:T(4,128)S(1)}, u32[]{:S(2)}, u32[]{:S(2)}) collective-permute-start(f32[3,128]{1,0:T(4,128)S(1)} %get-tuple-element.53), channel_id=1, source_target_pairs={{0,1},{1,0},{2,3},{3,2},{4,5},{5,4},{6,7},{7,6},{8,9},{9,8},{10,11... | collective-permute-start | bytes 4616 | tf_op jit(solution)/shard_map/ppermute | solution.py:414
  31.2 4.5 %collective-permute-start.11 = (f32[3,128]{1,0:T(4,128)S(1)}, f32[3,128]{1,0:T(4,128)S(1)}, u32[]{:S(2)}, u32[]{:S(2)}) collective-permute-start(f32[3,128]{1,0:T(4,128)S(1)} %add.3.one_ref), channel_id=1, source_target_pairs={{0,2},{1,3},{2,0},{3,1},{4,6},{5,7},{6,4},{7,5},{8,10},{9,11},{10,... | collective-permute-start | bytes 4616 | tf_op jit(solution)/shard_map/ppermute | solution.py:414

commit v11 on v8

--- a/solution.py
+++ b/solution.py
@@ -105,7 +105,8 @@
 
 
 def load_kernel(suffix, *refs):
-    sources, (sw_ref, uw_ref), loaded, tables, sems = refs[:4], refs[4:6], refs[6:8], refs[8:10], refs[10]
+    sources, (k_ref, v_ref), (sw_ref, uw_ref), rest = refs[:4], refs[4:6], refs[6:8], refs[8:]
+    loaded, o_ref, tables, sems = rest[:2], rest[2], rest[3:5], rest[5]
     copies = start_copies(sources, (*tables, *loaded), sems)
     slab_table, user_table = tables
     for copy in copies[:2]:
@@ -119,6 +120,7 @@
         uw_ref[user * suffix : (user + 1) * suffix] = matmul(user_table[user], same, ((0,), (0,)))
     for copy in copies[2:]:
         copy.wait()
+    attend(causal_mask(), loaded[0], k_ref, v_ref, sw_ref, o_ref)
 
 
 def scale_queries(q_ref, w_ref, scaled_ref):
@@ -133,16 +135,9 @@
             scaled_ref[level, :, cols] = query * weight
 
 
-def slab_kernel(*refs):
-    sources, (w_ref, q_ref, k_ref, v_ref), (o_ref, scaled_ref), loaded, sems = (
-        refs[:3],
-        refs[3:7],
-        refs[7:9],
-        refs[9:12],
-        refs[12],
-    )
+def scale_kernel(*refs):
+    sources, (w_ref, q_ref), scaled_ref, loaded, sems = refs[:3], refs[3:5], refs[5], refs[6:9], refs[9]
     copies = start_copies(sources, loaded, sems)
-    attend(causal_mask(), q_ref, k_ref, v_ref, w_ref, o_ref)
     scale_queries(q_ref, w_ref, scaled_ref)
     for copy in copies:
         copy.wait()
@@ -190,6 +185,7 @@
 
 def last_kernel(ss_ref, us_ref, sa_ref, ua_ref, state_ref, mate_ref, st_ref, ut_ref, square_ref):
     head_count = sa_ref.shape[1] // HD
+    square_ref[...] = jnp.zeros_like(square_ref)
     line = 0
     for q_ref, a_ref, t_ref in ((ss_ref, sa_ref, st_ref), (us_ref, ua_ref, ut_ref)):
         for start in range(0, a_ref.shape[0], ROWS):
@@ -264,15 +260,9 @@
     def cost(flops, moved):
         return pl.CostEstimate(flops=flops, bytes_accessed=moved, transcendentals=0)
 
-    held = {0: list(range(seq_count))}
-
-    def swap(value, bit, offset):
+    def swap(value, bit):
         other = depth - bit if bit else 0
-        pairs = [(i, i ^ (1 << (other if i & 1 else bit))) for i in range(seq_count)]
-        pairs = [(i, j) for i, j in pairs if held[offset][i] not in (None, seq_count - 1)]
-        came = {j: held[offset][i] for i, j in pairs}
-        held[offset | (1 << bit)] = [came.get(i) for i in range(seq_count)]
-        return lax.ppermute(value, "seq", pairs)
+        return lax.ppermute(value, "seq", [(i, i ^ (1 << (other if i & 1 else bit))) for i in range(seq_count)])
 
     def after(results, values):
         return list(lax.optimization_barrier((results, values))[1])
@@ -303,21 +293,22 @@
     ahead = [(bit, 0) for bit in outer[:-1]] + [(bit, 1) for bit in outer[1:]] or places
     sides = {1 << bit: [None, None] for bit in outer}
     for bit, side in ahead:
-        sides[1 << bit][side] = swap(halves[side], bit, 0)
+        sides[1 << bit][side] = swap(halves[side], bit)
     levels = depth + 1
     slab_table = slab_levels.reshape(-1, token_count)
     user_table = user_levels.reshape(user_count, -1, suffix)
     user_array = pltpu.VMEM((user_rows, width), jnp.bfloat16)
-    slab_weights, user_weights, slab_queries, lengths = pl.pallas_call(
+    slab_weights, user_weights, slab_queries, lengths, slab_acc = pl.pallas_call(
         functools.partial(load_kernel, suffix),
         out_shape=[
             pltpu.VMEM((token_count, levels * head_count), jnp.float32),
             pltpu.VMEM((user_rows, levels * head_count), jnp.float32),
             slab_rows,
             pltpu.VMEM((user_count,), jnp.int32),
+            pltpu.VMEM((token_count, width), jnp.float32),
         ],
-        in_specs=[hbm] * 4,
-        out_specs=[vmem] * 4,
+        in_specs=[hbm] * 4 + [vmem] * 2,
+        out_specs=[vmem] * 5,
         scratch_shapes=[
             pltpu.VMEM(slab_table.shape, jnp.bfloat16),
             pltpu.VMEM(user_table.shape, jnp.bfloat16),
@@ -325,20 +316,16 @@
         ],
         compiler_params=params,
         cost_estimate=cost(0, 0),
-    )(*pinned(slab_table, user_table, slab_query, prefix_lengths))
+    )(*pinned(slab_table, user_table, slab_query, prefix_lengths), slab_keys, slab_values)
     halves = after(slab_weights, halves)
     for bit, side in places:
         if (bit, side) not in ahead:
-            sides[1 << bit][side] = swap(halves[side], bit, 0)
-    slab_acc, slab_scaled, user_queries, user_keys, user_values = pl.pallas_call(
-        slab_kernel,
-        out_shape=[
-            pltpu.VMEM((token_count, width), jnp.float32),
-            pltpu.VMEM((levels, token_count, width), jnp.bfloat16),
-        ]
-        + [user_array] * 3,
-        in_specs=[hbm] * 3 + [vmem] * 4,
-        out_specs=[vmem] * 5,
+            sides[1 << bit][side] = swap(halves[side], bit)
+    slab_scaled, user_queries, user_keys, user_values = pl.pallas_call(
+        scale_kernel,
+        out_shape=[pltpu.VMEM((levels, token_count, width), jnp.bfloat16)] + [user_array] * 3,
+        in_specs=[hbm] * 3 + [vmem] * 2,
+        out_specs=[vmem] * 4,
         scratch_shapes=[pltpu.SemaphoreType.DMA((3,))],
         compiler_params=params,
         cost_estimate=cost(0, 0),
@@ -346,19 +333,14 @@
         *pinned(*[array.reshape(user_rows, width) for array in (user_query, user_key, user_value)]),
         slab_weights,
         slab_queries,
-        slab_keys,
-        slab_values,
     )
 
     later = sorted((m for m in range(0, seq_count, 2) if m.bit_count() > 1), key=lambda m: m.bit_count())
-    for (bit, side), value in zip(ahead, after(slab_acc, [sides[1 << bit][side] for bit, side in ahead])):
+    for (bit, side), value in zip(ahead, after(slab_scaled, [sides[1 << bit][side] for bit, side in ahead])):
         sides[1 << bit][side] = value
     for m in later:
         high, low = m.bit_length() - 1, (m & -m).bit_length() - 1
-        sides[m] = [
-            swap(sides[m ^ (1 << high)][0], high, m ^ (1 << high)),
-            swap(sides[m ^ (1 << low)][1], low, m ^ (1 << low)),
-        ]
+        sides[m] = [swap(sides[m ^ (1 << high)][0], high), swap(sides[m ^ (1 << low)][1], low)]
     user_weights = after([sides[1 << bit][side] for bit, side in ahead], [user_weights])[0]
     user_acc, user_scaled = pl.pallas_call(
         functools.partial(user_kernel, suffix),
@@ -389,22 +371,22 @@
         )(lengths, slab_scaled, user_scaled, *accs, *[whole[m] for m in offsets])
 
     state = after(slab_weights, [state])[0]
-    whole = {0: state, 1: swap(state, 0, 0)}
+    whole = {0: state, 1: swap(state, 0)}
     direct = [1 << bit for bit in outer]
     for m in direct:
         whole[m] = join(user_acc, sides[m])
-        whole[m | 1] = swap(whole[m], 0, m)
+        whole[m | 1] = swap(whole[m], 0)
     last = later[-1]
     *accs, slab_ahead, user_ahead = read([0, 1] + direct, (slab_acc, user_acc), (last, last | 1))
     for m in later:
         whole[m] = join(accs[0], sides[m])
-        whole[m | 1] = swap(whole[m], 0, m)
+        whole[m | 1] = swap(whole[m], 0)
     if later[:-1]:
         accs = read([n for m in later[:-1] for n in (m, m | 1)], accs)
     accs = read([m | 1 for m in direct], accs)
     slab_total, user_total, square = pl.pallas_call(
         last_kernel,
-        out_shape=totals + [pltpu.VMEM((lines, ROWS), jnp.float32)],
+        out_shape=totals + [pltpu.VMEM((-(-lines // 8) * 8, ROWS), jnp.float32)],
         in_specs=[vmem] * 6,
         out_specs=[vmem] * 3,
         compiler_params=params,

time: 53.4 us -> 37.3 us (0.70)
  starting transfers between devices: 32.4 us -> 14 us
  waiting for transfers between devices: 3.92 us -> 6.23 us
    ppermute x10, starting transfers between devices: 28.2 us -> 9.49 us  [swap(): lax.ppermute(value, 'seq', [(i, i ^ 1 << (other if i & 1 else bit)) for i...]
    ppermute x10, waiting for transfers between devices: 0.03 us -> 2.57 us  [swap(): lax.ppermute(value, 'seq', [(i, i ^ 1 << (other if i & 1 else bit)) for i...]
    pallas_call x1, Pallas kernels: 1.17 us -> 2.6 us  [local(): pl.pallas_call(functools.partial(load_kernel, suffix), out_shape=[pltpu.V...]
    pallas_call x2, Pallas kernels: 4.04 us -> 2.96 us  [the longest x1 1.88 us: local(): pl.pallas_call(scale_kernel, out_shape=[pltpu.VMEM((levels, token_count,...]
  transfers between devices with their start and end apart: 12 -> 12, of which waited for: 2 -> 6; matrix products, arithmetic and copies ran while one was open for 0% -> 0% of each run, Pallas kernels for 21% -> 31%
where the time goes in v11:
time: 37.3 us; the launch traced here: 37.2 us
  Pallas kernels  16.1 us (43%)
  starting transfers between devices  14 us (38%)
  waiting for transfers between devices  6.23 us (17%)
  between operations  0.76 us (2%)
    ppermute x10, starting transfers between devices, swap(): lax.ppermute(value, 'seq', [(i, i ^ 1 << (other if i & 1 else bit)) for i...  9.49 us
    pallas_call x2, Pallas kernels, read(): pl.pallas_call(functools.partial(read_kernel, depth, suffix, groups, ahea...  4.8 us
    ppermute x2, starting transfers between devices, local(): lax.ppermute(square, 'head', [(i, i ^ 1 << bit) for i in range(head_axis)])  4.51 us
    ppermute x2, waiting for transfers between devices, local(): lax.ppermute(square, 'head', [(i, i ^ 1 << bit) for i in range(head_axis)])  3.66 us
    pallas_call x1, Pallas kernels, local(): pl.pallas_call(functools.partial(load_kernel, suffix), out_shape=[pltpu.V...  2.6 us
    ppermute x10, waiting for transfers between devices, swap(): lax.ppermute(value, 'seq', [(i, i ^ 1 << (other if i & 1 else bit)) for i...  2.57 us
    pallas_call x1, Pallas kernels, local(): pl.pallas_call(functools.partial(user_kernel, suffix), out_shape=[pltpu.V...  2.22 us
    pallas_call x1, Pallas kernels, local(): pl.pallas_call(functools.partial(state_kernel, chunks), out_shape=[half_s...  1.95 us
  transfers between devices with their start and end apart: 12, of which 6 were waited for; matrix products, arithmetic and copies ran while one was open for 0% of the time, Pallas kernels for 31%

profile of v11, /device:TPU:0, one launch (start us, length us, event | category | flops | bytes accessed | tf_op | source)
XLA Modules:
  0.0 37.2 jit_solution(1813826047460426327)
XLA Ops:
  0.6 2.0 %shard_map.113 = (bf16[8,128,128]{2,1,0:T(8,128)(2,1)S(1)}, bf16[8,128,128]{2,1,0:T(8,128)(2,1)S(1)}, bf16[1,16,128,128]{3,2,1,0:T(8,128)(2,1)S(1)}, bf16[128,2048]{1,0:T(8,128)(2,1)S(1)}, bf16[128,2048]{1,0:T(8,128)(2,1)S(1)}) custom-call(bf16[128,2048]{1,0:T(8,128)(2,1)} %key_hbm.1, bf16[128,2048]{1,0:T(8,128)(2,1)} %value_hbm.1), custom_call_target="tpu_custom_call" | custom-call | tf_op jit(solution)/shard_map/pallas_call | solution.py:281
  2.6 3.0 %collective-permute-start = (bf16[8,128,128]{2,1,0:T(8,128)(2,1)S(1)}, bf16[8,128,128]{2,1,0:T(8,128)(2,1)S(1)}, u32[]{:S(2)}, u32[]{:S(2)}) collective-permute-start(bf16[8,128,128]{2,1,0:T(8,128)(2,1)S(1)} %get-tuple-element.56), channel_id=1, source_target_pairs={{0,8},{4,20},{8,0},{12,28},{16,24},{20,4},{24,16},{28,12},{1,9},{5... | collective-permute-start | bytes 786440 | tf_op jit(solution)/shard_map/ppermute | solution.py:265
  5.6 1.5 %collective-permute-start.1 = (bf16[8,128,128]{2,1,0:T(8,128)(2,1)S(1)}, bf16[8,128,128]{2,1,0:T(8,128)(2,1)S(1)}, u32[]{:S(2)}, u32[]{:S(2)}) collective-permute-start(bf16[8,128,128]{2,1,0:T(8,128)(2,1)S(1)} %get-tuple-element.55), channel_id=1, source_target_pairs={{0,16},{4,12},{8,24},{12,4},{16,0},{20,28},{24,8},{28,20},{1,17},{... | collective-permute-start | bytes 786440 | tf_op jit(solution)/shard_map/ppermute | solution.py:265
  7.1 2.6 %shard_map.114 = (f32[128,64]{1,0:T(8,128)S(1)}, f32[256,64]{1,0:T(8,128)S(1)}, bf16[128,2048]{1,0:T(8,128)(2,1)S(1)}, s32[4]{0:T(128)S(1)}, f32[128,2048]{1,0:T(8,128)S(1)}) custom-call(bf16[96,128]{1,0:T(8,128)(2,1)} %bitcast.10, bf16[4,96,64]{2,1,0:T(8,128)(2,1)} %bitcast.9, bf16[128,2048]{1,0:T(8,128)(2,1)} %refs_2_.1, s32[4]{0:T(128)} %refs_3_.1, ...), custom_call_target="tpu_custom_call" | custom-call | tf_op jit(solution)/shard_map/pallas_call | solution.py:301
  9.7 0.1 collective-permute-start.2
  9.8 0.6 %collective-permute-start.4 = (bf16[8,128,128]{2,1,0:T(8,128)(2,1)S(1)}, bf16[8,128,128]{2,1,0:T(8,128)(2,1)S(1)}, u32[]{:S(2)}, u32[]{:S(2)}) collective-permute-start(bf16[8,128,128]{2,1,0:T(8,128)(2,1)S(1)} %get-tuple-element.56), channel_id=1, source_target_pairs={{0,16},{4,12},{8,24},{12,4},{16,0},{20,28},{24,8},{28,20},{1,17},{... | collective-permute-start | bytes 786440 | tf_op jit(solution)/shard_map/ppermute | solution.py:265
  10.4 0.1 collective-permute-start.3
  10.5 1.9 %shard_map.115 = (bf16[4,128,2048]{2,1,0:T(8,128)(2,1)S(1)}, bf16[256,2048]{1,0:T(8,128)(2,1)S(1)}, bf16[256,2048]{1,0:T(8,128)(2,1)S(1)}, bf16[256,2048]{1,0:T(8,128)(2,1)S(1)}) custom-call(bf16[256,2048]{1,0:T(8,128)(2,1)} %bitcast.6, bf16[256,2048]{1,0:T(8,128)(2,1)} %bitcast.7, bf16[256,2048]{1,0:T(8,128)(2,1)} %bitcast.8, ...), custom_call_target="tpu_custom_call" | custom-call | tf_op jit(solution)/shard_map/pallas_call | solution.py:324
  12.4 0.0 collective-permute-done.refs_0_
  12.4 0.0 collective-permute-done.1.refs_1_
  12.4 2.0 %collective-permute-start.7 = (bf16[8,128,128]{2,1,0:T(8,128)(2,1)S(1)}, bf16[8,128,128]{2,1,0:T(8,128)(2,1)S(1)}, u32[]{:S(2)}, u32[]{:S(2)}) collective-permute-start(bf16[8,128,128]{2,1,0:T(8,128)(2,1)S(1)} %collective-permute-done.refs_0_), channel_id=1, source_target_pairs={{0,16},{4,12},{8,24},{12,4},{16,0},{20,28},{24,8},{28,20},{1,17},{... | collective-permute-start | bytes 786440 | tf_op jit(solution)/shard_map/ppermute | solution.py:265
  14.4 1.9 %collective-permute-start.8 = (bf16[8,128,128]{2,1,0:T(8,128)(2,1)S(1)}, bf16[8,128,128]{2,1,0:T(8,128)(2,1)S(1)}, u32[]{:S(2)}, u32[]{:S(2)}) collective-permute-start(bf16[8,128,128]{2,1,0:T(8,128)(2,1)S(1)} %collective-permute-done.1.refs_1_), channel_id=1, source_target_pairs={{0,8},{4,20},{8,0},{12,28},{16,24},{20,4},{24,16},{28,12},{1,9},{5... | collective-permute-start | bytes 786440 | tf_op jit(solution)/shard_map/ppermute | solution.py:265
  16.3 2.2 %shard_map.116 = (f32[256,2048]{1,0:T(8,128)S(1)}, bf16[4,256,2048]{2,1,0:T(8,128)(2,1)S(1)}) custom-call(f32[256,64]{1,0:T(8,128)S(1)} %get-tuple-element.46.w_ref, bf16[256,2048]{1,0:T(8,128)(2,1)S(1)} %get-tuple-element.47.q_ref, bf16[256,2048]{1,0:T(8,128)(2,1)S(1)} %get-tuple-element.48.k_ref, bf16[256,2048]{1,0:T(8,128)(2,1)S(1)} %get-tuple-element.49.v_ref), custom_call_target="tpu_custom_call" | custom-call | tf_op jit(solution)/shard_map/pallas_call | solution.py:345
  18.5 0.5 %collective-permute-done.4.refs_0_ = bf16[8,128,128]{2,1,0:T(8,128)(2,1)S(1)} collective-permute-done((bf16[8,128,128]{2,1,0:T(8,128)(2,1)S(1)}, bf16[8,128,128]{2,1,0:T(8,128)(2,1)S(1)}, u32[]{:S(2)}, u32[]{:S(2)}) %collective-permute-start.4) | collective-permute-done | bytes 262176 | tf_op jit(solution)/shard_map/ppermute | solution.py:265
  19.1 0.1 collective-permute-start.6
  19.2 0.4 %collective-permute-done.3.refs_1_ = bf16[8,128,128]{2,1,0:T(8,128)(2,1)S(1)} collective-permute-done((bf16[8,128,128]{2,1,0:T(8,128)(2,1)S(1)}, bf16[8,128,128]{2,1,0:T(8,128)(2,1)S(1)}, u32[]{:S(2)}, u32[]{:S(2)}) %collective-permute-start.3) | collective-permute-done | bytes 262176 | tf_op jit(solution)/shard_map/ppermute | solution.py:265
  19.6 0.2 collective-permute-start.5
  19.8 0.0 collective-permute-done.2.rest_1_
  19.8 3.2 %shard_map.119 = (f32[128,2048]{1,0:T(8,128)S(1)}, f32[256,2048]{1,0:T(8,128)S(1)}, bf16[128,4096]{1,0:T(8,128)(2,1)S(1)}, bf16[256,4096]{1,0:T(8,128)(2,1)S(1)}) custom-call(s32[4]{0:T(128)S(1)} %get-tuple-element.37.length_ref, bf16[4,128,2048]{2,1,0:T(8,128)(2,1)S(1)} %get-tuple-element.40.ss_ref, bf16[4,256,2048]{2,1,0:T(8,128)(2,1)S(1)} %get-tuple-element.50.us_ref, ...), custom_call_target="tpu_custom_call" | custom-call | tf_op jit(solution)/shard_map/pallas_call | solution.py:363
  23.0 1.4 %collective-permute-done.7.refs_0_ = bf16[8,128,128]{2,1,0:T(8,128)(2,1)S(1)} collective-permute-done((bf16[8,128,128]{2,1,0:T(8,128)(2,1)S(1)}, bf16[8,128,128]{2,1,0:T(8,128)(2,1)S(1)}, u32[]{:S(2)}, u32[]{:S(2)}) %collective-permute-start.7) | collective-permute-done | bytes 262176 | tf_op jit(solution)/shard_map/ppermute | solution.py:265
  24.4 0.0 collective-permute-done.8.refs_1_
  24.4 0.1 collective-permute-start.9
  24.5 0.0 collective-permute-done.6.rest_1_
  24.5 0.0 collective-permute-done.5.rest_0_
  24.5 1.6 %shard_map.120 = (f32[128,2048]{1,0:T(8,128)S(1)}, f32[256,2048]{1,0:T(8,128)S(1)}) custom-call(s32[4]{0:T(128)S(1)} %get-tuple-element.37.length_ref, bf16[4,128,2048]{2,1,0:T(8,128)(2,1)S(1)} %get-tuple-element.40.ss_ref, bf16[4,256,2048]{2,1,0:T(8,128)(2,1)S(1)} %get-tuple-element.50.us_ref, f32[128,2048]{1,0:T(8,128)S(1)} %get-tuple-element.59.sa_ref.order_ref, ...), custom_call_target="tpu_custom_call" | custom-call | tf_op jit(solution)/shard_map/pallas_call | solution.py:363
  26.2 0.2 collective-permute-done.9.mate_ref
  26.4 0.0 copy-start
  26.4 1.1 %shard_map.122 = (f32[128,2048]{1,0:T(8,128)S(1)}, f32[256,2048]{1,0:T(8,128)S(1)}, f32[8,128]{1,0:T(8,128)S(1)}) custom-call(bf16[128,4096]{1,0:T(8,128)(2,1)S(1)} %get-tuple-element.57.ss_ref, bf16[256,4096]{1,0:T(8,128)(2,1)S(1)} %get-tuple-element.58.us_ref, f32[128,2048]{1,0:T(8,128)S(1)} %get-tuple-element.61.sa_ref, ...), custom_call_target="tpu_custom_call" | custom-call | tf_op jit(solution)/shard_map/pallas_call | solution.py:387
  27.5 1.8 %collective-permute-start.10 = (f32[8,128]{1,0:T(8,128)S(1)}, f32[8,128]{1,0:T(8,128)S(1)}, u32[]{:S(2)}, u32[]{:S(2)}) collective-permute-start(f32[8,128]{1,0:T(8,128)S(1)} %get-tuple-element.65), channel_id=1, source_target_pairs={{0,1},{1,0},{2,3},{3,2},{4,5},{5,4},{6,7},{7,6},{8,9},{9,8},{10,11... | collective-permute-start | bytes 12296 | tf_op jit(solution)/shard_map/ppermute | solution.py:399
  29.3 1.9 %collective-permute-done.10 = f32[8,128]{1,0:T(8,128)S(1)} collective-permute-done((f32[8,128]{1,0:T(8,128)S(1)}, f32[8,128]{1,0:T(8,128)S(1)}, u32[]{:S(2)}, u32[]{:S(2)}) %collective-permute-start.10) | collective-permute-done | bytes 4128 | tf_op jit(solution)/shard_map/ppermute | solution.py:399
  31.2 2.7 %collective-permute-start.11 = (f32[8,128]{1,0:T(8,128)S(1)}, f32[8,128]{1,0:T(8,128)S(1)}, u32[]{:S(2)}, u32[]{:S(2)}) collective-permute-start(f32[8,128]{1,0:T(8,128)S(1)} %add.3.one_ref), channel_id=1, source_target_pairs={{0,2},{1,3},{2,0},{3,1},{4,6},{5,7},{6,4},{7,5},{8,10},{9,11},{10,... | collective-permute-start | bytes 12296 | tf_op jit(solution)/shard_map/ppermute | solution.py:399
  33.9 0.0 copy-done
  33.9 1.8 %collective-permute-done.11.two_ref = f32[8,128]{1,0:T(8,128)S(1)} collective-permute-done((f32[8,128]{1,0:T(8,128)S(1)}, f32[8,128]{1,0:T(8,128)S(1)}, u32[]{:S(2)}, u32[]{:S(2)}) %collective-permute-start.11) | collective-permute-done | bytes 4128 | tf_op jit(solution)/shard_map/ppermute | solution.py:399
  35.7 1.5 %shard_map.123 = (bf16[128,2048]{1,0:T(8,128)(2,1)}, bf16[256,2048]{1,0:T(8,128)(2,1)}) custom-call(f32[128,2048]{1,0:T(8,128)S(1)} %get-tuple-element.63.st_ref, f32[256,2048]{1,0:T(8,128)S(1)} %get-tuple-element.64.ut_ref, bf16[1,2048]{1,0:T(2,128)(2,1)S(1)} %reshape.30.gain_ref, f32[8,128]{1,0:T(8,128)S(1)} %add.3.one_ref, ...), custom_call_target="tpu_custom_call" | custom-call | tf_op jit(solution)/shard_map/pallas_call | solution.py:401
  (5 shorter events, 0.2 us)
Async XLA Ops:
  2.6 9.8 %collective-permute-start = (bf16[8,128,128]{2,1,0:T(8,128)(2,1)S(1)}, bf16[8,128,128]{2,1,0:T(8,128)(2,1)S(1)}, u32[]{:S(2)}, u32[]{:S(2)}) collective-permute-start(bf16[8,128,128]{2,1,0:T(8,128)(2,1)S(1)} %get-tuple-element.56), channel_id=1, source_target_pairs={{0,8},{4,20},{8,0},{12,28},{16,24},{20,4},{24,16},{28,12},{1,9},{5... | collective-permute-start | bytes 786440 | tf_op jit(solution)/shard_map/ppermute | solution.py:265
  5.6 6.8 %collective-permute-start.1 = (bf16[8,128,128]{2,1,0:T(8,128)(2,1)S(1)}, bf16[8,128,128]{2,1,0:T(8,128)(2,1)S(1)}, u32[]{:S(2)}, u32[]{:S(2)}) collective-permute-start(bf16[8,128,128]{2,1,0:T(8,128)(2,1)S(1)} %get-tuple-element.55), channel_id=1, source_target_pairs={{0,16},{4,12},{8,24},{12,4},{16,0},{20,28},{24,8},{28,20},{1,17},{... | collective-permute-start | bytes 786440 | tf_op jit(solution)/shard_map/ppermute | solution.py:265
  9.7 10.1 %collective-permute-start.2 = (bf16[1,16,128,128]{3,2,1,0:T(8,128)(2,1)S(1)}, bf16[1,16,128,128]{3,2,1,0:T(8,128)(2,1)S(1)}, u32[]{:S(2)}, u32[]{:S(2)}) collective-permute-start(bf16[1,16,128,128]{3,2,1,0:T(8,128)(2,1)S(1)} %get-tuple-element.54.rest_0_), channel_id=1, source_target_pairs={{0,4},{4,0},{8,12},{12,8},{16,20},{20,16},{24,28},{28,24},{1,5},{5... | collective-permute-start | bytes 1572872 | tf_op jit(solution)/shard_map/ppermute | solution.py:265
  9.8 9.2 %collective-permute-start.4 = (bf16[8,128,128]{2,1,0:T(8,128)(2,1)S(1)}, bf16[8,128,128]{2,1,0:T(8,128)(2,1)S(1)}, u32[]{:S(2)}, u32[]{:S(2)}) collective-permute-start(bf16[8,128,128]{2,1,0:T(8,128)(2,1)S(1)} %get-tuple-element.56), channel_id=1, source_target_pairs={{0,16},{4,12},{8,24},{12,4},{16,0},{20,28},{24,8},{28,20},{1,17},{... | collective-permute-start | bytes 786440 | tf_op jit(solution)/shard_map/ppermute | solution.py:265
  10.4 9.2 %collective-permute-start.3 = (bf16[8,128,128]{2,1,0:T(8,128)(2,1)S(1)}, bf16[8,128,128]{2,1,0:T(8,128)(2,1)S(1)}, u32[]{:S(2)}, u32[]{:S(2)}) collective-permute-start(bf16[8,128,128]{2,1,0:T(8,128)(2,1)S(1)} %get-tuple-element.55), channel_id=1, source_target_pairs={{0,8},{4,20},{8,0},{12,28},{16,24},{20,4},{24,16},{28,12},{1,9},{5... | collective-permute-start | bytes 786440 | tf_op jit(solution)/shard_map/ppermute | solution.py:265
  12.4 12.0 %collective-permute-start.7 = (bf16[8,128,128]{2,1,0:T(8,128)(2,1)S(1)}, bf16[8,128,128]{2,1,0:T(8,128)(2,1)S(1)}, u32[]{:S(2)}, u32[]{:S(2)}) collective-permute-start(bf16[8,128,128]{2,1,0:T(8,128)(2,1)S(1)} %collective-permute-done.refs_0_), channel_id=1, source_target_pairs={{0,16},{4,12},{8,24},{12,4},{16,0},{20,28},{24,8},{28,20},{1,17},{... | collective-permute-start | bytes 786440 | tf_op jit(solution)/shard_map/ppermute | solution.py:265
  14.4 10.0 %collective-permute-start.8 = (bf16[8,128,128]{2,1,0:T(8,128)(2,1)S(1)}, bf16[8,128,128]{2,1,0:T(8,128)(2,1)S(1)}, u32[]{:S(2)}, u32[]{:S(2)}) collective-permute-start(bf16[8,128,128]{2,1,0:T(8,128)(2,1)S(1)} %collective-permute-done.1.refs_1_), channel_id=1, source_target_pairs={{0,8},{4,20},{8,0},{12,28},{16,24},{20,4},{24,16},{28,12},{1,9},{5... | collective-permute-start | bytes 786440 | tf_op jit(solution)/shard_map/ppermute | solution.py:265
  19.1 5.4 %collective-permute-start.6 = (bf16[1,16,128,128]{3,2,1,0:T(8,128)(2,1)S(1)}, bf16[1,16,128,128]{3,2,1,0:T(8,128)(2,1)S(1)}, u32[]{:S(2)}, u32[]{:S(2)}) collective-permute-start(bf16[1,16,128,128]{3,2,1,0:T(8,128)(2,1)S(1)} %shard_map.118.rest_3_), channel_id=1, source_target_pairs={{0,4},{4,0},{8,12},{12,8},{16,20},{20,16},{24,28},{28,24},{1,5},{5... | collective-permute-start | bytes 1572872 | tf_op jit(solution)/shard_map/ppermute | solution.py:265
  19.6 4.9 %collective-permute-start.5 = (bf16[1,16,128,128]{3,2,1,0:T(8,128)(2,1)S(1)}, bf16[1,16,128,128]{3,2,1,0:T(8,128)(2,1)S(1)}, u32[]{:S(2)}, u32[]{:S(2)}) collective-permute-start(bf16[1,16,128,128]{3,2,1,0:T(8,128)(2,1)S(1)} %shard_map.117.rest_2_), channel_id=1, source_target_pairs={{0,4},{4,0},{8,12},{12,8},{16,20},{20,16},{24,28},{28,24},{1,5},{5... | collective-permute-start | bytes 1572872 | tf_op jit(solution)/shard_map/ppermute | solution.py:265
  24.4 2.0 %collective-permute-start.9 = (bf16[1,16,128,128]{3,2,1,0:T(8,128)(2,1)S(1)}, bf16[1,16,128,128]{3,2,1,0:T(8,128)(2,1)S(1)}, u32[]{:S(2)}, u32[]{:S(2)}) collective-permute-start(bf16[1,16,128,128]{3,2,1,0:T(8,128)(2,1)S(1)} %shard_map.121.state_ref), channel_id=1, source_target_pairs={{0,4},{4,0},{8,12},{12,8},{16,20},{20,16},{24,28},{28,24},{1,5},{5... | collective-permute-start | bytes 1572872 | tf_op jit(solution)/shard_map/ppermute | solution.py:265
  26.4 7.5 %copy-start = (bf16[2048]{0:T(1024)(128)(2,1)S(1)}, bf16[2048]{0:T(1024)(128)(2,1)}, u32[]{:S(2)}) copy-start(bf16[2048]{0:T(1024)(128)(2,1)} %param.14) | copy-start | bytes 12292
  27.5 3.7 %collective-permute-start.10 = (f32[8,128]{1,0:T(8,128)S(1)}, f32[8,128]{1,0:T(8,128)S(1)}, u32[]{:S(2)}, u32[]{:S(2)}) collective-permute-start(f32[8,128]{1,0:T(8,128)S(1)} %get-tuple-element.65), channel_id=1, source_target_pairs={{0,1},{1,0},{2,3},{3,2},{4,5},{5,4},{6,7},{7,6},{8,9},{9,8},{10,11... | collective-permute-start | bytes 12296 | tf_op jit(solution)/shard_map/ppermute | solution.py:399
  31.2 4.5 %collective-permute-start.11 = (f32[8,128]{1,0:T(8,128)S(1)}, f32[8,128]{1,0:T(8,128)S(1)}, u32[]{:S(2)}, u32[]{:S(2)}) collective-permute-start(f32[8,128]{1,0:T(8,128)S(1)} %add.3.one_ref), channel_id=1, source_target_pairs={{0,2},{1,3},{2,0},{3,1},{4,6},{5,7},{6,4},{7,5},{8,10},{9,11},{10,... | collective-permute-start | bytes 12296 | tf_op jit(solution)/shard_map/ppermute | solution.py:399

commit v12 on v11

--- a/solution.py
+++ b/solution.py
@@ -17,38 +17,22 @@
     return lax.dot_general(a, b, (contract, ((), ())), preferred_element_type=jnp.float32)
 
 
-def load_columns(sources, targets, sems, chunks):
+def state_kernel(key_hbm, value_hbm, first_ref, second_ref, key_ref, value_ref, sems):
+    half, width = first_ref.shape[0], key_ref.shape[2]
+    parity = lax.axis_index("seq") & 1
     copies = []
-    for chunk in range(chunks):
-        group = []
-        for i, (source, target) in enumerate(zip(sources, targets)):
-            size = source.shape[1] // chunks
-            cols = pl.ds(chunk * size, size)
-            group.append(pltpu.make_async_copy(source.at[:, cols], target.at[:, cols], sems.at[i, chunk]))
-            group[-1].start()
-        copies.append(group)
-
-    def wait(chunk):
-        for copy in copies[chunk]:
+    for part in range(2):
+        cols = pl.ds(pl.multiple_of((parity ^ part) * width, width), width)
+        for i, (source, target) in enumerate(((key_hbm, key_ref), (value_hbm, value_ref))):
+            copies.append(pltpu.make_async_copy(source.at[:, cols], target.at[part], sems.at[i, part]))
+            copies[-1].start()
+    for part, out_ref in enumerate((first_ref, second_ref)):
+        for copy in copies[2 * part : 2 * part + 2]:
             copy.wait()
-
-    return wait
-
-
-def state_kernel(chunks, key_hbm, value_hbm, first_ref, second_ref, whole_ref, key_ref, value_ref, sems):
-    half = first_ref.shape[0]
-    head_count = 2 * half
-    wait = load_columns((key_hbm, value_hbm), (key_ref, value_ref), sems, chunks)
-    for head in range(head_count):
-        if head % (head_count // chunks) == 0:
-            wait(head // (head_count // chunks))
-        cols = slice(head * HD, (head + 1) * HD)
-        state = matmul(key_ref[:, cols], value_ref[:, cols], ((0,), (0,)))
-        whole_ref[0, head] = state.astype(jnp.bfloat16)
-    parity = lax.axis_index("seq") & 1
-    for head in range(half):
-        first_ref[head] = whole_ref[0, parity * half + head]
-        second_ref[head] = whole_ref[0, (1 - parity) * half + head]
+        for head in range(half):
+            cols = slice(head * HD, (head + 1) * HD)
+            state = matmul(key_ref[part, :, cols], value_ref[part, :, cols], ((0,), (0,)))
+            out_ref[head] = state.astype(jnp.bfloat16)
 
 
 def join_kernel(order_ref, *refs):
@@ -73,8 +57,16 @@
     return jnp.where(block < target, level, 0)
 
 
-def attend(mask, q_ref, k_ref, v_ref, w_ref, o_ref):
+def attend(mask, q_ref, k_ref, v_ref, w_ref, o_ref, parity=None):
     head_count = q_ref.shape[1] // HD
+    half = head_count // 2
+
+    def pick(ref, head, rows, cols):
+        if parity is None:
+            return ref[rows, cols]
+        start = head % half * HD
+        return ref[(head // half) ^ parity, rows, start : start + HD]
+
     step = 2
     for first in range(0, head_count, step):
         units = [
@@ -82,9 +74,11 @@
             for head in range(first, first + step)
             for start in range(0, q_ref.shape[0], ROWS)
         ]
-        scores = [matmul(q_ref[rows, cols], k_ref[rows, cols], ((1,), (1,))) for _, cols, rows in units]
+        scores = [matmul(q_ref[rows, cols], pick(k_ref, head, rows, cols), ((1,), (1,))) for head, cols, rows in units]
         scores = [jnp.where(mask, score, 0.0).astype(jnp.bfloat16) for score in scores]
-        results = [matmul(score, v_ref[rows, cols], ((1,), (0,))) for score, (_, cols, rows) in zip(scores, units)]
+        results = [
+            matmul(score, pick(v_ref, head, rows, cols), ((1,), (0,))) for score, (head, cols, rows) in zip(scores, units)
+        ]
         for result, (head, cols, rows) in zip(results, units):
             o_ref[rows, cols] = result * w_ref[rows, head : head + 1]
 
@@ -105,9 +99,14 @@
 
 
 def load_kernel(suffix, *refs):
-    sources, (k_ref, v_ref), (sw_ref, uw_ref), rest = refs[:4], refs[4:6], refs[6:8], refs[8:]
-    loaded, o_ref, tables, sems = rest[:2], rest[2], rest[3:5], rest[5]
+    sources, (k_ref, v_ref), halves, (sw_ref, uw_ref), rest = refs[:4], refs[4:6], refs[6:8], refs[8:10], refs[10:]
+    loaded, o_ref, whole_ref, tables, sems = rest[:2], rest[2], rest[3], rest[4:6], rest[6]
     copies = start_copies(sources, (*tables, *loaded), sems)
+    parity = lax.axis_index("seq") & 1
+    half = halves[0].shape[0]
+    for part, half_ref in enumerate(halves):
+        for head in range(half):
+            whole_ref[0, (part ^ parity) * half + head] = half_ref[head]
     slab_table, user_table = tables
     for copy in copies[:2]:
         copy.wait()
@@ -120,7 +119,7 @@
         uw_ref[user * suffix : (user + 1) * suffix] = matmul(user_table[user], same, ((0,), (0,)))
     for copy in copies[2:]:
         copy.wait()
-    attend(causal_mask(), loaded[0], k_ref, v_ref, sw_ref, o_ref)
+    attend(causal_mask(), loaded[0], k_ref, v_ref, sw_ref, o_ref, parity)
 
 
 def scale_queries(q_ref, w_ref, scaled_ref):
@@ -278,12 +277,13 @@
 
     half_state = pltpu.VMEM((half, HD, HD), jnp.bfloat16)
     slab_rows = pltpu.VMEM((token_count, width), jnp.bfloat16)
-    first, second, state, slab_keys, slab_values = pl.pallas_call(
-        functools.partial(state_kernel, chunks),
-        out_shape=[half_state, half_state, pltpu.VMEM((1, head_count, HD, HD), jnp.bfloat16), slab_rows, slab_rows],
+    half_rows = pltpu.VMEM((2, token_count, width // 2), jnp.bfloat16)
+    first, second, slab_keys, slab_values = pl.pallas_call(
+        state_kernel,
+        out_shape=[half_state, half_state, half_rows, half_rows],
         in_specs=[hbm] * 2,
-        out_specs=[vmem] * 5,
-        scratch_shapes=[pltpu.SemaphoreType.DMA((2, chunks))],
+        out_specs=[vmem] * 4,
+        scratch_shapes=[pltpu.SemaphoreType.DMA((2, 2))],
         compiler_params=params,
     )(*pinned(slab_key, slab_value))
     halves = [first, second]
@@ -298,7 +298,7 @@
     slab_table = slab_levels.reshape(-1, token_count)
     user_table = user_levels.reshape(user_count, -1, suffix)
     user_array = pltpu.VMEM((user_rows, width), jnp.bfloat16)
-    slab_weights, user_weights, slab_queries, lengths, slab_acc = pl.pallas_call(
+    slab_weights, user_weights, slab_queries, lengths, slab_acc, state = pl.pallas_call(
         functools.partial(load_kernel, suffix),
         out_shape=[
             pltpu.VMEM((token_count, levels * head_count), jnp.float32),
@@ -306,9 +306,10 @@
             slab_rows,
             pltpu.VMEM((user_count,), jnp.int32),
             pltpu.VMEM((token_count, width), jnp.float32),
+            pltpu.VMEM((1, head_count, HD, HD), jnp.bfloat16),
         ],
-        in_specs=[hbm] * 4 + [vmem] * 2,
-        out_specs=[vmem] * 5,
+        in_specs=[hbm] * 4 + [vmem] * 4,
+        out_specs=[vmem] * 6,
         scratch_shapes=[
             pltpu.VMEM(slab_table.shape, jnp.bfloat16),
             pltpu.VMEM(user_table.shape, jnp.bfloat16),
@@ -316,7 +317,7 @@
         ],
         compiler_params=params,
         cost_estimate=cost(0, 0),
-    )(*pinned(slab_table, user_table, slab_query, prefix_lengths), slab_keys, slab_values)
+    )(*pinned(slab_table, user_table, slab_query, prefix_lengths), slab_keys, slab_values, first, second)
     halves = after(slab_weights, halves)
     for bit, side in places:
         if (bit, side) not in ahead:
@@ -370,7 +371,6 @@
             cost_estimate=cost(0, 0),
         )(lengths, slab_scaled, user_scaled, *accs, *[whole[m] for m in offsets])
 
-    state = after(slab_weights, [state])[0]
     whole = {0: state, 1: swap(state, 0)}
     direct = [1 << bit for bit in outer]
     for m in direct:

time: 37.3 us -> 37 us (level)
  transfers between devices with their start and end apart: 12 -> 12, of which waited for: 6 -> 6; matrix products, arithmetic and copies ran while one was open for 0% -> 0% of each run, Pallas kernels for 31% -> 32%
where the time goes in v12:
time: 37 us; the launch traced here: 36.8 us
  Pallas kernels  15.8 us (43%)
  starting transfers between devices  14 us (38%)
  waiting for transfers between devices  6.23 us (17%)
  between operations  0.76 us (2%)
    ppermute x10, starting transfers between devices, swap(): lax.ppermute(value, 'seq', [(i, i ^ 1 << (other if i & 1 else bit)) for i...  9.49 us
    pallas_call x2, Pallas kernels, read(): pl.pallas_call(functools.partial(read_kernel, depth, suffix, groups, ahea...  4.8 us
    ppermute x2, starting transfers between devices, local(): lax.ppermute(square, 'head', [(i, i ^ 1 << bit) for i in range(head_axis)])  4.51 us
    ppermute x2, waiting for transfers between devices, local(): lax.ppermute(square, 'head', [(i, i ^ 1 << bit) for i in range(head_axis)])  3.65 us
    pallas_call x1, Pallas kernels, local(): pl.pallas_call(functools.partial(load_kernel, suffix), out_shape=[pltpu.V...  2.59 us
    ppermute x10, waiting for transfers between devices, swap(): lax.ppermute(value, 'seq', [(i, i ^ 1 << (other if i & 1 else bit)) for i...  2.58 us
    pallas_call x1, Pallas kernels, local(): pl.pallas_call(functools.partial(user_kernel, suffix), out_shape=[pltpu.V...  2.22 us
    pallas_call x1, Pallas kernels, local(): pl.pallas_call(scale_kernel, out_shape=[pltpu.VMEM((levels, token_count,...  1.88 us
  transfers between devices with their start and end apart: 12, of which 6 were waited for; matrix products, arithmetic and copies ran while one was open for 0% of the time, Pallas kernels for 32%

profile of v12, /device:TPU:0, one launch (start us, length us, event | category | flops | bytes accessed | tf_op | source)
XLA Modules:
  0.0 36.8 jit_solution(12578773854512238299)
XLA Ops:
  0.6 1.6 %shard_map.113 = (bf16[8,128,128]{2,1,0:T(8,128)(2,1)S(1)}, bf16[8,128,128]{2,1,0:T(8,128)(2,1)S(1)}, bf16[2,128,1024]{2,1,0:T(8,128)(2,1)S(1)}, bf16[2,128,1024]{2,1,0:T(8,128)(2,1)S(1)}) custom-call(bf16[128,2048]{1,0:T(8,128)(2,1)} %key_hbm.1, bf16[128,2048]{1,0:T(8,128)(2,1)} %value_hbm.1), custom_call_target="tpu_custom_call" | custom-call | tf_op jit(solution)/shard_map/pallas_call | solution.py:281
  2.2 3.0 %collective-permute-start = (bf16[8,128,128]{2,1,0:T(8,128)(2,1)S(1)}, bf16[8,128,128]{2,1,0:T(8,128)(2,1)S(1)}, u32[]{:S(2)}, u32[]{:S(2)}) collective-permute-start(bf16[8,128,128]{2,1,0:T(8,128)(2,1)S(1)} %get-tuple-element.54.refs_6_), channel_id=1, source_target_pairs={{0,8},{4,20},{8,0},{12,28},{16,24},{20,4},{24,16},{28,12},{1,9},{5... | collective-permute-start | bytes 786440 | tf_op jit(solution)/shard_map/ppermute | solution.py:264
  5.2 1.5 %collective-permute-start.1 = (bf16[8,128,128]{2,1,0:T(8,128)(2,1)S(1)}, bf16[8,128,128]{2,1,0:T(8,128)(2,1)S(1)}, u32[]{:S(2)}, u32[]{:S(2)}) collective-permute-start(bf16[8,128,128]{2,1,0:T(8,128)(2,1)S(1)} %get-tuple-element.53.refs_7_), channel_id=1, source_target_pairs={{0,16},{4,12},{8,24},{12,4},{16,0},{20,28},{24,8},{28,20},{1,17},{... | collective-permute-start | bytes 786440 | tf_op jit(solution)/shard_map/ppermute | solution.py:264
  6.8 2.6 %shard_map.114 = (f32[128,64]{1,0:T(8,128)S(1)}, f32[256,64]{1,0:T(8,128)S(1)}, bf16[128,2048]{1,0:T(8,128)(2,1)S(1)}, s32[4]{0:T(128)S(1)}, f32[128,2048]{1,0:T...) custom-call(bf16[96,128]{1,0:T(8,128)(2,1)} %bitcast.10, bf16[4,96,64]{2,1,0:T(8,128)(2,1)} %bitcast.9, ...), custom_call_target="tpu_custom_call" | custom-call | tf_op jit(solution)/shard_map/pallas_call | solution.py:301
  9.4 0.1 collective-permute-start.2
  9.4 0.6 %collective-permute-start.4 = (bf16[8,128,128]{2,1,0:T(8,128)(2,1)S(1)}, bf16[8,128,128]{2,1,0:T(8,128)(2,1)S(1)}, u32[]{:S(2)}, u32[]{:S(2)}) collective-permute-start(bf16[8,128,128]{2,1,0:T(8,128)(2,1)S(1)} %get-tuple-element.54.refs_6_), channel_id=1, source_target_pairs={{0,16},{4,12},{8,24},{12,4},{16,0},{20,28},{24,8},{28,20},{1,17},{... | collective-permute-start | bytes 786440 | tf_op jit(solution)/shard_map/ppermute | solution.py:264
  10.0 0.1 collective-permute-start.3
  10.1 1.9 %shard_map.115 = (bf16[4,128,2048]{2,1,0:T(8,128)(2,1)S(1)}, bf16[256,2048]{1,0:T(8,128)(2,1)S(1)}, bf16[256,2048]{1,0:T(8,128)(2,1)S(1)}, bf16[256,2048]{1,0:T(8,128)(2,1)S(1)}) custom-call(bf16[256,2048]{1,0:T(8,128)(2,1)} %bitcast.6, bf16[256,2048]{1,0:T(8,128)(2,1)} %bitcast.7, bf16[256,2048]{1,0:T(8,128)(2,1)} %bitcast.8, ...), custom_call_target="tpu_custom_call" | custom-call | tf_op jit(solution)/shard_map/pallas_call | solution.py:325
  12.0 0.0 collective-permute-done.refs_0_
  12.0 0.0 collective-permute-done.1.refs_1_
  12.0 2.0 %collective-permute-start.7 = (bf16[8,128,128]{2,1,0:T(8,128)(2,1)S(1)}, bf16[8,128,128]{2,1,0:T(8,128)(2,1)S(1)}, u32[]{:S(2)}, u32[]{:S(2)}) collective-permute-start(bf16[8,128,128]{2,1,0:T(8,128)(2,1)S(1)} %collective-permute-done.refs_0_), channel_id=1, source_target_pairs={{0,16},{4,12},{8,24},{12,4},{16,0},{20,28},{24,8},{28,20},{1,17},{... | collective-permute-start | bytes 786440 | tf_op jit(solution)/shard_map/ppermute | solution.py:264
  14.1 1.9 %collective-permute-start.8 = (bf16[8,128,128]{2,1,0:T(8,128)(2,1)S(1)}, bf16[8,128,128]{2,1,0:T(8,128)(2,1)S(1)}, u32[]{:S(2)}, u32[]{:S(2)}) collective-permute-start(bf16[8,128,128]{2,1,0:T(8,128)(2,1)S(1)} %collective-permute-done.1.refs_1_), channel_id=1, source_target_pairs={{0,8},{4,20},{8,0},{12,28},{16,24},{20,4},{24,16},{28,12},{1,9},{5... | collective-permute-start | bytes 786440 | tf_op jit(solution)/shard_map/ppermute | solution.py:264
  15.9 2.2 %shard_map.116 = (f32[256,2048]{1,0:T(8,128)S(1)}, bf16[4,256,2048]{2,1,0:T(8,128)(2,1)S(1)}) custom-call(f32[256,64]{1,0:T(8,128)S(1)} %get-tuple-element.45.w_ref, bf16[256,2048]{1,0:T(8,128)(2,1)S(1)} %get-tuple-element.46.q_ref, bf16[256,2048]{1,0:T(8,128)(2,1)S(1)} %get-tuple-element.47.k_ref, bf16[256,2048]{1,0:T(8,128)(2,1)S(1)} %get-tuple-element.48.v_ref), custom_call_target="tpu_custom_call" | custom-call | tf_op jit(solution)/shard_map/pallas_call | solution.py:346
  18.2 0.5 %collective-permute-done.4.refs_0_ = bf16[8,128,128]{2,1,0:T(8,128)(2,1)S(1)} collective-permute-done((bf16[8,128,128]{2,1,0:T(8,128)(2,1)S(1)}, bf16[8,128,128]{2,1,0:T(8,128)(2,1)S(1)}, u32[]{:S(2)}, u32[]{:S(2)}) %collective-permute-start.4) | collective-permute-done | bytes 262176 | tf_op jit(solution)/shard_map/ppermute | solution.py:264
  18.7 0.1 collective-permute-start.6
  18.8 0.4 %collective-permute-done.3.refs_1_ = bf16[8,128,128]{2,1,0:T(8,128)(2,1)S(1)} collective-permute-done((bf16[8,128,128]{2,1,0:T(8,128)(2,1)S(1)}, bf16[8,128,128]{2,1,0:T(8,128)(2,1)S(1)}, u32[]{:S(2)}, u32[]{:S(2)}) %collective-permute-start.3) | collective-permute-done | bytes 262176 | tf_op jit(solution)/shard_map/ppermute | solution.py:264
  19.3 0.2 collective-permute-start.5
  19.4 0.0 collective-permute-done.2.rest_1_
  19.4 3.2 %shard_map.119 = (f32[128,2048]{1,0:T(8,128)S(1)}, f32[256,2048]{1,0:T(8,128)S(1)}, bf16[128,4096]{1,0:T(8,128)(2,1)S(1)}, bf16[256,4096]{1,0:T(8,128)(2,1)S(1)}) custom-call(s32[4]{0:T(128)S(1)} %get-tuple-element.38.length_ref, bf16[4,128,2048]{2,1,0:T(8,128)(2,1)S(1)} %get-tuple-element.41.ss_ref, bf16[4,256,2048]{2,1,0:T(8,128)(2,1)S(1)} %get-tuple-element.49.us_ref, ...), custom_call_target="tpu_custom_call" | custom-call | tf_op jit(solution)/shard_map/pallas_call | solution.py:364
  22.6 1.4 %collective-permute-done.7.refs_0_ = bf16[8,128,128]{2,1,0:T(8,128)(2,1)S(1)} collective-permute-done((bf16[8,128,128]{2,1,0:T(8,128)(2,1)S(1)}, bf16[8,128,128]{2,1,0:T(8,128)(2,1)S(1)}, u32[]{:S(2)}, u32[]{:S(2)}) %collective-permute-start.7) | collective-permute-done | bytes 262176 | tf_op jit(solution)/shard_map/ppermute | solution.py:264
  24.0 0.0 collective-permute-done.8.refs_1_
  24.1 0.1 collective-permute-start.9
  24.2 0.0 collective-permute-done.6.rest_1_
  24.2 0.0 collective-permute-done.5.rest_0_
  24.2 1.6 %shard_map.120 = (f32[128,2048]{1,0:T(8,128)S(1)}, f32[256,2048]{1,0:T(8,128)S(1)}) custom-call(s32[4]{0:T(128)S(1)} %get-tuple-element.38.length_ref, bf16[4,128,2048]{2,1,0:T(8,128)(2,1)S(1)} %get-tuple-element.41.ss_ref, bf16[4,256,2048]{2,1,0:T(8,128)(2,1)S(1)} %get-tuple-element.49.us_ref, f32[128,2048]{1,0:T(8,128)S(1)} %get-tuple-element.57.sa_ref.order_ref, ...), custom_call_target="tpu_custom_call" | custom-call | tf_op jit(solution)/shard_map/pallas_call | solution.py:364
  25.8 0.2 collective-permute-done.9.mate_ref
  26.1 0.0 copy-start
  26.1 1.1 %shard_map.122 = (f32[128,2048]{1,0:T(8,128)S(1)}, f32[256,2048]{1,0:T(8,128)S(1)}, f32[8,128]{1,0:T(8,128)S(1)}) custom-call(bf16[128,4096]{1,0:T(8,128)(2,1)S(1)} %get-tuple-element.55.ss_ref, bf16[256,4096]{1,0:T(8,128)(2,1)S(1)} %get-tuple-element.56.us_ref, f32[128,2048]{1,0:T(8,128)S(1)} %get-tuple-element.59.sa_ref, ...), custom_call_target="tpu_custom_call" | custom-call | tf_op jit(solution)/shard_map/pallas_call | solution.py:387
  27.1 1.8 %collective-permute-start.10 = (f32[8,128]{1,0:T(8,128)S(1)}, f32[8,128]{1,0:T(8,128)S(1)}, u32[]{:S(2)}, u32[]{:S(2)}) collective-permute-start(f32[8,128]{1,0:T(8,128)S(1)} %get-tuple-element.63), channel_id=1, source_target_pairs={{0,1},{1,0},{2,3},{3,2},{4,5},{5,4},{6,7},{7,6},{8,9},{9,8},{10,11... | collective-permute-start | bytes 12296 | tf_op jit(solution)/shard_map/ppermute | solution.py:399
  28.9 1.9 %collective-permute-done.10 = f32[8,128]{1,0:T(8,128)S(1)} collective-permute-done((f32[8,128]{1,0:T(8,128)S(1)}, f32[8,128]{1,0:T(8,128)S(1)}, u32[]{:S(2)}, u32[]{:S(2)}) %collective-permute-start.10) | collective-permute-done | bytes 4128 | tf_op jit(solution)/shard_map/ppermute | solution.py:399
  30.8 2.7 %collective-permute-start.11 = (f32[8,128]{1,0:T(8,128)S(1)}, f32[8,128]{1,0:T(8,128)S(1)}, u32[]{:S(2)}, u32[]{:S(2)}) collective-permute-start(f32[8,128]{1,0:T(8,128)S(1)} %add.3.one_ref), channel_id=1, source_target_pairs={{0,2},{1,3},{2,0},{3,1},{4,6},{5,7},{6,4},{7,5},{8,10},{9,11},{10,... | collective-permute-start | bytes 12296 | tf_op jit(solution)/shard_map/ppermute | solution.py:399
  33.5 0.0 copy-done
  33.6 1.8 %collective-permute-done.11.two_ref = f32[8,128]{1,0:T(8,128)S(1)} collective-permute-done((f32[8,128]{1,0:T(8,128)S(1)}, f32[8,128]{1,0:T(8,128)S(1)}, u32[]{:S(2)}, u32[]{:S(2)}) %collective-permute-start.11) | collective-permute-done | bytes 4128 | tf_op jit(solution)/shard_map/ppermute | solution.py:399
  35.3 1.5 %shard_map.123 = (bf16[128,2048]{1,0:T(8,128)(2,1)}, bf16[256,2048]{1,0:T(8,128)(2,1)}) custom-call(f32[128,2048]{1,0:T(8,128)S(1)} %get-tuple-element.61.st_ref, f32[256,2048]{1,0:T(8,128)S(1)} %get-tuple-element.62.ut_ref, bf16[1,2048]{1,0:T(2,128)(2,1)S(1)} %reshape.30.gain_ref, f32[8,128]{1,0:T(8,128)S(1)} %add.3.one_ref, ...), custom_call_target="tpu_custom_call" | custom-call | tf_op jit(solution)/shard_map/pallas_call | solution.py:401
  (5 shorter events, 0.2 us)
Async XLA Ops:
  2.2 9.8 %collective-permute-start = (bf16[8,128,128]{2,1,0:T(8,128)(2,1)S(1)}, bf16[8,128,128]{2,1,0:T(8,128)(2,1)S(1)}, u32[]{:S(2)}, u32[]{:S(2)}) collective-permute-start(bf16[8,128,128]{2,1,0:T(8,128)(2,1)S(1)} %get-tuple-element.54.refs_6_), channel_id=1, source_target_pairs={{0,8},{4,20},{8,0},{12,28},{16,24},{20,4},{24,16},{28,12},{1,9},{5... | collective-permute-start | bytes 786440 | tf_op jit(solution)/shard_map/ppermute | solution.py:264
  5.2 6.8 %collective-permute-start.1 = (bf16[8,128,128]{2,1,0:T(8,128)(2,1)S(1)}, bf16[8,128,128]{2,1,0:T(8,128)(2,1)S(1)}, u32[]{:S(2)}, u32[]{:S(2)}) collective-permute-start(bf16[8,128,128]{2,1,0:T(8,128)(2,1)S(1)} %get-tuple-element.53.refs_7_), channel_id=1, source_target_pairs={{0,16},{4,12},{8,24},{12,4},{16,0},{20,28},{24,8},{28,20},{1,17},{... | collective-permute-start | bytes 786440 | tf_op jit(solution)/shard_map/ppermute | solution.py:264
  9.4 10.1 %collective-permute-start.2 = (bf16[1,16,128,128]{3,2,1,0:T(8,128)(2,1)S(1)}, bf16[1,16,128,128]{3,2,1,0:T(8,128)(2,1)S(1)}, u32[]{:S(2)}, u32[]{:S(2)}) collective-permute-start(bf16[1,16,128,128]{3,2,1,0:T(8,128)(2,1)S(1)} %get-tuple-element.52.rest_0_), channel_id=1, source_target_pairs={{0,4},{4,0},{8,12},{12,8},{16,20},{20,16},{24,28},{28,24},{1,5},{5... | collective-permute-start | bytes 1572872 | tf_op jit(solution)/shard_map/ppermute | solution.py:264
  9.4 9.2 %collective-permute-start.4 = (bf16[8,128,128]{2,1,0:T(8,128)(2,1)S(1)}, bf16[8,128,128]{2,1,0:T(8,128)(2,1)S(1)}, u32[]{:S(2)}, u32[]{:S(2)}) collective-permute-start(bf16[8,128,128]{2,1,0:T(8,128)(2,1)S(1)} %get-tuple-element.54.refs_6_), channel_id=1, source_target_pairs={{0,16},{4,12},{8,24},{12,4},{16,0},{20,28},{24,8},{28,20},{1,17},{... | collective-permute-start | bytes 786440 | tf_op jit(solution)/shard_map/ppermute | solution.py:264
  10.0 9.2 %collective-permute-start.3 = (bf16[8,128,128]{2,1,0:T(8,128)(2,1)S(1)}, bf16[8,128,128]{2,1,0:T(8,128)(2,1)S(1)}, u32[]{:S(2)}, u32[]{:S(2)}) collective-permute-start(bf16[8,128,128]{2,1,0:T(8,128)(2,1)S(1)} %get-tuple-element.53.refs_7_), channel_id=1, source_target_pairs={{0,8},{4,20},{8,0},{12,28},{16,24},{20,4},{24,16},{28,12},{1,9},{5... | collective-permute-start | bytes 786440 | tf_op jit(solution)/shard_map/ppermute | solution.py:264
  12.0 12.0 %collective-permute-start.7 = (bf16[8,128,128]{2,1,0:T(8,128)(2,1)S(1)}, bf16[8,128,128]{2,1,0:T(8,128)(2,1)S(1)}, u32[]{:S(2)}, u32[]{:S(2)}) collective-permute-start(bf16[8,128,128]{2,1,0:T(8,128)(2,1)S(1)} %collective-permute-done.refs_0_), channel_id=1, source_target_pairs={{0,16},{4,12},{8,24},{12,4},{16,0},{20,28},{24,8},{28,20},{1,17},{... | collective-permute-start | bytes 786440 | tf_op jit(solution)/shard_map/ppermute | solution.py:264
  14.1 10.0 %collective-permute-start.8 = (bf16[8,128,128]{2,1,0:T(8,128)(2,1)S(1)}, bf16[8,128,128]{2,1,0:T(8,128)(2,1)S(1)}, u32[]{:S(2)}, u32[]{:S(2)}) collective-permute-start(bf16[8,128,128]{2,1,0:T(8,128)(2,1)S(1)} %collective-permute-done.1.refs_1_), channel_id=1, source_target_pairs={{0,8},{4,20},{8,0},{12,28},{16,24},{20,4},{24,16},{28,12},{1,9},{5... | collective-permute-start | bytes 786440 | tf_op jit(solution)/shard_map/ppermute | solution.py:264
  18.7 5.4 %collective-permute-start.6 = (bf16[1,16,128,128]{3,2,1,0:T(8,128)(2,1)S(1)}, bf16[1,16,128,128]{3,2,1,0:T(8,128)(2,1)S(1)}, u32[]{:S(2)}, u32[]{:S(2)}) collective-permute-start(bf16[1,16,128,128]{3,2,1,0:T(8,128)(2,1)S(1)} %shard_map.118.rest_3_), channel_id=1, source_target_pairs={{0,4},{4,0},{8,12},{12,8},{16,20},{20,16},{24,28},{28,24},{1,5},{5... | collective-permute-start | bytes 1572872 | tf_op jit(solution)/shard_map/ppermute | solution.py:264
  19.3 4.9 %collective-permute-start.5 = (bf16[1,16,128,128]{3,2,1,0:T(8,128)(2,1)S(1)}, bf16[1,16,128,128]{3,2,1,0:T(8,128)(2,1)S(1)}, u32[]{:S(2)}, u32[]{:S(2)}) collective-permute-start(bf16[1,16,128,128]{3,2,1,0:T(8,128)(2,1)S(1)} %shard_map.117.rest_2_), channel_id=1, source_target_pairs={{0,4},{4,0},{8,12},{12,8},{16,20},{20,16},{24,28},{28,24},{1,5},{5... | collective-permute-start | bytes 1572872 | tf_op jit(solution)/shard_map/ppermute | solution.py:264
  24.1 2.0 %collective-permute-start.9 = (bf16[1,16,128,128]{3,2,1,0:T(8,128)(2,1)S(1)}, bf16[1,16,128,128]{3,2,1,0:T(8,128)(2,1)S(1)}, u32[]{:S(2)}, u32[]{:S(2)}) collective-permute-start(bf16[1,16,128,128]{3,2,1,0:T(8,128)(2,1)S(1)} %shard_map.121.state_ref), channel_id=1, source_target_pairs={{0,4},{4,0},{8,12},{12,8},{16,20},{20,16},{24,28},{28,24},{1,5},{5... | collective-permute-start | bytes 1572872 | tf_op jit(solution)/shard_map/ppermute | solution.py:264
  26.1 7.5 %copy-start = (bf16[2048]{0:T(1024)(128)(2,1)S(1)}, bf16[2048]{0:T(1024)(128)(2,1)}, u32[]{:S(2)}) copy-start(bf16[2048]{0:T(1024)(128)(2,1)} %param.14) | copy-start | bytes 12292
  27.1 3.7 %collective-permute-start.10 = (f32[8,128]{1,0:T(8,128)S(1)}, f32[8,128]{1,0:T(8,128)S(1)}, u32[]{:S(2)}, u32[]{:S(2)}) collective-permute-start(f32[8,128]{1,0:T(8,128)S(1)} %get-tuple-element.63), channel_id=1, source_target_pairs={{0,1},{1,0},{2,3},{3,2},{4,5},{5,4},{6,7},{7,6},{8,9},{9,8},{10,11... | collective-permute-start | bytes 12296 | tf_op jit(solution)/shard_map/ppermute | solution.py:399
  30.8 4.5 %collective-permute-start.11 = (f32[8,128]{1,0:T(8,128)S(1)}, f32[8,128]{1,0:T(8,128)S(1)}, u32[]{:S(2)}, u32[]{:S(2)}) collective-permute-start(f32[8,128]{1,0:T(8,128)S(1)} %add.3.one_ref), channel_id=1, source_target_pairs={{0,2},{1,3},{2,0},{3,1},{4,6},{5,7},{6,4},{7,5},{8,10},{9,11},{10,... | collective-permute-start | bytes 12296 | tf_op jit(solution)/shard_map/ppermute | solution.py:399

commit v13 on v12

--- a/solution.py
+++ b/solution.py
@@ -201,8 +201,11 @@
             line += 1
 
 
-def norm_kernel(features, chunks, st_ref, ut_ref, gain_ref, one_ref, two_ref, so_hbm, uo_hbm, so_ref, uo_ref, sems):
-    square = one_ref[...] + two_ref[...]
+def norm_kernel(features, chunks, st_ref, ut_ref, gain_ref, *rest):
+    squares, (so_hbm, uo_hbm, so_ref, uo_ref, sems) = rest[:-5], rest[-5:]
+    square = squares[0][...]
+    for part_ref in squares[1:]:
+        square = square + part_ref[...]
     scale = lax.rsqrt(square / features + 1e-06)
     size = st_ref.shape[1] // chunks
     copies = []
@@ -393,15 +396,14 @@
         cost_estimate=cost(0, 0),
     )(slab_ahead, user_ahead, *accs, whole[last], whole[last | 1])
 
-    mate = jnp.zeros_like(square)
-    for bit in range(head_axis.bit_length() - 1):
-        square = square + mate
-        mate = lax.ppermute(square, "head", [(i, i ^ (1 << bit)) for i in range(head_axis)])
+    squares = [square]
+    for shift in range(1, head_axis):
+        squares.append(lax.ppermute(square, "head", [(i, (i + shift) % head_axis) for i in range(head_axis)]))
 
     slab_out, user_out = pl.pallas_call(
         functools.partial(norm_kernel, float(width * head_axis), chunks),
         out_shape=[bf16((token_count, width)), bf16((user_rows, width))],
-        in_specs=[vmem] * 5,
+        in_specs=[vmem] * (3 + head_axis),
         out_specs=[hbm] * 2,
         scratch_shapes=[
             pltpu.VMEM((token_count, width), jnp.bfloat16),
@@ -409,7 +411,7 @@
             pltpu.SemaphoreType.DMA((lines, chunks)),
         ],
         compiler_params=params,
-    )(slab_total, user_total, norm_gain.reshape(1, width), square, mate)
+    )(slab_total, user_total, norm_gain.reshape(1, width), *squares)
     return slab_out, user_out.reshape(user_count, suffix, width)
 
 

time: 37 us -> 36.8 us (level)
  waiting for transfers between devices: 6.23 us -> 4.82 us
  starting transfers between devices: 14 us -> 15.2 us
    ppermute x2 -> x3, waiting for transfers between devices: 3.65 us -> 2.24 us  [local(): lax.ppermute(square, 'head', [(i, (i + shift) % head_axis) for i in range...]
    ppermute x2 -> x3, starting transfers between devices: 4.51 us -> 5.71 us  [local(): lax.ppermute(square, 'head', [(i, (i + shift) % head_axis) for i in range...]
  transfers between devices with their start and end apart: 12 -> 13, of which waited for: 6 -> 6; matrix products, arithmetic and copies ran while one was open for 0% -> 0% of each run, Pallas kernels for 32% -> 32%
where the time goes in v13:
time: 36.8 us; the launch traced here: 36.6 us
  Pallas kernels  15.8 us (43%)
  starting transfers between devices  15.2 us (41%)
  waiting for transfers between devices  4.82 us (13%)
  between operations  0.77 us (2%)
    ppermute x10, starting transfers between devices, swap(): lax.ppermute(value, 'seq', [(i, i ^ 1 << (other if i & 1 else bit)) for i...  9.49 us
    ppermute x3, starting transfers between devices, local(): lax.ppermute(square, 'head', [(i, (i + shift) % head_axis) for i in range...  5.71 us
    pallas_call x2, Pallas kernels, read(): pl.pallas_call(functools.partial(read_kernel, depth, suffix, groups, ahea...  4.8 us
    pallas_call x1, Pallas kernels, local(): pl.pallas_call(functools.partial(load_kernel, suffix), out_shape=[pltpu.V...  2.59 us
    ppermute x10, waiting for transfers between devices, swap(): lax.ppermute(value, 'seq', [(i, i ^ 1 << (other if i & 1 else bit)) for i...  2.58 us
    ppermute x3, waiting for transfers between devices, local(): lax.ppermute(square, 'head', [(i, (i + shift) % head_axis) for i in range...  2.24 us
    pallas_call x1, Pallas kernels, local(): pl.pallas_call(functools.partial(user_kernel, suffix), out_shape=[pltpu.V...  2.22 us
    pallas_call x1, Pallas kernels, local(): pl.pallas_call(scale_kernel, out_shape=[pltpu.VMEM((levels, token_count,...  1.88 us
  transfers between devices with their start and end apart: 13, of which 6 were waited for; matrix products, arithmetic and copies ran while one was open for 0% of the time, Pallas kernels for 32%

profile of v13, /device:TPU:0, one launch (start us, length us, event | category | flops | bytes accessed | tf_op | source)
XLA Modules:
  0.0 36.6 jit_solution(5595699321119800194)
XLA Ops:
  0.6 1.6 %shard_map.113 = (bf16[8,128,128]{2,1,0:T(8,128)(2,1)S(1)}, bf16[8,128,128]{2,1,0:T(8,128)(2,1)S(1)}, bf16[2,128,1024]{2,1,0:T(8,128)(2,1)S(1)}, bf16[2,128,1024]{2,1,0:T(8,128)(2,1)S(1)}) custom-call(bf16[128,2048]{1,0:T(8,128)(2,1)} %key_hbm.1, bf16[128,2048]{1,0:T(8,128)(2,1)} %value_hbm.1), custom_call_target="tpu_custom_call" | custom-call | tf_op jit(solution)/shard_map/pallas_call | solution.py:284
  2.2 3.0 %collective-permute-start = (bf16[8,128,128]{2,1,0:T(8,128)(2,1)S(1)}, bf16[8,128,128]{2,1,0:T(8,128)(2,1)S(1)}, u32[]{:S(2)}, u32[]{:S(2)}) collective-permute-start(bf16[8,128,128]{2,1,0:T(8,128)(2,1)S(1)} %get-tuple-element.54.refs_6_), channel_id=1, source_target_pairs={{0,8},{4,20},{8,0},{12,28},{16,24},{20,4},{24,16},{28,12},{1,9},{5... | collective-permute-start | bytes 786440 | tf_op jit(solution)/shard_map/ppermute | solution.py:267
  5.2 1.5 %collective-permute-start.1 = (bf16[8,128,128]{2,1,0:T(8,128)(2,1)S(1)}, bf16[8,128,128]{2,1,0:T(8,128)(2,1)S(1)}, u32[]{:S(2)}, u32[]{:S(2)}) collective-permute-start(bf16[8,128,128]{2,1,0:T(8,128)(2,1)S(1)} %get-tuple-element.53.refs_7_), channel_id=1, source_target_pairs={{0,16},{4,12},{8,24},{12,4},{16,0},{20,28},{24,8},{28,20},{1,17},{... | collective-permute-start | bytes 786440 | tf_op jit(solution)/shard_map/ppermute | solution.py:267
  6.8 2.6 %shard_map.114 = (f32[128,64]{1,0:T(8,128)S(1)}, f32[256,64]{1,0:T(8,128)S(1)}, bf16[128,2048]{1,0:T(8,128)(2,1)S(1)}, s32[4]{0:T(128)S(1)}, f32[128,2048]{1,0:T...) custom-call(bf16[96,128]{1,0:T(8,128)(2,1)} %bitcast.10, bf16[4,96,64]{2,1,0:T(8,128)(2,1)} %bitcast.9, ...), custom_call_target="tpu_custom_call" | custom-call | tf_op jit(solution)/shard_map/pallas_call | solution.py:304
  9.4 0.1 collective-permute-start.2
  9.4 0.6 %collective-permute-start.4 = (bf16[8,128,128]{2,1,0:T(8,128)(2,1)S(1)}, bf16[8,128,128]{2,1,0:T(8,128)(2,1)S(1)}, u32[]{:S(2)}, u32[]{:S(2)}) collective-permute-start(bf16[8,128,128]{2,1,0:T(8,128)(2,1)S(1)} %get-tuple-element.54.refs_6_), channel_id=1, source_target_pairs={{0,16},{4,12},{8,24},{12,4},{16,0},{20,28},{24,8},{28,20},{1,17},{... | collective-permute-start | bytes 786440 | tf_op jit(solution)/shard_map/ppermute | solution.py:267
  10.0 0.1 collective-permute-start.3
  10.1 1.9 %shard_map.115 = (bf16[4,128,2048]{2,1,0:T(8,128)(2,1)S(1)}, bf16[256,2048]{1,0:T(8,128)(2,1)S(1)}, bf16[256,2048]{1,0:T(8,128)(2,1)S(1)}, bf16[256,2048]{1,0:T(8,128)(2,1)S(1)}) custom-call(bf16[256,2048]{1,0:T(8,128)(2,1)} %bitcast.6, bf16[256,2048]{1,0:T(8,128)(2,1)} %bitcast.7, bf16[256,2048]{1,0:T(8,128)(2,1)} %bitcast.8, ...), custom_call_target="tpu_custom_call" | custom-call | tf_op jit(solution)/shard_map/pallas_call | solution.py:328
  12.0 0.0 collective-permute-done.refs_0_
  12.0 0.0 collective-permute-done.1.refs_1_
  12.0 2.0 %collective-permute-start.7 = (bf16[8,128,128]{2,1,0:T(8,128)(2,1)S(1)}, bf16[8,128,128]{2,1,0:T(8,128)(2,1)S(1)}, u32[]{:S(2)}, u32[]{:S(2)}) collective-permute-start(bf16[8,128,128]{2,1,0:T(8,128)(2,1)S(1)} %collective-permute-done.refs_0_), channel_id=1, source_target_pairs={{0,16},{4,12},{8,24},{12,4},{16,0},{20,28},{24,8},{28,20},{1,17},{... | collective-permute-start | bytes 786440 | tf_op jit(solution)/shard_map/ppermute | solution.py:267
  14.1 1.9 %collective-permute-start.8 = (bf16[8,128,128]{2,1,0:T(8,128)(2,1)S(1)}, bf16[8,128,128]{2,1,0:T(8,128)(2,1)S(1)}, u32[]{:S(2)}, u32[]{:S(2)}) collective-permute-start(bf16[8,128,128]{2,1,0:T(8,128)(2,1)S(1)} %collective-permute-done.1.refs_1_), channel_id=1, source_target_pairs={{0,8},{4,20},{8,0},{12,28},{16,24},{20,4},{24,16},{28,12},{1,9},{5... | collective-permute-start | bytes 786440 | tf_op jit(solution)/shard_map/ppermute | solution.py:267
  15.9 2.2 %shard_map.116 = (f32[256,2048]{1,0:T(8,128)S(1)}, bf16[4,256,2048]{2,1,0:T(8,128)(2,1)S(1)}) custom-call(f32[256,64]{1,0:T(8,128)S(1)} %get-tuple-element.45.w_ref, bf16[256,2048]{1,0:T(8,128)(2,1)S(1)} %get-tuple-element.46.q_ref, bf16[256,2048]{1,0:T(8,128)(2,1)S(1)} %get-tuple-element.47.k_ref, bf16[256,2048]{1,0:T(8,128)(2,1)S(1)} %get-tuple-element.48.v_ref), custom_call_target="tpu_custom_call" | custom-call | tf_op jit(solution)/shard_map/pallas_call | solution.py:349
  18.2 0.5 %collective-permute-done.4.refs_0_ = bf16[8,128,128]{2,1,0:T(8,128)(2,1)S(1)} collective-permute-done((bf16[8,128,128]{2,1,0:T(8,128)(2,1)S(1)}, bf16[8,128,128]{2,1,0:T(8,128)(2,1)S(1)}, u32[]{:S(2)}, u32[]{:S(2)}) %collective-permute-start.4) | collective-permute-done | bytes 262176 | tf_op jit(solution)/shard_map/ppermute | solution.py:267
  18.7 0.1 collective-permute-start.6
  18.8 0.4 %collective-permute-done.3.refs_1_ = bf16[8,128,128]{2,1,0:T(8,128)(2,1)S(1)} collective-permute-done((bf16[8,128,128]{2,1,0:T(8,128)(2,1)S(1)}, bf16[8,128,128]{2,1,0:T(8,128)(2,1)S(1)}, u32[]{:S(2)}, u32[]{:S(2)}) %collective-permute-start.3) | collective-permute-done | bytes 262176 | tf_op jit(solution)/shard_map/ppermute | solution.py:267
  19.3 0.2 collective-permute-start.5
  19.4 0.0 collective-permute-done.2.rest_1_
  19.4 3.2 %shard_map.119 = (f32[128,2048]{1,0:T(8,128)S(1)}, f32[256,2048]{1,0:T(8,128)S(1)}, bf16[128,4096]{1,0:T(8,128)(2,1)S(1)}, bf16[256,4096]{1,0:T(8,128)(2,1)S(1)}) custom-call(s32[4]{0:T(128)S(1)} %get-tuple-element.38.length_ref, bf16[4,128,2048]{2,1,0:T(8,128)(2,1)S(1)} %get-tuple-element.41.ss_ref, bf16[4,256,2048]{2,1,0:T(8,128)(2,1)S(1)} %get-tuple-element.49.us_ref, ...), custom_call_target="tpu_custom_call" | custom-call | tf_op jit(solution)/shard_map/pallas_call | solution.py:367
  22.6 1.4 %collective-permute-done.7.refs_0_ = bf16[8,128,128]{2,1,0:T(8,128)(2,1)S(1)} collective-permute-done((bf16[8,128,128]{2,1,0:T(8,128)(2,1)S(1)}, bf16[8,128,128]{2,1,0:T(8,128)(2,1)S(1)}, u32[]{:S(2)}, u32[]{:S(2)}) %collective-permute-start.7) | collective-permute-done | bytes 262176 | tf_op jit(solution)/shard_map/ppermute | solution.py:267
  24.0 0.0 collective-permute-done.8.refs_1_
  24.1 0.1 collective-permute-start.9
  24.2 0.0 collective-permute-done.6.rest_1_
  24.2 0.0 collective-permute-done.5.rest_0_
  24.2 1.6 %shard_map.120 = (f32[128,2048]{1,0:T(8,128)S(1)}, f32[256,2048]{1,0:T(8,128)S(1)}) custom-call(s32[4]{0:T(128)S(1)} %get-tuple-element.38.length_ref, bf16[4,128,2048]{2,1,0:T(8,128)(2,1)S(1)} %get-tuple-element.41.ss_ref, bf16[4,256,2048]{2,1,0:T(8,128)(2,1)S(1)} %get-tuple-element.49.us_ref, f32[128,2048]{1,0:T(8,128)S(1)} %get-tuple-element.57.sa_ref.order_ref, ...), custom_call_target="tpu_custom_call" | custom-call | tf_op jit(solution)/shard_map/pallas_call | solution.py:367
  25.8 0.2 collective-permute-done.9.mate_ref
  26.1 0.0 copy-start
  26.1 1.1 %shard_map.122 = (f32[128,2048]{1,0:T(8,128)S(1)}, f32[256,2048]{1,0:T(8,128)S(1)}, f32[8,128]{1,0:T(8,128)S(1)}) custom-call(bf16[128,4096]{1,0:T(8,128)(2,1)S(1)} %get-tuple-element.55.ss_ref, bf16[256,4096]{1,0:T(8,128)(2,1)S(1)} %get-tuple-element.56.us_ref, f32[128,2048]{1,0:T(8,128)S(1)} %get-tuple-element.59.sa_ref, ...), custom_call_target="tpu_custom_call" | custom-call | tf_op jit(solution)/shard_map/pallas_call | solution.py:390
  27.1 1.8 %collective-permute-start.10 = (f32[8,128]{1,0:T(8,128)S(1)}, f32[8,128]{1,0:T(8,128)S(1)}, u32[]{:S(2)}, u32[]{:S(2)}) collective-permute-start(f32[8,128]{1,0:T(8,128)S(1)} %get-tuple-element.63.rest_0_), channel_id=1, source_target_pairs={{0,1},{1,2},{2,3},{3,0},{4,5},{5,6},{6,7},{7,4},{8,9},{9,10},{10,1... | collective-permute-start | bytes 12296 | tf_op jit(solution)/shard_map/ppermute | solution.py:401
  28.9 2.6 %collective-permute-start.11 = (f32[8,128]{1,0:T(8,128)S(1)}, f32[8,128]{1,0:T(8,128)S(1)}, u32[]{:S(2)}, u32[]{:S(2)}) collective-permute-start(f32[8,128]{1,0:T(8,128)S(1)} %get-tuple-element.63.rest_0_), channel_id=1, source_target_pairs={{0,2},{1,3},{2,0},{3,1},{4,6},{5,7},{6,4},{7,5},{8,10},{9,11},{10,... | collective-permute-start | bytes 12296 | tf_op jit(solution)/shard_map/ppermute | solution.py:401
  31.5 1.3 %collective-permute-start.12 = (f32[8,128]{1,0:T(8,128)S(1)}, f32[8,128]{1,0:T(8,128)S(1)}, u32[]{:S(2)}, u32[]{:S(2)}) collective-permute-start(f32[8,128]{1,0:T(8,128)S(1)} %get-tuple-element.63.rest_0_), channel_id=1, source_target_pairs={{0,3},{1,0},{2,1},{3,2},{4,7},{5,4},{6,5},{7,6},{8,11},{9,8},{10,9... | collective-permute-start | bytes 12296 | tf_op jit(solution)/shard_map/ppermute | solution.py:401
  32.9 0.0 copy-done
  32.9 0.0 collective-permute-done.10.rest_1_
  32.9 0.6 %collective-permute-done.11.rest_2_ = f32[8,128]{1,0:T(8,128)S(1)} collective-permute-done((f32[8,128]{1,0:T(8,128)S(1)}, f32[8,128]{1,0:T(8,128)S(1)}, u32[]{:S(2)}, u32[]{:S(2)}) %collective-permute-start.11) | collective-permute-done | bytes 4128 | tf_op jit(solution)/shard_map/ppermute | solution.py:401
  33.4 1.7 %collective-permute-done.12.rest_3_ = f32[8,128]{1,0:T(8,128)S(1)} collective-permute-done((f32[8,128]{1,0:T(8,128)S(1)}, f32[8,128]{1,0:T(8,128)S(1)}, u32[]{:S(2)}, u32[]{:S(2)}) %collective-permute-start.12) | collective-permute-done | bytes 4128 | tf_op jit(solution)/shard_map/ppermute | solution.py:401
  35.1 1.5 %shard_map.123 = (bf16[128,2048]{1,0:T(8,128)(2,1)}, bf16[256,2048]{1,0:T(8,128)(2,1)}) custom-call(f32[128,2048]{1,0:T(8,128)S(1)} %get-tuple-element.61.st_ref, f32[256,2048]{1,0:T(8,128)S(1)} %get-tuple-element.62.ut_ref, bf16[1,2048]{1,0:T(2,128)(2,1)S(1)} %reshape.30.gain_ref, f32[8,128]{1,0:T(8,128)S(1)} %get-tuple-element.63.rest_0_, ...), custom_call_target="tpu_custom_call" | custom-call | tf_op jit(solution)/shard_map/pallas_call | solution.py:403
  (4 shorter events, 0.1 us)
Async XLA Ops:
  2.2 9.8 %collective-permute-start = (bf16[8,128,128]{2,1,0:T(8,128)(2,1)S(1)}, bf16[8,128,128]{2,1,0:T(8,128)(2,1)S(1)}, u32[]{:S(2)}, u32[]{:S(2)}) collective-permute-start(bf16[8,128,128]{2,1,0:T(8,128)(2,1)S(1)} %get-tuple-element.54.refs_6_), channel_id=1, source_target_pairs={{0,8},{4,20},{8,0},{12,28},{16,24},{20,4},{24,16},{28,12},{1,9},{5... | collective-permute-start | bytes 786440 | tf_op jit(solution)/shard_map/ppermute | solution.py:267
  5.2 6.8 %collective-permute-start.1 = (bf16[8,128,128]{2,1,0:T(8,128)(2,1)S(1)}, bf16[8,128,128]{2,1,0:T(8,128)(2,1)S(1)}, u32[]{:S(2)}, u32[]{:S(2)}) collective-permute-start(bf16[8,128,128]{2,1,0:T(8,128)(2,1)S(1)} %get-tuple-element.53.refs_7_), channel_id=1, source_target_pairs={{0,16},{4,12},{8,24},{12,4},{16,0},{20,28},{24,8},{28,20},{1,17},{... | collective-permute-start | bytes 786440 | tf_op jit(solution)/shard_map/ppermute | solution.py:267
  9.4 10.1 %collective-permute-start.2 = (bf16[1,16,128,128]{3,2,1,0:T(8,128)(2,1)S(1)}, bf16[1,16,128,128]{3,2,1,0:T(8,128)(2,1)S(1)}, u32[]{:S(2)}, u32[]{:S(2)}) collective-permute-start(bf16[1,16,128,128]{3,2,1,0:T(8,128)(2,1)S(1)} %get-tuple-element.52.rest_0_), channel_id=1, source_target_pairs={{0,4},{4,0},{8,12},{12,8},{16,20},{20,16},{24,28},{28,24},{1,5},{5... | collective-permute-start | bytes 1572872 | tf_op jit(solution)/shard_map/ppermute | solution.py:267
  9.4 9.2 %collective-permute-start.4 = (bf16[8,128,128]{2,1,0:T(8,128)(2,1)S(1)}, bf16[8,128,128]{2,1,0:T(8,128)(2,1)S(1)}, u32[]{:S(2)}, u32[]{:S(2)}) collective-permute-start(bf16[8,128,128]{2,1,0:T(8,128)(2,1)S(1)} %get-tuple-element.54.refs_6_), channel_id=1, source_target_pairs={{0,16},{4,12},{8,24},{12,4},{16,0},{20,28},{24,8},{28,20},{1,17},{... | collective-permute-start | bytes 786440 | tf_op jit(solution)/shard_map/ppermute | solution.py:267
  10.0 9.2 %collective-permute-start.3 = (bf16[8,128,128]{2,1,0:T(8,128)(2,1)S(1)}, bf16[8,128,128]{2,1,0:T(8,128)(2,1)S(1)}, u32[]{:S(2)}, u32[]{:S(2)}) collective-permute-start(bf16[8,128,128]{2,1,0:T(8,128)(2,1)S(1)} %get-tuple-element.53.refs_7_), channel_id=1, source_target_pairs={{0,8},{4,20},{8,0},{12,28},{16,24},{20,4},{24,16},{28,12},{1,9},{5... | collective-permute-start | bytes 786440 | tf_op jit(solution)/shard_map/ppermute | solution.py:267
  12.0 12.0 %collective-permute-start.7 = (bf16[8,128,128]{2,1,0:T(8,128)(2,1)S(1)}, bf16[8,128,128]{2,1,0:T(8,128)(2,1)S(1)}, u32[]{:S(2)}, u32[]{:S(2)}) collective-permute-start(bf16[8,128,128]{2,1,0:T(8,128)(2,1)S(1)} %collective-permute-done.refs_0_), channel_id=1, source_target_pairs={{0,16},{4,12},{8,24},{12,4},{16,0},{20,28},{24,8},{28,20},{1,17},{... | collective-permute-start | bytes 786440 | tf_op jit(solution)/shard_map/ppermute | solution.py:267
  14.1 10.0 %collective-permute-start.8 = (bf16[8,128,128]{2,1,0:T(8,128)(2,1)S(1)}, bf16[8,128,128]{2,1,0:T(8,128)(2,1)S(1)}, u32[]{:S(2)}, u32[]{:S(2)}) collective-permute-start(bf16[8,128,128]{2,1,0:T(8,128)(2,1)S(1)} %collective-permute-done.1.refs_1_), channel_id=1, source_target_pairs={{0,8},{4,20},{8,0},{12,28},{16,24},{20,4},{24,16},{28,12},{1,9},{5... | collective-permute-start | bytes 786440 | tf_op jit(solution)/shard_map/ppermute | solution.py:267
  18.7 5.4 %collective-permute-start.6 = (bf16[1,16,128,128]{3,2,1,0:T(8,128)(2,1)S(1)}, bf16[1,16,128,128]{3,2,1,0:T(8,128)(2,1)S(1)}, u32[]{:S(2)}, u32[]{:S(2)}) collective-permute-start(bf16[1,16,128,128]{3,2,1,0:T(8,128)(2,1)S(1)} %shard_map.118.rest_3_), channel_id=1, source_target_pairs={{0,4},{4,0},{8,12},{12,8},{16,20},{20,16},{24,28},{28,24},{1,5},{5... | collective-permute-start | bytes 1572872 | tf_op jit(solution)/shard_map/ppermute | solution.py:267
  19.3 4.9 %collective-permute-start.5 = (bf16[1,16,128,128]{3,2,1,0:T(8,128)(2,1)S(1)}, bf16[1,16,128,128]{3,2,1,0:T(8,128)(2,1)S(1)}, u32[]{:S(2)}, u32[]{:S(2)}) collective-permute-start(bf16[1,16,128,128]{3,2,1,0:T(8,128)(2,1)S(1)} %shard_map.117.rest_2_), channel_id=1, source_target_pairs={{0,4},{4,0},{8,12},{12,8},{16,20},{20,16},{24,28},{28,24},{1,5},{5... | collective-permute-start | bytes 1572872 | tf_op jit(solution)/shard_map/ppermute | solution.py:267
  24.1 2.0 %collective-permute-start.9 = (bf16[1,16,128,128]{3,2,1,0:T(8,128)(2,1)S(1)}, bf16[1,16,128,128]{3,2,1,0:T(8,128)(2,1)S(1)}, u32[]{:S(2)}, u32[]{:S(2)}) collective-permute-start(bf16[1,16,128,128]{3,2,1,0:T(8,128)(2,1)S(1)} %shard_map.121.state_ref), channel_id=1, source_target_pairs={{0,4},{4,0},{8,12},{12,8},{16,20},{20,16},{24,28},{28,24},{1,5},{5... | collective-permute-start | bytes 1572872 | tf_op jit(solution)/shard_map/ppermute | solution.py:267
  26.1 6.8 %copy-start = (bf16[2048]{0:T(1024)(128)(2,1)S(1)}, bf16[2048]{0:T(1024)(128)(2,1)}, u32[]{:S(2)}) copy-start(bf16[2048]{0:T(1024)(128)(2,1)} %param.14) | copy-start | bytes 12292
  27.1 5.7 %collective-permute-start.10 = (f32[8,128]{1,0:T(8,128)S(1)}, f32[8,128]{1,0:T(8,128)S(1)}, u32[]{:S(2)}, u32[]{:S(2)}) collective-permute-start(f32[8,128]{1,0:T(8,128)S(1)} %get-tuple-element.63.rest_0_), channel_id=1, source_target_pairs={{0,1},{1,2},{2,3},{3,0},{4,5},{5,6},{6,7},{7,4},{8,9},{9,10},{10,1... | collective-permute-start | bytes 12296 | tf_op jit(solution)/shard_map/ppermute | solution.py:401
  28.9 4.5 %collective-permute-start.11 = (f32[8,128]{1,0:T(8,128)S(1)}, f32[8,128]{1,0:T(8,128)S(1)}, u32[]{:S(2)}, u32[]{:S(2)}) collective-permute-start(f32[8,128]{1,0:T(8,128)S(1)} %get-tuple-element.63.rest_0_), channel_id=1, source_target_pairs={{0,2},{1,3},{2,0},{3,1},{4,6},{5,7},{6,4},{7,5},{8,10},{9,11},{10,... | collective-permute-start | bytes 12296 | tf_op jit(solution)/shard_map/ppermute | solution.py:401
  31.5 3.6 %collective-permute-start.12 = (f32[8,128]{1,0:T(8,128)S(1)}, f32[8,128]{1,0:T(8,128)S(1)}, u32[]{:S(2)}, u32[]{:S(2)}) collective-permute-start(f32[8,128]{1,0:T(8,128)S(1)} %get-tuple-element.63.rest_0_), channel_id=1, source_target_pairs={{0,3},{1,0},{2,1},{3,2},{4,7},{5,4},{6,5},{7,6},{8,11},{9,8},{10,9... | collective-permute-start | bytes 12296 | tf_op jit(solution)/shard_map/ppermute | solution.py:401

commit v14 on v13

--- a/solution.py
+++ b/solution.py
@@ -374,7 +374,8 @@
             cost_estimate=cost(0, 0),
         )(lengths, slab_scaled, user_scaled, *accs, *[whole[m] for m in offsets])
 
-    whole = {0: state, 1: swap(state, 0)}
+    other = [swap(halves[side], 0) for side in (1, 0)]
+    whole = {0: state, 1: join(user_acc, other)}
     direct = [1 << bit for bit in outer]
     for m in direct:
         whole[m] = join(user_acc, sides[m])

time: 36.8 us -> 37.7 us (1.024)
  starting transfers between devices: 15.2 us -> 15.9 us
    ppermute x10 -> x11, starting transfers between devices: 9.49 us -> 10.3 us  [swap(): lax.ppermute(value, 'seq', [(i, i ^ 1 << (other if i & 1 else bit)) for i...]
    ppermute x10 -> x11, waiting for transfers between devices: 2.58 us -> 2.84 us  [swap(): lax.ppermute(value, 'seq', [(i, i ^ 1 << (other if i & 1 else bit)) for i...]
  transfers between devices with their start and end apart: 13 -> 14, of which waited for: 6 -> 4; matrix products, arithmetic and copies ran while one was open for 0% -> 0% of each run, Pallas kernels for 32% -> 31%
where the time goes in v14:
time: 37.7 us; the launch traced here: 37.5 us
  starting transfers between devices  15.9 us (42%)
  Pallas kernels  15.8 us (42%)
  waiting for transfers between devices  5.08 us (13%)
  between operations  0.78 us (2%)
    ppermute x11, starting transfers between devices, swap(): lax.ppermute(value, 'seq', [(i, i ^ 1 << (other if i & 1 else bit)) for i...  10.3 us
    ppermute x3, starting transfers between devices, local(): lax.ppermute(square, 'head', [(i, (i + shift) % head_axis) for i in range...  5.57 us
    pallas_call x2, Pallas kernels, read(): pl.pallas_call(functools.partial(read_kernel, depth, suffix, groups, ahea...  4.75 us
    ppermute x11, waiting for transfers between devices, swap(): lax.ppermute(value, 'seq', [(i, i ^ 1 << (other if i & 1 else bit)) for i...  2.84 us
    pallas_call x1, Pallas kernels, local(): pl.pallas_call(functools.partial(load_kernel, suffix), out_shape=[pltpu.V...  2.59 us
    ppermute x3, waiting for transfers between devices, local(): lax.ppermute(square, 'head', [(i, (i + shift) % head_axis) for i in range...  2.24 us
    pallas_call x1, Pallas kernels, local(): pl.pallas_call(functools.partial(user_kernel, suffix), out_shape=[pltpu.V...  2.22 us
    pallas_call x1, Pallas kernels, local(): pl.pallas_call(scale_kernel, out_shape=[pltpu.VMEM((levels, token_count,...  1.88 us
  transfers between devices with their start and end apart: 14, of which 4 were waited for; matrix products, arithmetic and copies ran while one was open for 0% of the time, Pallas kernels for 31%

profile of v14, /device:TPU:0, one launch (start us, length us, event | category | flops | bytes accessed | tf_op | source)
XLA Modules:
  0.0 37.5 jit_solution(14106620715026888149)
XLA Ops:
  0.6 1.6 %shard_map.113 = (bf16[8,128,128]{2,1,0:T(8,128)(2,1)S(1)}, bf16[8,128,128]{2,1,0:T(8,128)(2,1)S(1)}, bf16[2,128,1024]{2,1,0:T(8,128)(2,1)S(1)}, bf16[2,128,1024]{2,1,0:T(8,128)(2,1)S(1)}) custom-call(bf16[128,2048]{1,0:T(8,128)(2,1)} %key_hbm.1, bf16[128,2048]{1,0:T(8,128)(2,1)} %value_hbm.1), custom_call_target="tpu_custom_call" | custom-call | tf_op jit(solution)/shard_map/pallas_call | solution.py:284
  2.2 3.0 %collective-permute-start = (bf16[8,128,128]{2,1,0:T(8,128)(2,1)S(1)}, bf16[8,128,128]{2,1,0:T(8,128)(2,1)S(1)}, u32[]{:S(2)}, u32[]{:S(2)}) collective-permute-start(bf16[8,128,128]{2,1,0:T(8,128)(2,1)S(1)} %get-tuple-element.54.refs_6_), channel_id=1, source_target_pairs={{0,8},{4,20},{8,0},{12,28},{16,24},{20,4},{24,16},{28,12},{1,9},{5... | collective-permute-start | bytes 786440 | tf_op jit(solution)/shard_map/ppermute | solution.py:267
  5.2 1.5 %collective-permute-start.1 = (bf16[8,128,128]{2,1,0:T(8,128)(2,1)S(1)}, bf16[8,128,128]{2,1,0:T(8,128)(2,1)S(1)}, u32[]{:S(2)}, u32[]{:S(2)}) collective-permute-start(bf16[8,128,128]{2,1,0:T(8,128)(2,1)S(1)} %get-tuple-element.53.refs_7_), channel_id=1, source_target_pairs={{0,16},{4,12},{8,24},{12,4},{16,0},{20,28},{24,8},{28,20},{1,17},{... | collective-permute-start | bytes 786440 | tf_op jit(solution)/shard_map/ppermute | solution.py:267
  6.8 2.6 %shard_map.114 = (f32[128,64]{1,0:T(8,128)S(1)}, f32[256,64]{1,0:T(8,128)S(1)}, bf16[128,2048]{1,0:T(8,128)(2,1)S(1)}, s32[4]{0:T(128)S(1)}, f32[128,2048]{1,0:T...) custom-call(bf16[96,128]{1,0:T(8,128)(2,1)} %bitcast.10, bf16[4,96,64]{2,1,0:T(8,128)(2,1)} %bitcast.9, ...), custom_call_target="tpu_custom_call" | custom-call | tf_op jit(solution)/shard_map/pallas_call | solution.py:304
  9.4 0.6 %collective-permute-start.5 = (bf16[8,128,128]{2,1,0:T(8,128)(2,1)S(1)}, bf16[8,128,128]{2,1,0:T(8,128)(2,1)S(1)}, u32[]{:S(2)}, u32[]{:S(2)}) collective-permute-start(bf16[8,128,128]{2,1,0:T(8,128)(2,1)S(1)} %get-tuple-element.54.refs_6_), channel_id=1, source_target_pairs={{0,16},{4,12},{8,24},{12,4},{16,0},{20,28},{24,8},{28,20},{1,17},{... | collective-permute-start | bytes 786440 | tf_op jit(solution)/shard_map/ppermute | solution.py:267
  9.9 0.1 collective-permute-start.4
  10.0 0.0 collective-permute-start.2
  10.1 1.9 %shard_map.115 = (bf16[4,128,2048]{2,1,0:T(8,128)(2,1)S(1)}, bf16[256,2048]{1,0:T(8,128)(2,1)S(1)}, bf16[256,2048]{1,0:T(8,128)(2,1)S(1)}, bf16[256,2048]{1,0:T(8,128)(2,1)S(1)}) custom-call(bf16[256,2048]{1,0:T(8,128)(2,1)} %bitcast.6, bf16[256,2048]{1,0:T(8,128)(2,1)} %bitcast.7, bf16[256,2048]{1,0:T(8,128)(2,1)} %bitcast.8, ...), custom_call_target="tpu_custom_call" | custom-call | tf_op jit(solution)/shard_map/pallas_call | solution.py:328
  11.9 0.0 collective-permute-done.refs_0_
  12.0 0.6 %collective-permute-start.3 = (bf16[8,128,128]{2,1,0:T(8,128)(2,1)S(1)}, bf16[8,128,128]{2,1,0:T(8,128)(2,1)S(1)}, u32[]{:S(2)}, u32[]{:S(2)}) collective-permute-start(bf16[8,128,128]{2,1,0:T(8,128)(2,1)S(1)} %get-tuple-element.54.refs_6_), channel_id=1, source_target_pairs={{0,4},{4,0},{8,12},{12,8},{16,20},{20,16},{24,28},{28,24},{1,5},{5... | collective-permute-start | bytes 786440 | tf_op jit(solution)/shard_map/ppermute | solution.py:267
  12.5 0.0 collective-permute-done.1.refs_1_
  12.5 2.1 %collective-permute-start.8 = (bf16[8,128,128]{2,1,0:T(8,128)(2,1)S(1)}, bf16[8,128,128]{2,1,0:T(8,128)(2,1)S(1)}, u32[]{:S(2)}, u32[]{:S(2)}) collective-permute-start(bf16[8,128,128]{2,1,0:T(8,128)(2,1)S(1)} %collective-permute-done.refs_0_), channel_id=1, source_target_pairs={{0,16},{4,12},{8,24},{12,4},{16,0},{20,28},{24,8},{28,20},{1,17},{... | collective-permute-start | bytes 786440 | tf_op jit(solution)/shard_map/ppermute | solution.py:267
  14.7 2.6 %collective-permute-done.5.refs_0_ = bf16[8,128,128]{2,1,0:T(8,128)(2,1)S(1)} collective-permute-done((bf16[8,128,128]{2,1,0:T(8,128)(2,1)S(1)}, bf16[8,128,128]{2,1,0:T(8,128)(2,1)S(1)}, u32[]{:S(2)}, u32[]{:S(2)}) %collective-permute-start.5) | collective-permute-done | bytes 262176 | tf_op jit(solution)/shard_map/ppermute | solution.py:267
  17.2 1.7 %collective-permute-start.9 = (bf16[8,128,128]{2,1,0:T(8,128)(2,1)S(1)}, bf16[8,128,128]{2,1,0:T(8,128)(2,1)S(1)}, u32[]{:S(2)}, u32[]{:S(2)}) collective-permute-start(bf16[8,128,128]{2,1,0:T(8,128)(2,1)S(1)} %collective-permute-done.1.refs_1_), channel_id=1, source_target_pairs={{0,8},{4,20},{8,0},{12,28},{16,24},{20,4},{24,16},{28,12},{1,9},{5... | collective-permute-start | bytes 786440 | tf_op jit(solution)/shard_map/ppermute | solution.py:267
  18.9 2.2 %shard_map.116 = (f32[256,2048]{1,0:T(8,128)S(1)}, bf16[4,256,2048]{2,1,0:T(8,128)(2,1)S(1)}) custom-call(f32[256,64]{1,0:T(8,128)S(1)} %get-tuple-element.45.w_ref, bf16[256,2048]{1,0:T(8,128)(2,1)S(1)} %get-tuple-element.46.q_ref, bf16[256,2048]{1,0:T(8,128)(2,1)S(1)} %get-tuple-element.47.k_ref, bf16[256,2048]{1,0:T(8,128)(2,1)S(1)} %get-tuple-element.48.v_ref), custom_call_target="tpu_custom_call" | custom-call | tf_op jit(solution)/shard_map/pallas_call | solution.py:349
  21.2 0.0 collective-permute-done.4.refs_1_
  21.2 0.1 collective-permute-start.7
  21.3 0.0 collective-permute-done.2.refs_0_
  21.4 0.6 %collective-permute-start.6 = (bf16[1,16,128,128]{3,2,1,0:T(8,128)(2,1)S(1)}, bf16[1,16,128,128]{3,2,1,0:T(8,128)(2,1)S(1)}, u32[]{:S(2)}, u32[]{:S(2)}) collective-permute-start(bf16[1,16,128,128]{3,2,1,0:T(8,128)(2,1)S(1)} %shard_map.118.rest_2_), channel_id=1, source_target_pairs={{0,4},{4,0},{8,12},{12,8},{16,20},{20,16},{24,28},{28,24},{1,5},{5... | collective-permute-start | bytes 1572872 | tf_op jit(solution)/shard_map/ppermute | solution.py:267
  21.9 0.0 collective-permute-done.3.refs_1_
  22.0 3.1 %shard_map.120 = (f32[128,2048]{1,0:T(8,128)S(1)}, f32[256,2048]{1,0:T(8,128)S(1)}, bf16[128,4096]{1,0:T(8,128)(2,1)S(1)}, bf16[256,4096]{1,0:T(8,128)(2,1)S(1)}) custom-call(s32[4]{0:T(128)S(1)} %get-tuple-element.38.length_ref, bf16[4,128,2048]{2,1,0:T(8,128)(2,1)S(1)} %get-tuple-element.41.ss_ref, bf16[4,256,2048]{2,1,0:T(8,128)(2,1)S(1)} %get-tuple-element.49.us_ref, ...), custom_call_target="tpu_custom_call" | custom-call | tf_op jit(solution)/shard_map/pallas_call | solution.py:367
  25.1 0.0 collective-permute-done.8.refs_0_
  25.1 0.0 collective-permute-done.9.refs_1_
  25.2 0.1 collective-permute-start.10
  25.3 0.0 collective-permute-done.7.rest_1_
  25.3 0.0 collective-permute-done.6.rest_0_
  25.3 1.6 %shard_map.121 = (f32[128,2048]{1,0:T(8,128)S(1)}, f32[256,2048]{1,0:T(8,128)S(1)}) custom-call(s32[4]{0:T(128)S(1)} %get-tuple-element.38.length_ref, bf16[4,128,2048]{2,1,0:T(8,128)(2,1)S(1)} %get-tuple-element.41.ss_ref, bf16[4,256,2048]{2,1,0:T(8,128)(2,1)S(1)} %get-tuple-element.49.us_ref, f32[128,2048]{1,0:T(8,128)S(1)} %get-tuple-element.57.sa_ref.order_ref, ...), custom_call_target="tpu_custom_call" | custom-call | tf_op jit(solution)/shard_map/pallas_call | solution.py:367
  26.9 0.2 collective-permute-done.10.mate_ref
  27.1 0.0 copy-start
  27.1 1.1 %shard_map.123 = (f32[128,2048]{1,0:T(8,128)S(1)}, f32[256,2048]{1,0:T(8,128)S(1)}, f32[8,128]{1,0:T(8,128)S(1)}) custom-call(bf16[128,4096]{1,0:T(8,128)(2,1)S(1)} %get-tuple-element.55.ss_ref, bf16[256,4096]{1,0:T(8,128)(2,1)S(1)} %get-tuple-element.56.us_ref, f32[128,2048]{1,0:T(8,128)S(1)} %get-tuple-element.59.sa_ref, ...), custom_call_target="tpu_custom_call" | custom-call | tf_op jit(solution)/shard_map/pallas_call | solution.py:391
  28.2 1.6 %collective-permute-start.11 = (f32[8,128]{1,0:T(8,128)S(1)}, f32[8,128]{1,0:T(8,128)S(1)}, u32[]{:S(2)}, u32[]{:S(2)}) collective-permute-start(f32[8,128]{1,0:T(8,128)S(1)} %get-tuple-element.63.rest_0_), channel_id=1, source_target_pairs={{0,1},{1,2},{2,3},{3,0},{4,5},{5,6},{6,7},{7,4},{8,9},{9,10},{10,1... | collective-permute-start | bytes 12296 | tf_op jit(solution)/shard_map/ppermute | solution.py:402
  29.9 2.6 %collective-permute-start.12 = (f32[8,128]{1,0:T(8,128)S(1)}, f32[8,128]{1,0:T(8,128)S(1)}, u32[]{:S(2)}, u32[]{:S(2)}) collective-permute-start(f32[8,128]{1,0:T(8,128)S(1)} %get-tuple-element.63.rest_0_), channel_id=1, source_target_pairs={{0,2},{1,3},{2,0},{3,1},{4,6},{5,7},{6,4},{7,5},{8,10},{9,11},{10,... | collective-permute-start | bytes 12296 | tf_op jit(solution)/shard_map/ppermute | solution.py:402
  32.4 1.3 %collective-permute-start.13 = (f32[8,128]{1,0:T(8,128)S(1)}, f32[8,128]{1,0:T(8,128)S(1)}, u32[]{:S(2)}, u32[]{:S(2)}) collective-permute-start(f32[8,128]{1,0:T(8,128)S(1)} %get-tuple-element.63.rest_0_), channel_id=1, source_target_pairs={{0,3},{1,0},{2,1},{3,2},{4,7},{5,4},{6,5},{7,6},{8,11},{9,8},{10,9... | collective-permute-start | bytes 12296 | tf_op jit(solution)/shard_map/ppermute | solution.py:402
  33.8 0.0 copy-done
  33.8 0.0 collective-permute-done.11.rest_1_
  33.8 0.6 %collective-permute-done.12.rest_2_ = f32[8,128]{1,0:T(8,128)S(1)} collective-permute-done((f32[8,128]{1,0:T(8,128)S(1)}, f32[8,128]{1,0:T(8,128)S(1)}, u32[]{:S(2)}, u32[]{:S(2)}) %collective-permute-start.12) | collective-permute-done | bytes 4128 | tf_op jit(solution)/shard_map/ppermute | solution.py:402
  34.4 1.7 %collective-permute-done.13.rest_3_ = f32[8,128]{1,0:T(8,128)S(1)} collective-permute-done((f32[8,128]{1,0:T(8,128)S(1)}, f32[8,128]{1,0:T(8,128)S(1)}, u32[]{:S(2)}, u32[]{:S(2)}) %collective-permute-start.13) | collective-permute-done | bytes 4128 | tf_op jit(solution)/shard_map/ppermute | solution.py:402
  36.1 1.5 %shard_map.124 = (bf16[128,2048]{1,0:T(8,128)(2,1)}, bf16[256,2048]{1,0:T(8,128)(2,1)}) custom-call(f32[128,2048]{1,0:T(8,128)S(1)} %get-tuple-element.61.st_ref, f32[256,2048]{1,0:T(8,128)S(1)} %get-tuple-element.62.ut_ref, bf16[1,2048]{1,0:T(2,128)(2,1)S(1)} %reshape.30.gain_ref, f32[8,128]{1,0:T(8,128)S(1)} %get-tuple-element.63.rest_0_, ...), custom_call_target="tpu_custom_call" | custom-call | tf_op jit(solution)/shard_map/pallas_call | solution.py:404
  (5 shorter events, 0.2 us)
Async XLA Ops:
  2.2 9.7 %collective-permute-start = (bf16[8,128,128]{2,1,0:T(8,128)(2,1)S(1)}, bf16[8,128,128]{2,1,0:T(8,128)(2,1)S(1)}, u32[]{:S(2)}, u32[]{:S(2)}) collective-permute-start(bf16[8,128,128]{2,1,0:T(8,128)(2,1)S(1)} %get-tuple-element.54.refs_6_), channel_id=1, source_target_pairs={{0,8},{4,20},{8,0},{12,28},{16,24},{20,4},{24,16},{28,12},{1,9},{5... | collective-permute-start | bytes 786440 | tf_op jit(solution)/shard_map/ppermute | solution.py:267
  5.2 7.3 %collective-permute-start.1 = (bf16[8,128,128]{2,1,0:T(8,128)(2,1)S(1)}, bf16[8,128,128]{2,1,0:T(8,128)(2,1)S(1)}, u32[]{:S(2)}, u32[]{:S(2)}) collective-permute-start(bf16[8,128,128]{2,1,0:T(8,128)(2,1)S(1)} %get-tuple-element.53.refs_7_), channel_id=1, source_target_pairs={{0,16},{4,12},{8,24},{12,4},{16,0},{20,28},{24,8},{28,20},{1,17},{... | collective-permute-start | bytes 786440 | tf_op jit(solution)/shard_map/ppermute | solution.py:267
  9.4 7.9 %collective-permute-start.5 = (bf16[8,128,128]{2,1,0:T(8,128)(2,1)S(1)}, bf16[8,128,128]{2,1,0:T(8,128)(2,1)S(1)}, u32[]{:S(2)}, u32[]{:S(2)}) collective-permute-start(bf16[8,128,128]{2,1,0:T(8,128)(2,1)S(1)} %get-tuple-element.54.refs_6_), channel_id=1, source_target_pairs={{0,16},{4,12},{8,24},{12,4},{16,0},{20,28},{24,8},{28,20},{1,17},{... | collective-permute-start | bytes 786440 | tf_op jit(solution)/shard_map/ppermute | solution.py:267
  9.9 11.3 %collective-permute-start.4 = (bf16[8,128,128]{2,1,0:T(8,128)(2,1)S(1)}, bf16[8,128,128]{2,1,0:T(8,128)(2,1)S(1)}, u32[]{:S(2)}, u32[]{:S(2)}) collective-permute-start(bf16[8,128,128]{2,1,0:T(8,128)(2,1)S(1)} %get-tuple-element.53.refs_7_), channel_id=1, source_target_pairs={{0,8},{4,20},{8,0},{12,28},{16,24},{20,4},{24,16},{28,12},{1,9},{5... | collective-permute-start | bytes 786440 | tf_op jit(solution)/shard_map/ppermute | solution.py:267
  10.0 11.3 %collective-permute-start.2 = (bf16[8,128,128]{2,1,0:T(8,128)(2,1)S(1)}, bf16[8,128,128]{2,1,0:T(8,128)(2,1)S(1)}, u32[]{:S(2)}, u32[]{:S(2)}) collective-permute-start(bf16[8,128,128]{2,1,0:T(8,128)(2,1)S(1)} %get-tuple-element.53.refs_7_), channel_id=1, source_target_pairs={{0,4},{4,0},{8,12},{12,8},{16,20},{20,16},{24,28},{28,24},{1,5},{5... | collective-permute-start | bytes 786440 | tf_op jit(solution)/shard_map/ppermute | solution.py:267
  12.0 10.0 %collective-permute-start.3 = (bf16[8,128,128]{2,1,0:T(8,128)(2,1)S(1)}, bf16[8,128,128]{2,1,0:T(8,128)(2,1)S(1)}, u32[]{:S(2)}, u32[]{:S(2)}) collective-permute-start(bf16[8,128,128]{2,1,0:T(8,128)(2,1)S(1)} %get-tuple-element.54.refs_6_), channel_id=1, source_target_pairs={{0,4},{4,0},{8,12},{12,8},{16,20},{20,16},{24,28},{28,24},{1,5},{5... | collective-permute-start | bytes 786440 | tf_op jit(solution)/shard_map/ppermute | solution.py:267
  12.5 12.6 %collective-permute-start.8 = (bf16[8,128,128]{2,1,0:T(8,128)(2,1)S(1)}, bf16[8,128,128]{2,1,0:T(8,128)(2,1)S(1)}, u32[]{:S(2)}, u32[]{:S(2)}) collective-permute-start(bf16[8,128,128]{2,1,0:T(8,128)(2,1)S(1)} %collective-permute-done.refs_0_), channel_id=1, source_target_pairs={{0,16},{4,12},{8,24},{12,4},{16,0},{20,28},{24,8},{28,20},{1,17},{... | collective-permute-start | bytes 786440 | tf_op jit(solution)/shard_map/ppermute | solution.py:267
  17.2 7.9 %collective-permute-start.9 = (bf16[8,128,128]{2,1,0:T(8,128)(2,1)S(1)}, bf16[8,128,128]{2,1,0:T(8,128)(2,1)S(1)}, u32[]{:S(2)}, u32[]{:S(2)}) collective-permute-start(bf16[8,128,128]{2,1,0:T(8,128)(2,1)S(1)} %collective-permute-done.1.refs_1_), channel_id=1, source_target_pairs={{0,8},{4,20},{8,0},{12,28},{16,24},{20,4},{24,16},{28,12},{1,9},{5... | collective-permute-start | bytes 786440 | tf_op jit(solution)/shard_map/ppermute | solution.py:267
  21.2 4.1 %collective-permute-start.7 = (bf16[1,16,128,128]{3,2,1,0:T(8,128)(2,1)S(1)}, bf16[1,16,128,128]{3,2,1,0:T(8,128)(2,1)S(1)}, u32[]{:S(2)}, u32[]{:S(2)}) collective-permute-start(bf16[1,16,128,128]{3,2,1,0:T(8,128)(2,1)S(1)} %shard_map.119.rest_3_), channel_id=1, source_target_pairs={{0,4},{4,0},{8,12},{12,8},{16,20},{20,16},{24,28},{28,24},{1,5},{5... | collective-permute-start | bytes 1572872 | tf_op jit(solution)/shard_map/ppermute | solution.py:267
  21.4 3.9 %collective-permute-start.6 = (bf16[1,16,128,128]{3,2,1,0:T(8,128)(2,1)S(1)}, bf16[1,16,128,128]{3,2,1,0:T(8,128)(2,1)S(1)}, u32[]{:S(2)}, u32[]{:S(2)}) collective-permute-start(bf16[1,16,128,128]{3,2,1,0:T(8,128)(2,1)S(1)} %shard_map.118.rest_2_), channel_id=1, source_target_pairs={{0,4},{4,0},{8,12},{12,8},{16,20},{20,16},{24,28},{28,24},{1,5},{5... | collective-permute-start | bytes 1572872 | tf_op jit(solution)/shard_map/ppermute | solution.py:267
  25.2 2.0 %collective-permute-start.10 = (bf16[1,16,128,128]{3,2,1,0:T(8,128)(2,1)S(1)}, bf16[1,16,128,128]{3,2,1,0:T(8,128)(2,1)S(1)}, u32[]{:S(2)}, u32[]{:S(2)}) collective-permute-start(bf16[1,16,128,128]{3,2,1,0:T(8,128)(2,1)S(1)} %shard_map.122.state_ref), channel_id=1, source_target_pairs={{0,4},{4,0},{8,12},{12,8},{16,20},{20,16},{24,28},{28,24},{1,5},{5... | collective-permute-start | bytes 1572872 | tf_op jit(solution)/shard_map/ppermute | solution.py:267
  27.1 6.7 %copy-start = (bf16[2048]{0:T(1024)(128)(2,1)S(1)}, bf16[2048]{0:T(1024)(128)(2,1)}, u32[]{:S(2)}) copy-start(bf16[2048]{0:T(1024)(128)(2,1)} %param.14) | copy-start | bytes 12292
  28.2 5.6 %collective-permute-start.11 = (f32[8,128]{1,0:T(8,128)S(1)}, f32[8,128]{1,0:T(8,128)S(1)}, u32[]{:S(2)}, u32[]{:S(2)}) collective-permute-start(f32[8,128]{1,0:T(8,128)S(1)} %get-tuple-element.63.rest_0_), channel_id=1, source_target_pairs={{0,1},{1,2},{2,3},{3,0},{4,5},{5,6},{6,7},{7,4},{8,9},{9,10},{10,1... | collective-permute-start | bytes 12296 | tf_op jit(solution)/shard_map/ppermute | solution.py:402
  29.9 4.5 %collective-permute-start.12 = (f32[8,128]{1,0:T(8,128)S(1)}, f32[8,128]{1,0:T(8,128)S(1)}, u32[]{:S(2)}, u32[]{:S(2)}) collective-permute-start(f32[8,128]{1,0:T(8,128)S(1)} %get-tuple-element.63.rest_0_), channel_id=1, source_target_pairs={{0,2},{1,3},{2,0},{3,1},{4,6},{5,7},{6,4},{7,5},{8,10},{9,11},{10,... | collective-permute-start | bytes 12296 | tf_op jit(solution)/shard_map/ppermute | solution.py:402
  32.4 3.6 %collective-permute-start.13 = (f32[8,128]{1,0:T(8,128)S(1)}, f32[8,128]{1,0:T(8,128)S(1)}, u32[]{:S(2)}, u32[]{:S(2)}) collective-permute-start(f32[8,128]{1,0:T(8,128)S(1)} %get-tuple-element.63.rest_0_), channel_id=1, source_target_pairs={{0,3},{1,0},{2,1},{3,2},{4,7},{5,4},{6,5},{7,6},{8,11},{9,8},{10,9... | collective-permute-start | bytes 12296 | tf_op jit(solution)/shard_map/ppermute | solution.py:402
